TPU v7x, 32 devices: a whole 2x2x4 slice. The times are simulated.
32 devices in a mesh: row: 8 (over y, x, core), col: 4 (over z).
Axes of the slice: x: 2, y: 2, z: 4, core: 2. Of those that a mesh axis runs over, the one named last changes fastest.
Arguments:
- streams: bfloat16 [4, 8192, 2048], P(None, 'row', 'col')
- segments: int32 [8, 1024], P('row'), may hold values from 0 to 7, never falling along the last dimension, each value on 1 to 512 neighbouring positions
- attention_in: float32 [3, 2048, 2048], P(None, 'row', 'col'), may hold values from -0.125 to 0.125
- attention_out: float32 [2048, 2048], P('col', 'row'), may hold values from -0.75 to 0.75
- gate_up: float32 [2, 2048, 8192], P(None, 'row', 'col'), may hold values from -0.125 to 0.125
- down_weights: float32 [8192, 2048], P('col', 'row'), may hold values from -0.0625 to 0.0625
- hyper_mix: float32 [2, 4, 6], replicated
- moment_attention_in: float32 [3, 2048, 2048], P(None, 'row', 'col'), may hold values from -160 to 160
- moment_attention_out: float32 [2048, 2048], P('col', 'row'), may hold values from -160 to 160
- moment_gate_up: float32 [2, 2048, 8192], P(None, 'row', 'col'), may hold values from -160 to 160
- moment_down_weights: float32 [8192, 2048], P('col', 'row'), may hold values from -160 to 160
- moment_hyper_mix: float32 [2, 4, 6], replicated, may hold values from -12288 to 12288
- average_attention_in: float32 [3, 2048, 2048], P(None, 'row', 'col'), may hold values from -0.125 to 0.125
- average_attention_out: float32 [2048, 2048], P('col', 'row'), may hold values from -0.75 to 0.75
- average_gate_up: float32 [2, 2048, 8192], P(None, 'row', 'col'), may hold values from -0.125 to 0.125
- average_down_weights: float32 [8192, 2048], P('col', 'row'), may hold values from -0.0625 to 0.0625
- average_hyper_mix: float32 [2, 4, 6], replicated, may hold values from -3 to 3
- cotangent: bfloat16 [4, 8192, 2048], P(None, 'row', 'col')
Outputs:
- out_streams: bfloat16 [4, 8192, 2048], P(None, 'row', 'col')
- grad_streams: float32 [4, 8192, 2048], P(None, 'row', 'col')
- new_attention_in: float32 [3, 2048, 2048], P(None, 'row', 'col')
- new_moment_attention_in: float32 [3, 2048, 2048], P(None, 'row', 'col')
- new_average_attention_in: float32 [3, 2048, 2048], P(None, 'row', 'col')
- new_attention_out: float32 [2048, 2048], P('col', 'row')
- new_moment_attention_out: float32 [2048, 2048], P('col', 'row')
- new_average_attention_out: float32 [2048, 2048], P('col', 'row')
- new_gate_up: float32 [2, 2048, 8192], P(None, 'row', 'col')
- new_moment_gate_up: float32 [2, 2048, 8192], P(None, 'row', 'col')
- new_average_gate_up: float32 [2, 2048, 8192], P(None, 'row', 'col')
- new_down_weights: float32 [8192, 2048], P('col', 'row')
- new_moment_down_weights: float32 [8192, 2048], P('col', 'row')
- new_average_down_weights: float32 [8192, 2048], P('col', 'row')
- new_hyper_mix: float32 [2, 4, 6], replicated
- new_moment_hyper_mix: float32 [2, 4, 6], replicated
- new_average_hyper_mix: float32 [2, 4, 6], replicated
Inputs may be any that keep to these rules, and one draw needn't show every extreme that they name: `segments`: row s holds the document numbers of sequence s: 8 documents numbered 0 to 7 in order, each 1 to 512 tokens long, one of them exactly 512.
All inputs are finite; a program needn't handle non-finite values.
Results may differ from a plain program's by a relative error of at most 0.019.
Values may be sent and summed in bfloat16 or wider, within the bound.
A program may use at most 208 MiB of HBM per device.

v0:
```python
import jax
import jax.numpy as jnp
from jax import lax
from jax.sharding import PartitionSpec as P

D = 2048
HEAD_DIM = 128
FF = 8192
STEP = 8


HIGH = lax.Precision.HIGHEST
EPSILON = 1e-05
MASKED = -1e30
MOMENTUM = 0.9
DECAY = 0.01


def rope_tables(segments):
    length = segments.shape[-1]
    index = jnp.arange(length, dtype=jnp.int32)
    before = jnp.concatenate(
        [jnp.full(segments.shape[:-1] + (1,), -1, jnp.int32), segments[..., :-1]], -1
    )
    starts = jnp.where(segments != before, index, 0)
    places = index - lax.cummax(starts, axis=segments.ndim - 1)
    rates = 10000.0 ** (-2.0 * jnp.arange(HEAD_DIM // 2).astype(jnp.float32) / HEAD_DIM)
    angle = places[..., None].astype(jnp.float32) * rates
    angle = jnp.concatenate([angle, angle], -1)[..., None, :]
    return (jnp.cos(angle), jnp.sin(angle))


def rotate(values, cosine, sine):
    half = values.shape[-1] // 2
    turned = jnp.concatenate([-values[..., half:], values[..., :half]], -1)
    return values * cosine + turned * sine


def unrotate(values, cosine, sine):
    scaled = values * sine
    half = values.shape[-1] // 2
    return values * cosine + jnp.concatenate([scaled[..., half:], -scaled[..., :half]], -1)


def mix_in(streams, coeffs):
    return jnp.einsum("s,std->td", coeffs, streams, precision=HIGH)


def mix_out(streams, coeffs, branch):
    count = coeffs.shape[0]
    mixed = jnp.einsum("ij,itd->jtd", coeffs[:, 1 : 1 + count], streams, precision=HIGH)
    return mixed + coeffs[:, 1 + count][:, None, None] * branch[None]


def mix_back(coeffs, grad_after, grad_mixed):
    count = coeffs.shape[0]
    spread = jnp.einsum("ij,jtd->itd", coeffs[:, 1 : 1 + count], grad_after, precision=HIGH)
    return spread + coeffs[:, 0][:, None, None] * grad_mixed[None]


def mixing_grads(before, grad_mixed, grad_after, branch):
    into = jnp.sum(before * grad_mixed[None], (1, 2))
    across = jnp.einsum("itd,jtd->ij", before, grad_after, precision=HIGH)
    outward = jnp.sum(grad_after * branch[None], (1, 2))
    return jnp.concatenate([into[:, None], across, outward[:, None]], 1)


def normalize_gather(mixed):
    sums, squares = lax.psum((jnp.sum(mixed, -1), jnp.sum(mixed * mixed, -1)), "col")
    center = sums / D
    spread = squares / D - center * center
    scale = lax.rsqrt(spread + EPSILON)
    normal = (mixed - center[:, None]) * scale[:, None]
    whole = lax.all_gather(normal.astype(jnp.bfloat16), "col", axis=1, tiled=True)
    return (normal, scale, whole)


def norm_backward(grad_normal, normal, scale):
    sums, products = lax.psum((jnp.sum(grad_normal, -1), jnp.sum(grad_normal * normal, -1)), "col")
    inner = grad_normal - sums[:, None] / D - normal * (products[:, None] / D)
    return scale[:, None] * inner


def project_in(whole, weights):
    return jnp.einsum(
        "tn,knw->ktw",
        whole,
        lax.all_gather(weights, "row", axis=1, tiled=True),
        preferred_element_type=jnp.float32,
    )


def project_out(active, weights):
    partial_value = jnp.dot(
        active,
        lax.all_gather(weights, "row", axis=1, tiled=True),
        preferred_element_type=jnp.float32,
    )
    return lax.psum_scatter(partial_value, "col", scatter_dimension=1, tiled=True)


def back_out(grad_branch, active, weights):
    whole = lax.all_gather(grad_branch.astype(jnp.bfloat16), "col", axis=1, tiled=True)
    weight_grad = lax.psum_scatter(
        jnp.einsum("tw,td->wd", active, whole, preferred_element_type=jnp.float32).astype(
            jnp.bfloat16
        ),
        "row",
        scatter_dimension=1,
        tiled=True,
    ).astype(jnp.float32)
    grad_active = jnp.einsum(
        "tn,wn->tw",
        whole,
        lax.all_gather(weights, "row", axis=1, tiled=True),
        preferred_element_type=jnp.float32,
    )
    return (grad_active, weight_grad)


def back_in(grads, whole, weights):
    weight_grad = lax.psum_scatter(
        jnp.einsum("td,ktw->kdw", whole, grads, preferred_element_type=jnp.float32).astype(
            jnp.bfloat16
        ),
        "row",
        scatter_dimension=1,
        tiled=True,
    ).astype(jnp.float32)

    def rows(piece, start):
        return jnp.einsum("ktw,knw->tn", grads, piece, preferred_element_type=jnp.float32)

    partial_value = rows(lax.all_gather(weights, "row", axis=1, tiled=True), jnp.int32(0))
    grad_normal = lax.psum_scatter(
        partial_value.astype(jnp.bfloat16), "col", scatter_dimension=1, tiled=True
    ).astype(jnp.float32)
    return (grad_normal, weight_grad)


def block_scores(queries, key_heads, segment_row, start, block):
    length = key_heads.shape[0]
    index = jnp.arange(length)
    rows = lax.dynamic_slice_in_dim(index, start, block)
    own_docs = lax.dynamic_slice_in_dim(segment_row, start, block)
    allowed = (own_docs[:, None] == segment_row[None, :]) & (index[None, :] <= rows[:, None])
    part = lax.dynamic_slice_in_dim(queries, start, block, 0)
    raw = jnp.einsum("qhe,khe->hqk", part, key_heads, preferred_element_type=jnp.float32)
    raw = raw * queries.shape[-1] ** (-0.5)
    return (jnp.where(allowed[None], raw, MASKED), part)


def attend_forward(queries, key_heads, value_heads, segment_row):
    length = queries.shape[0]
    block = min(512, length)
    starts = jnp.arange(length // block) * block

    def one_block(start):
        scores, part = block_scores(queries, key_heads, segment_row, start, block)
        top = jnp.max(scores, -1, keepdims=True)
        expo = jnp.exp(scores - top)
        total = jnp.sum(expo, -1, keepdims=True)
        probs = (expo / total).astype(jnp.bfloat16)
        result = jnp.einsum("hqk,khe->qhe", probs, value_heads, preferred_element_type=jnp.float32)
        return (result, (top + jnp.log(total))[..., 0])

    results, log_totals = lax.map(one_block, starts)
    return (results.reshape(length, -1), log_totals)


def attend_back(queries, key_heads, value_heads, segment_row, log_totals, grad_result):
    length = queries.shape[0]
    block = min(512, length)
    starts = jnp.arange(length // block) * block
    factor = queries.shape[-1] ** (-0.5)

    def one_block(carry, packed):
        start, log_total = packed
        scores, part = block_scores(queries, key_heads, segment_row, start, block)
        probs = jnp.exp(scores - log_total[..., None])
        grad_part = lax.dynamic_slice_in_dim(grad_result, start, block, 0)
        grad_probs = jnp.einsum(
            "qhe,khe->hqk", grad_part, value_heads, preferred_element_type=jnp.float32
        )
        row_sum = jnp.sum(probs * grad_probs, -1, keepdims=True)
        grad_scores = (probs * (grad_probs - row_sum)).astype(jnp.bfloat16)
        grad_query = (
            jnp.einsum("hqk,khe->qhe", grad_scores, key_heads, preferred_element_type=jnp.float32)
            * factor
        )
        grad_keys = (
            carry[0]
            + jnp.einsum("hqk,qhe->khe", grad_scores, part, preferred_element_type=jnp.float32)
            * factor
        )
        grad_values = carry[1] + jnp.einsum(
            "hqk,qhe->khe",
            probs.astype(jnp.bfloat16),
            grad_part,
            preferred_element_type=jnp.float32,
        )
        return ((grad_keys, grad_values), grad_query)

    zeros = jnp.zeros(key_heads.shape, jnp.float32)
    (grad_keys, grad_values), grad_queries = lax.scan(
        one_block, (zeros, zeros), (starts, log_totals)
    )
    return (grad_queries.reshape(queries.shape), grad_keys, grad_values)


def forward(stream_values, hyper_mix, lowered, cosine, sine, segment_row):
    projections, output_rows, gate_rows, down_rows = lowered
    normal_one, scale_one, whole_one = normalize_gather(mix_in(stream_values, hyper_mix[0, :, 0]))
    projected = project_in(whole_one, projections)
    length = stream_values.shape[1]
    shape = (length, projected.shape[2] // HEAD_DIM, HEAD_DIM)
    queries = rotate(projected[0].reshape(shape), cosine, sine).astype(jnp.bfloat16)
    key_heads = rotate(projected[1].reshape(shape), cosine, sine).astype(jnp.bfloat16)
    value_heads = projected[2].reshape(shape).astype(jnp.bfloat16)
    attended, log_totals = attend_forward(queries, key_heads, value_heads, segment_row)
    attended = attended.astype(jnp.bfloat16)
    branch = project_out(attended, output_rows)
    middle = mix_out(stream_values, hyper_mix[0], branch)
    normal_two, scale_two, whole_two = normalize_gather(mix_in(middle, hyper_mix[1, :, 0]))
    gated = project_in(whole_two, gate_rows)
    active = (jax.nn.silu(gated[0]) * gated[1]).astype(jnp.bfloat16)
    branch_two = project_out(active, down_rows)
    final = mix_out(middle, hyper_mix[1], branch_two)
    kept = {
        "normal_one": normal_one,
        "scale_one": scale_one,
        "whole_one": whole_one,
        "queries": queries,
        "key_heads": key_heads,
        "value_heads": value_heads,
        "log_totals": log_totals,
        "attended": attended,
        "branch": branch,
        "middle": middle,
        "normal_two": normal_two,
        "scale_two": scale_two,
        "whole_two": whole_two,
        "gated": gated,
        "active": active,
        "branch_two": branch_two,
    }
    return (final, kept)


def update(weight, grad, moment, average, rate):
    step_grad = grad + DECAY * weight
    moment_new = MOMENTUM * moment + step_grad
    weight_new = weight - rate * (step_grad + MOMENTUM * moment_new)
    return (weight_new, moment_new, average + (weight_new - average) / (STEP + 1))


def per_device(
    streams,
    segments,
    attention_in,
    attention_out,
    gate_up,
    down_weights,
    hyper_mix,
    moment_attention_in,
    moment_attention_out,
    moment_gate_up,
    moment_down_weights,
    moment_hyper_mix,
    average_attention_in,
    average_attention_out,
    average_gate_up,
    average_down_weights,
    average_hyper_mix,
    cotangent,
):
    stream_values = streams.astype(jnp.float32)
    cosine, sine = rope_tables(segments)
    cosine = cosine[0]
    sine = sine[0]
    segment_row = segments[0]
    lowered = (
        attention_in.astype(jnp.bfloat16),
        attention_out.astype(jnp.bfloat16),
        gate_up.astype(jnp.bfloat16),
        down_weights.astype(jnp.bfloat16),
    )
    projections, output_rows, gate_rows, down_rows = lowered
    final, kept = forward(stream_values, hyper_mix, lowered, cosine, sine, segment_row)
    kept = forward(stream_values, hyper_mix, lowered, cosine, sine, segment_row)[1]
    count = hyper_mix.shape[1]
    mix_one = hyper_mix[0]
    mix_two = hyper_mix[1]
    grad_final = cotangent.astype(jnp.float32)
    grad_branch_two = jnp.einsum("j,jtd->td", mix_two[:, 1 + count], grad_final, precision=HIGH)
    grad_active, grad_down = back_out(grad_branch_two, kept["active"], down_rows)
    gate = kept["gated"][0]
    upper = kept["gated"][1]
    sigma = jax.nn.sigmoid(gate)
    grad_gate = grad_active * upper * sigma * (1.0 + gate * (1.0 - sigma))
    grad_upper = grad_active * gate * sigma
    grad_normal_two, grad_gate_up = back_in(
        jnp.stack([grad_gate, grad_upper]).astype(jnp.bfloat16), kept["whole_two"], gate_rows
    )
    grad_mixed_two = norm_backward(grad_normal_two, kept["normal_two"], kept["scale_two"])
    grad_middle = mix_back(mix_two, grad_final, grad_mixed_two)
    hyper_two = mixing_grads(kept["middle"], grad_mixed_two, grad_final, kept["branch_two"])
    grad_branch = jnp.einsum("j,jtd->td", mix_one[:, 1 + count], grad_middle, precision=HIGH)
    grad_attended, grad_output = back_out(grad_branch, kept["attended"], output_rows)
    shape = kept["queries"].shape
    length = shape[0]
    grad_attended = grad_attended.astype(jnp.bfloat16).reshape(shape)
    grad_queries, grad_keys, grad_values = attend_back(
        kept["queries"],
        kept["key_heads"],
        kept["value_heads"],
        segment_row,
        kept["log_totals"],
        grad_attended,
    )
    grad_heads = jnp.stack(
        [
            unrotate(grad_queries, cosine, sine).reshape(length, -1),
            unrotate(grad_keys, cosine, sine).reshape(length, -1),
            grad_values.reshape(length, -1),
        ]
    ).astype(jnp.bfloat16)
    grad_normal_one, grad_projections = back_in(grad_heads, kept["whole_one"], projections)
    grad_mixed_one = norm_backward(grad_normal_one, kept["normal_one"], kept["scale_one"])
    grad_streams = mix_back(mix_one, grad_middle, grad_mixed_one)
    hyper_one = mixing_grads(stream_values, grad_mixed_one, grad_middle, kept["branch"])
    grad_hyper = lax.psum(jnp.stack([hyper_one, hyper_two]), ("row", "col"))
    tokens_all = streams.shape[1] * lax.axis_size("row")
    token_scale = tokens_all ** (-0.5)
    model_rate = D ** (-0.5) * token_scale
    first = update(
        attention_in, grad_projections, moment_attention_in, average_attention_in, model_rate
    )
    second = update(
        attention_out, grad_output, moment_attention_out, average_attention_out, model_rate
    )
    third = update(gate_up, grad_gate_up, moment_gate_up, average_gate_up, model_rate)
    fourth = update(
        down_weights,
        grad_down,
        moment_down_weights,
        average_down_weights,
        FF ** (-0.5) * token_scale,
    )
    fifth = update(
        hyper_mix,
        grad_hyper,
        moment_hyper_mix,
        average_hyper_mix,
        0.05 * (tokens_all * D) ** (-0.5),
    )
    return (
        final.astype(jnp.bfloat16),
        grad_streams,
        first[0],
        first[1],
        first[2],
        second[0],
        second[1],
        second[2],
        third[0],
        third[1],
        third[2],
        fourth[0],
        fourth[1],
        fourth[2],
        fifth[0],
        fifth[1],
        fifth[2],
    )


def solution(mesh):
    in_specs = (
        P(None, "row", "col"),
        P("row", None),
        P(None, "row", "col"),
        P("col", "row"),
        P(None, "row", "col"),
        P("col", "row"),
        P(),
        P(None, "row", "col"),
        P("col", "row"),
        P(None, "row", "col"),
        P("col", "row"),
        P(),
        P(None, "row", "col"),
        P("col", "row"),
        P(None, "row", "col"),
        P("col", "row"),
        P(),
        P(None, "row", "col"),
    )
    out_specs = (
        P(None, "row", "col"),
        P(None, "row", "col"),
        P(None, "row", "col"),
        P(None, "row", "col"),
        P(None, "row", "col"),
        P("col", "row"),
        P("col", "row"),
        P("col", "row"),
        P(None, "row", "col"),
        P(None, "row", "col"),
        P(None, "row", "col"),
        P("col", "row"),
        P("col", "row"),
        P("col", "row"),
        P(),
        P(),
        P(),
    )
    return jax.shard_map(
        per_device, mesh=mesh, in_specs=in_specs, out_specs=out_specs, check_vma=False
    )
```

profile of v0, /device:TPU:0, one launch (start us, length us, event | category | flops | bytes accessed | tf_op | source)
XLA Modules:
  0.0 1899.3 jit_solution(6364101342961397694)
XLA Ops:
  47.2 67.2 %all-gather.10.cloned.1.call-done = bf16[1024,2048]{1,0:T(8,128)(2,1)} async-done(((bf16[1024,512]{1,0:T(8,128)(2,1)}), bf16[1024,2048]{1,0:T(8,128)(2,1)}) %all-gather.10.cloned.1.call-update) | async-done | bytes 4194320 | tf_op jit(solution)/shard_map/all_gather | solution.py:74
  114.4 47.7 %all-gather.12.cloned.1.call-done = bf16[3,2048,512]{1,2,0:T(8,128)(2,1)} async-done(((bf16[3,256,512]{1,2,0:T(8,128)(2,1)}), bf16[3,2048,512]{1,2,0:T(8,128)(2,1)}) %all-gather.12.cloned.1.call-update) | async-done | bytes 6291472 | tf_op jit(solution)/shard_map/all_gather | solution.py:88
  189.6 22.5 %while.41 = (s32[]{:T(128)}, bf16[2,512,4,128]{3,1,2,0:T(8,128)(2,1)}, f32[2,4,512]{2,1,0:T(4,128)S(1)}, s32[2]{0:T(128)S(1)}, s32[1024]{0:T(1024)S(1)}, /*index...) while((s32[]{:T(128)}, ...), condition=%wide.region_19.20_spmd.clone, body=%wide.region_16.19_spmd.sunk.clone | while | flops 1100478464 | bytes 31019676 | solution.py:167
  242.6 125.9 %reduce-scatter.15.cloned.1.call-done = f32[1024,512]{1,0:T(8,128)} async-done(((f32[1024,2048]{1,0:T(8,128)}), f32[1024,512]{1,0:T(8,128)}) %reduce-scatter.15.cloned.1.call-update) | async-done | bytes 2097168 | tf_op jit(solution)/shard_map/reduce_scatter | solution.py:99
  416.9 44.5 %all-gather.18.cloned.1.call-done = bf16[2,2048,2048]{2,1,0:T(8,128)(2,1)} async-done(((bf16[2,256,2048]{2,1,0:T(8,128)(2,1)}), bf16[2,2048,2048]{2,1,0:T(8,128)(2,1)}) %all-gather.18.cloned.1.call-update) | async-done | bytes 16777232 | tf_op jit(solution)/shard_map/all_gather | solution.py:88
  461.4 82.8 %all-gather.24.cloned.1.call-done = bf16[1024,2048]{1,0:T(8,128)(2,1)} async-done(((bf16[1024,512]{1,0:T(8,128)(2,1)}), bf16[1024,2048]{1,0:T(8,128)(2,1)}) %all-gather.24.cloned.1.call-update) | async-done | bytes 4194320 | tf_op jit(solution)/shard_map/all_gather | solution.py:74
  544.2 23.4 %convolution_bitcast_fusion = f32[2,1024,2048]{2,1,0:T(8,128)} fusion(bf16[2,2048,2048]{2,1,0:T(8,128)(2,1)} %all-gather.18.cloned.1.call-done, bf16[1024,2048]{1,0:T(8,128)(2,1)} %all-gather.24.cloned.1.call-done), kind=kOutput, calls=%fused_computation.91 | convolution fusion | flops 17179869184 | bytes 37748736 | tf_op jit(solution)/shard_map/tn,knw->ktw/dot_general | solution.py:85
  567.7 58.0 %all-gather.22.cloned.1.call-done = bf16[1024,2048]{1,0:T(8,128)(2,1)} async-done(((bf16[1024,512]{1,0:T(8,128)(2,1)}), bf16[1024,2048]{1,0:T(8,128)(2,1)}) %all-gather.22.cloned.1.call-update) | async-done | bytes 4194320 | tf_op jit(solution)/shard_map/all_gather | solution.py:103
  625.7 57.0 %all-gather.20.cloned.1.call-done = bf16[2048,2048]{1,0:T(8,128)(2,1)} async-done(((bf16[2048,256]{1,0:T(8,128)(2,1)}), bf16[2048,2048]{1,0:T(8,128)(2,1)}) %all-gather.20.cloned.1.call-update) | async-done | bytes 8388624 | tf_op jit(solution)/shard_map/all_gather | solution.py:96
  704.5 23.8 %bitcast_convert_fusion.1 = bf16[1024,2048]{1,0:T(8,128)(2,1)} fusion(bf16[2,2048,2048]{2,1,0:T(8,128)(2,1)} %all-gather.18.cloned.1.call-done, bf16[1,1024,2048]{2,1,0:T(8,128)(2,1)} %get-tuple-element.414, bf16[1,1024,2048]{2,1,0:T(8,128)(2,1)} %get-tuple-element.413), kind=kOutput, calls=%fused_computation.76 | convolution fusion | flops 17186160640 | bytes 29360128 | tf_op jit(solution)/shard_map/ktw,knw->tn/dot_general | solution.py:132
  728.5 76.7 %reduce-scatter.17.cloned.1.call-done = bf16[1024,512]{1,0:T(8,128)(2,1)} async-done(((bf16[1024,2048]{1,0:T(8,128)(2,1)}), bf16[1024,512]{1,0:T(8,128)(2,1)}) %reduce-scatter.17.cloned.1.call-update) | async-done | bytes 1048592 | tf_op jit(solution)/shard_map/reduce_scatter | solution.py:135
  861.1 32.1 %while.40 = (s32[]{:T(128)}, bf16[2,512,4,128]{3,1,2,0:T(8,128)(2,1)}, s32[2]{0:T(128)S(1)}, s32[1024]{0:T(1024)S(1)}, s32[1,1024]{1,0:T(1,128)S(1)}, /*index=5*...) while((s32[]{:T(128)}, ...), condition=%wide.region_9.10_spmd.clone, body=%wide.region_6.9_spmd.sunk.clone | while | flops 1087898624 | bytes 21533328 | solution.py:167
  909.0 30.5 %all-gather.26.cloned.1.call-done = bf16[1024,2048]{1,0:T(8,128)(2,1)} async-done(((bf16[1024,512]{1,0:T(8,128)(2,1)}), bf16[1024,2048]{1,0:T(8,128)(2,1)}) %all-gather.26.cloned.1.call-update) | async-done | bytes 4194320 | tf_op jit(solution)/shard_map/all_gather | solution.py:103
  945.7 49.9 %while.42 = (s32[]{:T(128)}, f32[1024,4,128]{0,2,1:T(8,128)S(1)}, f32[1024,4,128]{0,2,1:T(8,128)}, f32[2,512,4,128]{3,1,2,0:T(8,128)}, s32[2]{0:T(128)S(1)}, /*i...) while((s32[]{:T(128)}, f32[1024,4,128]{0,2,1:T(8,128)S(1)}, ...), condition=%wide.region_32.33_spmd.clone.clone, body=%wide.region_30.32_spmd.clone.sunk.clone | while | flops 2720266240 | bytes 180433872 | solution.py:205
  1037.7 47.8 %reduce-scatter.11.cloned.1.call-done = f32[1024,512]{1,0:T(8,128)} async-done(((f32[1024,2048]{1,0:T(8,128)}), f32[1024,512]{1,0:T(8,128)}) %reduce-scatter.11.cloned.1.call-update) | async-done | bytes 2097168 | tf_op jit(solution)/shard_map/reduce_scatter | solution.py:99
  1106.9 59.0 %reduce-scatter.19.cloned.1.call-done = bf16[1024,512]{1,0:T(8,128)(2,1)} async-done(((bf16[1024,2048]{1,0:T(8,128)(2,1)}), bf16[1024,512]{1,0:T(8,128)(2,1)}) %reduce-scatter.19.cloned.1.call-update) | async-done | bytes 1048592 | tf_op jit(solution)/shard_map/reduce_scatter | solution.py:135
  1237.2 24.7 %convert_bitcast_fusion = bf16[2,2048,2048]{1,2,0:T(8,128)(2,1)} fusion(bf16[1,1024,2048]{2,1,0:T(8,128)(2,1)} %get-tuple-element.414, bf16[1,1024,2048]{2,1,0:T(8,128)(2,1)} %get-tuple-element.413, bf16[1024,2048]{1,0:T(8,128)(2,1)} %all-gather.24.cloned.1.call-done), kind=kOutput, calls=%fused_computation.66 | convolution fusion | flops 17192452096 | bytes 29360128 | tf_op jit(solution)/shard_map/td,ktw->kdw/dot_general | solution.py:123
  1326.9 24.4 %fusion.121 = f32[4,4]{1,0:T(4,128)S(1)} fusion(bf16[4,1024,512]{2,1,0:T(8,128)(2,1)} %param.41, f32[4,1024,512]{2,0,1:T(4,128)} %fusion.116, f32[1024,512]{1,0:T(8,128)S(1)} %copy-done.33, f32[4]{0:T(128)S(1)} %copy-done.58), kind=kOutput, calls=%fused_computation.191 | convolution fusion | flops 104857600 | bytes 14680144 | tf_op jit(solution)/shard_map/itd,jtd->ij/dot_general | solution.py:63
  1351.5 22.8 %fusion.118 = f32[4,4]{1,0:T(4,128)S(1)} fusion(f32[4,1024,512]{2,0,1:T(4,128)} %get-tuple-element.444, bf16[4,1024,512]{2,1,0:T(8,128)(2,1)} %param.24), kind=kOutput, calls=%fused_computation.190 | convolution fusion | flops 100663296 | bytes 12582976 | tf_op jit(solution)/shard_map/itd,jtd->ij/dot_general | solution.py:63
  1380.3 109.2 %reduce-scatter.29.cloned.1.call-done = f32[1024,512]{1,0:T(8,128)} async-done(((f32[1024,2048]{1,0:T(8,128)}), f32[1024,512]{1,0:T(8,128)}) %reduce-scatter.29.cloned.1.call-update) | async-done | bytes 2097168 | tf_op jit(solution)/shard_map/reduce_scatter | solution.py:99
  1493.8 41.8 %reduce-scatter.23.cloned.1.call-done = bf16[512,256]{1,0:T(8,128)(2,1)} async-done(((bf16[512,2048]{1,0:T(8,128)(2,1)}), bf16[512,256]{1,0:T(8,128)(2,1)}) %reduce-scatter.23.cloned.1.call-update) | async-done | bytes 262160 | tf_op jit(solution)/shard_map/reduce_scatter | solution.py:104
  1581.0 39.7 %psum.93 = f32[2,4,6]{2,1,0:T(4,128)S(1)} all-reduce(f32[2,4,6]{2,1,0:T(4,128)S(1)} %pad_maximum_fusion.10), channel_id=1, replica_groups=mesh['row'=8,'col'=4] {'row','col'}, use_global_device_ids=true, to_apply=%region_47.48 | all-reduce | flops 48 | bytes 384 | tf_op jit(solution)/shard_map/psum | solution.py:332
  1633.2 87.4 %reduce-scatter.25.cloned.1.call-done = bf16[2,256,2048]{1,2,0:T(8,128)(2,1)} async-done(((bf16[2,2048,2048]{1,2,0:T(8,128)(2,1)}), bf16[2,256,2048]{1,2,0:T(8,128)(2,1)}) %reduce-scatter.25.cloned.1.call-update) | async-done | bytes 2097168 | tf_op jit(solution)/shard_map/reduce_scatter | solution.py:122
  1746.7 120.9 %reduce-scatter.13.cloned.1.call-done = f32[1024,512]{1,0:T(8,128)} async-done(((f32[1024,2048]{1,0:T(8,128)}), f32[1024,512]{1,0:T(8,128)}) %reduce-scatter.13.cloned.1.call-update) | async-done | bytes 2097168 | tf_op jit(solution)/shard_map/reduce_scatter | solution.py:99
  (386 shorter events, 656.8 us)
Async XLA Ops:
  7.2 107.2 %all-gather.10.cloned.1.call-start = ((), (), s32[]{:S(2)}) async-start(), calls=%async_computation.10 | async-start | bytes 5242880 | tf_op jit(solution)/shard_map/all_gather | solution.py:74
  8.1 360.4 %copy-start.61 = (f32[4]{0:T(128)}, f32[4]{0:T(128)S(1)}, u32[]{:S(2)}) copy-start(f32[4]{0:T(128)S(1)} %get-tuple-element.320) | copy-start | bytes 52
  35.2 126.8 %all-gather.12.cloned.1.call-start = ((), (), s32[]{:S(2)}) async-start(), calls=%async_computation.11 | async-start | bytes 7077888 | tf_op jit(solution)/shard_map/all_gather | solution.py:88
  40.7 175.2 %all-gather.14.cloned.1.call-start = ((), (), s32[]{:S(2)}) async-start(), calls=%async_computation.12 | async-start | bytes 2359296 | tf_op jit(solution)/shard_map/all_gather | solution.py:96
  41.6 326.9 %reduce-scatter.15.cloned.1.call-start = ((), (), s32[]{:S(2)}) async-start(), calls=%async_computation.18 | async-start | bytes 10485760 | tf_op jit(solution)/shard_map/reduce_scatter | solution.py:99
  223.7 237.8 %all-gather.18.cloned.1.call-start = ((), (), s32[]{:S(2)}) async-start(), calls=%async_computation.15 | async-start | bytes 18874368 | tf_op jit(solution)/shard_map/all_gather | solution.py:88
  227.6 316.6 %all-gather.24.cloned.1.call-start = ((), (), s32[]{:S(2)}) async-start(), calls=%async_computation.20 | async-start | bytes 5242880 | tf_op jit(solution)/shard_map/all_gather | solution.py:74
  227.7 594.1 %copy-start.59 = (f32[4,6]{1,0:T(4,128)}, f32[4,6]{1,0:T(4,128)S(1)}, u32[]{:S(2)}) copy-start(f32[4,6]{1,0:T(4,128)S(1)} %get-tuple-element.440) | copy-start | bytes 292
  228.4 613.6 %copy-start.56 = (f32[4]{0:T(128)}, f32[4]{0:T(128)S(1)}, u32[]{:S(2)}) copy-start(f32[4]{0:T(128)S(1)} %get-tuple-element.323) | copy-start | bytes 52
  400.9 224.8 %all-gather.22.cloned.1.call-start = ((), (), s32[]{:S(2)}) async-start(), calls=%async_computation.19 | async-start | bytes 5242880 | tf_op jit(solution)/shard_map/all_gather | solution.py:103
  414.0 268.7 %all-gather.20.cloned.1.call-start = ((), (), s32[]{:S(2)}) async-start(), calls=%async_computation.16 | async-start | bytes 9437184 | tf_op jit(solution)/shard_map/all_gather | solution.py:96
  416.8 388.4 %reduce-scatter.17.cloned.1.call-start = ((), (), s32[]{:S(2)}) async-start(), calls=%async_computation.21 | async-start | bytes 5242880 | tf_op jit(solution)/shard_map/reduce_scatter | solution.py:135
  728.3 211.2 %all-gather.26.cloned.1.call-start = ((), (), s32[]{:S(2)}) async-start(), calls=%async_computation.22 | async-start | bytes 5242880 | tf_op jit(solution)/shard_map/all_gather | solution.py:103
  860.2 225.4 %reduce-scatter.11.cloned.1.call-start = ((), (), s32[]{:S(2)}) async-start(), calls=%async_computation.13 | async-start | bytes 10485760 | tf_op jit(solution)/shard_map/reduce_scatter | solution.py:99
  902.6 263.3 %reduce-scatter.19.cloned.1.call-start = ((), (), s32[]{:S(2)}) async-start(), calls=%async_computation.23 | async-start | bytes 5242880 | tf_op jit(solution)/shard_map/reduce_scatter | solution.py:135
  1037.7 231.3 %all-gather.16.cloned.1.call-start = ((), (), s32[]{:S(2)}) async-start(), calls=%async_computation.14 | async-start | bytes 5242880 | tf_op jit(solution)/shard_map/all_gather | solution.py:74
  1189.7 184.7 %reduce-scatter.27.cloned.1.call-start = ((), (), s32[]{:S(2)}) async-start(), calls=%async_computation.27 | async-start | bytes 9437184 | tf_op jit(solution)/shard_map/reduce_scatter | solution.py:104
  1204.2 285.3 %reduce-scatter.29.cloned.1.call-start = ((), (), s32[]{:S(2)}) async-start(), calls=%async_computation.28 | async-start | bytes 10485760 | tf_op jit(solution)/shard_map/reduce_scatter | solution.py:99
  1218.8 316.8 %reduce-scatter.23.cloned.1.call-start = ((), (), s32[]{:S(2)}) async-start(), calls=%async_computation.25 | async-start | bytes 2359296 | tf_op jit(solution)/shard_map/reduce_scatter | solution.py:104
  1225.9 395.5 %reduce-scatter.21.cloned.1.call-start = ((), (), s32[]{:S(2)}) async-start(), calls=%async_computation.24 | async-start | bytes 7077888 | tf_op jit(solution)/shard_map/reduce_scatter | solution.py:122
  1237.2 483.4 %reduce-scatter.25.cloned.1.call-start = ((), (), s32[]{:S(2)}) async-start(), calls=%async_computation.26 | async-start | bytes 18874368 | tf_op jit(solution)/shard_map/reduce_scatter | solution.py:122
  1261.9 605.6 %reduce-scatter.13.cloned.1.call-start = ((), (), s32[]{:S(2)}) async-start(), calls=%async_computation.17 | async-start | bytes 10485760 | tf_op jit(solution)/shard_map/reduce_scatter | solution.py:99
  1380.3 158.2 %copy-start.48 = (f32[1024]{0:T(1024)S(1)}, f32[1024]{0:T(1024)}, u32[]{:S(2)}) copy-start(f32[1024]{0:T(1024)} %copy-done.46) | copy-start | bytes 12292
  1380.3 158.2 %copy-start.51 = (f32[1024]{0:T(1024)S(1)}, f32[1024]{0:T(1024)}, u32[]{:S(2)}) copy-start(f32[1024]{0:T(1024)} %copy-done.49) | copy-start | bytes 12292
  (77 other events, 2260.4 us)
Sparse Core Ops, SparseCore 0:
  35.3 78.9 all-gather.9
  116.8 45.1 all-gather.11
  164.5 28.1 all-gather.13
  223.8 144.6 reduce-scatter.14
  370.8 90.5 all-gather.17
  463.4 80.7 all-gather.23
  546.4 79.2 all-gather.21
  628.2 54.4 all-gather.19
  728.4 76.7 reduce-scatter.16
  860.3 79.1 all-gather.25
  942.5 142.9 reduce-scatter.10
  1088.4 77.4 reduce-scatter.18
  1189.8 79.1 all-gather.15
  1272.8 69.7 reduce-scatter.26
  1345.0 144.4 reduce-scatter.28
  1493.5 41.9 reduce-scatter.22
  1538.8 61.9 reduce-scatter.20
  1604.6 115.9 reduce-scatter.24
  1723.0 144.4 reduce-scatter.12
where the time goes:
time: 1910 us; the launch traced here: 1900 us
  waiting for transfers between devices  1060 us (55%)
  matrix products  488 us (26%)
  local copies, waits for them, and re-layouts  117 us (6%)
  other arithmetic  107 us (6%)
  blocking collectives  94.4 us (5%)
    reduce_scatter x4, waiting for transfers between devices, project_out(): lax.psum_scatter(partial_value, 'col', scatter_dimension=1, tiled=True)  404 us
    all_gather x3, waiting for transfers between devices, normalize_gather(): lax.all_gather(normal.astype(jnp.bfloat16), 'col', axis=1, tiled=True)  157 us
    reduce_scatter x2, waiting for transfers between devices, back_in(): lax.psum_scatter(partial_value.astype(jnp.bfloat16), 'col', scatter_dimen...  136 us
    all_gather x2, waiting for transfers between devices, project_in(): lax.all_gather(weights, 'row', axis=1, tiled=True)  92.2 us
    all_gather x2, waiting for transfers between devices, back_out(): lax.all_gather(grad_branch.astype(jnp.bfloat16), 'col', axis=1, tiled=True)  88.5 us
    reduce_scatter x2, waiting for transfers between devices, back_in(): lax.psum_scatter(jnp.einsum('td,ktw->kdw', whole, grads, preferred_elemen...  87.4 us
    unnamed x147, local copies, waits for them, and re-layouts  63.6 us
    all_gather x2, waiting for transfers between devices, project_out(): lax.all_gather(weights, 'row', axis=1, tiled=True)  57 us
  transfers between devices with their start and end apart: 19, of which 16 were waited for; matrix products, arithmetic and copies ran while one was open for 30% of the time, Pallas kernels for 0%

commit v1 on v0

--- a/solution.py
+++ b/solution.py
@@ -9,7 +9,6 @@
 STEP = 8
 
 
-HIGH = lax.Precision.HIGHEST
 EPSILON = 1e-05
 MASKED = -1e30
 MOMENTUM = 0.9
@@ -42,27 +41,40 @@
     return values * cosine + jnp.concatenate([scaled[..., half:], -scaled[..., :half]], -1)
 
 
-def mix_in(streams, coeffs):
-    return jnp.einsum("s,std->td", coeffs, streams, precision=HIGH)
+def weighted(coeffs, streams):
+    total = coeffs[0] * streams[0]
+    for index in range(1, len(streams)):
+        total = total + coeffs[index] * streams[index]
+    return total
 
 
 def mix_out(streams, coeffs, branch):
     count = coeffs.shape[0]
-    mixed = jnp.einsum("ij,itd->jtd", coeffs[:, 1 : 1 + count], streams, precision=HIGH)
-    return mixed + coeffs[:, 1 + count][:, None, None] * branch[None]
+    return [
+        weighted(coeffs[:, 1 + j], streams) + coeffs[j, 1 + count] * branch for j in range(count)
+    ]
 
 
 def mix_back(coeffs, grad_after, grad_mixed):
     count = coeffs.shape[0]
-    spread = jnp.einsum("ij,jtd->itd", coeffs[:, 1 : 1 + count], grad_after, precision=HIGH)
-    return spread + coeffs[:, 0][:, None, None] * grad_mixed[None]
+    return [
+        weighted(coeffs[i, 1 : 1 + count], grad_after) + coeffs[i, 0] * grad_mixed
+        for i in range(count)
+    ]
 
 
 def mixing_grads(before, grad_mixed, grad_after, branch):
-    into = jnp.sum(before * grad_mixed[None], (1, 2))
-    across = jnp.einsum("itd,jtd->ij", before, grad_after, precision=HIGH)
-    outward = jnp.sum(grad_after * branch[None], (1, 2))
-    return jnp.concatenate([into[:, None], across, outward[:, None]], 1)
+    rows = []
+    for i, own in enumerate(before):
+        row = [jnp.sum(own * grad_mixed)]
+        row = row + [jnp.sum(own * after) for after in grad_after]
+        row.append(jnp.sum(grad_after[i] * branch))
+        rows.append(jnp.stack(row))
+    return jnp.stack(rows)
+
+
+def gather_columns(values):
+    return lax.all_gather(values.astype(jnp.bfloat16), "col", axis=1, tiled=True)
 
 
 def normalize_gather(mixed):
@@ -71,8 +83,7 @@
     spread = squares / D - center * center
     scale = lax.rsqrt(spread + EPSILON)
     normal = (mixed - center[:, None]) * scale[:, None]
-    whole = lax.all_gather(normal.astype(jnp.bfloat16), "col", axis=1, tiled=True)
-    return (normal, scale, whole)
+    return (normal, scale, gather_columns(normal))
 
 
 def norm_backward(grad_normal, normal, scale):
@@ -82,25 +93,20 @@
 
 
 def project_in(whole, weights):
-    return jnp.einsum(
-        "tn,knw->ktw",
-        whole,
-        lax.all_gather(weights, "row", axis=1, tiled=True),
-        preferred_element_type=jnp.float32,
-    )
+    return jnp.einsum("tn,knw->ktw", whole, weights, preferred_element_type=jnp.float32)
+
+
+def scatter_columns(partial_value):
+    return lax.psum_scatter(
+        partial_value.astype(jnp.bfloat16), "col", scatter_dimension=1, tiled=True
+    ).astype(jnp.float32)
 
 
 def project_out(active, weights):
-    partial_value = jnp.dot(
-        active,
-        lax.all_gather(weights, "row", axis=1, tiled=True),
-        preferred_element_type=jnp.float32,
-    )
-    return lax.psum_scatter(partial_value, "col", scatter_dimension=1, tiled=True)
-
-
-def back_out(grad_branch, active, weights):
-    whole = lax.all_gather(grad_branch.astype(jnp.bfloat16), "col", axis=1, tiled=True)
+    return scatter_columns(jnp.dot(active, weights, preferred_element_type=jnp.float32))
+
+
+def back_out(whole, active, weights):
     weight_grad = lax.psum_scatter(
         jnp.einsum("tw,td->wd", active, whole, preferred_element_type=jnp.float32).astype(
             jnp.bfloat16
@@ -109,12 +115,7 @@
         scatter_dimension=1,
         tiled=True,
     ).astype(jnp.float32)
-    grad_active = jnp.einsum(
-        "tn,wn->tw",
-        whole,
-        lax.all_gather(weights, "row", axis=1, tiled=True),
-        preferred_element_type=jnp.float32,
-    )
+    grad_active = jnp.einsum("tn,wn->tw", whole, weights, preferred_element_type=jnp.float32)
     return (grad_active, weight_grad)
 
 
@@ -127,15 +128,8 @@
         scatter_dimension=1,
         tiled=True,
     ).astype(jnp.float32)
-
-    def rows(piece, start):
-        return jnp.einsum("ktw,knw->tn", grads, piece, preferred_element_type=jnp.float32)
-
-    partial_value = rows(lax.all_gather(weights, "row", axis=1, tiled=True), jnp.int32(0))
-    grad_normal = lax.psum_scatter(
-        partial_value.astype(jnp.bfloat16), "col", scatter_dimension=1, tiled=True
-    ).astype(jnp.float32)
-    return (grad_normal, weight_grad)
+    partial_value = jnp.einsum("ktw,knw->tn", grads, weights, preferred_element_type=jnp.float32)
+    return (scatter_columns(partial_value), weight_grad)
 
 
 def block_scores(queries, key_heads, segment_row, start, block):
@@ -210,9 +204,9 @@
 
 def forward(stream_values, hyper_mix, lowered, cosine, sine, segment_row):
     projections, output_rows, gate_rows, down_rows = lowered
-    normal_one, scale_one, whole_one = normalize_gather(mix_in(stream_values, hyper_mix[0, :, 0]))
+    normal_one, scale_one, whole_one = normalize_gather(weighted(hyper_mix[0, :, 0], stream_values))
     projected = project_in(whole_one, projections)
-    length = stream_values.shape[1]
+    length = stream_values[0].shape[0]
     shape = (length, projected.shape[2] // HEAD_DIM, HEAD_DIM)
     queries = rotate(projected[0].reshape(shape), cosine, sine).astype(jnp.bfloat16)
     key_heads = rotate(projected[1].reshape(shape), cosine, sine).astype(jnp.bfloat16)
@@ -221,7 +215,7 @@
     attended = attended.astype(jnp.bfloat16)
     branch = project_out(attended, output_rows)
     middle = mix_out(stream_values, hyper_mix[0], branch)
-    normal_two, scale_two, whole_two = normalize_gather(mix_in(middle, hyper_mix[1, :, 0]))
+    normal_two, scale_two, whole_two = normalize_gather(weighted(hyper_mix[1, :, 0], middle))
     gated = project_in(whole_two, gate_rows)
     active = (jax.nn.silu(gated[0]) * gated[1]).astype(jnp.bfloat16)
     branch_two = project_out(active, down_rows)
@@ -274,25 +268,22 @@
     average_hyper_mix,
     cotangent,
 ):
-    stream_values = streams.astype(jnp.float32)
+    stream_values = [streams[i].astype(jnp.float32) for i in range(streams.shape[0])]
     cosine, sine = rope_tables(segments)
     cosine = cosine[0]
     sine = sine[0]
     segment_row = segments[0]
-    lowered = (
-        attention_in.astype(jnp.bfloat16),
-        attention_out.astype(jnp.bfloat16),
-        gate_up.astype(jnp.bfloat16),
-        down_weights.astype(jnp.bfloat16),
+    lowered = tuple(
+        lax.all_gather(weights.astype(jnp.bfloat16), "row", axis=1, tiled=True)
+        for weights in (attention_in, attention_out, gate_up, down_weights)
     )
     projections, output_rows, gate_rows, down_rows = lowered
     final, kept = forward(stream_values, hyper_mix, lowered, cosine, sine, segment_row)
-    kept = forward(stream_values, hyper_mix, lowered, cosine, sine, segment_row)[1]
     count = hyper_mix.shape[1]
     mix_one = hyper_mix[0]
     mix_two = hyper_mix[1]
-    grad_final = cotangent.astype(jnp.float32)
-    grad_branch_two = jnp.einsum("j,jtd->td", mix_two[:, 1 + count], grad_final, precision=HIGH)
+    grad_final = [cotangent[j].astype(jnp.float32) for j in range(count)]
+    grad_branch_two = gather_columns(weighted(mix_two[:, 1 + count], grad_final))
     grad_active, grad_down = back_out(grad_branch_two, kept["active"], down_rows)
     gate = kept["gated"][0]
     upper = kept["gated"][1]
@@ -305,7 +296,7 @@
     grad_mixed_two = norm_backward(grad_normal_two, kept["normal_two"], kept["scale_two"])
     grad_middle = mix_back(mix_two, grad_final, grad_mixed_two)
     hyper_two = mixing_grads(kept["middle"], grad_mixed_two, grad_final, kept["branch_two"])
-    grad_branch = jnp.einsum("j,jtd->td", mix_one[:, 1 + count], grad_middle, precision=HIGH)
+    grad_branch = gather_columns(weighted(mix_one[:, 1 + count], grad_middle))
     grad_attended, grad_output = back_out(grad_branch, kept["attended"], output_rows)
     shape = kept["queries"].shape
     length = shape[0]
@@ -355,8 +346,8 @@
         0.05 * (tokens_all * D) ** (-0.5),
     )
     return (
-        final.astype(jnp.bfloat16),
-        grad_streams,
+        jnp.stack(final).astype(jnp.bfloat16),
+        jnp.stack(grad_streams),
         first[0],
         first[1],
         first[2],

time: 1910 us -> 1390 us (0.73)
  waiting for transfers between devices: 1060 us -> 717 us
  matrix products: 488 us -> 210 us
  other arithmetic: 107 us -> 210 us
    reduce_scatter x6 -> x4, waiting for transfers between devices: 539 us -> 211 us  [scatter_columns(): lax.psum_scatter(partial_value.astype(jnp.bfloat16), 'col', scatter_dimen...]
    dot_general x22 -> x8, matrix products: 363 us -> 118 us  [the longest x2 35.9 us: back_in(): jnp.einsum('ktw,knw->tn', grads, weights, preferred_element_type=jnp.floa...]
    another operation x6 -> x12, other arithmetic: 5.81 us -> 56.7 us  [the longest x3 27.6 us: per_device(): jnp.stack(grad_streams)]
    reduce_scatter x2, waiting for transfers between devices: 41.8 us -> 0.02 us  [back_out(): lax.psum_scatter(jnp.einsum('tw,td->wd', active, whole, preferred_element...]
    all_gather x9 -> x8, waiting for transfers between devices: 395 us -> 435 us  [the longest x4 239 us: gather_columns(): lax.all_gather(values.astype(jnp.bfloat16), 'col', axis=1, tiled=True)]
    another operation x3 -> x11, local copies, waits for them, and re-layouts: 0.89 us -> 31.5 us  [the longest x8 30.6 us: mixing_grads(): rows.append(jnp.stack(row))]
    reduce_sum x2, other arithmetic: 0.73 us -> 27.8 us  [normalize_gather(): jnp.sum(mixed, -1)]
    psum x3 -> x2, blocking collectives: 43.6 us -> 24.8 us  [normalize_gather(): lax.psum((jnp.sum(mixed, -1), jnp.sum(mixed * mixed, -1)), 'col')]
  transfers between devices with their start and end apart: 19 -> 16, of which waited for: 16 -> 11; matrix products, arithmetic and copies ran while one was open for 30% -> 29% of each run, Pallas kernels for 0% -> 0%
where the time goes in v1:
time: 1390 us; the launch traced here: 1380 us
  waiting for transfers between devices  717 us (52%)
  other arithmetic  210 us (15%)
  matrix products  210 us (15%)
  local copies, waits for them, and re-layouts  135 us (10%)
  blocking collectives  86 us (6%)
  between operations  15 us (1%)
    all_gather x4, waiting for transfers between devices, gather_columns(): lax.all_gather(values.astype(jnp.bfloat16), 'col', axis=1, tiled=True)  239 us
    reduce_scatter x4, waiting for transfers between devices, scatter_columns(): lax.psum_scatter(partial_value.astype(jnp.bfloat16), 'col', scatter_dimen...  211 us
    all_gather x4, waiting for transfers between devices, per_device(): lax.all_gather(weights.astype(jnp.bfloat16), 'row', axis=1, tiled=True)  196 us
    reduce_scatter x2, waiting for transfers between devices, back_in(): lax.psum_scatter(jnp.einsum('td,ktw->kdw', whole, grads, preferred_elemen...  70.7 us
    unnamed x140, local copies, waits for them, and re-layouts  51.9 us
    psum x1, blocking collectives, per_device(): grad_hyper = lax.psum(jnp.stack([hyper_one, hyper_two]), ('row', 'col'))  39 us
    dot_general x2, matrix products, back_in(): jnp.einsum('td,ktw->kdw', whole, grads, preferred_element_type=jnp.float32)  35.9 us
    dot_general x2, matrix products, back_in(): jnp.einsum('ktw,knw->tn', grads, weights, preferred_element_type=jnp.floa...  35.9 us
  transfers between devices with their start and end apart: 16, of which 11 were waited for; matrix products, arithmetic and copies ran while one was open for 29% of the time, Pallas kernels for 0%

profile of v1, /device:TPU:0, one launch (start us, length us, event | category | flops | bytes accessed | tf_op | source)
XLA Modules:
  0.0 1383.4 jit_solution(14971758775878073988)
XLA Ops:
  14.4 13.7 all-reduce.3
  39.5 69.7 %all-gather.9.cloned.1.call-done = bf16[1024,2048]{1,0:T(8,128)(2,1)} async-done(((bf16[1024,512]{1,0:T(8,128)(2,1)}), bf16[1024,2048]{1,0:T(8,128)(2,1)}) %all-gather.9.cloned.1.call-update) | async-done | bytes 4194320 | tf_op jit(solution)/shard_map/all_gather | solution.py:77
  109.3 47.7 %all-gather.11.cloned.1.call-done = bf16[3,2048,512]{1,2,0:T(8,128)(2,1)} async-done(((bf16[3,256,512]{1,2,0:T(8,128)(2,1)}), bf16[3,2048,512]{1,2,0:T(8,128)(2,1)}) %all-gather.11.cloned.1.call-update) | async-done | bytes 6291472 | tf_op jit(solution)/shard_map/all_gather | solution.py:277
  184.5 23.9 %while.29 = (s32[]{:T(128)}, bf16[2,512,4,128]{3,1,2,0:T(8,128)(2,1)}, f32[2,4,512]{2,1,0:T(4,128)S(1)}, s32[2]{0:T(128)S(1)}, s32[1024]{0:T(1024)S(1)}, /*index...) while((s32[]{:T(128)}, ...), condition=%wide.region_9.10_spmd.clone, body=%wide.region_6.9_spmd.sunk.clone | while | flops 1100478464 | bytes 39407840 | solution.py:161
  220.6 75.0 %reduce-scatter.9.cloned.1.call-done = bf16[1024,512]{1,0:T(8,128)(2,1)} async-done(((bf16[1024,2048]{1,0:T(8,128)(2,1)}), bf16[1024,512]{1,0:T(8,128)(2,1)}) %reduce-scatter.9.cloned.1.call-update) | async-done | bytes 1048592 | tf_op jit(solution)/shard_map/reduce_scatter | solution.py:100
  295.6 22.1 %fusion.164 = (f32[1024]{0:T(1024)S(1)}, f32[1024]{0:T(1024)S(1)}, f32[1024,512]{1,0:T(8,128)S(1)}, f32[1024,512]{1,0:T(8,128)}, f32[1024,512]{1,0:T(8,128)}, /*index=5*/f32[1024,512]{1,0:T(8,128)}, f32[1024,512]{1,0:T(8,128)}) fusion(f32[]{:T(128)} %bitcast.59, f32[]{:T(128)} %bitcast.58, f32[]{:T(128)} %bitcast.57, f32[]{:T(128)} %bitcast.56, ...), kind=kLoop, calls=%fused_computation.359 | loop fusion | flops 26736640 | bytes 15736928 | tf_op jit(solution)/shard_map/reduce_sum | solution.py:81
  344.4 65.1 %all-gather.15.cloned.1.call-done = bf16[1024,2048]{1,0:T(8,128)(2,1)} async-done(((bf16[1024,512]{1,0:T(8,128)(2,1)}), bf16[1024,2048]{1,0:T(8,128)(2,1)}) %all-gather.15.cloned.1.call-update) | async-done | bytes 4194320 | tf_op jit(solution)/shard_map/all_gather | solution.py:77
  409.5 90.9 %all-gather.17.cloned.1.call-done = bf16[2,2048,2048]{2,1,0:T(8,128)(2,1)} async-done(((bf16[2,256,2048]{2,1,0:T(8,128)(2,1)}), bf16[2,2048,2048]{2,1,0:T(8,128)(2,1)}) %all-gather.17.cloned.1.call-update) | async-done | bytes 16777232 | tf_op jit(solution)/shard_map/all_gather | solution.py:277
  500.4 23.8 %convolution_bitcast_fusion = f32[2,1024,2048]{2,1,0:T(8,128)} fusion(bf16[2,2048,2048]{2,1,0:T(8,128)(2,1)} %all-gather.17.cloned.1.call-done, bf16[1024,2048]{1,0:T(8,128)(2,1)} %all-gather.15.cloned.1.call-done), kind=kOutput, calls=%fused_computation.137 | convolution fusion | flops 17179869184 | bytes 37748736 | tf_op jit(solution)/shard_map/tn,knw->ktw/dot_general | solution.py:96
  524.2 59.2 %all-gather.21.cloned.1.call-done = bf16[1024,2048]{1,0:T(8,128)(2,1)} async-done(((bf16[1024,512]{1,0:T(8,128)(2,1)}), bf16[1024,2048]{1,0:T(8,128)(2,1)}) %all-gather.21.cloned.1.call-update) | async-done | bytes 4194320 | tf_op jit(solution)/shard_map/all_gather | solution.py:77
  583.4 57.1 %all-gather.19.cloned.1.call-done = bf16[2048,2048]{1,0:T(8,128)(2,1)} async-done(((bf16[2048,256]{1,0:T(8,128)(2,1)}), bf16[2048,2048]{1,0:T(8,128)(2,1)}) %all-gather.19.cloned.1.call-update) | async-done | bytes 8388624 | tf_op jit(solution)/shard_map/all_gather | solution.py:277
  640.5 21.8 %fusion.42 = (bf16[1,1024,2048]{2,1,0:T(8,128)(2,1)}, bf16[1,1024,2048]{2,1,0:T(8,128)(2,1)}, bf16[1024,2048]{1,0:T(8,128)(2,1)}) fusion(f32[2,1024,2048]{2,1,0:T(8,128)} %convolution_bitcast_fusion, bf16[1024,2048]{1,0:T(8,128)(2,1)} %all-gather.21.cloned.1.call-done, bf16[2048,2048]{1,0:T(8,128)(2,1)} %all-gather.19.cloned.1.call-done), kind=kOutput, calls=%fused_computation.163 | convolution fusion | flops 8623489024 | bytes 41943040 | tf_op jit(solution)/shard_map/tn,wn->tw/dot_general | solution.py:118
  662.4 23.8 %bitcast_convert_fusion.1 = bf16[1024,2048]{1,0:T(8,128)(2,1)} fusion(bf16[2,2048,2048]{2,1,0:T(8,128)(2,1)} %all-gather.17.cloned.1.call-done, bf16[1,1024,2048]{2,1,0:T(8,128)(2,1)} %get-tuple-element.410, bf16[1,1024,2048]{2,1,0:T(8,128)(2,1)} %get-tuple-element.409), kind=kOutput, calls=%fused_computation.51 | convolution fusion | flops 17186160640 | bytes 29360128 | tf_op jit(solution)/shard_map/ktw,knw->tn/dot_general | solution.py:131
  686.4 76.7 %reduce-scatter.13.cloned.1.call-done = bf16[1024,512]{1,0:T(8,128)(2,1)} async-done(((bf16[1024,2048]{1,0:T(8,128)(2,1)}), bf16[1024,512]{1,0:T(8,128)(2,1)}) %reduce-scatter.13.cloned.1.call-update) | async-done | bytes 1048592 | tf_op jit(solution)/shard_map/reduce_scatter | solution.py:100
  776.5 21.6 %fusion.87 = (f32[]{:T(128)}, f32[]{:T(128)}, f32[]{:T(128)}, f32[]{:T(128)}, f32[]{:T(128)}, /*index=5*/f32[]{:T(128)}, f32[]{:T(128)}, f32[]{:T(128)}, f32[]{:...) fusion(bf16[4,1024,512]{2,1,0:T(8,128)(2,1)} %param.22, ...), kind=kLoop, calls=%fused_computation.216 | loop fusion | flops 38273020 | bytes 20988024 | tf_op jit(solution)/shard_map/reduce_sum | solution.py:70
  807.3 13.8 convolution_convert_fusion.1
  821.4 14.0 %convolution_convert_fusion = bf16[2048,2048]{1,0:T(8,128)(2,1)} fusion(bf16[1024,2048]{1,0:T(8,128)(2,1)} %get-tuple-element.411, bf16[1024,2048]{1,0:T(8,128)(2,1)} %all-gather.21.cloned.1.call-done), kind=kOutput, calls=%fused_computation.56 | convolution fusion | flops 8594128896 | bytes 16777216 | tf_op jit(solution)/shard_map/tw,td->wd/dot_general | solution.py:111
  841.3 45.3 %all-gather.23.cloned.1.call-done = bf16[1024,2048]{1,0:T(8,128)(2,1)} async-done(((bf16[1024,512]{1,0:T(8,128)(2,1)}), bf16[1024,2048]{1,0:T(8,128)(2,1)}) %all-gather.23.cloned.1.call-update) | async-done | bytes 4194320 | tf_op jit(solution)/shard_map/all_gather | solution.py:77
  892.8 50.1 %while.30 = (s32[]{:T(128)}, f32[1024,4,128]{0,2,1:T(8,128)S(1)}, f32[1024,4,128]{0,2,1:T(8,128)}, f32[2,512,4,128]{3,1,2,0:T(8,128)}, s32[2]{0:T(128)S(1)}, /*i...) while((s32[]{:T(128)}, f32[1024,4,128]{0,2,1:T(8,128)S(1)}, ...), condition=%wide.region_23.24_spmd.clone.clone, body=%wide.region_21.23_spmd.clone.sunk.clone | while | flops 2720266240 | bytes 213987920 | solution.py:199
  1006.4 25.1 %convert_bitcast_fusion = bf16[2,2048,2048]{1,2,0:T(8,128)(2,1)} fusion(bf16[1,1024,2048]{2,1,0:T(8,128)(2,1)} %get-tuple-element.410, bf16[1,1024,2048]{2,1,0:T(8,128)(2,1)} %get-tuple-element.409, bf16[1024,2048]{1,0:T(8,128)(2,1)} %all-gather.15.cloned.1.call-done), kind=kOutput, calls=%fused_computation.45 | convolution fusion | flops 17192452096 | bytes 29360128 | tf_op jit(solution)/shard_map/td,ktw->kdw/dot_general | solution.py:124
  1105.4 59.6 %reduce-scatter.15.cloned.1.call-done = bf16[1024,512]{1,0:T(8,128)(2,1)} async-done(((bf16[1024,2048]{1,0:T(8,128)(2,1)}), bf16[1024,512]{1,0:T(8,128)(2,1)}) %reduce-scatter.15.cloned.1.call-update) | async-done | bytes 1048592 | tf_op jit(solution)/shard_map/reduce_scatter | solution.py:100
  1202.0 39.0 %psum.71 = f32[2,4,6]{2,1,0:T(4,128)S(1)} all-reduce(f32[2,4,6]{2,1,0:T(4,128)S(1)} %pad_maximum_fusion.12), channel_id=1, replica_groups=mesh['row'=8,'col'=4] {'row','col'}, use_global_device_ids=true, to_apply=%region_81.82 | all-reduce | flops 48 | bytes 384 | tf_op jit(solution)/shard_map/psum | solution.py:323
  1241.6 16.3 %add_bitcast_fusion.3 = (f32[1,1024,512]{2,1,0:T(8,128)S(1)}, f32[1,1024,512]{2,1,0:T(8,128)S(1)}) fusion(f32[1024,512]{1,0:T(8,128)} %get-tuple-element.386, f32[1024,512]{1,0:T(8,128)} %copy-done.23, f32[1024,512]{1,0:T(8,128)} %get-tuple-element.398, f32[1024,512]{1,0:T(8,128)} %copy-done.21, f32[1024,512]{1,0:T(8,128)} %copy-done.19, f32[]{:T(128)} %bitcast.98, ...), kind=kLoop, calls=%fused_computation.298 | loop fusion | flops 9437184 | bytes 14680104 | tf_op jit(solution)/shard_map/stack | solution.py:350
  1280.2 70.7 %reduce-scatter.21.cloned.1.call-done = bf16[2,256,2048]{1,2,0:T(8,128)(2,1)} async-done(((bf16[2,2048,2048]{1,2,0:T(8,128)(2,1)}), bf16[2,256,2048]{1,2,0:T(8,128)(2,1)}) %reduce-scatter.21.cloned.1.call-update) | async-done | bytes 2097168 | tf_op jit(solution)/shard_map/reduce_scatter | solution.py:123
  (371 shorter events, 407.3 us)
Async XLA Ops:
  7.2 102.1 %all-gather.9.cloned.1.call-start = ((), (), s32[]{:S(2)}) async-start(), calls=%async_computation.8 | async-start | bytes 5242880 | tf_op jit(solution)/shard_map/all_gather | solution.py:77
  30.1 126.8 %all-gather.11.cloned.1.call-start = ((), (), s32[]{:S(2)}) async-start(), calls=%async_computation.9 | async-start | bytes 7077888 | tf_op jit(solution)/shard_map/all_gather | solution.py:277
  33.1 179.1 %all-gather.13.cloned.1.call-start = ((), (), s32[]{:S(2)}) async-start(), calls=%async_computation.10 | async-start | bytes 2359296 | tf_op jit(solution)/shard_map/all_gather | solution.py:277
  34.3 261.4 %reduce-scatter.9.cloned.1.call-start = ((), (), s32[]{:S(2)}) async-start(), calls=%async_computation.11 | async-start | bytes 5242880 | tf_op jit(solution)/shard_map/reduce_scatter | solution.py:100
  218.6 190.9 %all-gather.15.cloned.1.call-start = ((), (), s32[]{:S(2)}) async-start(), calls=%async_computation.12 | async-start | bytes 5242880 | tf_op jit(solution)/shard_map/all_gather | solution.py:77
  330.1 170.2 %all-gather.17.cloned.1.call-start = ((), (), s32[]{:S(2)}) async-start(), calls=%async_computation.13 | async-start | bytes 18874368 | tf_op jit(solution)/shard_map/all_gather | solution.py:277
  334.0 249.4 %all-gather.21.cloned.1.call-start = ((), (), s32[]{:S(2)}) async-start(), calls=%async_computation.16 | async-start | bytes 5242880 | tf_op jit(solution)/shard_map/all_gather | solution.py:77
  341.7 298.9 %all-gather.19.cloned.1.call-start = ((), (), s32[]{:S(2)}) async-start(), calls=%async_computation.14 | async-start | bytes 9437184 | tf_op jit(solution)/shard_map/all_gather | solution.py:277
  344.4 418.7 %reduce-scatter.13.cloned.1.call-start = ((), (), s32[]{:S(2)}) async-start(), calls=%async_computation.17 | async-start | bytes 5242880 | tf_op jit(solution)/shard_map/reduce_scatter | solution.py:100
  686.2 90.3 %copy-start.30 = (bf16[1024,512]{1,0:T(8,128)(2,1)S(1)}, bf16[1024,512]{1,0:T(8,128)(2,1)}, u32[]{:S(2)}) copy-start(bf16[1024,512]{1,0:T(8,128)(2,1)} %reduce-scatter.9.cloned.1.call-done) | copy-start | bytes 3145732
  686.2 200.3 %all-gather.23.cloned.1.call-start = ((), (), s32[]{:S(2)}) async-start(), calls=%async_computation.18 | async-start | bytes 5242880 | tf_op jit(solution)/shard_map/all_gather | solution.py:77
  807.3 243.9 %reduce-scatter.11.cloned.1.call-start = ((), (), s32[]{:S(2)}) async-start(), calls=%async_computation.15 | async-start | bytes 5242880 | tf_op jit(solution)/shard_map/reduce_scatter | solution.py:100
  821.1 275.1 %reduce-scatter.23.cloned.1.call-start = ((), (), s32[]{:S(2)}) async-start(), calls=%async_computation.23 | async-start | bytes 9437184 | tf_op jit(solution)/shard_map/reduce_scatter | solution.py:110
  835.4 267.4 %reduce-scatter.19.cloned.1.call-start = ((), (), s32[]{:S(2)}) async-start(), calls=%async_computation.21 | async-start | bytes 2359296 | tf_op jit(solution)/shard_map/reduce_scatter | solution.py:110
  962.4 202.6 %reduce-scatter.15.cloned.1.call-start = ((), (), s32[]{:S(2)}) async-start(), calls=%async_computation.19 | async-start | bytes 5242880 | tf_op jit(solution)/shard_map/reduce_scatter | solution.py:100
  993.5 275.8 %reduce-scatter.17.cloned.1.call-start = ((), (), s32[]{:S(2)}) async-start(), calls=%async_computation.20 | async-start | bytes 7077888 | tf_op jit(solution)/shard_map/reduce_scatter | solution.py:123
  1006.3 344.7 %reduce-scatter.21.cloned.1.call-start = ((), (), s32[]{:S(2)}) async-start(), calls=%async_computation.22 | async-start | bytes 18874368 | tf_op jit(solution)/shard_map/reduce_scatter | solution.py:123
  1102.8 62.2 %copy-start.12 = (f32[1024,512]{1,0:T(8,128)S(1)}, f32[1024,512]{1,0:T(8,128)}, u32[]{:S(2)}) copy-start(f32[1024,512]{1,0:T(8,128)} %copy-done.11) | copy-start | bytes 6291460
  1102.8 62.2 %copy-start.68 = (f32[1024]{0:T(1024)S(1)}, f32[1024]{0:T(1024)}, u32[]{:S(2)}) copy-start(f32[1024]{0:T(1024)} %copy-done.67) | copy-start | bytes 12292
  1102.8 62.2 %copy-start.70 = (f32[1024]{0:T(1024)S(1)}, f32[1024]{0:T(1024)}, u32[]{:S(2)}) copy-start(f32[1024]{0:T(1024)} %copy-done.69) | copy-start | bytes 12292
  1105.4 73.0 %copy-start.31 = (bf16[1024,512]{1,0:T(8,128)(2,1)S(1)}, bf16[1024,512]{1,0:T(8,128)(2,1)}, u32[]{:S(2)}) copy-start(bf16[1024,512]{1,0:T(8,128)(2,1)} %reduce-scatter.9.cloned.1.call-done) | copy-start | bytes 3145732
  1178.4 62.5 %copy-start.72 = (f32[2,4,6]{2,1,0:T(4,128)S(1)}, f32[2,4,6]{2,1,0:T(4,128)}, u32[]{:S(2)}) copy-start(f32[2,4,6]{2,1,0:T(4,128)} %param.28) | copy-start | bytes 580
  1178.5 62.5 %copy-start.73 = (f32[2,4,6]{2,1,0:T(4,128)S(1)}, f32[2,4,6]{2,1,0:T(4,128)}, u32[]{:S(2)}) copy-start(f32[2,4,6]{2,1,0:T(4,128)} %param.38) | copy-start | bytes 580
  1178.5 62.5 %copy-start.74 = (f32[2,4,6]{2,1,0:T(4,128)S(1)}, f32[2,4,6]{2,1,0:T(4,128)}, u32[]{:S(2)}) copy-start(f32[2,4,6]{2,1,0:T(4,128)} %param.33) | copy-start | bytes 580
  (84 other events, 663.9 us)
Sparse Core Ops, SparseCore 0:
  30.2 78.9 all-gather.8
  111.7 45.1 all-gather.10
  159.4 28.1 all-gather.12
  218.7 76.9 reduce-scatter.8
  330.3 79.1 all-gather.14
  412.0 88.3 all-gather.16
  502.6 80.7 all-gather.20
  586.0 54.4 all-gather.18
  686.3 76.7 reduce-scatter.12
  807.4 79.1 all-gather.22
  889.4 75.2 reduce-scatter.10
  969.0 71.8 reduce-scatter.22
  1044.1 41.2 reduce-scatter.18
  1088.2 76.7 reduce-scatter.14
  1168.2 62.8 reduce-scatter.16
  1235.0 115.9 reduce-scatter.20

commit v2 on v1

v2 whole, which is shorter than its diff:
```python
import functools

import jax
import jax.numpy as jnp
from jax import lax
from jax.experimental import pallas as pl
from jax.experimental.pallas import tpu as pltpu
from jax.sharding import PartitionSpec as P

D = 2048
HEAD_DIM = 128
FF = 8192
STEP = 8


EPSILON = 1e-05
MASKED = -1e30
MOMENTUM = 0.9
DECAY = 0.01
GROUP = 128
MESH = pl.DeviceIdType.MESH
VM, SM = pltpu.VMEM, pltpu.SMEM
f32 = jnp.float32
LANES = (((1,), (1,)), ((), ()))
ROWS = (((0,), (0,)), ((), ()))


def rope_tables(segments):
    segments = segments[0]
    length = segments.shape[0]
    index = jnp.arange(length, dtype=jnp.int32)
    before = jnp.concatenate([jnp.full((1,), -1, jnp.int32), segments[:-1]])
    starts = jnp.where(segments != before, index, 0)
    places = index - lax.cummax(starts)
    rates = 10000.0 ** (-2.0 * jnp.arange(HEAD_DIM // 2).astype(jnp.float32) / HEAD_DIM)
    angle = places[:, None].astype(jnp.float32) * rates
    cosine, sine = jnp.cos(angle), jnp.sin(angle)
    return (jnp.concatenate([cosine, cosine], 1), jnp.concatenate([-sine, sine], 1))


def exchange(
    size, tokens, width, chunk, hop, scatter, gather, prepare, finish, scratch, during=None, rows_too=0
):
    send, recv, blocks, facts, own_facts, sums_sent, sums_got, blocks_sent, blocks_got, facts_sent, facts_got = scratch
    me = lax.axis_index("col")
    chunks = tokens // chunk
    per_group = GROUP // chunk
    edge = size - 1

    def far(place):
        return jnp.maximum(place, edge - place) * hop if scatter is not None else place * 0

    def remote(source, target, sent, got, device):
        return pltpu.make_async_remote_copy(
            src_ref=source,
            dst_ref=target,
            send_sem=sent,
            recv_sem=got,
            device_id={"col": device},
            device_id_type=MESH,
        )

    def rows(index):
        return pl.ds(pl.multiple_of(index * chunk, chunk), chunk)

    def sum_copy(shard, slot, index, device):
        return remote(
            send.at[shard, rows(index)],
            recv.at[slot, rows(index)],
            sums_sent.at[shard, index],
            sums_got.at[slot, index],
            device,
        )

    def block_copy(place, index, way, device):
        return remote(
            blocks.at[place, rows(index)],
            blocks.at[place, rows(index)],
            blocks_sent.at[way, place, index],
            blocks_got.at[place, index],
            device,
        )

    def fact_copy(place, group, device):
        return remote(
            facts.at[group, pl.ds(pl.multiple_of(place * 8, 8), 8)],
            facts.at[group, pl.ds(pl.multiple_of(place * 8, 8), 8)],
            facts_sent.at[device, group],
            facts_got.at[place, group],
            device,
        )

    right = jnp.minimum(me + 1, edge)
    left = jnp.maximum(me - 1, 0)
    other = jnp.where(me == edge, left, right)

    def inside(index):
        return (index >= 0) & (index < chunks)

    def relay_sums(step):
        index = step - me * hop

        @pl.when(inside(index))
        def _():
            for shard in range(size - 1, 0, -1):

                @pl.when(shard > me)
                def _():
                    mine = scatter[rows(index), shard * width : (shard + 1) * width]

                    @pl.when(me > 0)
                    def _():
                        sum_copy(shard, shard, index, other).wait_recv()
                        total = mine.astype(jnp.float32) + recv[shard, rows(index)].astype(
                            jnp.float32
                        )
                        send[shard, rows(index)] = total.astype(jnp.bfloat16)

                    @pl.when(me == 0)
                    def _():
                        send[shard, rows(index)] = mine

                    slot = jnp.where(me + 1 == shard, size, shard)
                    sum_copy(shard, slot, index, right).start()

        back = step - (edge - me) * hop

        @pl.when(inside(back))
        def _():
            for shard in range(size - 1):

                @pl.when(shard < me)
                def _():
                    mine = scatter[rows(back), shard * width : (shard + 1) * width]

                    @pl.when(me < edge)
                    def _():
                        sum_copy(shard, shard, back, other).wait_recv()
                        total = mine.astype(jnp.float32) + recv[shard, rows(back)].astype(
                            jnp.float32
                        )
                        send[shard, rows(back)] = total.astype(jnp.bfloat16)

                    @pl.when(me == edge)
                    def _():
                        send[shard, rows(back)] = mine

                    sum_copy(shard, shard, back, left).start()

    def ready(step):
        index = step - far(me)

        @pl.when(inside(index))
        def _():
            if scatter is not None:

                @pl.when(me > 0)
                def _():
                    sum_copy(0, size, index, other).wait_recv()

                @pl.when(me < edge)
                def _():
                    sum_copy(0, me, index, other).wait_recv()

                start = pl.multiple_of(me * width, width)
                total = scatter[rows(index), pl.ds(start, width)].astype(jnp.float32)
                total = total + jnp.where(me > 0, recv[size, rows(index)].astype(jnp.float32), 0.0)
                total = total + jnp.where(
                    me < edge, recv[me, rows(index)].astype(jnp.float32), 0.0
                )
            else:
                total = None
            columns, block = prepare(rows(index), total)
            lane = lax.broadcasted_iota(jnp.int32, (chunk, 128), 1)
            packed = jnp.zeros((chunk, 128), jnp.float32)
            for place, column in enumerate(columns):
                packed = jnp.where(lane == place, column, packed)
            within = lax.rem(index, per_group)
            own_facts[pl.ds(pl.multiple_of(within * chunk, chunk), chunk), :] = packed
            if gather:
                blocks[me, rows(index)] = block

                @pl.when(me < edge)
                def _():
                    block_copy(me, index, 0, right).start()

                @pl.when(me > 0)
                def _():
                    block_copy(me, index, 1, left).start()

            @pl.when(within == per_group - 1)
            def _():
                group = index // per_group
                turned = own_facts[...].T
                facts[group, pl.ds(pl.multiple_of(me * 8, 8), 8), :] = turned[:8]
                for place in range(size):

                    @pl.when(place != me)
                    def _():
                        fact_copy(me, group, place).start()

    def relay_blocks(step):
        for near in range(1, size):
            for way, place in ((0, me - near), (1, me + near)):
                index = step - far(place) - near * hop

                @pl.when((place >= 0) & (place < size) & inside(index))
                def _():
                    block_copy(place, index, way, other).wait_recv()
                    onward = (me < edge) if way == 0 else (me > 0)

                    @pl.when(onward)
                    def _():
                        block_copy(place, index, way, right if way == 0 else left).start()

    longest = 2 * edge * hop if scatter is not None else edge * hop
    if not gather:
        longest = edge * hop

    def conclude(step):
        index = step - longest

        @pl.when(inside(index) & (lax.rem(index, per_group) == per_group - 1))
        def _():
            group = index // per_group
            for place in range(size):

                @pl.when(place != me)
                def _():
                    fact_copy(place, group, other).wait_recv()

            turned = facts[group].T
            finish(group, pl.ds(pl.multiple_of(group * GROUP, GROUP), GROUP), turned)

    barrier = pltpu.get_barrier_semaphore()
    for place in range(size):

        @pl.when(place != me)
        def _():
            pl.semaphore_signal(barrier, inc=1, device_id={"col": place}, device_id_type=MESH)

    line = lax.axis_index("row")
    for place in range(rows_too):

        @pl.when(place != line)
        def _():
            pl.semaphore_signal(barrier, inc=1, device_id={"row": place}, device_id_type=MESH)

    pl.semaphore_wait(barrier, size - 1 + max(rows_too - 1, 0))

    def step_all(step, carry):
        if scatter is not None:
            relay_sums(step)
        ready(step)
        if gather:
            relay_blocks(step)
        conclude(step)
        if during is not None:

            @pl.when(inside(step))
            def _():
                during(rows(step))

        return carry

    lax.fori_loop(0, chunks + longest, step_all, 0)

    def drain(index, carry):
        if scatter is not None:
            for shard in range(size):

                @pl.when(shard != me)
                def _():
                    sum_copy(shard, shard, index, other).wait_send()

        if gather:
            for place in range(size):

                @pl.when((place <= me) & (me < edge))
                def _():
                    block_copy(place, index, 0, other).wait_send()

                @pl.when((place >= me) & (me > 0))
                def _():
                    block_copy(place, index, 1, other).wait_send()

        return carry

    lax.fori_loop(0, chunks, drain, 0)

    def drain_facts(group, carry):
        for place in range(size):

            @pl.when(place != me)
            def _():
                fact_copy(me, group, place).wait_send()

        return carry

    lax.fori_loop(0, tokens // GROUP, drain_facts, 0)


def exchange_scratch(size, tokens, width, chunk, scatter, gather):
    chunks = tokens // chunk
    groups = tokens // GROUP
    dma = pltpu.SemaphoreType.DMA
    tiny = (1, chunk, 128)
    return [
        pltpu.VMEM((size, tokens, width) if scatter else tiny, jnp.bfloat16),
        pltpu.VMEM((size + 1, tokens, width) if scatter else tiny, jnp.bfloat16),
        pltpu.VMEM((size, tokens, width) if gather else tiny, jnp.bfloat16),
        pltpu.VMEM((groups, 128, 128), jnp.float32),
        pltpu.VMEM((GROUP, 128), jnp.float32),
        dma((size, chunks) if scatter else (1, 1)),
        dma((size + 1, chunks) if scatter else (1, 1)),
        dma((2, size, chunks) if gather else (1, 1, 1)),
        dma((size, chunks) if gather else (1, 1)),
        dma((size, groups)),
        dma((size, groups)),
    ]


def call(body, operands, places, outs, scratch, name, ident):
    moved = sum(array.size * array.dtype.itemsize for array in list(operands) + outs)
    return pl.pallas_call(
        body,
        out_shape=outs,
        in_specs=[pl.BlockSpec(memory_space=place) for place in places],
        out_specs=[pl.BlockSpec(memory_space=pltpu.VMEM)] * len(outs),
        scratch_shapes=scratch,
        compiler_params=pltpu.CompilerParams(
            collective_id=ident, has_side_effects=True, vmem_limit_bytes=58 * 2**20
        ),
        cost_estimate=pl.CostEstimate(
            flops=10**11, bytes_accessed=moved, transcendentals=0
        ),
        name=name,
    )(*operands)


def norm_stats(value):
    mean = jnp.sum(value, -1, keepdims=True) * (1.0 / value.shape[-1])
    center = value - mean
    return mean, center, jnp.sum(center * center, -1, keepdims=True)


def norm_whole(size, width, turned):
    means = [turned[:, 8 * z : 8 * z + 1] for z in range(size)]
    squares = [turned[:, 8 * z + 1 : 8 * z + 2] for z in range(size)]
    mean = sum(means[1:], means[0]) * (1.0 / size)
    shifts = [own - mean for own in means]
    spread = sum(squares[1:], squares[0])
    for shift in shifts:
        spread = spread + width * shift * shift
    return shifts, lax.rsqrt(spread * (1.0 / (size * width)) + EPSILON)


def norm_in_kernel(size, chunk, hop, coeffs, streams, whole, scale, *scratch):
    count, tokens, width = streams.shape
    blocks = scratch[2]

    def prepare(rows, total):
        mixed = coeffs[0] * streams[0, rows].astype(f32)
        for k in range(1, count):
            mixed = mixed + coeffs[k] * streams[k, rows].astype(f32)
        mean, center, square = norm_stats(mixed)
        return (mean, square), center.astype(jnp.bfloat16)

    def finish(group, rows, turned):
        shifts, rate = norm_whole(size, width, turned)
        scale[rows, :] = rate
        for z in range(size):
            value = (blocks[z, rows].astype(f32) + shifts[z]) * rate
            whole[rows, z * width : (z + 1) * width] = value.astype(jnp.bfloat16)

    exchange(size, tokens, width, chunk, hop, None, True, prepare, finish, scratch)


def norm_in(size, streams, coeffs, chunk=64, hop=1):
    _, tokens, width = streams.shape
    return call(
        functools.partial(norm_in_kernel, size, chunk, hop),
        (coeffs, streams),
        (SM, VM),
        [
            jax.ShapeDtypeStruct((tokens, size * width), jnp.bfloat16),
            jax.ShapeDtypeStruct((tokens, 1), f32),
        ],
        exchange_scratch(size, tokens, width, chunk, False, True),
        "norm_in",
        1,
    )


def norm_mid_kernel(size, chunk, hop, coeffs, partial, streams, whole, scale, branch, *scratch):
    count, tokens, width = streams.shape
    blocks = scratch[2]

    def prepare(rows, total):
        branch[rows, :] = total
        mixed = coeffs[count] * total
        for k in range(count):
            mixed = mixed + coeffs[k] * streams[k, rows].astype(f32)
        mean, center, square = norm_stats(mixed)
        return (mean, square), center.astype(jnp.bfloat16)

    def finish(group, rows, turned):
        shifts, rate = norm_whole(size, width, turned)
        scale[rows, :] = rate
        for z in range(size):
            value = (blocks[z, rows].astype(f32) + shifts[z]) * rate
            whole[rows, z * width : (z + 1) * width] = value.astype(jnp.bfloat16)

    exchange(size, tokens, width, chunk, hop, partial, True, prepare, finish, scratch)


def norm_mid(size, partial, streams, coeffs, chunk=64, hop=1):
    _, tokens, width = streams.shape
    return call(
        functools.partial(norm_mid_kernel, size, chunk, hop),
        (coeffs, partial, streams),
        (SM, VM, VM),
        [
            jax.ShapeDtypeStruct((tokens, size * width), jnp.bfloat16),
            jax.ShapeDtypeStruct((tokens, 1), f32),
            jax.ShapeDtypeStruct((tokens, width), f32),
        ],
        exchange_scratch(size, tokens, width, chunk, True, True),
        "norm_mid",
        2,
    )


def back_mid_kernel(
    size, chunk, hop, coeffs, partial, grads, whole_normal, scale, whole, inner, *scratch
):
    count, tokens, width = grads.shape
    blocks = scratch[2]
    me = lax.axis_index("col")

    def own_normal(rows):
        return whole_normal[rows, pl.ds(pl.multiple_of(me * width, width), width)].astype(f32)

    def prepare(rows, total):
        inner[rows, :] = total
        normal = own_normal(rows)
        part = 1.0 / width
        first = jnp.sum(total, -1, keepdims=True)
        second = jnp.sum(total * normal, -1, keepdims=True)
        plain = jnp.sum(normal, -1, keepdims=True)
        square = jnp.sum(normal * normal, -1, keepdims=True)
        spread = square - plain * plain * part
        cross = second - first * plain * part
        slope = jnp.where(spread > 1e-3, cross / jnp.maximum(spread, 1e-3), 0.0)
        level = (first - slope * plain) * part
        known = coeffs[0] * grads[0, rows].astype(f32)
        for k in range(1, count):
            known = known + coeffs[k] * grads[k, rows].astype(f32)
        block = known + (coeffs[count] * scale[rows, :]) * (total - level - slope * normal)
        return (first, second, level, slope), block.astype(jnp.bfloat16)

    def finish(group, rows, turned):
        first = turned[:, 0:1]
        second = turned[:, 1:2]
        for z in range(1, size):
            first = first + turned[:, 8 * z : 8 * z + 1]
            second = second + turned[:, 8 * z + 1 : 8 * z + 2]
        first = first * (1.0 / (size * width))
        second = second * (1.0 / (size * width))
        rate = scale[rows, :]
        gain = coeffs[count] * rate
        for z in range(size):
            level = gain * (turned[:, 8 * z + 2 : 8 * z + 3] - first)
            slope = gain * (turned[:, 8 * z + 3 : 8 * z + 4] - second)
            columns = slice(z * width, (z + 1) * width)
            value = blocks[z, rows].astype(f32) + level + slope * whole_normal[rows, columns].astype(f32)
            whole[rows, columns] = value.astype(jnp.bfloat16)
        inner[rows, :] = rate * (inner[rows, :] - first - second * own_normal(rows))

    exchange(size, tokens, width, chunk, hop, partial, True, prepare, finish, scratch)


def back_mid(size, partial, grads, whole_normal, scale, coeffs, chunk=64, hop=1):
    _, tokens, width = grads.shape
    return call(
        functools.partial(back_mid_kernel, size, chunk, hop),
        (coeffs, partial, grads, whole_normal, scale),
        (SM, VM, VM, VM, VM),
        [
            jax.ShapeDtypeStruct((tokens, size * width), jnp.bfloat16),
            jax.ShapeDtypeStruct((tokens, width), f32),
        ],
        exchange_scratch(size, tokens, width, chunk, True, True),
        "back_mid",
        3,
    )


def tile_sum(product):
    height, width = product.shape
    folded = jnp.sum(product.reshape(height // 8, 8, width), 0)
    total = folded[:, :128]
    for start in range(128, width, 128):
        total = total + folded[:, start : start + 128]
    return total


def back_in_kernel(
    size,
    chunk,
    hop,
    coeffs,
    partial,
    whole_normal,
    scale,
    streams,
    grads,
    branch_one,
    branch_two,
    inner_two,
    final,
    grad_streams,
    whole_sums,
    inner,
    sums,
    shares,
    shares_sent,
    shares_got,
    *scratch,
):
    count, tokens, width = streams.shape
    me = lax.axis_index("col")
    square = count * count
    sums[...] = jnp.zeros_like(sums)

    def own_normal(rows):
        return whole_normal[rows, pl.ds(pl.multiple_of(me * width, width), width)].astype(f32)

    def prepare(rows, total):
        inner[rows, :] = total
        first = jnp.sum(total, -1, keepdims=True)
        second = jnp.sum(total * own_normal(rows), -1, keepdims=True)
        return (first, second), None

    def finish(group, rows, turned):
        first = turned[:, 0:1]
        second = turned[:, 1:2]
        for z in range(1, size):
            first = first + turned[:, 8 * z : 8 * z + 1]
            second = second + turned[:, 8 * z + 1 : 8 * z + 2]
        first = first * (1.0 / (size * width))
        second = second * (1.0 / (size * width))
        own = scale[rows, :] * (inner[rows, :] - first - second * own_normal(rows))
        below = inner_two[rows, :]
        for i in range(count):
            value = coeffs[square + i] * below + coeffs[square + 3 * count + i] * own
            for k in range(count):
                value = value + coeffs[i * count + k] * grads[k, rows].astype(f32)
            grad_streams[i, rows] = value
            place = square + 3 * count + 1 + i
            sums[place] = sums[place] + tile_sum(streams[i, rows].astype(f32) * own)

    def during(rows):
        values = [streams[i, rows].astype(f32) for i in range(count)]
        above = [grads[i, rows].astype(f32) for i in range(count)]
        one = branch_one[rows, :]
        two = branch_two[rows, :]
        below = inner_two[rows, :]
        for j in range(count):
            value = coeffs[square + count + j] * one + coeffs[square + 2 * count + j] * two
            for k in range(count):
                value = value + coeffs[k * count + j] * values[k]
            final[j, rows] = value.astype(jnp.bfloat16)
        pairs = [(a, b) for a in values for b in above]
        pairs = pairs + [(a, below) for a in values]
        pairs = pairs + [(one, b) for b in above]
        pairs = pairs + [(a, two) for a in above]
        pairs = pairs + [(one, below)]
        for place, (a, b) in enumerate(pairs):
            sums[place] = sums[place] + tile_sum(a * b)

    count_rows = lax.axis_size("row")
    exchange(
        size,
        tokens,
        width,
        chunk,
        hop,
        partial,
        False,
        prepare,
        finish,
        scratch,
        during,
        count_rows,
    )
    total = jnp.sum(jnp.sum(sums[...], 1), -1, keepdims=True)
    total = jnp.broadcast_to(total, whole_sums.shape)
    for axis, members, base in (("col", size, 0), ("row", count_rows, size)):
        here = lax.axis_index(axis)

        def share_copy(member, target):
            return pltpu.make_async_remote_copy(
                src_ref=shares.at[base + here],
                dst_ref=shares.at[base + here],
                send_sem=shares_sent.at[base + member],
                recv_sem=shares_got.at[base + here],
                device_id={axis: target},
                device_id_type=MESH,
            )

        shares[base + here] = total
        for member in range(members):

            @pl.when(member != here)
            def _():
                share_copy(member, member).start()

        for member in range(members):

            @pl.when(member != here)
            def _():
                pltpu.make_async_remote_copy(
                    src_ref=shares.at[base + member],
                    dst_ref=shares.at[base + member],
                    send_sem=shares_sent.at[base + member],
                    recv_sem=shares_got.at[base + member],
                    device_id={axis: member},
                    device_id_type=MESH,
                ).wait()

        total = shares[base]
        for member in range(1, members):
            total = total + shares[base + member]
    whole_sums[...] = total


def back_in(
    size,
    coeffs,
    partial,
    whole_normal,
    scale,
    streams,
    grads,
    branch_one,
    branch_two,
    inner_two,
    chunk=64,
    hop=1,
):
    count, tokens, width = streams.shape
    products = -(-(count * count + 4 * count + 1) // 8) * 8
    return call(
        functools.partial(back_in_kernel, size, chunk, hop),
        (
            coeffs,
            partial,
            whole_normal,
            scale,
            streams,
            grads,
            branch_one,
            branch_two,
            inner_two,
        ),
        (SM,) + (VM,) * 8,
        [
            jax.ShapeDtypeStruct(streams.shape, jnp.bfloat16),
            jax.ShapeDtypeStruct(streams.shape, f32),
            jax.ShapeDtypeStruct((products, 128), f32),
        ],
        [
            pltpu.VMEM((tokens, width), f32),
            pltpu.VMEM((products, 8, 128), f32),
            pltpu.VMEM((size + lax.axis_size("row"), products, 128), f32),
            pltpu.SemaphoreType.DMA((size + lax.axis_size("row"),)),
            pltpu.SemaphoreType.DMA((size + lax.axis_size("row"),)),
        ]
        + exchange_scratch(size, tokens, width, chunk, True, False),
        "back_in",
        4,
    )


def block_probs(queries, key_heads, rows_docs, columns_docs, start):
    scores = lax.dot_general(queries, key_heads, LANES, preferred_element_type=f32)
    scores = scores * HEAD_DIM ** (-0.5)
    row = lax.broadcasted_iota(jnp.int32, scores.shape, 0) + start
    column = lax.broadcasted_iota(jnp.int32, scores.shape, 1)
    scores = jnp.where((rows_docs == columns_docs) & (column <= row), scores, MASKED)
    expo = jnp.exp(scores - jnp.max(scores, -1, keepdims=True))
    return expo * (1.0 / jnp.sum(expo, -1, keepdims=True))


def attend_forward_kernel(
    block, query, key, value, cosine, sine, column, row, queries, key_heads, value_heads, attended
):
    length = query.shape[0]

    def turn(values):
        return (values * cosine[...] + pltpu.roll(values, HEAD_DIM // 2, 1) * sine[...]).astype(
            jnp.bfloat16
        )

    queries[...] = turn(query[...])
    key_heads[...] = turn(key[...])
    value_heads[...] = value[...].astype(jnp.bfloat16)
    for start in range(0, length, block):
        end = start + block
        probs = block_probs(
            queries[start:end], key_heads[:end], column[start:end], row[:, :end], start
        )
        result = jnp.dot(
            probs.astype(jnp.bfloat16), value_heads[:end], preferred_element_type=f32
        )
        attended[start:end, :] = result.astype(jnp.bfloat16)


def attend_forward(projected, cosine, sine, column, row):
    length, width = projected.shape
    width = width // 3
    heads = width // HEAD_DIM
    block = min(256, length)

    def head(offset):
        return pl.BlockSpec((length, HEAD_DIM), lambda h: (0, h + offset))

    def fixed(array):
        return pl.BlockSpec(array.shape, lambda h: (0, 0))

    return pl.pallas_call(
        functools.partial(attend_forward_kernel, block),
        grid=(heads,),
        out_shape=[jax.ShapeDtypeStruct((length, width), jnp.bfloat16)] * 4,
        in_specs=[head(0), head(heads), head(2 * heads)]
        + [fixed(array) for array in (cosine, sine, column, row)],
        out_specs=[head(0)] * 4,
        compiler_params=pltpu.CompilerParams(vmem_limit_bytes=48 * 2**20),
        name="attend_forward",
    )(projected, projected, projected, cosine, sine, column, row)


def attend_back_kernel(
    block,
    queries,
    key_heads,
    value_heads,
    grad_result,
    cosine,
    sine,
    column,
    row,
    grad_query,
    grad_key,
    grad_value,
    key_sum,
    value_sum,
):
    length = queries.shape[0]
    factor = HEAD_DIM ** (-0.5)

    def turn_back(values, rows):
        values = values * factor
        return (
            values * cosine[rows] - pltpu.roll(values, HEAD_DIM // 2, 1) * sine[rows]
        ).astype(jnp.bfloat16)

    for start in range(length - block, -1, -block):
        end = start + block
        query, grad_part = queries[start:end], grad_result[start:end]
        probs = block_probs(query, key_heads[:end], column[start:end], row[:, :end], start)
        grad_probs = lax.dot_general(
            grad_part, value_heads[:end], LANES, preferred_element_type=f32
        )
        row_sum = jnp.sum(probs * grad_probs, -1, keepdims=True)
        grad_scores = (probs * (grad_probs - row_sum)).astype(jnp.bfloat16)
        grad_part_query = jnp.dot(grad_scores, key_heads[:end], preferred_element_type=f32)
        grad_query[start:end, :] = turn_back(grad_part_query, pl.ds(start, block))
        key_part = lax.dot_general(grad_scores, query, ROWS, preferred_element_type=f32)
        value_part = lax.dot_general(
            probs.astype(jnp.bfloat16), grad_part, ROWS, preferred_element_type=f32
        )
        if end == length:
            key_sum[...] = key_part
            value_sum[...] = value_part
        else:
            key_sum[:end, :] += key_part
            value_sum[:end, :] += value_part
    grad_key[...] = turn_back(key_sum[...], pl.ds(0, length))
    grad_value[...] = value_sum[...].astype(jnp.bfloat16)


def attend_back(queries, key_heads, value_heads, grad_result, cosine, sine, column, row):
    length, width = queries.shape
    heads = width // HEAD_DIM
    block = min(256, length)
    head = pl.BlockSpec((length, HEAD_DIM), lambda h: (0, h))

    def fixed(array):
        return pl.BlockSpec(array.shape, lambda h: (0, 0))

    grads = pl.pallas_call(
        functools.partial(attend_back_kernel, block),
        grid=(heads,),
        out_shape=[jax.ShapeDtypeStruct((length, width), jnp.bfloat16)] * 3,
        in_specs=[head] * 4 + [fixed(array) for array in (cosine, sine, column, row)],
        out_specs=[head] * 3,
        scratch_shapes=[pltpu.VMEM((length, HEAD_DIM), f32)] * 2,
        compiler_params=pltpu.CompilerParams(vmem_limit_bytes=48 * 2**20),
        name="attend_back",
    )(queries, key_heads, value_heads, grad_result, cosine, sine, column, row)
    return jnp.concatenate(grads, 1)


def update(weight, grad, moment, average, rate):
    step_grad = grad + DECAY * weight
    moment_new = MOMENTUM * moment + step_grad
    weight_new = weight - rate * (step_grad + MOMENTUM * moment_new)
    return (weight_new, moment_new, average + (weight_new - average) / (STEP + 1))


def tie(*values):
    return lax.optimization_barrier(values)


def line_ways():
    size = lax.axis_size("col")
    up = [(i, i + 1) for i in range(size - 1)]
    down = [(i + 1, i) for i in range(size - 1)]
    return size, lax.axis_index("col"), up, down


def gather_steps(values):
    size, me, up, down = line_ways()
    width = values.shape[1]
    before, after = [values], [values]
    for _ in range(size - 1):
        step = (lax.ppermute(before[-1], "col", up), lax.ppermute(after[-1], "col", down))
        step = yield step
        before.append(step[0])
        after.append(step[1])
    row = jnp.concatenate(before[:0:-1] + after, 1)
    yield lax.dynamic_slice_in_dim(row, (size - 1 - me) * width, size * width, 1)


def scatter_steps(partial):
    size, me, up, down = line_ways()
    width = partial.shape[1] // size

    def share(place):
        return lax.dynamic_slice_in_dim(partial, place * width, width, 1)

    first = share(jnp.minimum(me + size - 1, size - 1))
    last = share(jnp.maximum(me - size + 1, 0))
    for step in range(1, size):
        if step > 1:
            first = share(jnp.minimum(me + size - step, size - 1)).astype(f32) + first.astype(f32)
            last = share(jnp.maximum(me - size + step, 0)).astype(f32) + last.astype(f32)
            first = first.astype(jnp.bfloat16)
            last = last.astype(jnp.bfloat16)
        first, last = yield (lax.ppermute(first, "col", up), lax.ppermute(last, "col", down))
    yield share(me).astype(f32) + first.astype(f32) + last.astype(f32)


def advance(steps, got, *values):
    moved = next(steps) if got is None else steps.send(got)
    tied = tie(*moved, *values)
    return tied[: len(moved)], tied[len(moved) :]


def finish_line(steps, got):
    moved = steps.send(got)
    while isinstance(moved, tuple):
        moved = steps.send(moved)
    return moved


def weighted(coeffs, streams):
    total = coeffs[0] * streams[0].astype(f32)
    for index in range(1, len(streams)):
        total = total + coeffs[index] * streams[index].astype(f32)
    return total


def small_matmul(left, right):
    return jnp.sum(left[:, :, None] * right[None, :, :], 1)


def matmul(spec, left, right, kind=jnp.float32):
    return jnp.einsum(spec, left, right, preferred_element_type=f32).astype(kind)


def scatter_rows(grad, axis):
    return lax.psum_scatter(grad, "row", scatter_dimension=axis, tiled=True).astype(f32)


def side_by_side(weights):
    return jnp.concatenate([weights[k] for k in range(weights.shape[0])], 1)


def one_by_one(values, count):
    width = values.shape[1] // count
    return jnp.stack([values[:, k * width : (k + 1) * width] for k in range(count)])


def per_device(
    streams,
    segments,
    attention_in,
    attention_out,
    gate_up,
    down_weights,
    hyper_mix,
    moment_attention_in,
    moment_attention_out,
    moment_gate_up,
    moment_down_weights,
    moment_hyper_mix,
    average_attention_in,
    average_attention_out,
    average_gate_up,
    average_down_weights,
    average_hyper_mix,
    cotangent,
):
    size = lax.axis_size("col")
    low = jnp.bfloat16
    count, length, width = streams.shape
    cosine, sine = rope_tables(segments)

    def gather_rows(weights, axis):
        return lax.all_gather(weights.astype(low), "row", axis=axis, tiled=True)

    projections = gather_rows(side_by_side(attention_in), 0)
    output_rows = gather_rows(attention_out, 1)
    gate_rows = gather_rows(side_by_side(gate_up), 0)
    down_rows = gather_rows(down_weights, 1)

    one, two = hyper_mix[0], hyper_mix[1]
    across_one, across_two = one[:, 1 : 1 + count], two[:, 1 : 1 + count]
    through = small_matmul(across_one, across_two)
    in_two = small_matmul(across_one, two[:, :1])[:, 0]
    out_one = small_matmul(one[None, :, 1 + count], across_two)[0]
    turn = jnp.sum(one[:, 1 + count] * two[:, 0])

    whole_one, scale_one = norm_in(size, streams, one[:, 0])
    whole_one, grads_tied = tie(whole_one, cotangent)

    steps = gather_steps(
        weighted(two[:, 1 + count], [grads_tied[i] for i in range(count)]).astype(low)
    )
    got, (projected,) = advance(steps, None, matmul("tn,nw->tw", whole_one, projections))
    queries, key_heads, value_heads, attended = attend_forward(
        projected, cosine, sine, segments.T, segments
    )
    got, (attended,) = advance(steps, got, attended)

    mid_coeffs = jnp.concatenate([in_two, turn[None]])
    whole_two, scale_two, branch_one = norm_mid(
        size, matmul("tw,wd->td", attended, output_rows, low), streams, mid_coeffs
    )
    whole_two, *got = tie(whole_two, *got)

    gated = matmul("tn,nw->tw", whole_two, gate_rows)
    whole_grad_two = finish_line(steps, tuple(got))
    hidden = gated.shape[1] // 2
    gate, upper = gated[:, :hidden], gated[:, hidden:]
    sigma = jax.nn.sigmoid(gate)
    active = (gate * sigma * upper).astype(low)
    partial_two = matmul("tw,wd->td", active, down_rows, low)
    grad_down = matmul("tw,td->wd", active, whole_grad_two, low)
    grad_down, partial_two, whole_grad_two = tie(grad_down, partial_two, whole_grad_two)
    grad_down = scatter_rows(grad_down, 1)

    steps = scatter_steps(partial_two)
    grad_active = matmul("tn,wn->tw", whole_grad_two, down_rows)
    grad_gate = grad_active * upper * sigma * (1.0 + gate * (1.0 - sigma))
    grad_upper = grad_active * gate * sigma
    grad_gated = jnp.concatenate([grad_gate, grad_upper], 1).astype(low)
    got, (grad_gated,) = advance(steps, None, grad_gated)
    grad_gate_up = matmul("td,tw->dw", whole_two, grad_gated, low)
    got, (grad_gate_up, grad_gated) = advance(steps, got, grad_gate_up, grad_gated)
    grad_gate_up, grad_down = tie(grad_gate_up, grad_down)
    grad_gate_up = scatter_rows(grad_gate_up, 0)
    partial_mid = matmul("tw,nw->tn", grad_gated, gate_rows, low)
    branch_two = finish_line(steps, got)
    partial_mid, branch_two = tie(partial_mid, branch_two)
    back_coeffs = jnp.concatenate([out_one, turn[None]])
    whole_grad_one, inner_two = back_mid(
        size, partial_mid, cotangent, whole_two, scale_two, back_coeffs
    )

    grad_output = matmul("tw,td->wd", attended, whole_grad_one, low)
    grad_output, whole_grad_one = tie(grad_output, whole_grad_one)
    grad_output, grad_gate_up = tie(grad_output, grad_gate_up)
    grad_output = scatter_rows(grad_output, 1)
    grad_attended = matmul("tn,wn->tw", whole_grad_one, output_rows, low)
    grad_heads = attend_back(
        queries, key_heads, value_heads, grad_attended, cosine, sine, segments.T, segments
    )
    grad_projections = matmul("td,tw->dw", whole_one, grad_heads, low)
    grad_projections, grad_heads = tie(grad_projections, grad_heads)
    grad_projections, grad_output = tie(grad_projections, grad_output)
    grad_projections = scatter_rows(grad_projections, 0)
    end_coeffs = jnp.concatenate(
        [through.reshape(-1), in_two, out_one, two[:, 1 + count], one[:, 0]]
    )
    final, grad_streams, products = back_in(
        size,
        end_coeffs,
        matmul("tw,nw->tn", grad_heads, projections, low),
        whole_one,
        scale_one,
        streams,
        cotangent,
        branch_one,
        branch_two,
        inner_two,
    )

    products = products[:, 0]
    cuts = [count * count, count, count, count, 1, count]
    parts = []
    start = 0
    for cut in cuts:
        parts.append(products[start : start + cut])
        start = start + cut
    streams_grads, streams_two, branch_grads, grads_branch, branch_inner, streams_one = parts
    streams_grads = streams_grads.reshape(count, count)
    hyper_one = jnp.concatenate(
        [
            streams_one[:, None],
            small_matmul(streams_grads, across_two.T) + streams_two[:, None] * two[None, :, 0],
            small_matmul(across_two, branch_grads[:, None]) + (two[:, 0] * branch_inner)[:, None],
        ],
        1,
    )
    hyper_two = jnp.concatenate(
        [
            small_matmul(across_one.T, streams_two[:, None])
            + (one[:, 1 + count] * branch_inner)[:, None],
            small_matmul(across_one.T, streams_grads)
            + one[:, 1 + count][:, None] * branch_grads[None, :],
            grads_branch[:, None],
        ],
        1,
    )
    grad_hyper = jnp.stack([hyper_one, hyper_two])
    grad_projections = one_by_one(grad_projections, attention_in.shape[0])
    grad_gate_up = one_by_one(grad_gate_up, gate_up.shape[0])
    tokens_all = length * lax.axis_size("row")
    token_scale = tokens_all ** (-0.5)
    model_rate = D ** (-0.5) * token_scale
    first = update(
        attention_in, grad_projections, moment_attention_in, average_attention_in, model_rate
    )
    second = update(
        attention_out, grad_output, moment_attention_out, average_attention_out, model_rate
    )
    third = update(gate_up, grad_gate_up, moment_gate_up, average_gate_up, model_rate)
    fourth = update(
        down_weights,
        grad_down,
        moment_down_weights,
        average_down_weights,
        FF ** (-0.5) * token_scale,
    )
    fifth = update(
        hyper_mix,
        grad_hyper,
        moment_hyper_mix,
        average_hyper_mix,
        0.05 * (tokens_all * D) ** (-0.5),
    )
    return (
        final,
        grad_streams,
        first[0],
        first[1],
        first[2],
        second[0],
        second[1],
        second[2],
        third[0],
        third[1],
        third[2],
        fourth[0],
        fourth[1],
        fourth[2],
        fifth[0],
        fifth[1],
        fifth[2],
    )


def solution(mesh):
    in_specs = (
        P(None, "row", "col"),
        P("row", None),
        P(None, "row", "col"),
        P("col", "row"),
        P(None, "row", "col"),
        P("col", "row"),
        P(),
        P(None, "row", "col"),
        P("col", "row"),
        P(None, "row", "col"),
        P("col", "row"),
        P(),
        P(None, "row", "col"),
        P("col", "row"),
        P(None, "row", "col"),
        P("col", "row"),
        P(),
        P(None, "row", "col"),
    )
    out_specs = (
        P(None, "row", "col"),
        P(None, "row", "col"),
        P(None, "row", "col"),
        P(None, "row", "col"),
        P(None, "row", "col"),
        P("col", "row"),
        P("col", "row"),
        P("col", "row"),
        P(None, "row", "col"),
        P(None, "row", "col"),
        P(None, "row", "col"),
        P("col", "row"),
        P("col", "row"),
        P("col", "row"),
        P(),
        P(),
        P(),
    )
    return jax.shard_map(
        per_device, mesh=mesh, in_specs=in_specs, out_specs=out_specs, check_vma=False
    )
```

time: 1390 us -> 854 us (0.61)
  waiting for transfers between devices: 717 us -> 37.5 us
  Pallas kernels: 0 us -> 473 us
  other arithmetic: 210 us -> 72.1 us
  local copies, waits for them, and re-layouts: 135 us -> 41 us
  blocking collectives: 86 us -> 0 us
  matrix products: 210 us -> 173 us
  starting transfers between devices: 1.05 us -> 35.8 us
    pallas_call x0 -> x6, Pallas kernels: none -> 473 us  [the longest x4 444 us: call(): pl.pallas_call(body, out_shape=outs, in_specs=[pl.BlockSpec(memory_space=...]
    all_gather x8 -> x4, waiting for transfers between devices: 435 us -> 0.03 us  [gather_rows(): return lax.all_gather(weights.astype(low), 'row', axis=axis, tiled=True)]
    reduce_scatter x8 -> x4, waiting for transfers between devices: 282 us -> 20 us  [scatter_rows(): lax.psum_scatter(grad, 'row', scatter_dimension=axis, tiled=True)]
    psum x5 -> x0, blocking collectives: 86 us -> none  [the longest x1 39 us: per_device(): grad_hyper = lax.psum(jnp.stack([hyper_one, hyper_two]), ('row', 'col'))]
    reduce_sum x9 -> x6, other arithmetic: 75.6 us -> 1.21 us  [the longest x1 0.67 us: per_device(): turn = jnp.sum(one[:, 1 + count] * two[:, 0])]
    another operation x15 -> x6, other arithmetic: 56.7 us -> 4.52 us  [the longest x3 27.6 us: per_device(): jnp.stack(grad_streams)]
    another operation x15 -> x3, local copies, waits for them, and re-layouts: 39.7 us -> 0.72 us  [the longest x2 0.61 us: one_by_one(): jnp.stack([values[:, k * width:(k + 1) * width] for k in range(count)])]
    dot_general x26 -> x12, matrix products: 210 us -> 173 us  [matmul(): jnp.einsum(spec, left, right, preferred_element_type=f32).astype(kind)]
  transfers between devices with their start and end apart: 16 -> 20, of which waited for: 11 -> 5; matrix products, arithmetic and copies ran while one was open for 29% -> 28% of each run, Pallas kernels for 0% -> 56%
where the time goes in v2:
time: 854 us; the launch traced here: 847 us
  Pallas kernels  473 us (55%)
  matrix products  173 us (20%)
  other arithmetic  72.1 us (8%)
  local copies, waits for them, and re-layouts  41 us (5%)
  waiting for transfers between devices  37.5 us (4%)
  starting transfers between devices  35.8 us (4%)
  between operations  15.1 us (2%)
    pallas_call x4, Pallas kernels, call(): pl.pallas_call(body, out_shape=outs, in_specs=[pl.BlockSpec(memory_space=...  444 us
    dot_general x12, matrix products, matmul(): jnp.einsum(spec, left, right, preferred_element_type=f32).astype(kind)  173 us
    unnamed x113, local copies, waits for them, and re-layouts  27.5 us
    reduce_scatter x4, waiting for transfers between devices, scatter_rows(): lax.psum_scatter(grad, 'row', scatter_dimension=axis, tiled=True)  20 us
    add x5, other arithmetic, update(): average + (weight_new - average) / (STEP + 1)  17.6 us
  transfers between devices with their start and end apart: 20, of which 5 were waited for; matrix products, arithmetic and copies ran while one was open for 28% of the time, Pallas kernels for 56%

profile of v2, /device:TPU:0, one launch (start us, length us, event | category | flops | bytes accessed | tf_op | source)
XLA Modules:
  0.0 847.2 jit_solution(8631715220939880895)
XLA Ops:
  15.7 83.6 %norm_in.1 = (bf16[1024,2048]{1,0:T(8,128)(2,1)}, f32[1024,1]{1,0:T(8,128)}) custom-call(f32[4]{0:T(128)} %get-tuple-element.121.coeffs, bf16[4,1024,512]{2,1,0:T(8,128)(2,1)} %streams.5), custom_call_target="tpu_custom_call" | custom-call | flops 99999997952 | bytes 8392720 | tf_op jit(solution)/shard_map/norm_in/pallas_call | solution.py:325
  114.7 11.7 %fusion.6.query.key.value = f32[1024,1536]{1,0:T(8,128)} fusion(bf16[1024,2048]{1,0:T(8,128)(2,1)} %get-tuple-element.68.whole_normal, bf16[2048,1536]{1,0:T(8,128)(2,1)} %all-gather.5.cloned.1.call-done), kind=kOutput, calls=%fused_computation.107 | convolution fusion | flops 6442450944 | bytes 16777216 | tf_op jit(solution)/shard_map/tn,nw->tw/dot_general | solution.py:891
  141.1 13.4 %attend_forward.1 = (bf16[1024,512]{1,0:T(8,128)(2,1)S(1)}, bf16[1024,512]{1,0:T(8,128)(2,1)S(1)}, bf16[1024,512]{1,0:T(8,128)(2,1)S(1)}, bf16[1024,512]{1,0:T(8,128)(2,1)S(1)}) custom-call(f32[1024,1536]{1,0:T(8,128)} %fusion.6.query.key.value, f32[1024,1536]{1,0:T(8,128)} %fusion.6.query.key.value, f32[1024,1536]{1,0:T(8,128)} %fusion.6.query.key.value, ...), custom_call_target="tpu_custom_call" | custom-call | tf_op jit(solution)/shard_map/attend_forward/pallas_call | solution.py:732
  159.6 6.0 convolution_convert_fusion.6.partial
  165.6 117.8 %norm_mid.1 = (bf16[1024,2048]{1,0:T(8,128)(2,1)}, f32[1024,1]{1,0:T(8,128)}, f32[1024,512]{1,0:T(8,128)}) custom-call(f32[5]{0:T(128)} %pad_maximum_fusion.6.coeffs, bf16[1024,2048]{1,0:T(8,128)(2,1)} %convolution_convert_fusion.6.partial, bf16[4,1024,512]{2,1,0:T(8,128)(2,1)} %streams.5), custom_call_target="tpu_custom_call" | custom-call | flops 99999997952 | bytes 14684180 | tf_op jit(solution)/shard_map/norm_mid/pallas_call | solution.py:325
  287.0 10.4 %collective-permute-done.4 = bf16[1024,512]{1,0:T(8,128)(2,1)} collective-permute-done((bf16[1024,512]{1,0:T(8,128)(2,1)}, bf16[1024,512]{1,0:T(8,128)(2,1)}, u32[]{:S(2)}, u32[]{:S(2)}) %collective-permute-start.4) | collective-permute-done | bytes 1048608 | tf_op jit(solution)/shard_map/ppermute | solution.py:839
  310.1 22.0 %fusion.7 = f32[1024,4096]{1,0:T(8,128)S(1)} fusion(bf16[1024,2048]{1,0:T(8,128)(2,1)} %get-tuple-element.81.whole_normal, bf16[2048,4096]{1,0:T(8,128)(2,1)} %all-gather.9.cloned.1.call-done), kind=kOutput, calls=%fused_computation.108 | convolution fusion | flops 17179869184 | bytes 37748736 | tf_op jit(solution)/shard_map/tn,nw->tw/dot_general | solution.py:891
  342.5 11.4 %convolution_convert_fusion.2 = bf16[2048,2048]{1,0:T(8,128)(2,1)} fusion(bf16[1024,2048]{1,0:T(8,128)(2,1)S(1)} %multiply_convert_fusion.2, bf16[1024,2048]{1,0:T(8,128)(2,1)S(1)} %copy-done.21), kind=kOutput, calls=%fused_computation.7 | convolution fusion | flops 8594128896 | bytes 16777216 | tf_op jit(solution)/shard_map/tw,td->wd/dot_general | solution.py:891
  354.0 13.8 %convolution_convert_fusion.5 = bf16[1024,2048]{1,0:T(8,128)(2,1)} fusion(bf16[1024,2048]{1,0:T(8,128)(2,1)} %copy-done.19, bf16[2048,2048]{1,0:T(8,128)(2,1)} %all-gather.11.cloned.1.call-done), kind=kOutput, calls=%fused_computation.14 | convolution fusion | flops 8592031744 | bytes 16777216 | tf_op jit(solution)/shard_map/tw,wd->td/dot_general | solution.py:891
  371.9 6.0 collective-permute-start.6
  378.0 23.4 %multiply_convert_fusion.1 = (bf16[1024,2048]{1,0:T(8,128)(2,1)}, bf16[1024,2048]{1,0:T(8,128)(2,1)}) fusion(f32[1024,4096]{1,0:T(8,128)} %copy-done.9, bf16[1024,2048]{1,0:T(8,128)(2,1)} %constant_dynamic-slice_fusion.2, bf16[2048,2048]{1,0:T(8,128)(2,1)} %all-gather.11.cloned.1.call-done), kind=kOutput, calls=%fused_computation.3 | convolution fusion | flops 8617197568 | bytes 37748736 | tf_op jit(solution)/shard_map/tn,wn->tw/dot_general | solution.py:891
  401.3 8.2 pad_maximum_fusion
  420.8 23.8 %convolution_convert_fusion = bf16[2048,4096]{1,0:T(8,128)(2,1)} fusion(bf16[1024,2048]{1,0:T(8,128)(2,1)S(1)} %copy-done.49, bf16[1024,4096]{1,0:T(8,128)(2,1)} %pad_maximum_fusion), kind=kOutput, calls=%fused_computation | convolution fusion | flops 17188257792 | bytes 29360128 | tf_op jit(solution)/shard_map/td,tw->dw/dot_general | solution.py:891
  457.3 26.0 %convolution_convert_fusion.3.partial = bf16[1024,2048]{1,0:T(8,128)(2,1)} fusion(bf16[1024,4096]{1,0:T(8,128)(2,1)} %pad_maximum_fusion, bf16[2048,4096]{1,0:T(8,128)(2,1)} %all-gather.9.cloned.1.call-done), kind=kOutput, calls=%fused_computation.12 | convolution fusion | flops 17181966336 | bytes 29360128 | tf_op jit(solution)/shard_map/tw,nw->tn/dot_general | solution.py:891
  486.4 121.2 %back_mid.1 = (bf16[1024,2048]{1,0:T(8,128)(2,1)}, f32[1024,512]{1,0:T(8,128)}) custom-call(f32[5]{0:T(128)} %pad_maximum_fusion.5.coeffs, bf16[1024,2048]{1,0:T(8,128)(2,1)} %convolution_convert_fusion.3.partial, bf16[4,1024,512]{2,1,0:T(8,128)(2,1)} %grads.3, bf16[1024,2048]{1,0:T(8,128)(2,1)} %get-tuple-element.81.whole_normal, ...), custom_call_target="tpu_custom_call" | custom-call | flops 99999997952 | bytes 18878484 | tf_op jit(solution)/shard_map/back_mid/pallas_call | solution.py:325
  607.5 5.9 convolution_convert_fusion.7
  613.5 6.3 convolution_convert_fusion.8.grad_result
  619.7 16.3 %attend_back.1 = (bf16[1024,512]{1,0:T(8,128)(2,1)S(1)}, bf16[1024,512]{1,0:T(8,128)(2,1)S(1)}, bf16[1024,512]{1,0:T(8,128)(2,1)S(1)}) custom-call(bf16[1024,512]{1,0:T(8,128)(2,1)S(1)} %get-tuple-element.71.queries, bf16[1024,512]{1,0:T(8,128)(2,1)} %copy-done.4, bf16[1024,512]{1,0:T(8,128)(2,1)} %copy-done.5, ...), custom_call_target="tpu_custom_call" | custom-call | tf_op jit(solution)/shard_map/attend_back/pallas_call | solution.py:803
  640.9 11.0 %convolution_convert_fusion.1 = bf16[2048,1536]{1,0:T(8,128)(2,1)} fusion(bf16[1024,2048]{1,0:T(8,128)(2,1)} %get-tuple-element.68.whole_normal, bf16[1024,1536]{1,0:T(8,128)(2,1)S(1)} %constant_dynamic-update-slice_fusion.7), kind=kOutput, calls=%fused_computation.6 | convolution fusion | flops 6445596672 | bytes 13631488 | tf_op jit(solution)/shard_map/td,tw->dw/dot_general | solution.py:891
  651.9 11.3 %convolution_convert_fusion.4.partial = bf16[1024,2048]{1,0:T(8,128)(2,1)} fusion(bf16[1024,1536]{1,0:T(8,128)(2,1)S(1)} %constant_dynamic-update-slice_fusion.7, bf16[2048,1536]{1,0:T(8,128)(2,1)} %all-gather.5.cloned.1.call-done), kind=kOutput, calls=%fused_computation.13 | convolution fusion | flops 6444548096 | bytes 13631488 | tf_op jit(solution)/shard_map/tw,nw->tn/dot_general | solution.py:891
  663.1 20.0 %reduce-scatter.9.cloned.1.call-done = bf16[512,256]{1,0:T(8,128)(2,1)} async-done(((bf16[512,2048]{1,0:T(8,128)(2,1)}), bf16[512,256]{1,0:T(8,128)(2,1)}) %reduce-scatter.9.cloned.1.call-update) | async-done | bytes 262160 | tf_op jit(solution)/shard_map/reduce_scatter | solution.py:895
  684.3 121.0 %back_in.1 = (bf16[4,1024,512]{2,1,0:T(8,128)(2,1)}, f32[4,1024,512]{2,1,0:T(8,128)}, f32[40,128]{1,0:T(8,128)}) custom-call(f32[32]{0:T(128)} %concatenate.44.coeffs, bf16[1024,2048]{1,0:T(8,128)(2,1)} %convolution_convert_fusion.4.partial, bf16[1024,2048]{1,0:T(8,128)(2,1)} %get-tuple-element.68.whole_normal, f32[1024,1]{1,0:T(8,128)} %get-tuple-element.100.scale, ...), custom_call_target="tpu_custom_call" | custom-call | flops 99999997952 | bytes 35676288 | tf_op jit(solution)/shard_map/back_in/pallas_call | solution.py:325
  810.5 6.5 multiply_add_fusion.2
  820.5 6.2 multiply_add_fusion
  (224 shorter events, 129.1 us)
Async XLA Ops:
  7.2 107.5 %all-gather.5.cloned.1.call-start = ((), (), s32[]{:S(2)}) async-start(), calls=%async_computation.4 | async-start | bytes 7077888 | tf_op jit(solution)/shard_map/all_gather | solution.py:933
  9.8 149.8 %all-gather.7.cloned.1.call-start = ((), (), s32[]{:S(2)}) async-start(), calls=%async_computation.5 | async-start | bytes 2359296 | tf_op jit(solution)/shard_map/all_gather | solution.py:933
  10.6 299.5 %all-gather.9.cloned.1.call-start = ((), (), s32[]{:S(2)}) async-start(), calls=%async_computation.6 | async-start | bytes 18874368 | tf_op jit(solution)/shard_map/all_gather | solution.py:933
  14.9 339.0 %all-gather.11.cloned.1.call-start = ((), (), s32[]{:S(2)}) async-start(), calls=%async_computation.7 | async-start | bytes 9437184 | tf_op jit(solution)/shard_map/all_gather | solution.py:933
  103.9 25.2 %collective-permute-start.1 = (bf16[1024,512]{1,0:T(8,128)(2,1)S(1)}, bf16[1024,512]{1,0:T(8,128)(2,1)}, u32[]{:S(2)}, u32[]{:S(2)}) collective-permute-start(bf16[1024,512]{1,0:T(8,128)(2,1)S(1)} %fusion), channel_id=1, source_target_pairs={{1,0},{2,1},{3,2},{5,4},{6,5},{7,6},{9,8},{10,9},{11,10},{13,12},{... | collective-permute-start | bytes 3145736 | tf_op jit(solution)/shard_map/ppermute | solution.py:839
  105.2 25.0 %collective-permute-start = (bf16[1024,512]{1,0:T(8,128)(2,1)S(1)}, bf16[1024,512]{1,0:T(8,128)(2,1)}, u32[]{:S(2)}, u32[]{:S(2)}) collective-permute-start(bf16[1024,512]{1,0:T(8,128)(2,1)S(1)} %fusion), channel_id=1, source_target_pairs={{0,1},{1,2},{2,3},{4,5},{5,6},{6,7},{8,9},{9,10},{10,11},{12,13},{... | collective-permute-start | bytes 3145736 | tf_op jit(solution)/shard_map/ppermute | solution.py:839
  111.8 332.9 %reduce-scatter.5.cloned.1.call-start = ((), (), s32[]{:S(2)}) async-start(), calls=%async_computation.8 | async-start | bytes 9437184 | tf_op jit(solution)/shard_map/reduce_scatter | solution.py:895
  130.2 26.3 %collective-permute-start.2 = (bf16[1024,512]{1,0:T(8,128)(2,1)}, bf16[1024,512]{1,0:T(8,128)(2,1)}, u32[]{:S(2)}, u32[]{:S(2)}) collective-permute-start(bf16[1024,512]{1,0:T(8,128)(2,1)} %collective-permute-done), channel_id=1, source_target_pairs={{0,1},{1,2},{2,3},{4,5},{5,6},{6,7},{8,9},{9,10},{10,11},{12,13},{... | collective-permute-start | bytes 3145736 | tf_op jit(solution)/shard_map/ppermute | solution.py:839
  135.7 23.9 %collective-permute-start.3 = (bf16[1024,512]{1,0:T(8,128)(2,1)}, bf16[1024,512]{1,0:T(8,128)(2,1)}, u32[]{:S(2)}, u32[]{:S(2)}) collective-permute-start(bf16[1024,512]{1,0:T(8,128)(2,1)} %collective-permute-done.1), channel_id=1, source_target_pairs={{1,0},{2,1},{3,2},{5,4},{6,5},{7,6},{9,8},{10,9},{11,10},{13,12},{... | collective-permute-start | bytes 3145736 | tf_op jit(solution)/shard_map/ppermute | solution.py:839
  283.4 14.0 %collective-permute-start.4 = (bf16[1024,512]{1,0:T(8,128)(2,1)}, bf16[1024,512]{1,0:T(8,128)(2,1)}, u32[]{:S(2)}, u32[]{:S(2)}) collective-permute-start(bf16[1024,512]{1,0:T(8,128)(2,1)} %collective-permute-done.2), channel_id=1, source_target_pairs={{0,1},{1,2},{2,3},{4,5},{5,6},{6,7},{8,9},{9,10},{10,11},{12,13},{... | collective-permute-start | bytes 3145736 | tf_op jit(solution)/shard_map/ppermute | solution.py:839
  285.7 21.6 %collective-permute-start.5 = (bf16[1024,512]{1,0:T(8,128)(2,1)}, bf16[1024,512]{1,0:T(8,128)(2,1)S(1)}, u32[]{:S(2)}, u32[]{:S(2)}) collective-permute-start(bf16[1024,512]{1,0:T(8,128)(2,1)} %collective-permute-done.3), channel_id=1, source_target_pairs={{1,0},{2,1},{3,2},{5,4},{6,5},{7,6},{9,8},{10,9},{11,10},{13,12},{... | collective-permute-start | bytes 3145736 | tf_op jit(solution)/shard_map/ppermute | solution.py:839
  367.8 268.5 %reduce-scatter.7.cloned.1.call-start = ((), (), s32[]{:S(2)}) async-start(), calls=%async_computation.9 | async-start | bytes 18874368 | tf_op jit(solution)/shard_map/reduce_scatter | solution.py:895
  370.7 38.8 %collective-permute-start.7 = (bf16[1024,512]{1,0:T(8,128)(2,1)}, bf16[1024,512]{1,0:T(8,128)(2,1)}, u32[]{:S(2)}, u32[]{:S(2)}) collective-permute-start(bf16[1024,512]{1,0:T(8,128)(2,1)} %get-tuple-element.148), channel_id=1, source_target_pairs={{1,0},{2,1},{3,2},{5,4},{6,5},{7,6},{9,8},{10,9},{11,10},{13,12},{... | collective-permute-start | bytes 3145736 | tf_op jit(solution)/shard_map/ppermute | solution.py:862
  371.9 37.6 %collective-permute-start.6 = (bf16[1024,512]{1,0:T(8,128)(2,1)S(1)}, bf16[1024,512]{1,0:T(8,128)(2,1)}, u32[]{:S(2)}, u32[]{:S(2)}) collective-permute-start(bf16[1024,512]{1,0:T(8,128)(2,1)S(1)} %get-tuple-element.149), channel_id=1, source_target_pairs={{0,1},{1,2},{2,3},{4,5},{5,6},{6,7},{8,9},{9,10},{10,11},{12,13},{... | collective-permute-start | bytes 3145736 | tf_op jit(solution)/shard_map/ppermute | solution.py:862
  414.0 30.7 %collective-permute-start.9 = (bf16[1024,512]{1,0:T(8,128)(2,1)}, bf16[1024,512]{1,0:T(8,128)(2,1)S(1)}, u32[]{:S(2)}, u32[]{:S(2)}) collective-permute-start(bf16[1024,512]{1,0:T(8,128)(2,1)} %get-tuple-element.146), channel_id=1, source_target_pairs={{1,0},{2,1},{3,2},{5,4},{6,5},{7,6},{9,8},{10,9},{11,10},{13,12},{... | collective-permute-start | bytes 3145736 | tf_op jit(solution)/shard_map/ppermute | solution.py:862
  415.3 29.4 %collective-permute-start.8 = (bf16[1024,512]{1,0:T(8,128)(2,1)}, bf16[1024,512]{1,0:T(8,128)(2,1)}, u32[]{:S(2)}, u32[]{:S(2)}) collective-permute-start(bf16[1024,512]{1,0:T(8,128)(2,1)} %get-tuple-element.147), channel_id=1, source_target_pairs={{0,1},{1,2},{2,3},{4,5},{5,6},{6,7},{8,9},{9,10},{10,11},{12,13},{... | collective-permute-start | bytes 3145736 | tf_op jit(solution)/shard_map/ppermute | solution.py:862
  447.4 235.7 %reduce-scatter.9.cloned.1.call-start = ((), (), s32[]{:S(2)}) async-start(), calls=%async_computation.10 | async-start | bytes 2359296 | tf_op jit(solution)/shard_map/reduce_scatter | solution.py:895
  454.0 29.3 %collective-permute-start.10 = (bf16[1024,512]{1,0:T(8,128)(2,1)S(1)}, bf16[1024,512]{1,0:T(8,128)(2,1)S(1)}, u32[]{:S(2)}, u32[]{:S(2)}) collective-permute-start(bf16[1024,512]{1,0:T(8,128)(2,1)S(1)} %get-tuple-element.144), channel_id=1, source_target_pairs={{0,1},{1,2},{2,3},{4,5},{5,6},{6,7},{8,9},{9,10},{10,11},{12,13},{... | collective-permute-start | bytes 3145736 | tf_op jit(solution)/shard_map/ppermute | solution.py:862
  456.0 27.3 %collective-permute-start.11 = (bf16[1024,512]{1,0:T(8,128)(2,1)S(1)}, bf16[1024,512]{1,0:T(8,128)(2,1)S(1)}, u32[]{:S(2)}, u32[]{:S(2)}) collective-permute-start(bf16[1024,512]{1,0:T(8,128)(2,1)S(1)} %get-tuple-element.145), channel_id=1, source_target_pairs={{1,0},{2,1},{3,2},{5,4},{6,5},{7,6},{9,8},{10,9},{11,10},{13,12},{... | collective-permute-start | bytes 3145736 | tf_op jit(solution)/shard_map/ppermute | solution.py:862
  640.4 187.6 %reduce-scatter.11.cloned.1.call-start = ((), (), s32[]{:S(2)}) async-start(), calls=%async_computation.11 | async-start | bytes 7077888 | tf_op jit(solution)/shard_map/reduce_scatter | solution.py:895
  684.2 125.7 %copy-start.34 = (f32[2,4,6]{2,1,0:T(4,128)S(1)}, f32[2,4,6]{2,1,0:T(4,128)}, u32[]{:S(2)}) copy-start(f32[2,4,6]{2,1,0:T(4,128)} %param.24) | copy-start | bytes 580
  684.2 125.7 %copy-start.43 = (f32[2,4,6]{2,1,0:T(4,128)S(1)}, f32[2,4,6]{2,1,0:T(4,128)}, u32[]{:S(2)}) copy-start(f32[2,4,6]{2,1,0:T(4,128)} %param.34) | copy-start | bytes 580
  684.2 125.7 %copy-start.44 = (f32[2,4,6]{2,1,0:T(4,128)S(1)}, f32[2,4,6]{2,1,0:T(4,128)}, u32[]{:S(2)}) copy-start(f32[2,4,6]{2,1,0:T(4,128)} %param.29) | copy-start | bytes 580
  684.2 126.3 %copy-start.15 = (f32[2048,256]{1,0:T(8,128)S(1)}, f32[2048,256]{1,0:T(8,128)}, u32[]{:S(2)}) copy-start(f32[2048,256]{1,0:T(8,128)} %param.23) | copy-start | bytes 6291460
  (48 other events, 1334.4 us)
Sparse Core Ops, SparseCore 0:
  10.5 48.3 all-gather.4
  61.3 28.0 all-gather.6
  91.9 89.8 all-gather.8
  184.1 55.9 all-gather.10
  367.9 73.4 reduce-scatter.4
  447.6 114.8 reduce-scatter.6
  640.5 42.5 reduce-scatter.8
  687.1 61.7 reduce-scatter.10

commit v3 on v2

--- a/solution.py
+++ b/solution.py
@@ -38,13 +38,14 @@
     return (jnp.concatenate([cosine, cosine], 1), jnp.concatenate([-sine, sine], 1))
 
 
-def exchange(
-    size, tokens, width, chunk, hop, scatter, gather, prepare, finish, scratch, during=None, rows_too=0
+def line_exchange(
+    size, tokens, width, chunk, hop, scatter, gather, produce, prepare, finish, scratch, during=None, rows_too=0
 ):
-    send, recv, blocks, facts, own_facts, sums_sent, sums_got, blocks_sent, blocks_got, facts_sent, facts_got = scratch
+    recv, blocks, facts, own_facts, sums_sent, sums_got, blocks_sent, blocks_got, facts_sent, facts_got = scratch
     me = lax.axis_index("col")
     chunks = tokens // chunk
     per_group = GROUP // chunk
+    groups = tokens // GROUP
     edge = size - 1
 
     def far(place):
@@ -63,9 +64,12 @@
     def rows(index):
         return pl.ds(pl.multiple_of(index * chunk, chunk), chunk)
 
+    def group_rows(group):
+        return pl.ds(pl.multiple_of(group * GROUP, GROUP), GROUP)
+
     def sum_copy(shard, slot, index, device):
         return remote(
-            send.at[shard, rows(index)],
+            scatter.at[rows(index), pl.ds(shard * width, width)],
             recv.at[slot, rows(index)],
             sums_sent.at[shard, index],
             sums_got.at[slot, index],
@@ -97,6 +101,17 @@
     def inside(index):
         return (index >= 0) & (index < chunks)
 
+    def relay_sum(shard, slot, index, fresh, target):
+        columns = slice(shard * width, (shard + 1) * width)
+
+        @pl.when(jnp.logical_not(fresh))
+        def _():
+            sum_copy(shard, shard, index, other).wait_recv()
+            total = scatter[rows(index), columns].astype(f32) + recv[shard, rows(index)].astype(f32)
+            scatter[rows(index), columns] = total.astype(jnp.bfloat16)
+
+        sum_copy(shard, slot, index, target).start()
+
     def relay_sums(step):
         index = step - me * hop
 
@@ -106,22 +121,8 @@
 
                 @pl.when(shard > me)
                 def _():
-                    mine = scatter[rows(index), shard * width : (shard + 1) * width]
-
-                    @pl.when(me > 0)
-                    def _():
-                        sum_copy(shard, shard, index, other).wait_recv()
-                        total = mine.astype(jnp.float32) + recv[shard, rows(index)].astype(
-                            jnp.float32
-                        )
-                        send[shard, rows(index)] = total.astype(jnp.bfloat16)
-
-                    @pl.when(me == 0)
-                    def _():
-                        send[shard, rows(index)] = mine
-
                     slot = jnp.where(me + 1 == shard, size, shard)
-                    sum_copy(shard, slot, index, right).start()
+                    relay_sum(shard, slot, index, me == 0, right)
 
         back = step - (edge - me) * hop
 
@@ -131,21 +132,7 @@
 
                 @pl.when(shard < me)
                 def _():
-                    mine = scatter[rows(back), shard * width : (shard + 1) * width]
-
-                    @pl.when(me < edge)
-                    def _():
-                        sum_copy(shard, shard, back, other).wait_recv()
-                        total = mine.astype(jnp.float32) + recv[shard, rows(back)].astype(
-                            jnp.float32
-                        )
-                        send[shard, rows(back)] = total.astype(jnp.bfloat16)
-
-                    @pl.when(me == edge)
-                    def _():
-                        send[shard, rows(back)] = mine
-
-                    sum_copy(shard, shard, back, left).start()
+                    relay_sum(shard, shard, back, me == edge, left)
 
     def ready(step):
         index = step - far(me)
@@ -163,16 +150,14 @@
                     sum_copy(0, me, index, other).wait_recv()
 
                 start = pl.multiple_of(me * width, width)
-                total = scatter[rows(index), pl.ds(start, width)].astype(jnp.float32)
-                total = total + jnp.where(me > 0, recv[size, rows(index)].astype(jnp.float32), 0.0)
-                total = total + jnp.where(
-                    me < edge, recv[me, rows(index)].astype(jnp.float32), 0.0
-                )
+                total = scatter[rows(index), pl.ds(start, width)].astype(f32)
+                total = total + jnp.where(me > 0, recv[size, rows(index)].astype(f32), 0.0)
+                total = total + jnp.where(me < edge, recv[me, rows(index)].astype(f32), 0.0)
             else:
                 total = None
             columns, block = prepare(rows(index), total)
             lane = lax.broadcasted_iota(jnp.int32, (chunk, 128), 1)
-            packed = jnp.zeros((chunk, 128), jnp.float32)
+            packed = jnp.zeros((chunk, 128), f32)
             for place, column in enumerate(columns):
                 packed = jnp.where(lane == place, column, packed)
             within = lax.rem(index, per_group)
@@ -213,9 +198,7 @@
                     def _():
                         block_copy(place, index, way, right if way == 0 else left).start()
 
-    longest = 2 * edge * hop if scatter is not None else edge * hop
-    if not gather:
-        longest = edge * hop
+    longest = 2 * edge * hop if scatter is not None and gather else edge * hop
 
     def conclude(step):
         index = step - longest
@@ -229,8 +212,7 @@
                 def _():
                     fact_copy(place, group, other).wait_recv()
 
-            turned = facts[group].T
-            finish(group, pl.ds(pl.multiple_of(group * GROUP, GROUP), GROUP), turned)
+            finish(group, group_rows(group), facts[group].T)
 
     barrier = pltpu.get_barrier_semaphore()
     for place in range(size):
@@ -246,6 +228,10 @@
         def _():
             pl.semaphore_signal(barrier, inc=1, device_id={"row": place}, device_id_type=MESH)
 
+    if scatter is not None:
+        order = sorted(range(size), key=lambda shard: -max(shard, edge - shard))
+        for shard in order:
+            produce(group_rows(0), shard, True)
     pl.semaphore_wait(barrier, size - 1 + max(rows_too - 1, 0))
 
     def step_all(step, carry):
@@ -255,6 +241,15 @@
         if gather:
             relay_blocks(step)
         conclude(step)
+        if scatter is not None:
+            following = step // per_group + 1
+            for part in range(per_group):
+
+                @pl.when((following < groups) & (lax.rem(step, per_group) == part))
+                def _():
+                    for shard in range(part * size // per_group, (part + 1) * size // per_group):
+                        produce(group_rows(following), shard, False)
+
         if during is not None:
 
             @pl.when(inside(step))
@@ -297,7 +292,7 @@
 
         return carry
 
-    lax.fori_loop(0, tokens // GROUP, drain_facts, 0)
+    lax.fori_loop(0, groups, drain_facts, 0)
 
 
 def exchange_scratch(size, tokens, width, chunk, scatter, gather):
@@ -306,11 +301,10 @@
     dma = pltpu.SemaphoreType.DMA
     tiny = (1, chunk, 128)
     return [
-        pltpu.VMEM((size, tokens, width) if scatter else tiny, jnp.bfloat16),
         pltpu.VMEM((size + 1, tokens, width) if scatter else tiny, jnp.bfloat16),
         pltpu.VMEM((size, tokens, width) if gather else tiny, jnp.bfloat16),
-        pltpu.VMEM((groups, 128, 128), jnp.float32),
-        pltpu.VMEM((GROUP, 128), jnp.float32),
+        pltpu.VMEM((groups, 128, 128), f32),
+        pltpu.VMEM((GROUP, 128), f32),
         dma((size, chunks) if scatter else (1, 1)),
         dma((size + 1, chunks) if scatter else (1, 1)),
         dma((2, size, chunks) if gather else (1, 1, 1)),
@@ -320,22 +314,51 @@
     ]
 
 
-def call(body, operands, places, outs, scratch, name, ident):
+def call(body, operands, places, outs, out_places, scratch, name, ident, cost=10**11):
     moved = sum(array.size * array.dtype.itemsize for array in list(operands) + outs)
     return pl.pallas_call(
         body,
         out_shape=outs,
         in_specs=[pl.BlockSpec(memory_space=place) for place in places],
-        out_specs=[pl.BlockSpec(memory_space=pltpu.VMEM)] * len(outs),
+        out_specs=[pl.BlockSpec(memory_space=place) for place in out_places],
         scratch_shapes=scratch,
         compiler_params=pltpu.CompilerParams(
-            collective_id=ident, has_side_effects=True, vmem_limit_bytes=58 * 2**20
+            collective_id=ident, has_side_effects=True, vmem_limit_bytes=60 * 2**20
         ),
-        cost_estimate=pl.CostEstimate(
-            flops=10**11, bytes_accessed=moved, transcendentals=0
-        ),
+        cost_estimate=pl.CostEstimate(flops=cost, bytes_accessed=moved, transcendentals=0),
         name=name,
     )(*operands)
+
+
+def held(*arrays):
+    return [pltpu.VMEM(array.shape, array.dtype) for array in arrays]
+
+
+def start_loads(pairs, sems):
+    copies = [
+        pltpu.make_async_copy(source, target, sems.at[place])
+        for place, (source, target) in enumerate(pairs)
+    ]
+    for copy in copies:
+        copy.start()
+    return copies
+
+
+def group_store(source, target, sems):
+    groups = source.shape[0] // GROUP
+
+    def copy(group):
+        rows = pl.ds(pl.multiple_of(group * GROUP, GROUP), GROUP)
+        return pltpu.make_async_copy(source.at[rows], target.at[rows], sems.at[group])
+
+    def wait_all():
+        def one(group, carry):
+            copy(group).wait()
+            return carry
+
+        lax.fori_loop(0, groups, one, 0)
+
+    return lambda group: copy(group).start(), wait_all
 
 
 def norm_stats(value):
@@ -355,9 +378,37 @@
     return shifts, lax.rsqrt(spread * (1.0 / (size * width)) + EPSILON)
 
 
-def norm_in_kernel(size, chunk, hop, coeffs, streams, whole, scale, *scratch):
+def norm_finish(size, width, blocks, scale, whole, store):
+    def finish(group, rows, turned):
+        shifts, rate = norm_whole(size, width, turned)
+        scale[rows, :] = rate
+        for z in range(size):
+            value = (blocks[z, rows].astype(f32) + shifts[z]) * rate
+            whole[rows, z * width : (z + 1) * width] = value.astype(jnp.bfloat16)
+        store(group)
+
+    return finish
+
+
+def norm_in_kernel(
+    size,
+    chunk,
+    hop,
+    coeffs,
+    streams,
+    grads_in,
+    whole_out,
+    scale,
+    branch_grad,
+    whole,
+    grads,
+    loads,
+    stores,
+    *scratch,
+):
     count, tokens, width = streams.shape
-    blocks = scratch[2]
+    waits = start_loads(((grads_in, grads),), loads)
+    store, wait_stores = group_store(whole, whole_out, stores)
 
     def prepare(rows, total):
         mixed = coeffs[0] * streams[0, rows].astype(f32)
@@ -366,35 +417,81 @@
         mean, center, square = norm_stats(mixed)
         return (mean, square), center.astype(jnp.bfloat16)
 
-    def finish(group, rows, turned):
-        shifts, rate = norm_whole(size, width, turned)
-        scale[rows, :] = rate
-        for z in range(size):
-            value = (blocks[z, rows].astype(f32) + shifts[z]) * rate
-            whole[rows, z * width : (z + 1) * width] = value.astype(jnp.bfloat16)
-
-    exchange(size, tokens, width, chunk, hop, None, True, prepare, finish, scratch)
-
-
-def norm_in(size, streams, coeffs, chunk=64, hop=1):
+    def during(rows):
+        @pl.when(rows.start == 0)
+        def _():
+            waits[0].wait()
+
+        value = coeffs[count] * grads[0, rows].astype(f32)
+        for k in range(1, count):
+            value = value + coeffs[count + k] * grads[k, rows].astype(f32)
+        branch_grad[rows, :] = value.astype(jnp.bfloat16)
+
+    finish = norm_finish(size, width, scratch[1], scale, whole, store)
+    line_exchange(
+        size, tokens, width, chunk, hop, None, True, None, prepare, finish, scratch, during
+    )
+    wait_stores()
+
+
+def norm_in(size, streams, grads, coeffs, chunk=64, hop=1):
     _, tokens, width = streams.shape
+    whole = jax.ShapeDtypeStruct((tokens, size * width), jnp.bfloat16)
     return call(
         functools.partial(norm_in_kernel, size, chunk, hop),
-        (coeffs, streams),
-        (SM, VM),
+        (coeffs, streams, grads),
+        (SM, VM, pl.ANY),
         [
-            jax.ShapeDtypeStruct((tokens, size * width), jnp.bfloat16),
+            whole,
             jax.ShapeDtypeStruct((tokens, 1), f32),
+            jax.ShapeDtypeStruct((tokens, width), jnp.bfloat16),
         ],
-        exchange_scratch(size, tokens, width, chunk, False, True),
+        (pl.ANY, VM, VM),
+        held(whole, grads)
+        + [pltpu.SemaphoreType.DMA((1,)), pltpu.SemaphoreType.DMA((tokens // GROUP,))]
+        + exchange_scratch(size, tokens, width, chunk, False, True),
         "norm_in",
         1,
     )
 
 
-def norm_mid_kernel(size, chunk, hop, coeffs, partial, streams, whole, scale, branch, *scratch):
+def norm_mid_kernel(
+    size,
+    chunk,
+    hop,
+    coeffs,
+    attended_in,
+    rows_in,
+    streams_in,
+    whole_out,
+    scale,
+    branch,
+    attended,
+    weights,
+    streams,
+    scatter,
+    whole,
+    loads,
+    stores,
+    *scratch,
+):
     count, tokens, width = streams.shape
-    blocks = scratch[2]
+    heads = attended.shape[1]
+    own_columns = rows_in.at[:, pl.ds(rows_in.shape[1] - heads, heads)]
+    waits = start_loads(
+        ((attended_in, attended), (own_columns, weights), (streams_in, streams)), loads
+    )
+    store, wait_stores = group_store(whole, whole_out, stores)
+    waits[0].wait()
+    waits[1].wait()
+
+    def produce(rows, shard, first):
+        columns = slice(shard * width, (shard + 1) * width)
+        scatter[rows, columns] = lax.dot_general(
+            attended[rows, :], weights[columns, :], LANES, preferred_element_type=f32
+        ).astype(jnp.bfloat16)
+        if first and shard == size // 2:
+            waits[2].wait()
 
     def prepare(rows, total):
         branch[rows, :] = total
@@ -404,39 +501,92 @@
         mean, center, square = norm_stats(mixed)
         return (mean, square), center.astype(jnp.bfloat16)
 
-    def finish(group, rows, turned):
-        shifts, rate = norm_whole(size, width, turned)
-        scale[rows, :] = rate
-        for z in range(size):
-            value = (blocks[z, rows].astype(f32) + shifts[z]) * rate
-            whole[rows, z * width : (z + 1) * width] = value.astype(jnp.bfloat16)
-
-    exchange(size, tokens, width, chunk, hop, partial, True, prepare, finish, scratch)
-
-
-def norm_mid(size, partial, streams, coeffs, chunk=64, hop=1):
+    finish = norm_finish(size, width, scratch[1], scale, whole, store)
+    line_exchange(size, tokens, width, chunk, hop, scatter, True, produce, prepare, finish, scratch)
+    wait_stores()
+
+
+def norm_mid(size, attended, rows, streams, coeffs, chunk=64, hop=1):
     _, tokens, width = streams.shape
+    weights = jax.ShapeDtypeStruct((size * width, attended.shape[1]), jnp.bfloat16)
+    whole = jax.ShapeDtypeStruct((tokens, size * width), jnp.bfloat16)
     return call(
         functools.partial(norm_mid_kernel, size, chunk, hop),
-        (coeffs, partial, streams),
-        (SM, VM, VM),
+        (coeffs, attended, rows, streams),
+        (SM, pl.ANY, pl.ANY, pl.ANY),
         [
-            jax.ShapeDtypeStruct((tokens, size * width), jnp.bfloat16),
+            whole,
             jax.ShapeDtypeStruct((tokens, 1), f32),
             jax.ShapeDtypeStruct((tokens, width), f32),
         ],
-        exchange_scratch(size, tokens, width, chunk, True, True),
+        (pl.ANY, VM, VM),
+        held(attended, weights, streams, whole, whole)
+        + [pltpu.SemaphoreType.DMA((3,)), pltpu.SemaphoreType.DMA((tokens // GROUP,))]
+        + exchange_scratch(size, tokens, width, chunk, True, True),
         "norm_mid",
         2,
     )
 
 
 def back_mid_kernel(
-    size, chunk, hop, coeffs, partial, grads, whole_normal, scale, whole, inner, *scratch
+    size,
+    chunk,
+    hop,
+    coeffs,
+    gated_in,
+    rows_in,
+    grads_in,
+    normal_in,
+    scale,
+    whole_out,
+    inner_out,
+    gated,
+    weights,
+    grads,
+    whole_normal,
+    scatter,
+    inner,
+    whole,
+    loads,
+    stores,
+    inner_stores,
+    *scratch,
 ):
     count, tokens, width = grads.shape
-    blocks = scratch[2]
+    blocks = scratch[1]
+    hidden = gated.shape[2]
     me = lax.axis_index("col")
+    edge = size - 1
+    order = sorted(range(size), key=lambda shard: -max(shard, edge - shard))
+    pairs = [(gated_in.at[:, pl.ds(0, GROUP)], gated.at[:, pl.ds(0, GROUP)])]
+    for shard in order:
+        shard_rows = pl.ds(shard * width, width)
+        pairs.append((rows_in.at[shard_rows, pl.ds(0, 2 * hidden)], weights.at[shard_rows]))
+    rest = pl.ds(GROUP, tokens - GROUP)
+    pairs = pairs + [
+        (gated_in.at[:, rest], gated.at[:, rest]),
+        (grads_in, grads),
+        (normal_in, whole_normal),
+    ]
+    waits = start_loads(pairs, loads)
+    store, wait_stores = group_store(whole, whole_out, stores)
+    store_inner, wait_inner = group_store(inner, inner_out, inner_stores)
+    waits[0].wait()
+
+    def produce(rows, shard, first):
+        if first:
+            waits[1 + order.index(shard)].wait()
+        shard_rows = slice(shard * width, (shard + 1) * width)
+        total = lax.dot_general(
+            gated[0, rows], weights[shard_rows, :hidden], LANES, preferred_element_type=f32
+        )
+        total = total + lax.dot_general(
+            gated[1, rows], weights[shard_rows, hidden:], LANES, preferred_element_type=f32
+        )
+        scatter[rows, shard_rows] = total.astype(jnp.bfloat16)
+        if first and shard == order[-1]:
+            for wait in waits[1 + size :]:
+                wait.wait()
 
     def own_normal(rows):
         return whole_normal[rows, pl.ds(pl.multiple_of(me * width, width), width)].astype(f32)
@@ -460,39 +610,56 @@
         return (first, second, level, slope), block.astype(jnp.bfloat16)
 
     def finish(group, rows, turned):
-        first = turned[:, 0:1]
-        second = turned[:, 1:2]
-        for z in range(1, size):
-            first = first + turned[:, 8 * z : 8 * z + 1]
-            second = second + turned[:, 8 * z + 1 : 8 * z + 2]
-        first = first * (1.0 / (size * width))
-        second = second * (1.0 / (size * width))
+        first, second = whole_sums(size, width, turned)
         rate = scale[rows, :]
         gain = coeffs[count] * rate
         for z in range(size):
             level = gain * (turned[:, 8 * z + 2 : 8 * z + 3] - first)
             slope = gain * (turned[:, 8 * z + 3 : 8 * z + 4] - second)
             columns = slice(z * width, (z + 1) * width)
-            value = blocks[z, rows].astype(f32) + level + slope * whole_normal[rows, columns].astype(f32)
+            value = blocks[z, rows].astype(f32) + level
+            value = value + slope * whole_normal[rows, columns].astype(f32)
             whole[rows, columns] = value.astype(jnp.bfloat16)
+        store(group)
         inner[rows, :] = rate * (inner[rows, :] - first - second * own_normal(rows))
-
-    exchange(size, tokens, width, chunk, hop, partial, True, prepare, finish, scratch)
-
-
-def back_mid(size, partial, grads, whole_normal, scale, coeffs, chunk=64, hop=1):
+        store_inner(group)
+
+    line_exchange(size, tokens, width, chunk, hop, scatter, True, produce, prepare, finish, scratch)
+    wait_stores()
+    wait_inner()
+
+
+def whole_sums(size, width, turned):
+    first = turned[:, 0:1]
+    second = turned[:, 1:2]
+    for z in range(1, size):
+        first = first + turned[:, 8 * z : 8 * z + 1]
+        second = second + turned[:, 8 * z + 1 : 8 * z + 2]
+    return first * (1.0 / (size * width)), second * (1.0 / (size * width))
+
+
+def back_mid(size, gated, rows, grads, whole_normal, scale, coeffs, chunk=64, hop=1):
     _, tokens, width = grads.shape
+    whole = jax.ShapeDtypeStruct((tokens, size * width), jnp.bfloat16)
+    inner = jax.ShapeDtypeStruct((tokens, width), f32)
+    groups = tokens // GROUP
+    weights = jax.ShapeDtypeStruct((size * width, 2 * gated.shape[2]), jnp.bfloat16)
     return call(
         functools.partial(back_mid_kernel, size, chunk, hop),
-        (coeffs, partial, grads, whole_normal, scale),
-        (SM, VM, VM, VM, VM),
-        [
-            jax.ShapeDtypeStruct((tokens, size * width), jnp.bfloat16),
-            jax.ShapeDtypeStruct((tokens, width), f32),
-        ],
-        exchange_scratch(size, tokens, width, chunk, True, True),
+        (coeffs, gated, rows, grads, whole_normal, scale),
+        (SM,) + (pl.ANY,) * 4 + (VM,),
+        [whole, inner],
+        (pl.ANY, pl.ANY),
+        held(gated, weights, grads, whole_normal, whole, inner, whole)
+        + [
+            pltpu.SemaphoreType.DMA((size + 4,)),
+            pltpu.SemaphoreType.DMA((groups,)),
+            pltpu.SemaphoreType.DMA((groups,)),
+        ]
+        + exchange_scratch(size, tokens, width, chunk, True, True),
         "back_mid",
         3,
+        10**9,
     )
 
 
@@ -510,9 +677,20 @@
     chunk,
     hop,
     coeffs,
-    partial,
-    whole_normal,
+    heads_in,
+    rows_in,
+    normal,
     scale,
+    streams_in,
+    grads_in,
+    branch_one_in,
+    branch_two_in,
+    inner_two_in,
+    final_out,
+    grad_streams_out,
+    whole_products,
+    heads,
+    weights,
     streams,
     grads,
     branch_one,
@@ -520,51 +698,86 @@
     inner_two,
     final,
     grad_streams,
-    whole_sums,
+    scatter,
     inner,
-    sums,
+    products,
     shares,
+    loads,
+    final_stores,
+    stores,
     shares_sent,
     shares_got,
     *scratch,
 ):
     count, tokens, width = streams.shape
-    me = lax.axis_index("col")
     square = count * count
-    sums[...] = jnp.zeros_like(sums)
-
-    def own_normal(rows):
-        return whole_normal[rows, pl.ds(pl.multiple_of(me * width, width), width)].astype(f32)
+    edge = size - 1
+    order = sorted(range(size), key=lambda shard: -max(shard, edge - shard))
+    pairs = [(heads_in.at[pl.ds(0, GROUP)], heads.at[pl.ds(0, GROUP)])]
+    for shard in order:
+        shard_rows = pl.ds(shard * width, width)
+        own_columns = pl.ds(0, heads.shape[1])
+        pairs.append((rows_in.at[shard_rows, own_columns], weights.at[shard_rows]))
+    rest = pl.ds(GROUP, tokens - GROUP)
+    pairs = pairs + [
+        (heads_in.at[rest], heads.at[rest]),
+        (streams_in, streams),
+        (grads_in, grads),
+        (branch_one_in, branch_one),
+        (branch_two_in, branch_two),
+        (inner_two_in, inner_two),
+    ]
+    waits = start_loads(pairs, loads)
+    products[...] = jnp.zeros_like(products)
+    waits[0].wait()
+
+    def produce(rows, shard, first):
+        if first:
+            waits[1 + order.index(shard)].wait()
+        shard_rows = slice(shard * width, (shard + 1) * width)
+        total = lax.dot_general(
+            heads[rows, :], weights[shard_rows, :], LANES, preferred_element_type=f32
+        )
+        scatter[rows, shard_rows] = total.astype(jnp.bfloat16)
+        if first and shard == order[-1]:
+            for wait in waits[1 + size :]:
+                wait.wait()
 
     def prepare(rows, total):
         inner[rows, :] = total
         first = jnp.sum(total, -1, keepdims=True)
-        second = jnp.sum(total * own_normal(rows), -1, keepdims=True)
+        second = jnp.sum(total * normal[rows, :].astype(f32), -1, keepdims=True)
         return (first, second), None
 
+    def store(stream, group):
+        rows = pl.ds(pl.multiple_of(group * GROUP, GROUP), GROUP)
+        return pltpu.make_async_copy(
+            grad_streams.at[stream, rows], grad_streams_out.at[stream, rows], stores.at[stream, group]
+        )
+
     def finish(group, rows, turned):
-        first = turned[:, 0:1]
-        second = turned[:, 1:2]
-        for z in range(1, size):
-            first = first + turned[:, 8 * z : 8 * z + 1]
-            second = second + turned[:, 8 * z + 1 : 8 * z + 2]
-        first = first * (1.0 / (size * width))
-        second = second * (1.0 / (size * width))
-        own = scale[rows, :] * (inner[rows, :] - first - second * own_normal(rows))
+        first, second = whole_sums(size, width, turned)
+        own = scale[rows, :] * (inner[rows, :] - first - second * normal[rows, :].astype(f32))
         below = inner_two[rows, :]
         for i in range(count):
             value = coeffs[square + i] * below + coeffs[square + 3 * count + i] * own
             for k in range(count):
                 value = value + coeffs[i * count + k] * grads[k, rows].astype(f32)
             grad_streams[i, rows] = value
+            store(i, group).start()
             place = square + 3 * count + 1 + i
-            sums[place] = sums[place] + tile_sum(streams[i, rows].astype(f32) * own)
+            products[place] = products[place] + tile_sum(streams[i, rows].astype(f32) * own)
+
+    def store_final(rows, index):
+        return pltpu.make_async_copy(
+            final.at[:, rows], final_out.at[:, rows], final_stores.at[index]
+        )
 
     def during(rows):
         values = [streams[i, rows].astype(f32) for i in range(count)]
         above = [grads[i, rows].astype(f32) for i in range(count)]
         one = branch_one[rows, :]
-        two = branch_two[rows, :]
+        two = branch_two[rows, :].astype(f32)
         below = inner_two[rows, :]
         for j in range(count):
             value = coeffs[square + count + j] * one + coeffs[square + 2 * count + j] * two
@@ -577,35 +790,37 @@
         pairs = pairs + [(a, two) for a in above]
         pairs = pairs + [(one, below)]
         for place, (a, b) in enumerate(pairs):
-            sums[place] = sums[place] + tile_sum(a * b)
+            products[place] = products[place] + tile_sum(a * b)
+        store_final(rows, rows.start // chunk).start()
 
     count_rows = lax.axis_size("row")
-    exchange(
+    line_exchange(
         size,
         tokens,
         width,
         chunk,
         hop,
-        partial,
+        scatter,
         False,
+        produce,
         prepare,
         finish,
         scratch,
         during,
         count_rows,
     )
-    total = jnp.sum(jnp.sum(sums[...], 1), -1, keepdims=True)
-    total = jnp.broadcast_to(total, whole_sums.shape)
+    total = jnp.sum(jnp.sum(products[...], 1), -1, keepdims=True)
+    total = jnp.broadcast_to(total, whole_products.shape)
     for axis, members, base in (("col", size, 0), ("row", count_rows, size)):
         here = lax.axis_index(axis)
 
-        def share_copy(member, target):
+        def share_copy(source, member):
             return pltpu.make_async_remote_copy(
-                src_ref=shares.at[base + here],
-                dst_ref=shares.at[base + here],
+                src_ref=shares.at[base + source],
+                dst_ref=shares.at[base + source],
                 send_sem=shares_sent.at[base + member],
-                recv_sem=shares_got.at[base + here],
-                device_id={axis: target},
+                recv_sem=shares_got.at[base + source],
+                device_id={axis: member},
                 device_id_type=MESH,
             )
 
@@ -614,32 +829,39 @@
 
             @pl.when(member != here)
             def _():
-                share_copy(member, member).start()
+                share_copy(here, member).start()
 
         for member in range(members):
 
             @pl.when(member != here)
             def _():
-                pltpu.make_async_remote_copy(
-                    src_ref=shares.at[base + member],
-                    dst_ref=shares.at[base + member],
-                    send_sem=shares_sent.at[base + member],
-                    recv_sem=shares_got.at[base + member],
-                    device_id={axis: member},
-                    device_id_type=MESH,
-                ).wait()
+                share_copy(member, member).wait()
 
         total = shares[base]
         for member in range(1, members):
             total = total + shares[base + member]
-    whole_sums[...] = total
+    whole_products[...] = total
+
+    def wait_final(index, carry):
+        store_final(pl.ds(pl.multiple_of(index * chunk, chunk), chunk), index).wait()
+        return carry
+
+    lax.fori_loop(0, tokens // chunk, wait_final, 0)
+
+    def wait_streams(group, carry):
+        for i in range(count):
+            store(i, group).wait()
+        return carry
+
+    lax.fori_loop(0, tokens // GROUP, wait_streams, 0)
 
 
 def back_in(
     size,
     coeffs,
-    partial,
-    whole_normal,
+    heads,
+    rows,
+    normal,
     scale,
     streams,
     grads,
@@ -647,16 +869,21 @@
     branch_two,
     inner_two,
     chunk=64,
-    hop=1,
+    hop=2,
 ):
     count, tokens, width = streams.shape
     products = -(-(count * count + 4 * count + 1) // 8) * 8
+    final = jax.ShapeDtypeStruct(streams.shape, jnp.bfloat16)
+    grad_streams = jax.ShapeDtypeStruct(streams.shape, f32)
+    members = size + lax.axis_size("row")
+    dma = pltpu.SemaphoreType.DMA
     return call(
         functools.partial(back_in_kernel, size, chunk, hop),
         (
             coeffs,
-            partial,
-            whole_normal,
+            heads,
+            rows,
+            normal,
             scale,
             streams,
             grads,
@@ -664,22 +891,205 @@
             branch_two,
             inner_two,
         ),
-        (SM,) + (VM,) * 8,
-        [
-            jax.ShapeDtypeStruct(streams.shape, jnp.bfloat16),
-            jax.ShapeDtypeStruct(streams.shape, f32),
-            jax.ShapeDtypeStruct((products, 128), f32),
-        ],
-        [
+        (SM, pl.ANY, pl.ANY, VM, VM) + (pl.ANY,) * 5,
+        [final, grad_streams, jax.ShapeDtypeStruct((products, 128), f32)],
+        (pl.ANY, pl.ANY, VM),
+        held(
+            heads,
+            jax.ShapeDtypeStruct((size * width, heads.shape[1]), jnp.bfloat16),
+            streams,
+            grads,
+            branch_one,
+            branch_two,
+            inner_two,
+            final,
+            grad_streams,
+        )
+        + [
+            pltpu.VMEM((tokens, size * width), jnp.bfloat16),
             pltpu.VMEM((tokens, width), f32),
             pltpu.VMEM((products, 8, 128), f32),
-            pltpu.VMEM((size + lax.axis_size("row"), products, 128), f32),
-            pltpu.SemaphoreType.DMA((size + lax.axis_size("row"),)),
-            pltpu.SemaphoreType.DMA((size + lax.axis_size("row"),)),
+            pltpu.VMEM((members, products, 128), f32),
+            dma((size + 7,)),
+            dma((tokens // chunk,)),
+            dma((count, tokens // GROUP)),
+            dma((members,)),
+            dma((members,)),
         ]
         + exchange_scratch(size, tokens, width, chunk, True, False),
         "back_in",
         4,
+    )
+
+
+def tiled(body, grid, operands, specs, outs, out_specs, scratch, flops, name):
+    moved = sum(array.size * array.dtype.itemsize for array in list(operands) + (list(outs) if isinstance(outs, list) else [outs]))
+    return pl.pallas_call(
+        body,
+        grid=grid,
+        out_shape=outs,
+        in_specs=specs,
+        out_specs=out_specs,
+        scratch_shapes=scratch,
+        compiler_params=pltpu.CompilerParams(vmem_limit_bytes=60 * 2**20),
+        cost_estimate=pl.CostEstimate(flops=flops, bytes_accessed=moved, transcendentals=0),
+        name=name,
+    )(*operands)
+
+
+def gate_kernel(whole, gate_rows, upper_rows, active, by_gate, by_upper):
+    gate = jnp.dot(whole[...], gate_rows[...], preferred_element_type=f32)
+    upper = jnp.dot(whole[...], upper_rows[...], preferred_element_type=f32)
+    sigma = jax.nn.sigmoid(gate)
+    silu = gate * sigma
+    active[...] = (silu * upper).astype(jnp.bfloat16)
+    by_gate[...] = (upper * sigma * (1.0 + gate * (1.0 - sigma))).astype(jnp.bfloat16)
+    by_upper[...] = silu.astype(jnp.bfloat16)
+
+
+def gate_forward(whole, weights, tile=256):
+    tokens, features = whole.shape
+    hidden = weights.shape[1] // 3
+    tile = min(tile, hidden)
+    tiles = hidden // tile
+    out = pl.BlockSpec((tokens, tile), lambda j: (0, j))
+    return tiled(
+        gate_kernel,
+        (tiles,),
+        (whole, weights, weights),
+        [
+            pl.BlockSpec((tokens, features), lambda j: (0, 0)),
+            pl.BlockSpec((features, tile), lambda j: (0, j)),
+            pl.BlockSpec((features, tile), lambda j: (0, j + tiles)),
+        ],
+        [jax.ShapeDtypeStruct((tokens, hidden), jnp.bfloat16)] * 3,
+        [out] * 3,
+        [],
+        4 * tokens * features * hidden,
+        "gate_forward",
+    )
+
+
+def gate_back_kernel(whole, rows, by_gate, by_upper, grads):
+    grad = jnp.dot(whole[...], rows[...], preferred_element_type=f32)
+    grads[0] = (grad * by_gate[...].astype(f32)).astype(jnp.bfloat16)
+    grads[1] = (grad * by_upper[...].astype(f32)).astype(jnp.bfloat16)
+
+
+def gate_back(whole, weights, by_gate, by_upper, tile=512):
+    tokens, features = whole.shape
+    hidden = weights.shape[1] // 3
+    tile = min(tile, hidden)
+    tiles = hidden // tile
+    part = pl.BlockSpec((tokens, tile), lambda j: (0, j))
+    return tiled(
+        gate_back_kernel,
+        (tiles,),
+        (whole, weights, by_gate, by_upper),
+        [
+            pl.BlockSpec((tokens, features), lambda j: (0, 0)),
+            pl.BlockSpec((features, tile), lambda j: (0, 2 * tiles + j)),
+            part,
+            part,
+        ],
+        jax.ShapeDtypeStruct((2, tokens, hidden), jnp.bfloat16),
+        pl.BlockSpec((2, tokens, tile), lambda j: (0, 0, j)),
+        [],
+        2 * tokens * features * hidden,
+        "gate_back",
+    )
+
+
+def outer_kernel(cut, left, right, other_left, other_right, out, turned):
+    step = pl.program_id(0)
+
+    @pl.when(step == 0)
+    def _():
+        turned[...] = left[...].T
+
+    @pl.when(step == cut)
+    def _():
+        turned[...] = other_left[...].T
+
+    @pl.when(step < cut)
+    def _():
+        out[...] = jnp.dot(turned[...], right[...], preferred_element_type=f32).astype(jnp.bfloat16)
+
+    @pl.when(step >= cut)
+    def _():
+        out[...] = jnp.dot(turned[...], other_right[...], preferred_element_type=f32).astype(
+            jnp.bfloat16
+        )
+
+
+def outer(left, right, other_left, other_right, tile=512, name="outer"):
+    tokens, rows = left.shape
+    tile = min(tile, other_right.shape[1])
+    other = other_right.shape[1] // tile
+    if right.ndim == 3:
+        tiles = right.shape[2] // tile
+        cut = right.shape[0] * tiles
+        clip = lambda j: jnp.minimum(j, cut - 1)
+        spec = pl.BlockSpec((None, tokens, tile), lambda j: (clip(j) // tiles, 0, clip(j) % tiles))
+    else:
+        cut = right.shape[1] // tile
+        spec = pl.BlockSpec((tokens, tile), lambda j: (0, jnp.minimum(j, cut - 1)))
+    whole = pl.BlockSpec((tokens, rows), lambda j: (0, 0))
+    return tiled(
+        functools.partial(outer_kernel, cut),
+        (cut + other,),
+        (left, right, other_left, other_right),
+        [whole, spec, whole, pl.BlockSpec((tokens, tile), lambda j: (0, jnp.maximum(j - cut, 0)))],
+        jax.ShapeDtypeStruct((rows, (cut + other) * tile), jnp.bfloat16),
+        pl.BlockSpec((rows, tile), lambda j: (0, j)),
+        [pltpu.VMEM((rows, tokens), jnp.bfloat16)],
+        2 * tokens * rows * (cut + other) * tile,
+        name,
+    )
+
+
+def product_kernel(dims, left, right, out):
+    total = lax.dot_general(left[...], right[...], dims, preferred_element_type=f32)
+    out[...] = total.astype(out.dtype)
+
+
+def product(left, right, start, columns, kind=jnp.bfloat16, tile=512, name="product"):
+    tokens, depth = left.shape
+    tile = min(tile, columns)
+    first = start // tile
+    return tiled(
+        functools.partial(product_kernel, (((1,), (0,)), ((), ()))),
+        (columns // tile,),
+        (left, right),
+        [
+            pl.BlockSpec((tokens, depth), lambda j: (0, 0)),
+            pl.BlockSpec((depth, tile), lambda j: (0, first + j)),
+        ],
+        jax.ShapeDtypeStruct((tokens, columns), kind),
+        pl.BlockSpec((tokens, tile), lambda j: (0, j)),
+        [],
+        2 * tokens * depth * columns,
+        name,
+    )
+
+
+def product_turned(left, right, place, tile=512, name="product_turned"):
+    tokens, depth = left.shape
+    rows = right.shape[0]
+    tile = min(tile, rows)
+    return tiled(
+        functools.partial(product_kernel, LANES),
+        (rows // tile,),
+        (left, right),
+        [
+            pl.BlockSpec((tokens, depth), lambda j: (0, 0)),
+            pl.BlockSpec((tile, depth), lambda j: (j, place)),
+        ],
+        jax.ShapeDtypeStruct((tokens, rows), jnp.bfloat16),
+        pl.BlockSpec((tokens, tile), lambda j: (0, j)),
+        [],
+        2 * tokens * depth * rows,
+        name,
     )
 
 
@@ -736,7 +1146,7 @@
         in_specs=[head(0), head(heads), head(2 * heads)]
         + [fixed(array) for array in (cosine, sine, column, row)],
         out_specs=[head(0)] * 4,
-        compiler_params=pltpu.CompilerParams(vmem_limit_bytes=48 * 2**20),
+        compiler_params=pltpu.CompilerParams(vmem_limit_bytes=60 * 2**20),
         name="attend_forward",
     )(projected, projected, projected, cosine, sine, column, row)
 
@@ -807,7 +1217,7 @@
         in_specs=[head] * 4 + [fixed(array) for array in (cosine, sine, column, row)],
         out_specs=[head] * 3,
         scratch_shapes=[pltpu.VMEM((length, HEAD_DIM), f32)] * 2,
-        compiler_params=pltpu.CompilerParams(vmem_limit_bytes=48 * 2**20),
+        compiler_params=pltpu.CompilerParams(vmem_limit_bytes=60 * 2**20),
         name="attend_back",
     )(queries, key_heads, value_heads, grad_result, cosine, sine, column, row)
     return jnp.concatenate(grads, 1)
@@ -820,47 +1230,90 @@
     return (weight_new, moment_new, average + (weight_new - average) / (STEP + 1))
 
 
+def update_kernel(rate, turned, weight, grad, moment, average, *outs):
+    value = grad[...].astype(f32)
+    results = update(weight[...], value.T if turned else value, moment[...], average[...], rate)
+    for out, result in zip(outs, results):
+        out[...] = result
+
+
+def update_blocks(weight, grad, moment, average, rate, start):
+    turned = weight.ndim == 2
+    rows = grad.shape[0]
+    columns = weight.shape[0] if turned else weight.shape[2]
+    tile = min(columns, 512)
+    tiles = columns // tile
+    first = start // tile
+    if turned:
+        grid = (tiles,)
+        own = pl.BlockSpec((tile, rows), lambda j: (j, 0))
+        place = pl.BlockSpec((rows, tile), lambda j: (0, first + j))
+    else:
+        grid = (weight.shape[0], tiles)
+        own = pl.BlockSpec((None, rows, tile), lambda k, j: (k, 0, j))
+        place = pl.BlockSpec((rows, tile), lambda k, j: (0, first + k * tiles + j))
+    return pl.pallas_call(
+        functools.partial(update_kernel, rate, turned),
+        grid=grid,
+        out_shape=[jax.ShapeDtypeStruct(weight.shape, f32)] * 3,
+        in_specs=[own, place, own, own],
+        out_specs=[own] * 3,
+        compiler_params=pltpu.CompilerParams(vmem_limit_bytes=60 * 2**20),
+        cost_estimate=pl.CostEstimate(
+            flops=10 * weight.size, bytes_accessed=26 * weight.size, transcendentals=0
+        ),
+        name="update",
+    )(weight, grad, moment, average)
+
+
 def tie(*values):
     return lax.optimization_barrier(values)
+
+
+def assemble_kernel(size, *refs):
+    pieces, whole = refs[:-1], refs[-1]
+    width = whole.shape[1] // size
+    me = lax.axis_index("col")
+    for here in range(size):
+
+        @pl.when(me == here)
+        def _():
+            for place in range(size):
+                columns = slice(place * width, (place + 1) * width)
+                whole[:, columns] = pieces[size - 1 + place - here][...]
+
+
+def assemble(pieces):
+    size = (len(pieces) + 1) // 2
+    tokens, width = pieces[0].shape
+    tile = min(256, tokens)
+    return pl.pallas_call(
+        functools.partial(assemble_kernel, size),
+        grid=(tokens // tile,),
+        out_shape=jax.ShapeDtypeStruct((tokens, size * width), pieces[0].dtype),
+        in_specs=[pl.BlockSpec((tile, width), lambda i: (i, 0))] * len(pieces),
+        out_specs=pl.BlockSpec((tile, size * width), lambda i: (i, 0)),
+        compiler_params=pltpu.CompilerParams(vmem_limit_bytes=60 * 2**20),
+        name="assemble",
+    )(*pieces)
 
 
 def line_ways():
     size = lax.axis_size("col")
     up = [(i, i + 1) for i in range(size - 1)]
     down = [(i + 1, i) for i in range(size - 1)]
-    return size, lax.axis_index("col"), up, down
+    return size, up, down
 
 
 def gather_steps(values):
-    size, me, up, down = line_ways()
-    width = values.shape[1]
+    size, up, down = line_ways()
     before, after = [values], [values]
     for _ in range(size - 1):
         step = (lax.ppermute(before[-1], "col", up), lax.ppermute(after[-1], "col", down))
         step = yield step
         before.append(step[0])
         after.append(step[1])
-    row = jnp.concatenate(before[:0:-1] + after, 1)
-    yield lax.dynamic_slice_in_dim(row, (size - 1 - me) * width, size * width, 1)
-
-
-def scatter_steps(partial):
-    size, me, up, down = line_ways()
-    width = partial.shape[1] // size
-
-    def share(place):
-        return lax.dynamic_slice_in_dim(partial, place * width, width, 1)
-
-    first = share(jnp.minimum(me + size - 1, size - 1))
-    last = share(jnp.maximum(me - size + 1, 0))
-    for step in range(1, size):
-        if step > 1:
-            first = share(jnp.minimum(me + size - step, size - 1)).astype(f32) + first.astype(f32)
-            last = share(jnp.maximum(me - size + step, 0)).astype(f32) + last.astype(f32)
-            first = first.astype(jnp.bfloat16)
-            last = last.astype(jnp.bfloat16)
-        first, last = yield (lax.ppermute(first, "col", up), lax.ppermute(last, "col", down))
-    yield share(me).astype(f32) + first.astype(f32) + last.astype(f32)
+    yield assemble(before[:0:-1] + after)
 
 
 def advance(steps, got, *values):
@@ -876,32 +1329,16 @@
     return moved
 
 
-def weighted(coeffs, streams):
-    total = coeffs[0] * streams[0].astype(f32)
-    for index in range(1, len(streams)):
-        total = total + coeffs[index] * streams[index].astype(f32)
-    return total
-
-
 def small_matmul(left, right):
     return jnp.sum(left[:, :, None] * right[None, :, :], 1)
 
 
-def matmul(spec, left, right, kind=jnp.float32):
-    return jnp.einsum(spec, left, right, preferred_element_type=f32).astype(kind)
-
-
-def scatter_rows(grad, axis):
-    return lax.psum_scatter(grad, "row", scatter_dimension=axis, tiled=True).astype(f32)
-
-
-def side_by_side(weights):
-    return jnp.concatenate([weights[k] for k in range(weights.shape[0])], 1)
-
-
-def one_by_one(values, count):
-    width = values.shape[1] // count
-    return jnp.stack([values[:, k * width : (k + 1) * width] for k in range(count)])
+def scatter_rows(grad):
+    return lax.psum_scatter(grad, "row", scatter_dimension=0, tiled=True)
+
+
+def side_by_side(weights, turned):
+    return jnp.concatenate([weights[k] for k in range(weights.shape[0])] + [turned.T], 1)
 
 
 def per_device(
@@ -929,13 +1366,11 @@
     count, length, width = streams.shape
     cosine, sine = rope_tables(segments)
 
-    def gather_rows(weights, axis):
-        return lax.all_gather(weights.astype(low), "row", axis=axis, tiled=True)
-
-    projections = gather_rows(side_by_side(attention_in), 0)
-    output_rows = gather_rows(attention_out, 1)
-    gate_rows = gather_rows(side_by_side(gate_up), 0)
-    down_rows = gather_rows(down_weights, 1)
+    def gather_rows(weights):
+        return lax.all_gather(weights.astype(low), "row", axis=0, tiled=True)
+
+    attention_weights = gather_rows(side_by_side(attention_in, attention_out))
+    hidden_weights = gather_rows(side_by_side(gate_up, down_weights))
 
     one, two = hyper_mix[0], hyper_mix[1]
     across_one, across_two = one[:, 1 : 1 + count], two[:, 1 : 1 + count]
@@ -944,73 +1379,59 @@
     out_one = small_matmul(one[None, :, 1 + count], across_two)[0]
     turn = jnp.sum(one[:, 1 + count] * two[:, 0])
 
-    whole_one, scale_one = norm_in(size, streams, one[:, 0])
-    whole_one, grads_tied = tie(whole_one, cotangent)
-
-    steps = gather_steps(
-        weighted(two[:, 1 + count], [grads_tied[i] for i in range(count)]).astype(low)
-    )
-    got, (projected,) = advance(steps, None, matmul("tn,nw->tw", whole_one, projections))
+    whole_one, scale_one, grad_two = norm_in(
+        size, streams, cotangent, jnp.concatenate([one[:, 0], two[:, 1 + count]])
+    )
+    heads = attention_in.shape[2]
+    steps = gather_steps(grad_two)
+    projected = product(whole_one, attention_weights, 0, 3 * heads, f32, heads, "project_in")
     queries, key_heads, value_heads, attended = attend_forward(
         projected, cosine, sine, segments.T, segments
     )
-    got, (attended,) = advance(steps, got, attended)
-
+    got, (attended,) = advance(steps, None, attended)
     mid_coeffs = jnp.concatenate([in_two, turn[None]])
     whole_two, scale_two, branch_one = norm_mid(
-        size, matmul("tw,wd->td", attended, output_rows, low), streams, mid_coeffs
-    )
+        size, attended, attention_weights, streams, mid_coeffs
+    )
+
     whole_two, *got = tie(whole_two, *got)
-
-    gated = matmul("tn,nw->tw", whole_two, gate_rows)
-    whole_grad_two = finish_line(steps, tuple(got))
-    hidden = gated.shape[1] // 2
-    gate, upper = gated[:, :hidden], gated[:, hidden:]
-    sigma = jax.nn.sigmoid(gate)
-    active = (gate * sigma * upper).astype(low)
-    partial_two = matmul("tw,wd->td", active, down_rows, low)
-    grad_down = matmul("tw,td->wd", active, whole_grad_two, low)
-    grad_down, partial_two, whole_grad_two = tie(grad_down, partial_two, whole_grad_two)
-    grad_down = scatter_rows(grad_down, 1)
-
-    steps = scatter_steps(partial_two)
-    grad_active = matmul("tn,wn->tw", whole_grad_two, down_rows)
-    grad_gate = grad_active * upper * sigma * (1.0 + gate * (1.0 - sigma))
-    grad_upper = grad_active * gate * sigma
-    grad_gated = jnp.concatenate([grad_gate, grad_upper], 1).astype(low)
-    got, (grad_gated,) = advance(steps, None, grad_gated)
-    grad_gate_up = matmul("td,tw->dw", whole_two, grad_gated, low)
-    got, (grad_gate_up, grad_gated) = advance(steps, got, grad_gate_up, grad_gated)
-    grad_gate_up, grad_down = tie(grad_gate_up, grad_down)
-    grad_gate_up = scatter_rows(grad_gate_up, 0)
-    partial_mid = matmul("tw,nw->tn", grad_gated, gate_rows, low)
-    branch_two = finish_line(steps, got)
-    partial_mid, branch_two = tie(partial_mid, branch_two)
+    active, by_gate, by_upper = gate_forward(whole_two, hidden_weights)
+    got, (active,) = advance(steps, tuple(got), active)
+    partial_two = product_turned(active, hidden_weights, 2, name="project_out")
+    got, (partial_two,) = advance(steps, got, partial_two)
+    whole_grad_two = finish_line(steps, got)
+    branch_two = lax.psum_scatter(partial_two, "col", scatter_dimension=1, tiled=True)
+    grad_gated = gate_back(whole_grad_two, hidden_weights, by_gate, by_upper)
+    grad_hidden = outer(whole_two, grad_gated, whole_grad_two, active, name="outer_hidden")
+    grad_hidden, grad_gated = tie(grad_hidden, grad_gated)
+    grad_hidden = scatter_rows(grad_hidden)
     back_coeffs = jnp.concatenate([out_one, turn[None]])
     whole_grad_one, inner_two = back_mid(
-        size, partial_mid, cotangent, whole_two, scale_two, back_coeffs
-    )
-
-    grad_output = matmul("tw,td->wd", attended, whole_grad_one, low)
-    grad_output, whole_grad_one = tie(grad_output, whole_grad_one)
-    grad_output, grad_gate_up = tie(grad_output, grad_gate_up)
-    grad_output = scatter_rows(grad_output, 1)
-    grad_attended = matmul("tn,wn->tw", whole_grad_one, output_rows, low)
+        size, grad_gated, hidden_weights, cotangent, whole_two, scale_two, back_coeffs
+    )
+
+    whole_grad_one, branch_two = tie(whole_grad_one, branch_two)
+    grad_attended = product(
+        whole_grad_one, attention_weights, 3 * heads, heads, low, heads, "back_out"
+    )
     grad_heads = attend_back(
         queries, key_heads, value_heads, grad_attended, cosine, sine, segments.T, segments
     )
-    grad_projections = matmul("td,tw->dw", whole_one, grad_heads, low)
-    grad_projections, grad_heads = tie(grad_projections, grad_heads)
-    grad_projections, grad_output = tie(grad_projections, grad_output)
-    grad_projections = scatter_rows(grad_projections, 0)
+    grad_attention = outer(
+        whole_one, grad_heads, whole_grad_one, attended, name="outer_attention"
+    )
+    grad_attention, grad_heads, grad_hidden = tie(grad_attention, grad_heads, grad_hidden)
+    grad_attention = scatter_rows(grad_attention)
     end_coeffs = jnp.concatenate(
         [through.reshape(-1), in_two, out_one, two[:, 1 + count], one[:, 0]]
     )
+    own_normal = lax.dynamic_slice_in_dim(whole_one, lax.axis_index("col") * width, width, 1)
     final, grad_streams, products = back_in(
         size,
         end_coeffs,
-        matmul("tw,nw->tn", grad_heads, projections, low),
-        whole_one,
+        grad_heads,
+        attention_weights,
+        own_normal,
         scale_one,
         streams,
         cotangent,
@@ -1047,24 +1468,28 @@
         1,
     )
     grad_hyper = jnp.stack([hyper_one, hyper_two])
-    grad_projections = one_by_one(grad_projections, attention_in.shape[0])
-    grad_gate_up = one_by_one(grad_gate_up, gate_up.shape[0])
     tokens_all = length * lax.axis_size("row")
     token_scale = tokens_all ** (-0.5)
     model_rate = D ** (-0.5) * token_scale
-    first = update(
-        attention_in, grad_projections, moment_attention_in, average_attention_in, model_rate
-    )
-    second = update(
-        attention_out, grad_output, moment_attention_out, average_attention_out, model_rate
-    )
-    third = update(gate_up, grad_gate_up, moment_gate_up, average_gate_up, model_rate)
-    fourth = update(
+    first = update_blocks(
+        attention_in, grad_attention, moment_attention_in, average_attention_in, model_rate, 0
+    )
+    second = update_blocks(
+        attention_out,
+        grad_attention,
+        moment_attention_out,
+        average_attention_out,
+        model_rate,
+        attention_in.shape[0] * heads,
+    )
+    third = update_blocks(gate_up, grad_hidden, moment_gate_up, average_gate_up, model_rate, 0)
+    fourth = update_blocks(
         down_weights,
-        grad_down,
+        grad_hidden,
         moment_down_weights,
         average_down_weights,
         FF ** (-0.5) * token_scale,
+        gate_up.shape[0] * gate_up.shape[2],
     )
     fifth = update(
         hyper_mix,

time: 854 us -> 741 us (0.87)
  matrix products: 173 us -> 0 us
  Pallas kernels: 473 us -> 642 us
  other arithmetic: 72.1 us -> 17.9 us
  waiting for transfers between devices: 37.5 us -> 15.5 us
  starting transfers between devices: 35.8 us -> 15.2 us
  local copies, waits for them, and re-layouts: 41 us -> 28.6 us
    dot_general x12 -> x0, matrix products: 173 us -> none  [matmul(): jnp.einsum(spec, left, right, preferred_element_type=f32).astype(kind)]
    pallas_call x0 -> x12, Pallas kernels: none -> 158 us  [the longest x7 126 us: tiled(): pl.pallas_call(body, grid=grid, out_shape=outs, in_specs=specs, out_specs...]
    convert_element_type x10 -> x0, other arithmetic: 25.1 us -> none  [the longest x4 9.24 us: scatter_rows(): lax.psum_scatter(grad, 'row', scatter_dimension=axis, tiled=True)]
    ppermute x6 -> x0, starting transfers between devices: 17.4 us -> none  [the longest x3 13.5 us: scatter_steps(): lax.ppermute(first, 'col', up)]
    add x5 -> x1, other arithmetic: 17.6 us -> 0.61 us  [update(): average + (weight_new - average) / (STEP + 1)]
    reduce_scatter x4 -> x3, waiting for transfers between devices: 20 us -> 8.66 us  [the longest x2 8.64 us: scatter_rows(): return lax.psum_scatter(grad, 'row', scatter_dimension=0, tiled=True)]
    ppermute x3, waiting for transfers between devices: 11.4 us -> 2.33 us  [gather_steps(): lax.ppermute(before[-1], 'col', up)]
    unnamed x113 -> x64, local copies, waits for them, and re-layouts: 27.5 us -> 20.4 us
  transfers between devices with their start and end apart: 20 -> 11, of which waited for: 5 -> 3; matrix products, arithmetic and copies ran while one was open for 28% -> 4% of each run, Pallas kernels for 56% -> 86%
where the time goes in v3:
time: 741 us; the launch traced here: 733 us
  Pallas kernels  642 us (87%)
  local copies, waits for them, and re-layouts  28.6 us (4%)
  other arithmetic  17.9 us (2%)
  waiting for transfers between devices  15.5 us (2%)
  starting transfers between devices  15.2 us (2%)
  between operations  14.5 us (2%)
    pallas_call x4, Pallas kernels, call(): pl.pallas_call(body, out_shape=outs, in_specs=[pl.BlockSpec(memory_space=...  451 us
    pallas_call x7, Pallas kernels, tiled(): pl.pallas_call(body, grid=grid, out_shape=outs, in_specs=specs, out_specs...  126 us
    pallas_call x4, Pallas kernels, update_blocks(): pl.pallas_call(functools.partial(update_kernel, rate, turned), grid=grid,...  26.3 us
    unnamed x64, local copies, waits for them, and re-layouts  20.4 us
    pallas_call x1, Pallas kernels, attend_back(): pl.pallas_call(functools.partial(attend_back_kernel, block), grid=(heads,...  17.8 us
    pallas_call x1, Pallas kernels, attend_forward(): pl.pallas_call(functools.partial(attend_forward_kernel, block), grid=(hea...  15.1 us
  transfers between devices with their start and end apart: 11, of which 3 were waited for; matrix products, arithmetic and copies ran while one was open for 4% of the time, Pallas kernels for 86%

profile of v3, /device:TPU:0, one launch (start us, length us, event | category | flops | bytes accessed | tf_op | source)
XLA Modules:
  0.0 733.2 jit_solution(9015628827905935778)
XLA Ops:
  18.2 83.4 %norm_in.1 = (bf16[1024,2048]{1,0:T(8,128)(2,1)}, f32[1024,1]{1,0:T(8,128)}, bf16[1024,512]{1,0:T(8,128)(2,1)}) custom-call(f32[8]{0:T(128)} %pad_maximum_fusion.4.coeffs, bf16[4,1024,512]{2,1,0:T(8,128)(2,1)} %streams_in.3, bf16[4,1024,512]{2,1,0:T(8,128)(2,1)} %grads_in.5), custom_call_target="tpu_custom_call" | custom-call | flops 99999997952 | bytes 13635616 | tf_op jit(solution)/shard_map/norm_in/pallas_call | solution.py:319
  103.0 4.6 collective-permute-start
  115.8 11.2 %project_in.1.query.key.value = f32[1024,1536]{1,0:T(8,128)} custom-call(bf16[1024,2048]{1,0:T(8,128)(2,1)} %get-tuple-element.69.left, bf16[2048,2048]{1,0:T(8,128)(2,1)} %all-gather.3.cloned.1.call-done.right.rows_in), custom_call_target="tpu_custom_call" | custom-call | flops 6442450944 | bytes 18874368 | tf_op jit(solution)/shard_map/project_in/pallas_call | solution.py:927
  127.1 15.1 %attend_forward.1 = (bf16[1024,512]{1,0:T(8,128)(2,1)}, bf16[1024,512]{1,0:T(8,128)(2,1)}, bf16[1024,512]{1,0:T(8,128)(2,1)}, bf16[1024,512]{1,0:T(8,128)(2,1)}) custom-call(f32[1024,1536]{1,0:T(8,128)} %project_in.1.query.key.value, f32[1024,1536]{1,0:T(8,128)} %project_in.1.query.key.value, f32[1024,1536]{1,0:T(8,128)} %project_in.1.query.key.value, ...), custom_call_target="tpu_custom_call" | custom-call | tf_op jit(solution)/shard_map/attend_forward/pallas_call | solution.py:1142
  142.1 116.9 %norm_mid.1 = (bf16[1024,2048]{1,0:T(8,128)(2,1)}, f32[1024,1]{1,0:T(8,128)}, f32[1024,512]{1,0:T(8,128)}) custom-call(f32[5]{0:T(128)} %pad_maximum_fusion.6.coeffs, bf16[1024,512]{1,0:T(8,128)(2,1)} %get-tuple-element.75.attended_in.other_right, bf16[2048,2048]{1,0:T(8,128)(2,1)} %all-gather.3.cloned.1.call-done.right.rows_in, bf16[4,1024,512]{2,1,0:T(8,128)(2,1)} %streams_in.3), custom_call_target="tpu_custom_call" | custom-call | flops 99999997952 | bytes 19927060 | tf_op jit(solution)/shard_map/norm_mid/pallas_call | solution.py:319
  261.8 24.5 %gate_forward.1 = (bf16[1024,2048]{1,0:T(8,128)(2,1)}, bf16[1024,2048]{1,0:T(8,128)(2,1)}, bf16[1024,2048]{1,0:T(8,128)(2,1)}) custom-call(bf16[1024,2048]{1,0:T(8,128)(2,1)} %get-tuple-element.79.whole.left.normal_in, bf16[2048,6144]{1,0:T(8,128)(2,1)} %all-gather.5.cloned.1.call-done.gate_rows.upper_rows.right.rows.rows_in, ...), custom_call_target="tpu_custom_call" | custom-call | flops 17179869184 | bytes 67108864 | tf_op jit(solution)/shard_map/gate_forward/pallas_call | solution.py:927
  286.3 4.6 collective-permute-start.4
  292.2 13.4 %project_out.1 = bf16[1024,2048]{1,0:T(8,128)(2,1)} custom-call(bf16[1024,2048]{1,0:T(8,128)(2,1)} %get-tuple-element.85.left.other_right, bf16[2048,6144]{1,0:T(8,128)(2,1)} %all-gather.5.cloned.1.call-done.gate_rows.upper_rows.right.rows.rows_in), custom_call_target="tpu_custom_call" | custom-call | flops 8589934592 | bytes 33554432 | tf_op jit(solution)/shard_map/project_out/pallas_call | solution.py:927
  307.9 4.4 collective-permute-done.5.refs_6_
  313.3 5.4 assemble.1.whole.other_left
  318.7 16.1 %gate_back.1.right.gated_in = bf16[2,1024,2048]{2,1,0:T(8,128)(2,1)} custom-call(bf16[1024,2048]{1,0:T(8,128)(2,1)} %assemble.1.whole.other_left, bf16[2048,6144]{1,0:T(8,128)(2,1)} %all-gather.5.cloned.1.call-done.gate_rows.upper_rows.right.rows.rows_in, bf16[1024,2048]{1,0:T(8,128)(2,1)} %get-tuple-element.88.by_gate, ...), custom_call_target="tpu_custom_call" | custom-call | flops 8589934592 | bytes 46137344 | tf_op jit(solution)/shard_map/gate_back/pallas_call | solution.py:927
  334.7 36.9 %outer_hidden.1 = bf16[2048,6144]{1,0:T(8,128)(2,1)} custom-call(bf16[1024,2048]{1,0:T(8,128)(2,1)} %get-tuple-element.79.whole.left.normal_in, bf16[2,1024,2048]{2,1,0:T(8,128)(2,1)} %gate_back.1.right.gated_in, bf16[1024,2048]{1,0:T(8,128)(2,1)} %assemble.1.whole.other_left, bf16[1024,2048]{1,0:T(8,128)(2,1)} %get-tuple-element.85.left.other_right), custom_call_target="tpu_custom_call" | custom-call | flops 25769803776 | bytes 46137344 | tf_op jit(solution)/shard_map/outer_hidden/pallas_call | solution.py:927
  373.7 129.7 %back_mid.1 = (bf16[1024,2048]{1,0:T(8,128)(2,1)}, f32[1024,512]{1,0:T(8,128)}) custom-call(f32[5]{0:T(128)} %pad_maximum_fusion.5.coeffs, bf16[2,1024,2048]{2,1,0:T(8,128)(2,1)} %gate_back.1.right.gated_in, bf16[2048,6144]{1,0:T(8,128)(2,1)} %all-gather.5.cloned.1.call-done.gate_rows.upper_rows.right.rows.rows_in, bf16[4,1024,512]{2,1,0:T(8,128)(2,1)} %grads_in.5, ...), custom_call_target="tpu_custom_call" | custom-call | flops 1000000000 | bytes 48238612 | tf_op jit(solution)/shard_map/back_mid/pallas_call | solution.py:319
  503.4 6.2 back_out.1.grad_result
  509.6 17.8 %attend_back.1 = (bf16[1024,512]{1,0:T(8,128)(2,1)}, bf16[1024,512]{1,0:T(8,128)(2,1)}, bf16[1024,512]{1,0:T(8,128)(2,1)}) custom-call(bf16[1024,512]{1,0:T(8,128)(2,1)} %get-tuple-element.70.queries, bf16[1024,512]{1,0:T(8,128)(2,1)} %get-tuple-element.71.key_heads, bf16[1024,512]{1,0:T(8,128)(2,1)} %get-tuple-element.72.value_heads, ...), custom_call_target="tpu_custom_call" | custom-call | tf_op jit(solution)/shard_map/attend_back/pallas_call | solution.py:1213
  532.0 18.0 %outer_attention.1 = bf16[2048,2048]{1,0:T(8,128)(2,1)} custom-call(bf16[1024,2048]{1,0:T(8,128)(2,1)} %get-tuple-element.69.left, bf16[1024,1536]{1,0:T(8,128)(2,1)} %copy-done.7, bf16[1024,2048]{1,0:T(8,128)(2,1)} %get-tuple-element.94.left.other_left, bf16[1024,512]{1,0:T(8,128)(2,1)} %get-tuple-element.75.attended_in.other_right), custom_call_target="tpu_custom_call" | custom-call | flops 8589934592 | bytes 20971520 | tf_op jit(solution)/shard_map/outer_attention/pallas_call | solution.py:927
  550.1 8.6 %reduce-scatter.6.cloned.1.call-done.grad = bf16[256,6144]{1,0:T(8,128)(2,1)} async-done(((bf16[2048,6144]{1,0:T(8,128)(2,1)}), bf16[256,6144]{1,0:T(8,128)(2,1)}) %reduce-scatter.6.cloned.1.call-update) | async-done | bytes 3145744 | tf_op jit(solution)/shard_map/reduce_scatter | solution.py:1337
  561.9 120.7 %back_in.1 = (bf16[4,1024,512]{2,1,0:T(8,128)(2,1)}, f32[4,1024,512]{2,1,0:T(8,128)}, f32[40,128]{1,0:T(8,128)}) custom-call(f32[32]{0:T(128)} %concatenate.40.coeffs, bf16[1024,1536]{1,0:T(8,128)(2,1)} %copy-done.7, bf16[2048,2048]{1,0:T(8,128)(2,1)} %all-gather.3.cloned.1.call-done.right.rows_in, bf16[1024,512]{1,0:T(8,128)(2,1)} %constant_dynamic-slice_fusion.normal, ...), custom_call_target="tpu_custom_call" | custom-call | flops 99999997952 | bytes 38822016 | tf_op jit(solution)/shard_map/back_in/pallas_call | solution.py:319
  686.2 6.3 update.7
  692.5 11.6 %update.6 = (f32[2,256,2048]{2,1,0:T(8,128)}, f32[2,256,2048]{2,1,0:T(8,128)}, f32[2,256,2048]{2,1,0:T(8,128)}) custom-call(f32[2,256,2048]{2,1,0:T(8,128)} %weight.6, bf16[256,6144]{1,0:T(8,128)(2,1)} %reduce-scatter.6.cloned.1.call-done.grad, f32[2,256,2048]{2,1,0:T(8,128)} %moment.6, f32[2,256,2048]{2,1,0:T(8,128)} %average.6), custom_call_target="tpu_custom_call" | custom-call | flops 10485760 | bytes 27262976 | tf_op jit(solution)/shard_map/update/pallas_call | solution.py:1255
  705.8 2.8 update.5
  708.6 5.6 update.4
  714.2 4.5 copy.61
  718.7 7.8 %copy.62 = f32[4,1024,512]{2,1,0:T(8,128)} copy(f32[4,1024,512]{2,1,0:T(8,128)} %get-tuple-element.175) | data formatting | bytes 16777216
  (132 shorter events, 42.7 us)
Async XLA Ops:
  7.2 108.6 %all-gather.3.cloned.1.call-start = ((), (), s32[]{:S(2)}) async-start(), calls=%async_computation.3 | async-start | bytes 9437184 | tf_op jit(solution)/shard_map/all_gather | solution.py:1370
  11.3 250.5 %all-gather.5.cloned.1.call-start = ((), (), s32[]{:S(2)}) async-start(), calls=%async_computation.4 | async-start | bytes 28311552 | tf_op jit(solution)/shard_map/all_gather | solution.py:1370
  16.4 487.0 %reduce-scatter.4.cloned.1.call-start = ((), (), s32[]{:S(2)}) async-start(), calls=%async_computation.5 | async-start | bytes 5242880 | tf_op jit(solution)/shard_map/reduce_scatter | solution.py:1403
  17.1 92.6 %copy-start.9 = (f32[4,6]{1,0:T(4,128)}, f32[4,6]{1,0:T(4,128)S(1)}, u32[]{:S(2)}) copy-start(f32[4,6]{1,0:T(4,128)S(1)} %get-tuple-element.144) | copy-start | bytes 292
  17.3 84.4 %copy-start.25 = (f32[4]{0:T(128)}, f32[4]{0:T(128)S(1)}, u32[]{:S(2)}) copy-start(f32[4]{0:T(128)S(1)} %get-tuple-element.125) | copy-start | bytes 52
  17.3 91.8 %copy-start.19 = (f32[4]{0:T(128)}, f32[4]{0:T(128)S(1)}, u32[]{:S(2)}) copy-start(f32[4]{0:T(128)S(1)} %get-tuple-element.126) | copy-start | bytes 52
  17.5 84.2 %copy-start.27 = (f32[4]{0:T(128)}, f32[4]{0:T(128)S(1)}, u32[]{:S(2)}) copy-start(f32[4]{0:T(128)S(1)} %get-tuple-element.127) | copy-start | bytes 52
  17.5 92.3 %copy-start.17 = (f32[4]{0:T(128)}, f32[4]{0:T(128)S(1)}, u32[]{:S(2)}) copy-start(f32[4]{0:T(128)S(1)} %get-tuple-element.128) | copy-start | bytes 52
  18.2 89.3 %copy-start.8 = (s32[1,1024]{1,0:T(1,128)S(1)}, s32[1,1024]{1,0:T(1,128)}, u32[]{:S(2)}) copy-start(s32[1,1024]{1,0:T(1,128)} %row.3) | copy-start | bytes 12292
  101.7 40.5 %collective-permute-start.1 = (bf16[1024,512]{1,0:T(8,128)(2,1)}, bf16[1024,512]{1,0:T(8,128)(2,1)S(1)}, u32[]{:S(2)}, u32[]{:S(2)}) collective-permute-start(bf16[1024,512]{1,0:T(8,128)(2,1)} %get-tuple-element.73.refs_3_), channel_id=1, source_target_pairs={{1,0},{2,1},{3,2},{5,4},{6,5},{7,6},{9,8},{10,9},{11,10},{13,12},{... | collective-permute-start | bytes 3145736 | tf_op jit(solution)/shard_map/ppermute | solution.py:1312
  103.0 39.2 %collective-permute-start = (bf16[1024,512]{1,0:T(8,128)(2,1)}, bf16[1024,512]{1,0:T(8,128)(2,1)S(1)}, u32[]{:S(2)}, u32[]{:S(2)}) collective-permute-start(bf16[1024,512]{1,0:T(8,128)(2,1)} %get-tuple-element.73.refs_3_), channel_id=1, source_target_pairs={{0,1},{1,2},{2,3},{4,5},{5,6},{6,7},{8,9},{9,10},{10,11},{12,13},{... | collective-permute-start | bytes 3145736 | tf_op jit(solution)/shard_map/ppermute | solution.py:1312
  142.1 118.3 %copy-start.2 = (bf16[1024,512]{1,0:T(8,128)(2,1)}, bf16[1024,512]{1,0:T(8,128)(2,1)S(1)}, u32[]{:S(2)}) copy-start(bf16[1024,512]{1,0:T(8,128)(2,1)S(1)} %collective-permute-done.1.refs_4_) | copy-start | bytes 3145732
  142.1 116.9 %copy-start.3 = (bf16[1024,512]{1,0:T(8,128)(2,1)}, bf16[1024,512]{1,0:T(8,128)(2,1)S(1)}, u32[]{:S(2)}) copy-start(bf16[1024,512]{1,0:T(8,128)(2,1)S(1)} %collective-permute-done.refs_2_) | copy-start | bytes 3145732
  259.1 27.2 %collective-permute-start.2 = (bf16[1024,512]{1,0:T(8,128)(2,1)S(1)}, bf16[1024,512]{1,0:T(8,128)(2,1)S(1)}, u32[]{:S(2)}, u32[]{:S(2)}) collective-permute-start(bf16[1024,512]{1,0:T(8,128)(2,1)S(1)} %collective-permute-done.refs_2_), channel_id=1, source_target_pairs={{0,1},{1,2},{2,3},{4,5},{5,6},{6,7},{8,9},{9,10},{10,11},{12,13},{... | collective-permute-start | bytes 3145736 | tf_op jit(solution)/shard_map/ppermute | solution.py:1312
  260.5 25.8 %collective-permute-start.3 = (bf16[1024,512]{1,0:T(8,128)(2,1)S(1)}, bf16[1024,512]{1,0:T(8,128)(2,1)}, u32[]{:S(2)}, u32[]{:S(2)}) collective-permute-start(bf16[1024,512]{1,0:T(8,128)(2,1)S(1)} %collective-permute-done.1.refs_4_), channel_id=1, source_target_pairs={{1,0},{2,1},{3,2},{5,4},{6,5},{7,6},{9,8},{10,9},{11,10},{13,12},{... | collective-permute-start | bytes 3145736 | tf_op jit(solution)/shard_map/ppermute | solution.py:1312
  286.3 19.3 %copy-start.4 = (bf16[1024,512]{1,0:T(8,128)(2,1)}, bf16[1024,512]{1,0:T(8,128)(2,1)S(1)}, u32[]{:S(2)}) copy-start(bf16[1024,512]{1,0:T(8,128)(2,1)S(1)} %collective-permute-done.2.refs_1_) | copy-start | bytes 3145732
  286.3 21.6 %collective-permute-start.4 = (bf16[1024,512]{1,0:T(8,128)(2,1)S(1)}, bf16[1024,512]{1,0:T(8,128)(2,1)S(1)}, u32[]{:S(2)}, u32[]{:S(2)}) collective-permute-start(bf16[1024,512]{1,0:T(8,128)(2,1)S(1)} %collective-permute-done.2.refs_1_), channel_id=1, source_target_pairs={{0,1},{1,2},{2,3},{4,5},{5,6},{6,7},{8,9},{9,10},{10,11},{12,13},{... | collective-permute-start | bytes 3145736 | tf_op jit(solution)/shard_map/ppermute | solution.py:1312
  290.9 21.4 %collective-permute-start.5 = (bf16[1024,512]{1,0:T(8,128)(2,1)}, bf16[1024,512]{1,0:T(8,128)(2,1)S(1)}, u32[]{:S(2)}, u32[]{:S(2)}) collective-permute-start(bf16[1024,512]{1,0:T(8,128)(2,1)} %collective-permute-done.3.refs_5_), channel_id=1, source_target_pairs={{1,0},{2,1},{3,2},{5,4},{6,5},{7,6},{9,8},{10,9},{11,10},{13,12},{... | collective-permute-start | bytes 3145736 | tf_op jit(solution)/shard_map/ppermute | solution.py:1312
  312.3 246.4 %reduce-scatter.6.cloned.1.call-start = ((), (), s32[]{:S(2)}) async-start(), calls=%async_computation.6 | async-start | bytes 28311552 | tf_op jit(solution)/shard_map/reduce_scatter | solution.py:1337
  371.7 334.1 %reduce-scatter.8.cloned.1.call-start = ((), (), s32[]{:S(2)}) async-start(), calls=%async_computation.7 | async-start | bytes 9437184 | tf_op jit(solution)/shard_map/reduce_scatter | solution.py:1337
  561.9 122.8 %copy-start.10 = (f32[4,6]{1,0:T(4,128)S(1)}, f32[4,6]{1,0:T(4,128)}, u32[]{:S(2)}) copy-start(f32[4,6]{1,0:T(4,128)} %copy-done.9) | copy-start | bytes 292
  692.5 12.7 %copy-start.14 = (f32[2,4,6]{2,1,0:T(4,128)S(1)}, f32[2,4,6]{2,1,0:T(4,128)}, u32[]{:S(2)}) copy-start(f32[2,4,6]{2,1,0:T(4,128)} %param.24) | copy-start | bytes 580
  692.5 12.7 %copy-start.21 = (f32[2,4,6]{2,1,0:T(4,128)S(1)}, f32[2,4,6]{2,1,0:T(4,128)}, u32[]{:S(2)}) copy-start(f32[2,4,6]{2,1,0:T(4,128)} %param.34) | copy-start | bytes 580
  692.5 12.7 %copy-start.22 = (f32[2,4,6]{2,1,0:T(4,128)S(1)}, f32[2,4,6]{2,1,0:T(4,128)}, u32[]{:S(2)}) copy-start(f32[2,4,6]{2,1,0:T(4,128)} %param.29) | copy-start | bytes 580
  (16 other events, 73.5 us)
Sparse Core Ops, SparseCore 0:
  11.4 57.0 all-gather.2
  71.0 125.4 all-gather.4
  312.5 81.7 reduce-scatter.3
  398.2 160.4 reduce-scatter.5
  563.0 71.2 reduce-scatter.7

commit v4 on v3

--- a/solution.py
+++ b/solution.py
@@ -21,6 +21,8 @@
 MESH = pl.DeviceIdType.MESH
 VM, SM = pltpu.VMEM, pltpu.SMEM
 f32 = jnp.float32
+LONGEST = 512
+LOG2E = 1.4426950408889634
 LANES = (((1,), (1,)), ((), ()))
 ROWS = (((0,), (0,)), ((), ()))
 
@@ -34,8 +36,7 @@
     places = index - lax.cummax(starts)
     rates = 10000.0 ** (-2.0 * jnp.arange(HEAD_DIM // 2).astype(jnp.float32) / HEAD_DIM)
     angle = places[:, None].astype(jnp.float32) * rates
-    cosine, sine = jnp.cos(angle), jnp.sin(angle)
-    return (jnp.concatenate([cosine, cosine], 1), jnp.concatenate([-sine, sine], 1))
+    return (jnp.cos(angle), jnp.sin(angle))
 
 
 def line_exchange(
@@ -48,8 +49,11 @@
     groups = tokens // GROUP
     edge = size - 1
 
+    hop, wait_hop, pass_hop = hop
+
     def far(place):
-        return jnp.maximum(place, edge - place) * hop if scatter is not None else place * 0
+        lag = jnp.maximum(place, edge - place) * hop + wait_hop
+        return lag if scatter is not None else place * 0
 
     def remote(source, target, sent, got, device):
         return pltpu.make_async_remote_copy(
@@ -187,7 +191,7 @@
     def relay_blocks(step):
         for near in range(1, size):
             for way, place in ((0, me - near), (1, me + near)):
-                index = step - far(place) - near * hop
+                index = step - far(place) - near * pass_hop
 
                 @pl.when((place >= 0) & (place < size) & inside(index))
                 def _():
@@ -198,7 +202,7 @@
                     def _():
                         block_copy(place, index, way, right if way == 0 else left).start()
 
-    longest = 2 * edge * hop if scatter is not None and gather else edge * hop
+    longest = (edge * hop + wait_hop if scatter is not None else 0) + edge * pass_hop
 
     def conclude(step):
         index = step - longest
@@ -390,42 +394,92 @@
     return finish
 
 
+def mixings(mix):
+    count = mix.shape[1]
+    span = range(count)
+
+    def dot(left, right):
+        total = left[0] * right[0]
+        for a, b in zip(left[1:], right[1:]):
+            total = total + a * b
+        return total
+
+    across_one = [[mix[0, k, 1 + i] for i in span] for k in span]
+    across_two = [[mix[1, i, 1 + j] for i in span] for j in span]
+    through = [[dot(across_one[k], across_two[j]) for j in span] for k in span]
+    second = [mix[1, i, 0] for i in span]
+    outward = [mix[0, i, 1 + count] for i in span]
+    in_two = [dot(across_one[k], second) for k in span]
+    out_one = [dot(outward, across_two[j]) for j in span]
+    return through, in_two, out_one, dot(outward, second)
+
+
 def norm_in_kernel(
     size,
     chunk,
     hop,
-    coeffs,
+    mix,
     streams,
     grads_in,
+    gate_in,
+    down_in,
     whole_out,
     scale,
     branch_grad,
+    products,
+    packed,
     whole,
     grads,
+    gate_up,
+    down,
     loads,
     stores,
     *scratch,
 ):
     count, tokens, width = streams.shape
-    waits = start_loads(((grads_in, grads),), loads)
+    kinds, _, hidden = gate_up.shape
+    tile = min(512, hidden)
+    tiles = hidden // tile
+    into = [mix[0, k, 0] for k in range(count)]
+    onto = [mix[1, k, 1 + count] for k in range(count)]
+    products[...] = jnp.zeros_like(products)
+    waits = start_loads(((grads_in, grads), (gate_in, gate_up), (down_in, down)), loads)
     store, wait_stores = group_store(whole, whole_out, stores)
 
     def prepare(rows, total):
-        mixed = coeffs[0] * streams[0, rows].astype(f32)
+        mixed = into[0] * streams[0, rows].astype(f32)
         for k in range(1, count):
-            mixed = mixed + coeffs[k] * streams[k, rows].astype(f32)
+            mixed = mixed + into[k] * streams[k, rows].astype(f32)
         mean, center, square = norm_stats(mixed)
         return (mean, square), center.astype(jnp.bfloat16)
 
     def during(rows):
         @pl.when(rows.start == 0)
         def _():
-            waits[0].wait()
-
-        value = coeffs[count] * grads[0, rows].astype(f32)
+            for wait in waits:
+                wait.wait()
+
+        for piece in range((kinds + 1) * tiles):
+
+            @pl.when(rows.start == piece * chunk)
+            def _():
+                kind, start = piece // tiles, piece % tiles * tile
+                if kind < kinds:
+                    value = gate_up[kind, :, start : start + tile]
+                else:
+                    value = down[start : start + tile, :].T
+                packed[:, piece * tile : (piece + 1) * tile] = value.astype(jnp.bfloat16)
+
+        above = [grads[k, rows].astype(f32) for k in range(count)]
+        value = onto[0] * above[0]
         for k in range(1, count):
-            value = value + coeffs[count + k] * grads[k, rows].astype(f32)
+            value = value + onto[k] * above[k]
         branch_grad[rows, :] = value.astype(jnp.bfloat16)
+        for i in range(count):
+            own = streams[i, rows].astype(f32)
+            for k in range(count):
+                place = i * count + k
+                products[place] = products[place] + tile_sum(own * above[k])
 
     finish = norm_finish(size, width, scratch[1], scale, whole, store)
     line_exchange(
@@ -434,21 +488,25 @@
     wait_stores()
 
 
-def norm_in(size, streams, grads, coeffs, chunk=64, hop=1):
+def norm_in(size, streams, grads, gate_up, down, mix, chunk=64, hop=(1, 0, 1)):
     _, tokens, width = streams.shape
     whole = jax.ShapeDtypeStruct((tokens, size * width), jnp.bfloat16)
     return call(
         functools.partial(norm_in_kernel, size, chunk, hop),
-        (coeffs, streams, grads),
-        (SM, VM, pl.ANY),
+        (mix, streams, grads, gate_up, down),
+        (SM, VM, pl.ANY, pl.ANY, pl.ANY),
         [
             whole,
             jax.ShapeDtypeStruct((tokens, 1), f32),
             jax.ShapeDtypeStruct((tokens, width), jnp.bfloat16),
+            jax.ShapeDtypeStruct((streams.shape[0] * grads.shape[0], 8, 128), f32),
+            jax.ShapeDtypeStruct(
+                (gate_up.shape[1], (gate_up.shape[0] + 1) * gate_up.shape[2]), jnp.bfloat16
+            ),
         ],
-        (pl.ANY, VM, VM),
-        held(whole, grads)
-        + [pltpu.SemaphoreType.DMA((1,)), pltpu.SemaphoreType.DMA((tokens // GROUP,))]
+        (pl.ANY, VM, VM, VM, VM),
+        held(whole, grads, gate_up, down)
+        + [pltpu.SemaphoreType.DMA((3,)), pltpu.SemaphoreType.DMA((tokens // GROUP,))]
         + exchange_scratch(size, tokens, width, chunk, False, True),
         "norm_in",
         1,
@@ -459,7 +517,7 @@
     size,
     chunk,
     hop,
-    coeffs,
+    mix,
     attended_in,
     rows_in,
     streams_in,
@@ -476,6 +534,7 @@
     *scratch,
 ):
     count, tokens, width = streams.shape
+    in_two, turn = mixings(mix)[1::2]
     heads = attended.shape[1]
     own_columns = rows_in.at[:, pl.ds(rows_in.shape[1] - heads, heads)]
     waits = start_loads(
@@ -495,9 +554,9 @@
 
     def prepare(rows, total):
         branch[rows, :] = total
-        mixed = coeffs[count] * total
+        mixed = turn * total
         for k in range(count):
-            mixed = mixed + coeffs[k] * streams[k, rows].astype(f32)
+            mixed = mixed + in_two[k] * streams[k, rows].astype(f32)
         mean, center, square = norm_stats(mixed)
         return (mean, square), center.astype(jnp.bfloat16)
 
@@ -506,13 +565,13 @@
     wait_stores()
 
 
-def norm_mid(size, attended, rows, streams, coeffs, chunk=64, hop=1):
+def norm_mid(size, attended, rows, streams, mix, chunk=64, hop=(1, 0, 1)):
     _, tokens, width = streams.shape
     weights = jax.ShapeDtypeStruct((size * width, attended.shape[1]), jnp.bfloat16)
     whole = jax.ShapeDtypeStruct((tokens, size * width), jnp.bfloat16)
     return call(
         functools.partial(norm_mid_kernel, size, chunk, hop),
-        (coeffs, attended, rows, streams),
+        (mix, attended, rows, streams),
         (SM, pl.ANY, pl.ANY, pl.ANY),
         [
             whole,
@@ -532,18 +591,21 @@
     size,
     chunk,
     hop,
-    coeffs,
+    mix,
     gated_in,
     rows_in,
     grads_in,
     normal_in,
     scale,
+    output_in,
     whole_out,
     inner_out,
+    grad_attended,
     gated,
     weights,
     grads,
     whole_normal,
+    output_rows,
     scatter,
     inner,
     whole,
@@ -553,8 +615,10 @@
     *scratch,
 ):
     count, tokens, width = grads.shape
+    out_one, turn = mixings(mix)[2:]
     blocks = scratch[1]
     hidden = gated.shape[2]
+    heads = output_rows.shape[1]
     me = lax.axis_index("col")
     edge = size - 1
     order = sorted(range(size), key=lambda shard: -max(shard, edge - shard))
@@ -567,6 +631,7 @@
         (gated_in.at[:, rest], gated.at[:, rest]),
         (grads_in, grads),
         (normal_in, whole_normal),
+        (output_in.at[:, pl.ds(output_in.shape[1] - heads, heads)], output_rows),
     ]
     waits = start_loads(pairs, loads)
     store, wait_stores = group_store(whole, whole_out, stores)
@@ -603,16 +668,16 @@
         cross = second - first * plain * part
         slope = jnp.where(spread > 1e-3, cross / jnp.maximum(spread, 1e-3), 0.0)
         level = (first - slope * plain) * part
-        known = coeffs[0] * grads[0, rows].astype(f32)
+        known = out_one[0] * grads[0, rows].astype(f32)
         for k in range(1, count):
-            known = known + coeffs[k] * grads[k, rows].astype(f32)
-        block = known + (coeffs[count] * scale[rows, :]) * (total - level - slope * normal)
+            known = known + out_one[k] * grads[k, rows].astype(f32)
+        block = known + (turn * scale[rows, :]) * (total - level - slope * normal)
         return (first, second, level, slope), block.astype(jnp.bfloat16)
 
     def finish(group, rows, turned):
         first, second = whole_sums(size, width, turned)
         rate = scale[rows, :]
-        gain = coeffs[count] * rate
+        gain = turn * rate
         for z in range(size):
             level = gain * (turned[:, 8 * z + 2 : 8 * z + 3] - first)
             slope = gain * (turned[:, 8 * z + 3 : 8 * z + 4] - second)
@@ -621,6 +686,9 @@
             value = value + slope * whole_normal[rows, columns].astype(f32)
             whole[rows, columns] = value.astype(jnp.bfloat16)
         store(group)
+        grad_attended[rows, :] = jnp.dot(
+            whole[rows, :], output_rows[...], preferred_element_type=f32
+        ).astype(jnp.bfloat16)
         inner[rows, :] = rate * (inner[rows, :] - first - second * own_normal(rows))
         store_inner(group)
 
@@ -638,21 +706,25 @@
     return first * (1.0 / (size * width)), second * (1.0 / (size * width))
 
 
-def back_mid(size, gated, rows, grads, whole_normal, scale, coeffs, chunk=64, hop=1):
+def back_mid(
+    size, gated, rows, grads, whole_normal, scale, output_rows, mix, chunk=64, hop=(1, 0, 1)
+):
     _, tokens, width = grads.shape
     whole = jax.ShapeDtypeStruct((tokens, size * width), jnp.bfloat16)
     inner = jax.ShapeDtypeStruct((tokens, width), f32)
     groups = tokens // GROUP
     weights = jax.ShapeDtypeStruct((size * width, 2 * gated.shape[2]), jnp.bfloat16)
+    heads = output_rows.shape[1] // 4
+    output_own = jax.ShapeDtypeStruct((size * width, heads), jnp.bfloat16)
     return call(
         functools.partial(back_mid_kernel, size, chunk, hop),
-        (coeffs, gated, rows, grads, whole_normal, scale),
-        (SM,) + (pl.ANY,) * 4 + (VM,),
-        [whole, inner],
-        (pl.ANY, pl.ANY),
-        held(gated, weights, grads, whole_normal, whole, inner, whole)
+        (mix, gated, rows, grads, whole_normal, scale, output_rows),
+        (SM,) + (pl.ANY,) * 4 + (VM, pl.ANY),
+        [whole, inner, jax.ShapeDtypeStruct((tokens, heads), jnp.bfloat16)],
+        (pl.ANY, pl.ANY, VM),
+        held(gated, weights, grads, whole_normal, output_own, whole, inner, whole)
         + [
-            pltpu.SemaphoreType.DMA((size + 4,)),
+            pltpu.SemaphoreType.DMA((size + 5,)),
             pltpu.SemaphoreType.DMA((groups,)),
             pltpu.SemaphoreType.DMA((groups,)),
         ]
@@ -674,143 +746,120 @@
 
 def back_in_kernel(
     size,
-    chunk,
-    hop,
-    coeffs,
-    heads_in,
-    rows_in,
-    normal,
+    partial_in,
+    first_in,
+    last_in,
+    normal_in,
     scale,
     streams_in,
-    grads_in,
-    branch_one_in,
-    branch_two_in,
-    inner_two_in,
-    final_out,
-    grad_streams_out,
+    streams_grads,
+    other_products,
+    inner,
     whole_products,
-    heads,
-    weights,
+    share,
+    first,
+    last,
+    normal,
     streams,
-    grads,
-    branch_one,
-    branch_two,
-    inner_two,
-    final,
-    grad_streams,
-    scatter,
-    inner,
+    facts,
     products,
     shares,
     loads,
-    final_stores,
-    stores,
+    facts_sent,
+    facts_got,
     shares_sent,
     shares_got,
-    *scratch,
 ):
     count, tokens, width = streams.shape
-    square = count * count
-    edge = size - 1
-    order = sorted(range(size), key=lambda shard: -max(shard, edge - shard))
-    pairs = [(heads_in.at[pl.ds(0, GROUP)], heads.at[pl.ds(0, GROUP)])]
-    for shard in order:
-        shard_rows = pl.ds(shard * width, width)
-        own_columns = pl.ds(0, heads.shape[1])
-        pairs.append((rows_in.at[shard_rows, own_columns], weights.at[shard_rows]))
-    rest = pl.ds(GROUP, tokens - GROUP)
-    pairs = pairs + [
-        (heads_in.at[rest], heads.at[rest]),
-        (streams_in, streams),
-        (grads_in, grads),
-        (branch_one_in, branch_one),
-        (branch_two_in, branch_two),
-        (inner_two_in, inner_two),
-    ]
-    waits = start_loads(pairs, loads)
+    groups = tokens // GROUP
+    me = lax.axis_index("col")
+    count_rows = lax.axis_size("row")
+    own_columns = pl.ds(pl.multiple_of(me * width, width), width)
+    waits = start_loads(
+        (
+            (partial_in.at[:, own_columns], share),
+            (first_in, first),
+            (last_in, last),
+            (normal_in.at[:, own_columns], normal),
+            (streams_in, streams),
+        ),
+        loads,
+    )
+    barrier = pltpu.get_barrier_semaphore()
+    for axis, members in (("col", size), ("row", count_rows)):
+        for member in range(members):
+
+            @pl.when(member != lax.axis_index(axis))
+            def _():
+                pl.semaphore_signal(
+                    barrier, inc=1, device_id={axis: member}, device_id_type=MESH
+                )
+
+    for wait in waits[:4]:
+        wait.wait()
+
+    def rows_of(group):
+        return pl.ds(pl.multiple_of(group * GROUP, GROUP), GROUP)
+
+    def sums(group, carry):
+        rows = rows_of(group)
+        total = share[rows, :].astype(f32) + first[rows, :].astype(f32) + last[rows, :].astype(f32)
+        inner[rows, :] = total
+        one = jnp.sum(total, -1, keepdims=True)
+        two = jnp.sum(total * normal[rows, :].astype(f32), -1, keepdims=True)
+        lane = lax.broadcasted_iota(jnp.int32, (GROUP, 128), 1)
+        packed = jnp.where(lane == 0, one, jnp.where(lane == 1, two, 0.0))
+        facts[me, pl.ds(pl.multiple_of(group * 8, 8), 8)] = packed.T[:8]
+        return carry
+
+    lax.fori_loop(0, groups, sums, 0)
+    pl.semaphore_wait(barrier, size - 1 + count_rows - 1)
+
+    def fact_copy(place, member):
+        return pltpu.make_async_remote_copy(
+            src_ref=facts.at[place],
+            dst_ref=facts.at[place],
+            send_sem=facts_sent.at[member],
+            recv_sem=facts_got.at[place],
+            device_id={"col": member},
+            device_id_type=MESH,
+        )
+
+    for member in range(size):
+
+        @pl.when(member != me)
+        def _():
+            fact_copy(me, member).start()
+
     products[...] = jnp.zeros_like(products)
-    waits[0].wait()
-
-    def produce(rows, shard, first):
-        if first:
-            waits[1 + order.index(shard)].wait()
-        shard_rows = slice(shard * width, (shard + 1) * width)
-        total = lax.dot_general(
-            heads[rows, :], weights[shard_rows, :], LANES, preferred_element_type=f32
-        )
-        scatter[rows, shard_rows] = total.astype(jnp.bfloat16)
-        if first and shard == order[-1]:
-            for wait in waits[1 + size :]:
-                wait.wait()
-
-    def prepare(rows, total):
-        inner[rows, :] = total
-        first = jnp.sum(total, -1, keepdims=True)
-        second = jnp.sum(total * normal[rows, :].astype(f32), -1, keepdims=True)
-        return (first, second), None
-
-    def store(stream, group):
-        rows = pl.ds(pl.multiple_of(group * GROUP, GROUP), GROUP)
-        return pltpu.make_async_copy(
-            grad_streams.at[stream, rows], grad_streams_out.at[stream, rows], stores.at[stream, group]
-        )
-
-    def finish(group, rows, turned):
-        first, second = whole_sums(size, width, turned)
-        own = scale[rows, :] * (inner[rows, :] - first - second * normal[rows, :].astype(f32))
-        below = inner_two[rows, :]
+    waits[4].wait()
+    for member in range(size):
+
+        @pl.when(member != me)
+        def _():
+            fact_copy(member, member).wait()
+
+    def conclude(group, carry):
+        rows = rows_of(group)
+        fact_rows = pl.ds(pl.multiple_of(group * 8, 8), 8)
+        total = facts[0, fact_rows]
+        for place in range(1, size):
+            total = total + facts[place, fact_rows]
+        total = total * (1.0 / (size * width))
+        turned = jnp.concatenate([total, jnp.zeros((GROUP - 8, 128), f32)], 0).T
+        own = scale[rows, :] * (
+            inner[rows, :] - turned[:, :1] - turned[:, 1:2] * normal[rows, :].astype(f32)
+        )
+        inner[rows, :] = own
         for i in range(count):
-            value = coeffs[square + i] * below + coeffs[square + 3 * count + i] * own
-            for k in range(count):
-                value = value + coeffs[i * count + k] * grads[k, rows].astype(f32)
-            grad_streams[i, rows] = value
-            store(i, group).start()
-            place = square + 3 * count + 1 + i
-            products[place] = products[place] + tile_sum(streams[i, rows].astype(f32) * own)
-
-    def store_final(rows, index):
-        return pltpu.make_async_copy(
-            final.at[:, rows], final_out.at[:, rows], final_stores.at[index]
-        )
-
-    def during(rows):
-        values = [streams[i, rows].astype(f32) for i in range(count)]
-        above = [grads[i, rows].astype(f32) for i in range(count)]
-        one = branch_one[rows, :]
-        two = branch_two[rows, :].astype(f32)
-        below = inner_two[rows, :]
-        for j in range(count):
-            value = coeffs[square + count + j] * one + coeffs[square + 2 * count + j] * two
-            for k in range(count):
-                value = value + coeffs[k * count + j] * values[k]
-            final[j, rows] = value.astype(jnp.bfloat16)
-        pairs = [(a, b) for a in values for b in above]
-        pairs = pairs + [(a, below) for a in values]
-        pairs = pairs + [(one, b) for b in above]
-        pairs = pairs + [(a, two) for a in above]
-        pairs = pairs + [(one, below)]
-        for place, (a, b) in enumerate(pairs):
-            products[place] = products[place] + tile_sum(a * b)
-        store_final(rows, rows.start // chunk).start()
-
-    count_rows = lax.axis_size("row")
-    line_exchange(
-        size,
-        tokens,
-        width,
-        chunk,
-        hop,
-        scatter,
-        False,
-        produce,
-        prepare,
-        finish,
-        scratch,
-        during,
-        count_rows,
-    )
-    total = jnp.sum(jnp.sum(products[...], 1), -1, keepdims=True)
-    total = jnp.broadcast_to(total, whole_products.shape)
+            products[i] = products[i] + tile_sum(streams[i, rows].astype(f32) * own)
+        return carry
+
+    lax.fori_loop(0, groups, conclude, 0)
+    parts = [streams_grads[...], other_products[...], products[...]]
+    total = jnp.concatenate([jnp.sum(jnp.sum(part, 1), -1, keepdims=True) for part in parts], 0)
+    total = jnp.concatenate([total, jnp.zeros((128 - total.shape[0], 1), f32)], 0)
+    total = jnp.broadcast_to(total, (128, 128)).T[:8]
     for axis, members, base in (("col", size, 0), ("row", count_rows, size)):
         here = lax.axis_index(axis)
 
@@ -842,84 +891,127 @@
             total = total + shares[base + member]
     whole_products[...] = total
 
-    def wait_final(index, carry):
-        store_final(pl.ds(pl.multiple_of(index * chunk, chunk), chunk), index).wait()
-        return carry
-
-    lax.fori_loop(0, tokens // chunk, wait_final, 0)
-
-    def wait_streams(group, carry):
-        for i in range(count):
-            store(i, group).wait()
-        return carry
-
-    lax.fori_loop(0, tokens // GROUP, wait_streams, 0)
-
-
-def back_in(
-    size,
-    coeffs,
-    heads,
-    rows,
-    normal,
-    scale,
-    streams,
-    grads,
-    branch_one,
-    branch_two,
-    inner_two,
-    chunk=64,
-    hop=2,
-):
+
+def back_in(size, partial, first, last, normal, scale, streams, streams_grads, other_products):
     count, tokens, width = streams.shape
-    products = -(-(count * count + 4 * count + 1) // 8) * 8
-    final = jax.ShapeDtypeStruct(streams.shape, jnp.bfloat16)
-    grad_streams = jax.ShapeDtypeStruct(streams.shape, f32)
+    own = -(-count // 8) * 8
     members = size + lax.axis_size("row")
     dma = pltpu.SemaphoreType.DMA
     return call(
-        functools.partial(back_in_kernel, size, chunk, hop),
-        (
-            coeffs,
-            heads,
-            rows,
-            normal,
-            scale,
-            streams,
-            grads,
-            branch_one,
-            branch_two,
-            inner_two,
-        ),
-        (SM, pl.ANY, pl.ANY, VM, VM) + (pl.ANY,) * 5,
-        [final, grad_streams, jax.ShapeDtypeStruct((products, 128), f32)],
-        (pl.ANY, pl.ANY, VM),
-        held(
-            heads,
-            jax.ShapeDtypeStruct((size * width, heads.shape[1]), jnp.bfloat16),
-            streams,
-            grads,
-            branch_one,
-            branch_two,
-            inner_two,
-            final,
-            grad_streams,
-        )
+        functools.partial(back_in_kernel, size),
+        (partial, first, last, normal, scale, streams, streams_grads, other_products),
+        (pl.ANY, pl.ANY, pl.ANY, pl.ANY, VM, pl.ANY, VM, VM),
+        [
+            jax.ShapeDtypeStruct((tokens, width), f32),
+            jax.ShapeDtypeStruct((8, 128), f32),
+        ],
+        (VM, VM),
+        held(first, first, last, first, streams)
         + [
-            pltpu.VMEM((tokens, size * width), jnp.bfloat16),
-            pltpu.VMEM((tokens, width), f32),
-            pltpu.VMEM((products, 8, 128), f32),
-            pltpu.VMEM((members, products, 128), f32),
-            dma((size + 7,)),
-            dma((tokens // chunk,)),
-            dma((count, tokens // GROUP)),
+            pltpu.VMEM((size, tokens // GROUP * 8, 128), f32),
+            pltpu.VMEM((own, 8, 128), f32),
+            pltpu.VMEM((members, 8, 128), f32),
+            dma((5,)),
+            dma((size,)),
+            dma((size,)),
             dma((members,)),
             dma((members,)),
-        ]
-        + exchange_scratch(size, tokens, width, chunk, True, False),
+        ],
         "back_in",
         4,
-    )
+        10**9,
+    )
+
+
+def end_kernel(mix, streams, grads, branch_one, branch_two, inner_two, final, products):
+    count, tokens, width = streams.shape
+    through, _, out_one, _ = mixings(mix)
+    out_two = [mix[1, j, 1 + count] for j in range(count)]
+
+    @pl.when(pl.program_id(0) == 0)
+    def _():
+        products[...] = jnp.zeros_like(products)
+
+    def slab(index, sums):
+        rows = pl.ds(pl.multiple_of(index * 16, 16), 16)
+        sums = list(sums)
+        for start in range(0, width, 128):
+            columns = slice(start, start + 128)
+            values = [streams[i, rows, columns].astype(f32) for i in range(count)]
+            above = [grads[i, rows, columns].astype(f32) for i in range(count)]
+            one = branch_one[rows, columns]
+            two = branch_two[rows, columns].astype(f32)
+            below = inner_two[rows, columns]
+            for j in range(count):
+                value = out_one[j] * one + out_two[j] * two
+                for k in range(count):
+                    value = value + through[k][j] * values[k]
+                final[j, rows, columns] = value.astype(jnp.bfloat16)
+            pairs = [(a, below) for a in values]
+            pairs = pairs + [(one, b) for b in above]
+            pairs = pairs + [(a, two) for a in above]
+            pairs = pairs + [(one, below)]
+            for place, (a, b) in enumerate(pairs):
+                product = a * b
+                sums[place] = sums[place] + product[:8] + product[8:]
+        return tuple(sums)
+
+    used = 3 * count + 1
+    sums = lax.fori_loop(0, tokens // 16, slab, (jnp.zeros((8, 128), f32),) * used)
+    for place in range(used):
+        products[place] = products[place] + sums[place]
+
+
+def end_streams(mix, streams, grads, branch_one, branch_two, inner_two, tile=256):
+    count, tokens, width = streams.shape
+    used = -(-(3 * count + 1) // 8) * 8
+    many = pl.BlockSpec((count, tile, width), lambda i: (0, i, 0))
+    own = pl.BlockSpec((tile, width), lambda i: (i, 0))
+    return pl.pallas_call(
+        end_kernel,
+        grid=(tokens // tile,),
+        out_shape=[
+            jax.ShapeDtypeStruct(streams.shape, jnp.bfloat16),
+            jax.ShapeDtypeStruct((used, 8, 128), f32),
+        ],
+        in_specs=[pl.BlockSpec(memory_space=SM), many, many, own, own, own],
+        out_specs=[many, pl.BlockSpec((used, 8, 128), lambda i: (0, 0, 0))],
+        compiler_params=pltpu.CompilerParams(vmem_limit_bytes=60 * 2**20),
+        cost_estimate=pl.CostEstimate(
+            flops=60 * streams.size, bytes_accessed=9 * streams.size, transcendentals=0
+        ),
+        name="end_streams",
+    )(mix, streams, grads, branch_one, branch_two, inner_two)
+
+
+def grad_kernel(mix, grads, inner_two, inner_one, out):
+    count = grads.shape[0]
+    through, in_two, _, _ = mixings(mix)
+    above = [grads[k].astype(f32) for k in range(count)]
+    below, own = inner_two[...], inner_one[...]
+    for i in range(count):
+        value = in_two[i] * below + mix[0, i, 0] * own
+        for k in range(count):
+            value = value + through[i][k] * above[k]
+        out[i] = value
+
+
+def grad_streams_of(mix, grads, inner_two, inner_one, tile=256):
+    count, tokens, width = grads.shape
+    many = pl.BlockSpec((count, tile, width), lambda i: (0, i, 0))
+    own = pl.BlockSpec((tile, width), lambda i: (i, 0))
+    return pl.pallas_call(
+        grad_kernel,
+        grid=(tokens // tile,),
+        out_shape=jax.ShapeDtypeStruct(grads.shape, f32),
+        in_specs=[pl.BlockSpec(memory_space=SM), many, own, own],
+        out_specs=many,
+        compiler_params=pltpu.CompilerParams(vmem_limit_bytes=60 * 2**20),
+        cost_estimate=pl.CostEstimate(
+            flops=10 * grads.size, bytes_accessed=8 * grads.size, transcendentals=0
+        ),
+        name="grad_streams",
+    )(mix, grads, inner_two, inner_one)
 
 
 def tiled(body, grid, operands, specs, outs, out_specs, scratch, flops, name):
@@ -937,37 +1029,205 @@
     )(*operands)
 
 
-def gate_kernel(whole, gate_rows, upper_rows, active, by_gate, by_upper):
-    gate = jnp.dot(whole[...], gate_rows[...], preferred_element_type=f32)
-    upper = jnp.dot(whole[...], upper_rows[...], preferred_element_type=f32)
-    sigma = jax.nn.sigmoid(gate)
-    silu = gate * sigma
-    active[...] = (silu * upper).astype(jnp.bfloat16)
-    by_gate[...] = (upper * sigma * (1.0 + gate * (1.0 - sigma))).astype(jnp.bfloat16)
-    by_upper[...] = silu.astype(jnp.bfloat16)
-
-
-def gate_forward(whole, weights, tile=256):
+def gate_kernel(
+    size,
+    steps,
+    chunks,
+    whole,
+    gate_rows,
+    upper_rows,
+    down_rows,
+    own_in,
+    before_in,
+    after_in,
+    active_out,
+    by_gate,
+    by_upper,
+    partial,
+    gathered,
+    active,
+    blocks,
+    loads,
+    stores,
+    sent,
+    got,
+):
+    step = pl.program_id(0)
+    me = lax.axis_index("col")
+    tiles, tile = active.shape[1] // gate_rows.shape[1], gate_rows.shape[1]
+    tokens, width = blocks.shape[1:]
+    chunk = tokens // chunks
+    edge = size - 1
+    right, left = jnp.minimum(me + 1, edge), jnp.maximum(me - 1, 0)
+    other = jnp.where(me == edge, left, right)
+
+    def load(place, way):
+        source = (own_in, before_in, after_in)[way]
+        return pltpu.make_async_copy(source, blocks.at[place], loads.at[way])
+
+    def store(place):
+        return pltpu.make_async_copy(
+            blocks.at[place],
+            gathered.at[:, pl.ds(pl.multiple_of(place * width, width), width)],
+            stores.at[place],
+        )
+
+    def send(place, index, way, device):
+        rows = pl.ds(pl.multiple_of(index * chunk, chunk), chunk)
+        return pltpu.make_async_remote_copy(
+            src_ref=blocks.at[place, rows],
+            dst_ref=blocks.at[place, rows],
+            send_sem=sent.at[way, place, index],
+            recv_sem=got.at[place, index],
+            device_id={"col": device},
+            device_id_type=MESH,
+        )
+
+    def both_ways(near, act):
+        for way, place, target, onward in (
+            (0, me - near, right, me < edge),
+            (1, me + near, left, me > 0),
+        ):
+
+            @pl.when((place >= 0) & (place < size))
+            def _():
+                act(way, place, target, onward)
+
+    @pl.when(step == 0)
+    def _():
+        load(me, 0).start()
+        both_ways(1, lambda way, place, target, onward: load(place, 1 + way).start())
+        barrier = pltpu.get_barrier_semaphore()
+        both_ways(
+            1,
+            lambda way, place, target, onward: pl.semaphore_signal(
+                barrier, inc=1, device_id={"col": place}, device_id_type=MESH
+            ),
+        )
+        load(me, 0).wait()
+        store(me).start()
+        both_ways(1, lambda way, place, target, onward: load(place, 1 + way).wait())
+
+        @pl.when((me > 0) & (me < edge))
+        def _():
+            pl.semaphore_wait(barrier, 2)
+
+        @pl.when((me == 0) | (me == edge))
+        def _():
+            pl.semaphore_wait(barrier, 1)
+
+
+        def begin(way, place, target, onward):
+            store(place).start()
+
+            @pl.when(onward)
+            def _():
+                for index in range(chunks):
+                    send(place, index, way, target).start()
+
+        both_ways(1, begin)
+
+    for near in range(2, size - 1):
+        index = step - (steps - chunks - (size - 2 - near))
+
+        def forward(way, place, target, onward):
+            send(place, index, way, other).wait_recv()
+
+            @pl.when(onward)
+            def _():
+                send(place, index, way, target).start()
+
+        @pl.when((index >= 0) & (index < chunks))
+        def _():
+            both_ways(near, forward)
+
+    @pl.when(step < tiles)
+    def _():
+        gate = jnp.dot(whole[...], gate_rows[...], preferred_element_type=f32)
+        upper = jnp.dot(whole[...], upper_rows[...], preferred_element_type=f32)
+        sigma = jax.nn.sigmoid(gate)
+        silu = gate * sigma
+        value = (silu * upper).astype(jnp.bfloat16)
+        active_out[...] = value
+        active[:, pl.ds(pl.multiple_of(step * tile, tile), tile)] = value
+        by_gate[...] = (upper * sigma * (1.0 + gate * (1.0 - sigma))).astype(jnp.bfloat16)
+        by_upper[...] = silu.astype(jnp.bfloat16)
+
+    @pl.when(step >= tiles)
+    def _():
+        partial[...] = lax.dot_general(
+            active[...], down_rows[...], LANES, preferred_element_type=f32
+        ).astype(jnp.bfloat16)
+
+    @pl.when(step == steps - 1)
+    def _():
+        def last(way, place, target, onward):
+            for index in range(chunks):
+                send(place, index, way, other).wait_recv()
+
+        both_ways(size - 1, last)
+        for near in range(2, size):
+            both_ways(near, lambda way, place, target, onward: store(place).start())
+
+        def sends_done(way, place, target, onward):
+            @pl.when(onward)
+            def _():
+                for index in range(chunks):
+                    send(place, index, way, other).wait_send()
+
+        for near in range(1, size - 1):
+            both_ways(near, sends_done)
+        for place in range(size):
+            store(place).wait()
+
+
+def gate_forward(size, whole, weights, own, before, after, tile=256):
     tokens, features = whole.shape
     hidden = weights.shape[1] // 3
     tile = min(tile, hidden)
     tiles = hidden // tile
-    out = pl.BlockSpec((tokens, tile), lambda j: (0, j))
-    return tiled(
-        gate_kernel,
-        (tiles,),
-        (whole, weights, weights),
-        [
+    down_tile = min(512, features)
+    steps = tiles + features // down_tile
+    chunks = 1
+    while 2 * chunks <= min(8, steps - size + 3):
+        chunks = 2 * chunks
+    wide = pl.BlockSpec((tokens, tile), lambda j: (0, jnp.minimum(j, tiles - 1)))
+    plain = pl.BlockSpec(memory_space=pl.ANY)
+    dma = pltpu.SemaphoreType.DMA
+    wide_shape = jax.ShapeDtypeStruct((tokens, hidden), jnp.bfloat16)
+    return pl.pallas_call(
+        functools.partial(gate_kernel, size, steps, chunks),
+        grid=(steps,),
+        out_shape=[wide_shape] * 3 + [jax.ShapeDtypeStruct((tokens, features), jnp.bfloat16)] * 2,
+        in_specs=[
             pl.BlockSpec((tokens, features), lambda j: (0, 0)),
-            pl.BlockSpec((features, tile), lambda j: (0, j)),
-            pl.BlockSpec((features, tile), lambda j: (0, j + tiles)),
+            pl.BlockSpec((features, tile), lambda j: (0, jnp.minimum(j, tiles - 1))),
+            pl.BlockSpec((features, tile), lambda j: (0, tiles + jnp.minimum(j, tiles - 1))),
+            pl.BlockSpec((down_tile, hidden), lambda j: (jnp.maximum(j - tiles, 0), 2)),
+            plain,
+            plain,
+            plain,
         ],
-        [jax.ShapeDtypeStruct((tokens, hidden), jnp.bfloat16)] * 3,
-        [out] * 3,
-        [],
-        4 * tokens * features * hidden,
-        "gate_forward",
-    )
+        out_specs=[wide] * 3
+        + [pl.BlockSpec((tokens, down_tile), lambda j: (0, jnp.maximum(j - tiles, 0))), plain],
+        scratch_shapes=[
+            pltpu.VMEM((tokens, hidden), jnp.bfloat16),
+            pltpu.VMEM((size, tokens, own.shape[1]), jnp.bfloat16),
+            dma((3,)),
+            dma((size,)),
+            dma((2, size, chunks)),
+            dma((size, chunks)),
+        ],
+        compiler_params=pltpu.CompilerParams(
+            collective_id=5, has_side_effects=True, vmem_limit_bytes=60 * 2**20
+        ),
+        cost_estimate=pl.CostEstimate(
+            flops=6 * tokens * features * hidden,
+            bytes_accessed=2 * weights.size,
+            transcendentals=0,
+        ),
+        name="gate_forward",
+    )(whole, weights, weights, weights, own, before, after)
 
 
 def gate_back_kernel(whole, rows, by_gate, by_upper, grads):
@@ -1073,56 +1333,94 @@
     )
 
 
-def product_turned(left, right, place, tile=512, name="product_turned"):
-    tokens, depth = left.shape
-    rows = right.shape[0]
+def heads_kernel(grads, rows, out):
+    width = grads.shape[2]
+    total = 0.0
+    for k in range(grads.shape[0]):
+        total = total + lax.dot_general(
+            grads[k], rows[:, k * width : (k + 1) * width], LANES, preferred_element_type=f32
+        )
+    out[...] = total.astype(jnp.bfloat16)
+
+
+def heads_product(grads, weights, tile=512):
+    count, tokens, width = grads.shape
+    rows = weights.shape[0]
     tile = min(tile, rows)
     return tiled(
-        functools.partial(product_kernel, LANES),
+        heads_kernel,
         (rows // tile,),
-        (left, right),
+        (grads, weights),
         [
-            pl.BlockSpec((tokens, depth), lambda j: (0, 0)),
-            pl.BlockSpec((tile, depth), lambda j: (j, place)),
+            pl.BlockSpec((count, tokens, width), lambda j: (0, 0, 0)),
+            pl.BlockSpec((tile, count * width), lambda j: (j, 0)),
         ],
         jax.ShapeDtypeStruct((tokens, rows), jnp.bfloat16),
         pl.BlockSpec((tokens, tile), lambda j: (0, j)),
         [],
-        2 * tokens * depth * rows,
-        name,
-    )
-
-
-def block_probs(queries, key_heads, rows_docs, columns_docs, start):
-    scores = lax.dot_general(queries, key_heads, LANES, preferred_element_type=f32)
-    scores = scores * HEAD_DIM ** (-0.5)
-    row = lax.broadcasted_iota(jnp.int32, scores.shape, 0) + start
-    column = lax.broadcasted_iota(jnp.int32, scores.shape, 1)
-    scores = jnp.where((rows_docs == columns_docs) & (column <= row), scores, MASKED)
-    expo = jnp.exp(scores - jnp.max(scores, -1, keepdims=True))
+        2 * count * tokens * width * rows,
+        "heads_product",
+    )
+
+
+def fill_bias(bias, column, row):
+    tile = min(256, bias.shape[0])
+    for start in range(0, bias.shape[0], tile):
+        shape = (tile, bias.shape[1])
+        index = lax.broadcasted_iota(jnp.int32, shape, 0) + start
+        allowed = (column[start : start + tile] == row[...]) & (
+            lax.broadcasted_iota(jnp.int32, shape, 1) <= index
+        )
+        bias[start : start + tile] = jnp.where(allowed, 0.0, MASKED)
+
+
+def key_span(start, block):
+    return max(0, start + 1 - LONGEST) // 128 * 128, start + block
+
+
+def block_probs(queries, key_heads, bias):
+    scores = lax.dot_general(queries, key_heads, LANES, preferred_element_type=f32) + bias
+    expo = jnp.exp2(scores - jnp.max(scores, -1, keepdims=True))
     return expo * (1.0 / jnp.sum(expo, -1, keepdims=True))
 
 
 def attend_forward_kernel(
-    block, query, key, value, cosine, sine, column, row, queries, key_heads, value_heads, attended
+    block,
+    query,
+    key,
+    value,
+    cosine,
+    sine,
+    column,
+    row,
+    queries,
+    key_heads,
+    value_heads,
+    attended,
+    bias,
 ):
     length = query.shape[0]
 
+    @pl.when(pl.program_id(0) == 0)
+    def _():
+        fill_bias(bias, column, row)
+
+    cosines = jnp.concatenate([cosine[...], cosine[...]], 1)
+    sines = jnp.concatenate([-sine[...], sine[...]], 1)
+
     def turn(values):
-        return (values * cosine[...] + pltpu.roll(values, HEAD_DIM // 2, 1) * sine[...]).astype(
-            jnp.bfloat16
-        )
-
-    queries[...] = turn(query[...])
-    key_heads[...] = turn(key[...])
+        return values * cosines + pltpu.roll(values, HEAD_DIM // 2, 1) * sines
+
+    queries[...] = (turn(query[...]) * (HEAD_DIM ** (-0.5) * LOG2E)).astype(jnp.bfloat16)
+    key_heads[...] = turn(key[...]).astype(jnp.bfloat16)
     value_heads[...] = value[...].astype(jnp.bfloat16)
     for start in range(0, length, block):
-        end = start + block
+        first, end = key_span(start, block)
         probs = block_probs(
-            queries[start:end], key_heads[:end], column[start:end], row[:, :end], start
+            queries[start:end], key_heads[first:end], bias[start:end, first:end]
         )
         result = jnp.dot(
-            probs.astype(jnp.bfloat16), value_heads[:end], preferred_element_type=f32
+            probs.astype(jnp.bfloat16), value_heads[first:end], preferred_element_type=f32
         )
         attended[start:end, :] = result.astype(jnp.bfloat16)
 
@@ -1146,6 +1444,7 @@
         in_specs=[head(0), head(heads), head(2 * heads)]
         + [fixed(array) for array in (cosine, sine, column, row)],
         out_specs=[head(0)] * 4,
+        scratch_shapes=[pltpu.VMEM((length, length), f32)],
         compiler_params=pltpu.CompilerParams(vmem_limit_bytes=60 * 2**20),
         name="attend_forward",
     )(projected, projected, projected, cosine, sine, column, row)
@@ -1161,44 +1460,49 @@
     sine,
     column,
     row,
-    grad_query,
-    grad_key,
-    grad_value,
+    grads,
     key_sum,
     value_sum,
+    bias,
 ):
     length = queries.shape[0]
-    factor = HEAD_DIM ** (-0.5)
-
-    def turn_back(values, rows):
+
+    @pl.when(pl.program_id(0) == 0)
+    def _():
+        fill_bias(bias, column, row)
+
+    key_sum[...] = jnp.zeros_like(key_sum)
+    value_sum[...] = jnp.zeros_like(value_sum)
+
+    def turn_back(values, rows, factor):
         values = values * factor
-        return (
-            values * cosine[rows] - pltpu.roll(values, HEAD_DIM // 2, 1) * sine[rows]
-        ).astype(jnp.bfloat16)
-
-    for start in range(length - block, -1, -block):
-        end = start + block
+        cosines = jnp.concatenate([cosine[rows], cosine[rows]], 1)
+        sines = jnp.concatenate([-sine[rows], sine[rows]], 1)
+        return (values * cosines - pltpu.roll(values, HEAD_DIM // 2, 1) * sines).astype(
+            jnp.bfloat16
+        )
+
+    for start in range(0, length, block):
+        first, end = key_span(start, block)
         query, grad_part = queries[start:end], grad_result[start:end]
-        probs = block_probs(query, key_heads[:end], column[start:end], row[:, :end], start)
+        probs = block_probs(query, key_heads[first:end], bias[start:end, first:end])
         grad_probs = lax.dot_general(
-            grad_part, value_heads[:end], LANES, preferred_element_type=f32
+            grad_part, value_heads[first:end], LANES, preferred_element_type=f32
         )
         row_sum = jnp.sum(probs * grad_probs, -1, keepdims=True)
         grad_scores = (probs * (grad_probs - row_sum)).astype(jnp.bfloat16)
-        grad_part_query = jnp.dot(grad_scores, key_heads[:end], preferred_element_type=f32)
-        grad_query[start:end, :] = turn_back(grad_part_query, pl.ds(start, block))
-        key_part = lax.dot_general(grad_scores, query, ROWS, preferred_element_type=f32)
-        value_part = lax.dot_general(
+        grad_part_query = jnp.dot(grad_scores, key_heads[first:end], preferred_element_type=f32)
+        grads[0, start:end] = turn_back(
+            grad_part_query, pl.ds(start, block), HEAD_DIM ** (-0.5)
+        )
+        key_sum[first:end, :] += lax.dot_general(
+            grad_scores, query, ROWS, preferred_element_type=f32
+        )
+        value_sum[first:end, :] += lax.dot_general(
             probs.astype(jnp.bfloat16), grad_part, ROWS, preferred_element_type=f32
         )
-        if end == length:
-            key_sum[...] = key_part
-            value_sum[...] = value_part
-        else:
-            key_sum[:end, :] += key_part
-            value_sum[:end, :] += value_part
-    grad_key[...] = turn_back(key_sum[...], pl.ds(0, length))
-    grad_value[...] = value_sum[...].astype(jnp.bfloat16)
+    grads[1] = turn_back(key_sum[...], pl.ds(0, length), 1.0 / LOG2E)
+    grads[2] = value_sum[...].astype(jnp.bfloat16)
 
 
 def attend_back(queries, key_heads, value_heads, grad_result, cosine, sine, column, row):
@@ -1210,17 +1514,17 @@
     def fixed(array):
         return pl.BlockSpec(array.shape, lambda h: (0, 0))
 
-    grads = pl.pallas_call(
+    return pl.pallas_call(
         functools.partial(attend_back_kernel, block),
         grid=(heads,),
-        out_shape=[jax.ShapeDtypeStruct((length, width), jnp.bfloat16)] * 3,
+        out_shape=jax.ShapeDtypeStruct((3, length, width), jnp.bfloat16),
         in_specs=[head] * 4 + [fixed(array) for array in (cosine, sine, column, row)],
-        out_specs=[head] * 3,
-        scratch_shapes=[pltpu.VMEM((length, HEAD_DIM), f32)] * 2,
+        out_specs=pl.BlockSpec((3, length, HEAD_DIM), lambda h: (0, 0, h)),
+        scratch_shapes=[pltpu.VMEM((length, HEAD_DIM), f32)] * 2
+        + [pltpu.VMEM((length, length), f32)],
         compiler_params=pltpu.CompilerParams(vmem_limit_bytes=60 * 2**20),
         name="attend_back",
     )(queries, key_heads, value_heads, grad_result, cosine, sine, column, row)
-    return jnp.concatenate(grads, 1)
 
 
 def update(weight, grad, moment, average, rate):
@@ -1270,34 +1574,6 @@
     return lax.optimization_barrier(values)
 
 
-def assemble_kernel(size, *refs):
-    pieces, whole = refs[:-1], refs[-1]
-    width = whole.shape[1] // size
-    me = lax.axis_index("col")
-    for here in range(size):
-
-        @pl.when(me == here)
-        def _():
-            for place in range(size):
-                columns = slice(place * width, (place + 1) * width)
-                whole[:, columns] = pieces[size - 1 + place - here][...]
-
-
-def assemble(pieces):
-    size = (len(pieces) + 1) // 2
-    tokens, width = pieces[0].shape
-    tile = min(256, tokens)
-    return pl.pallas_call(
-        functools.partial(assemble_kernel, size),
-        grid=(tokens // tile,),
-        out_shape=jax.ShapeDtypeStruct((tokens, size * width), pieces[0].dtype),
-        in_specs=[pl.BlockSpec((tile, width), lambda i: (i, 0))] * len(pieces),
-        out_specs=pl.BlockSpec((tile, size * width), lambda i: (i, 0)),
-        compiler_params=pltpu.CompilerParams(vmem_limit_bytes=60 * 2**20),
-        name="assemble",
-    )(*pieces)
-
-
 def line_ways():
     size = lax.axis_size("col")
     up = [(i, i + 1) for i in range(size - 1)]
@@ -1305,15 +1581,24 @@
     return size, up, down
 
 
-def gather_steps(values):
+def scatter_steps(partial):
     size, up, down = line_ways()
-    before, after = [values], [values]
-    for _ in range(size - 1):
-        step = (lax.ppermute(before[-1], "col", up), lax.ppermute(after[-1], "col", down))
-        step = yield step
-        before.append(step[0])
-        after.append(step[1])
-    yield assemble(before[:0:-1] + after)
+    me = lax.axis_index("col")
+    width = partial.shape[1] // size
+
+    def share(place):
+        return lax.dynamic_slice_in_dim(partial, place * width, width, 1)
+
+    first = share(jnp.minimum(me + size - 1, size - 1))
+    last = share(jnp.maximum(me - size + 1, 0))
+    for step in range(1, size):
+        if step > 1:
+            first = share(jnp.minimum(me + size - step, size - 1)).astype(f32) + first.astype(f32)
+            last = share(jnp.maximum(me - size + step, 0)).astype(f32) + last.astype(f32)
+            first = first.astype(jnp.bfloat16)
+            last = last.astype(jnp.bfloat16)
+        first, last = yield (lax.ppermute(first, "col", up), lax.ppermute(last, "col", down))
+    yield [first, last]
 
 
 def advance(steps, got, *values):
@@ -1370,84 +1655,103 @@
         return lax.all_gather(weights.astype(low), "row", axis=0, tiled=True)
 
     attention_weights = gather_rows(side_by_side(attention_in, attention_out))
-    hidden_weights = gather_rows(side_by_side(gate_up, down_weights))
 
     one, two = hyper_mix[0], hyper_mix[1]
     across_one, across_two = one[:, 1 : 1 + count], two[:, 1 : 1 + count]
-    through = small_matmul(across_one, across_two)
-    in_two = small_matmul(across_one, two[:, :1])[:, 0]
-    out_one = small_matmul(one[None, :, 1 + count], across_two)[0]
-    turn = jnp.sum(one[:, 1 + count] * two[:, 0])
-
-    whole_one, scale_one, grad_two = norm_in(
-        size, streams, cotangent, jnp.concatenate([one[:, 0], two[:, 1 + count]])
-    )
+    whole_one, scale_one, grad_two, streams_grads, hidden_weights = norm_in(
+        size, streams, cotangent, gate_up, down_weights, hyper_mix
+    )
+    hidden_weights = lax.all_gather(hidden_weights, "row", axis=0, tiled=True)
     heads = attention_in.shape[2]
-    steps = gather_steps(grad_two)
+    _, up, down = line_ways()
+    before = lax.ppermute(grad_two, "col", up)
+    after = lax.ppermute(grad_two, "col", down)
     projected = product(whole_one, attention_weights, 0, 3 * heads, f32, heads, "project_in")
     queries, key_heads, value_heads, attended = attend_forward(
         projected, cosine, sine, segments.T, segments
     )
-    got, (attended,) = advance(steps, None, attended)
-    mid_coeffs = jnp.concatenate([in_two, turn[None]])
+    attended, before, after = tie(attended, before, after)
     whole_two, scale_two, branch_one = norm_mid(
-        size, attended, attention_weights, streams, mid_coeffs
-    )
-
-    whole_two, *got = tie(whole_two, *got)
-    active, by_gate, by_upper = gate_forward(whole_two, hidden_weights)
-    got, (active,) = advance(steps, tuple(got), active)
-    partial_two = product_turned(active, hidden_weights, 2, name="project_out")
-    got, (partial_two,) = advance(steps, got, partial_two)
-    whole_grad_two = finish_line(steps, got)
+        size, attended, attention_weights, streams, hyper_mix
+    )
+
+    active, by_gate, by_upper, partial_two, whole_grad_two = gate_forward(
+        size, whole_two, hidden_weights, grad_two, before, after
+    )
     branch_two = lax.psum_scatter(partial_two, "col", scatter_dimension=1, tiled=True)
     grad_gated = gate_back(whole_grad_two, hidden_weights, by_gate, by_upper)
     grad_hidden = outer(whole_two, grad_gated, whole_grad_two, active, name="outer_hidden")
     grad_hidden, grad_gated = tie(grad_hidden, grad_gated)
     grad_hidden = scatter_rows(grad_hidden)
-    back_coeffs = jnp.concatenate([out_one, turn[None]])
-    whole_grad_one, inner_two = back_mid(
-        size, grad_gated, hidden_weights, cotangent, whole_two, scale_two, back_coeffs
-    )
-
-    whole_grad_one, branch_two = tie(whole_grad_one, branch_two)
-    grad_attended = product(
-        whole_grad_one, attention_weights, 3 * heads, heads, low, heads, "back_out"
-    )
+    whole_grad_one, inner_two, grad_attended = back_mid(
+        size,
+        grad_gated,
+        hidden_weights,
+        cotangent,
+        whole_two,
+        scale_two,
+        attention_weights,
+        hyper_mix,
+    )
+
+    grad_attended, branch_two = tie(grad_attended, branch_two)
     grad_heads = attend_back(
         queries, key_heads, value_heads, grad_attended, cosine, sine, segments.T, segments
     )
+    tokens_all = length * lax.axis_size("row")
+    token_scale = tokens_all ** (-0.5)
+    model_rate = D ** (-0.5) * token_scale
+    partial_one = heads_product(grad_heads, attention_weights)
+    steps = scatter_steps(partial_one)
     grad_attention = outer(
         whole_one, grad_heads, whole_grad_one, attended, name="outer_attention"
     )
-    grad_attention, grad_heads, grad_hidden = tie(grad_attention, grad_heads, grad_hidden)
+    got, (grad_attention,) = advance(steps, None, grad_attention)
+    grad_attention, grad_hidden = tie(grad_attention, grad_hidden)
     grad_attention = scatter_rows(grad_attention)
-    end_coeffs = jnp.concatenate(
-        [through.reshape(-1), in_two, out_one, two[:, 1 + count], one[:, 0]]
-    )
-    own_normal = lax.dynamic_slice_in_dim(whole_one, lax.axis_index("col") * width, width, 1)
-    final, grad_streams, products = back_in(
-        size,
-        end_coeffs,
-        grad_heads,
-        attention_weights,
-        own_normal,
-        scale_one,
+    third = update_blocks(gate_up, grad_hidden, moment_gate_up, average_gate_up, model_rate, 0)
+    fourth = update_blocks(
+        down_weights,
+        grad_hidden,
+        moment_down_weights,
+        average_down_weights,
+        FF ** (-0.5) * token_scale,
+        gate_up.shape[0] * gate_up.shape[2],
+    )
+    got, hidden = advance(steps, got, *third, *fourth)
+    third, fourth = hidden[:3], hidden[3:]
+    final, other_products = end_streams(
+        hyper_mix,
         streams,
         cotangent,
         branch_one,
         branch_two,
         inner_two,
     )
-
-    products = products[:, 0]
-    cuts = [count * count, count, count, count, 1, count]
+    got, (other_products,) = advance(steps, got, other_products)
+    first_part, last_part = finish_line(steps, got)
+    inner_one, products = back_in(
+        size,
+        partial_one,
+        first_part,
+        last_part,
+        whole_one,
+        scale_one,
+        streams,
+        streams_grads,
+        other_products,
+    )
+    grad_streams = grad_streams_of(hyper_mix, cotangent, inner_two, inner_one)
+
+    products = products[0]
+    streams_one = products[count * count + other_products.shape[0] :][:count]
+    cuts = [count * count, count, count, count, 1]
     parts = []
     start = 0
     for cut in cuts:
         parts.append(products[start : start + cut])
         start = start + cut
-    streams_grads, streams_two, branch_grads, grads_branch, branch_inner, streams_one = parts
+    streams_grads, streams_two, branch_grads, grads_branch, branch_inner = parts
     streams_grads = streams_grads.reshape(count, count)
     hyper_one = jnp.concatenate(
         [
@@ -1468,9 +1772,6 @@
         1,
     )
     grad_hyper = jnp.stack([hyper_one, hyper_two])
-    tokens_all = length * lax.axis_size("row")
-    token_scale = tokens_all ** (-0.5)
-    model_rate = D ** (-0.5) * token_scale
     first = update_blocks(
         attention_in, grad_attention, moment_attention_in, average_attention_in, model_rate, 0
     )
@@ -1481,15 +1782,6 @@
         average_attention_out,
         model_rate,
         attention_in.shape[0] * heads,
-    )
-    third = update_blocks(gate_up, grad_hidden, moment_gate_up, average_gate_up, model_rate, 0)
-    fourth = update_blocks(
-        down_weights,
-        grad_hidden,
-        moment_down_weights,
-        average_down_weights,
-        FF ** (-0.5) * token_scale,
-        gate_up.shape[0] * gate_up.shape[2],
     )
     fifth = update(
         hyper_mix,

time: 741 us -> 674 us (0.910)
  Pallas kernels: 642 us -> 584 us
  local copies, waits for them, and re-layouts: 28.6 us -> 9.86 us
  starting transfers between devices: 15.2 us -> 25.4 us
    pallas_call x4, Pallas kernels: 451 us -> 360 us  [call(): pl.pallas_call(body, out_shape=outs, in_specs=[pl.BlockSpec(memory_space=...]
    pallas_call x1 -> x3, Pallas kernels: 5.37 us -> 69.5 us  [the longest x1 50.5 us: gate_forward(): pl.pallas_call(functools.partial(gate_kernel, size, steps, chunks), grid=...]
    pallas_call x7 -> x5, Pallas kernels: 126 us -> 93.6 us  [tiled(): pl.pallas_call(body, grid=grid, out_shape=outs, in_specs=specs, out_specs...]
    unnamed x64 -> x21, local copies, waits for them, and re-layouts: 20.4 us -> 3.31 us
    ppermute x6 -> x8, starting transfers between devices: 14.5 us -> 25 us  [the longest x3 15.2 us: scatter_steps(): lax.ppermute(first, 'col', up)]
  transfers between devices with their start and end apart: 11 -> 13, of which waited for: 3 -> 5; matrix products, arithmetic and copies ran while one was open for 4% -> 3% of each run, Pallas kernels for 86% -> 79%
where the time goes in v4:
time: 674 us; the launch traced here: 667 us
  Pallas kernels  584 us (87%)
  starting transfers between devices  25.4 us (4%)
  waiting for transfers between devices  18 us (3%)
  other arithmetic  15.5 us (2%)
  between operations  14.5 us (2%)
  local copies, waits for them, and re-layouts  9.86 us (1%)
    pallas_call x4, Pallas kernels, call(): pl.pallas_call(body, out_shape=outs, in_specs=[pl.BlockSpec(memory_space=...  360 us
    pallas_call x5, Pallas kernels, tiled(): pl.pallas_call(body, grid=grid, out_shape=outs, in_specs=specs, out_specs...  93.6 us
    pallas_call x1, Pallas kernels, gate_forward(): pl.pallas_call(functools.partial(gate_kernel, size, steps, chunks), grid=...  50.5 us
    pallas_call x4, Pallas kernels, update_blocks(): pl.pallas_call(functools.partial(update_kernel, rate, turned), grid=grid,...  27.5 us
    pallas_call x1, Pallas kernels, attend_back(): pl.pallas_call(functools.partial(attend_back_kernel, block), grid=(heads,...  18.2 us
    ppermute x3, starting transfers between devices, scatter_steps(): lax.ppermute(first, 'col', up)  15.2 us
    pallas_call x1, Pallas kernels, attend_forward(): pl.pallas_call(functools.partial(attend_forward_kernel, block), grid=(hea...  14.5 us
  transfers between devices with their start and end apart: 13, of which 5 were waited for; matrix products, arithmetic and copies ran while one was open for 3% of the time, Pallas kernels for 79%

profile of v4, /device:TPU:0, one launch (start us, length us, event | category | flops | bytes accessed | tf_op | source)
XLA Modules:
  0.0 666.9 jit_solution(14447346637159788406)
XLA Ops:
  11.2 84.7 %norm_in.1 = (bf16[1024,2048]{1,0:T(8,128)(2,1)}, f32[1024,1]{1,0:T(8,128)}, bf16[1024,512]{1,0:T(8,128)(2,1)}, f32[16,8,128]{2,1,0:T(8,128)}, bf16[256,6144]{1,0:T(8,128)(2,1)}) custom-call(f32[2,4,6]{2,1,0:T(4,128)} %mix.9, bf16[4,1024,512]{2,1,0:T(8,128)(2,1)} %streams_in.3, bf16[4,1024,512]{2,1,0:T(8,128)(2,1)} %grads.3, f32[2,256,2048]{2,1,0:T(8,128)} %weight.4, ...), custom_call_target="tpu_custom_call" | custom-call | flops 99999997952 | bytes 23138496 | tf_op jit(solution)/shard_map/norm_in/pallas_call | solution.py:323
  98.4 4.6 collective-permute-start
  107.8 12.0 %project_in.1.query.key.value = f32[1024,1536]{1,0:T(8,128)} custom-call(bf16[1024,2048]{1,0:T(8,128)(2,1)} %get-tuple-element.76.left.normal_in, bf16[2048,2048]{1,0:T(8,128)(2,1)} %all-gather.3.cloned.1.call-done.right.rows_in.output_in.rows), custom_call_target="tpu_custom_call" | custom-call | flops 6442450944 | bytes 18874368 | tf_op jit(solution)/shard_map/project_in/pallas_call | solution.py:1019
  119.8 14.5 %attend_forward.1 = (bf16[1024,512]{1,0:T(8,128)(2,1)}, bf16[1024,512]{1,0:T(8,128)(2,1)}, bf16[1024,512]{1,0:T(8,128)(2,1)}, bf16[1024,512]{1,0:T(8,128)(2,1)}) custom-call(f32[1024,1536]{1,0:T(8,128)} %project_in.1.query.key.value, f32[1024,1536]{1,0:T(8,128)} %project_in.1.query.key.value, f32[1024,1536]{1,0:T(8,128)} %project_in.1.query.key.value, ...), custom_call_target="tpu_custom_call" | custom-call | tf_op jit(solution)/shard_map/attend_forward/pallas_call | solution.py:1440
  134.3 116.9 %norm_mid.1 = (bf16[1024,2048]{1,0:T(8,128)(2,1)}, f32[1024,1]{1,0:T(8,128)}, f32[1024,512]{1,0:T(8,128)}) custom-call(f32[2,4,6]{2,1,0:T(4,128)} %mix.9, bf16[1024,512]{1,0:T(8,128)(2,1)} %get-tuple-element.79.attended_in.other_right, bf16[2048,2048]{1,0:T(8,128)(2,1)} %all-gather.3.cloned.1.call-done.right.rows_in.output_in.rows, ...), custom_call_target="tpu_custom_call" | custom-call | flops 99999997952 | bytes 19927232 | tf_op jit(solution)/shard_map/norm_mid/pallas_call | solution.py:323
  251.2 50.5 %gate_forward.1 = (bf16[1024,2048]{1,0:T(8,128)(2,1)}, bf16[1024,2048]{1,0:T(8,128)(2,1)}, bf16[1024,2048]{1,0:T(8,128)(2,1)}, bf16[1024,2048]{1,0:T(8,128)(2,1)}, bf16[1024,2048]{1,0:T(8,128)(2,1)}) custom-call(bf16[1024,2048]{1,0:T(8,128)(2,1)} %get-tuple-element.81.whole.left.normal_in, ...), custom_call_target="tpu_custom_call" | custom-call | flops 25769803776 | bytes 25165824 | tf_op jit(solution)/shard_map/gate_forward/pallas_call | solution.py:1198
  302.0 15.5 %gate_back.1.right.gated_in = bf16[2,1024,2048]{2,1,0:T(8,128)(2,1)} custom-call(bf16[1024,2048]{1,0:T(8,128)(2,1)} %get-tuple-element.85.whole.other_left, bf16[2048,6144]{1,0:T(8,128)(2,1)} %all-gather.5.cloned.1.call-done.gate_rows.upper_rows.down_rows.rows.rows_in, bf16[1024,2048]{1,0:T(8,128)(2,1)} %get-tuple-element.86.by_gate, ...), custom_call_target="tpu_custom_call" | custom-call | flops 8589934592 | bytes 46137344 | tf_op jit(solution)/shard_map/gate_back/pallas_call | solution.py:1019
  317.5 36.9 %outer_hidden.1 = bf16[2048,6144]{1,0:T(8,128)(2,1)} custom-call(bf16[1024,2048]{1,0:T(8,128)(2,1)} %get-tuple-element.81.whole.left.normal_in, bf16[2,1024,2048]{2,1,0:T(8,128)(2,1)} %gate_back.1.right.gated_in, bf16[1024,2048]{1,0:T(8,128)(2,1)} %get-tuple-element.85.whole.other_left, bf16[1024,2048]{1,0:T(8,128)(2,1)} %get-tuple-element.88.other_right), custom_call_target="tpu_custom_call" | custom-call | flops 25769803776 | bytes 46137344 | tf_op jit(solution)/shard_map/outer_hidden/pallas_call | solution.py:1019
  354.5 137.2 %back_mid.1 = (bf16[1024,2048]{1,0:T(8,128)(2,1)}, f32[1024,512]{1,0:T(8,128)}, bf16[1024,512]{1,0:T(8,128)(2,1)}) custom-call(f32[2,4,6]{2,1,0:T(4,128)} %mix.9, bf16[2,1024,2048]{2,1,0:T(8,128)(2,1)} %gate_back.1.right.gated_in, bf16[2048,6144]{1,0:T(8,128)(2,1)} %all-gather.5.cloned.1.call-done.gate_rows.upper_rows.down_rows.rows.rows_in, ...), custom_call_target="tpu_custom_call" | custom-call | flops 1000000000 | bytes 57675968 | tf_op jit(solution)/shard_map/back_mid/pallas_call | solution.py:323
  491.8 18.2 %attend_back.1.grads.right = bf16[3,1024,512]{2,1,0:T(8,128)(2,1)} custom-call(bf16[1024,512]{1,0:T(8,128)(2,1)} %get-tuple-element.96.queries, bf16[1024,512]{1,0:T(8,128)(2,1)} %get-tuple-element.97.key_heads, bf16[1024,512]{1,0:T(8,128)(2,1)} %get-tuple-element.98.value_heads, bf16[1024,512]{1,0:T(8,128)(2,1)} %get-tuple-element.99.grad_result, ...), custom_call_target="tpu_custom_call" | custom-call | tf_op jit(solution)/shard_map/attend_back/pallas_call | solution.py:1517
  509.9 11.0 %heads_product.1.partial_in = bf16[1024,2048]{1,0:T(8,128)(2,1)} custom-call(bf16[3,1024,512]{2,1,0:T(8,128)(2,1)} %attend_back.1.grads.right, bf16[2048,2048]{1,0:T(8,128)(2,1)} %all-gather.3.cloned.1.call-done.right.rows_in.output_in.rows), custom_call_target="tpu_custom_call" | custom-call | flops 6442450944 | bytes 15728640 | tf_op jit(solution)/shard_map/heads_product/pallas_call | solution.py:1019
  523.9 5.5 collective-permute-start.2
  529.4 18.2 %outer_attention.1 = bf16[2048,2048]{1,0:T(8,128)(2,1)} custom-call(bf16[1024,2048]{1,0:T(8,128)(2,1)} %get-tuple-element.76.left.normal_in, bf16[3,1024,512]{2,1,0:T(8,128)(2,1)} %attend_back.1.grads.right, bf16[1024,2048]{1,0:T(8,128)(2,1)} %get-tuple-element.100.other_left, bf16[1024,512]{1,0:T(8,128)(2,1)} %get-tuple-element.79.attended_in.other_right), custom_call_target="tpu_custom_call" | custom-call | flops 8589934592 | bytes 20971520 | tf_op jit(solution)/shard_map/outer_attention/pallas_call | solution.py:1019
  547.6 4.5 reduce-scatter.6.cloned.1.call-done.grad
  552.2 3.4 add_convert_fusion.2
  556.9 4.6 collective-permute-start.4
  561.5 6.9 %update.5 = (f32[2048,256]{1,0:T(8,128)}, f32[2048,256]{1,0:T(8,128)}, f32[2048,256]{1,0:T(8,128)}) custom-call(f32[2048,256]{1,0:T(8,128)} %weight.5, bf16[256,6144]{1,0:T(8,128)(2,1)} %reduce-scatter.6.cloned.1.call-done.grad, f32[2048,256]{1,0:T(8,128)} %moment.5, f32[2048,256]{1,0:T(8,128)} %average.5), custom_call_target="tpu_custom_call" | custom-call | flops 5242880 | bytes 13631488 | tf_op jit(solution)/shard_map/update/pallas_call | solution.py:1559
  568.5 12.1 %update.4 = (f32[2,256,2048]{2,1,0:T(8,128)}, f32[2,256,2048]{2,1,0:T(8,128)}, f32[2,256,2048]{2,1,0:T(8,128)}) custom-call(f32[2,256,2048]{2,1,0:T(8,128)} %weight.4, bf16[256,6144]{1,0:T(8,128)(2,1)} %reduce-scatter.6.cloned.1.call-done.grad, f32[2,256,2048]{2,1,0:T(8,128)} %moment.4, f32[2,256,2048]{2,1,0:T(8,128)} %average.4), custom_call_target="tpu_custom_call" | custom-call | flops 10485760 | bytes 27262976 | tf_op jit(solution)/shard_map/update/pallas_call | solution.py:1559
  588.0 5.1 collective-permute-start.6
  593.3 10.6 %end_streams.1 = (bf16[4,1024,512]{2,1,0:T(8,128)(2,1)}, f32[16,8,128]{2,1,0:T(8,128)}) custom-call(f32[2,4,6]{2,1,0:T(4,128)} %mix.9, bf16[4,1024,512]{2,1,0:T(8,128)(2,1)} %streams_in.3, bf16[4,1024,512]{2,1,0:T(8,128)(2,1)} %grads.3, f32[1024,512]{1,0:T(8,128)} %get-tuple-element.80.branch_one, ...), custom_call_target="tpu_custom_call" | custom-call | flops 125829120 | bytes 18874368 | tf_op jit(solution)/shard_map/end_streams/pallas_call | solution.py:970
  603.9 9.4 %collective-permute-done.7.last_in = bf16[1024,512]{1,0:T(8,128)(2,1)S(1)} collective-permute-done((bf16[1024,512]{1,0:T(8,128)(2,1)}, bf16[1024,512]{1,0:T(8,128)(2,1)S(1)}, u32[]{:S(2)}, u32[]{:S(2)}) %collective-permute-start.7) | collective-permute-done | bytes 1048608 | tf_op jit(solution)/shard_map/ppermute | solution.py:1600
  615.2 21.6 %back_in.1 = (f32[1024,512]{1,0:T(8,128)}, f32[8,128]{1,0:T(8,128)}) custom-call(bf16[1024,2048]{1,0:T(8,128)(2,1)} %heads_product.1.partial_in, bf16[1024,512]{1,0:T(8,128)(2,1)} %copy-done.1, bf16[1024,512]{1,0:T(8,128)(2,1)} %copy-done, bf16[1024,2048]{1,0:T(8,128)(2,1)} %get-tuple-element.76.left.normal_in, f32[1024,1]{1,0:T(8,128)} %get-tuple-element.117.scale, ...), custom_call_target="tpu_custom_call" | custom-call | flops 1000000000 | bytes 16916480 | tf_op jit(solution)/shard_map/back_in/pallas_call | solution.py:323
  640.5 8.5 %grad_streams.1 = f32[4,1024,512]{2,1,0:T(8,128)} custom-call(f32[2,4,6]{2,1,0:T(4,128)} %mix.9, bf16[4,1024,512]{2,1,0:T(8,128)(2,1)} %grads.3, f32[1024,512]{1,0:T(8,128)} %get-tuple-element.94.inner_two, f32[1024,512]{1,0:T(8,128)} %get-tuple-element.120.inner_one), custom_call_target="tpu_custom_call" | custom-call | flops 20971520 | bytes 16777216 | tf_op jit(solution)/shard_map/grad_streams/pallas_call | solution.py:1003
  654.4 5.6 update.6
  (82 shorter events, 34.3 us)
Async XLA Ops:
  7.2 100.6 %all-gather.3.cloned.1.call-start = ((), (), s32[]{:S(2)}) async-start(), calls=%async_computation.3 | async-start | bytes 9437184 | tf_op jit(solution)/shard_map/all_gather | solution.py:1655
  11.1 240.1 %all-gather.5.cloned.1.call-start = ((), (), s32[]{:S(2)}) async-start(), calls=%async_computation.4 | async-start | bytes 28311552 | tf_op jit(solution)/shard_map/all_gather | solution.py:1664
  95.9 1.2 copy-start.7
  95.9 7.1 %copy-start.4 = (s32[1,1024]{1,0:T(1,128)S(1)}, s32[1,1024]{1,0:T(1,128)}, u32[]{:S(2)}) copy-start(s32[1,1024]{1,0:T(1,128)} %row.3) | copy-start | bytes 12292
  96.0 395.8 %reduce-scatter.4.cloned.1.call-start = ((), (), s32[]{:S(2)}) async-start(), calls=%async_computation.5 | async-start | bytes 5242880 | tf_op jit(solution)/shard_map/reduce_scatter | solution.py:1681
  97.1 37.2 %collective-permute-start.1 = (bf16[1024,512]{1,0:T(8,128)(2,1)S(1)}, bf16[1024,512]{1,0:T(8,128)(2,1)S(1)}, u32[]{:S(2)}, u32[]{:S(2)}) collective-permute-start(bf16[1024,512]{1,0:T(8,128)(2,1)S(1)} %copy-done.7), channel_id=1, source_target_pairs={{1,0},{2,1},{3,2},{5,4},{6,5},{7,6},{9,8},{10,9},{11,10},{13,12},{... | collective-permute-start | bytes 3145736 | tf_op jit(solution)/shard_map/ppermute | solution.py:1668
  98.4 35.9 %collective-permute-start = (bf16[1024,512]{1,0:T(8,128)(2,1)S(1)}, bf16[1024,512]{1,0:T(8,128)(2,1)S(1)}, u32[]{:S(2)}, u32[]{:S(2)}) collective-permute-start(bf16[1024,512]{1,0:T(8,128)(2,1)S(1)} %copy-done.7), channel_id=1, source_target_pairs={{0,1},{1,2},{2,3},{4,5},{5,6},{6,7},{8,9},{9,10},{10,11},{12,13},{... | collective-permute-start | bytes 3145736 | tf_op jit(solution)/shard_map/ppermute | solution.py:1667
  134.3 116.9 %copy-start.8 = (bf16[1024,512]{1,0:T(8,128)(2,1)}, bf16[1024,512]{1,0:T(8,128)(2,1)S(1)}, u32[]{:S(2)}) copy-start(bf16[1024,512]{1,0:T(8,128)(2,1)S(1)} %collective-permute-done.1.after_in) | copy-start | bytes 3145732
  134.3 116.9 %copy-start.9 = (bf16[1024,512]{1,0:T(8,128)(2,1)}, bf16[1024,512]{1,0:T(8,128)(2,1)S(1)}, u32[]{:S(2)}) copy-start(bf16[1024,512]{1,0:T(8,128)(2,1)S(1)} %collective-permute-done.before_in) | copy-start | bytes 3145732
  301.7 250.4 %reduce-scatter.6.cloned.1.call-start = ((), (), s32[]{:S(2)}) async-start(), calls=%async_computation.6 | async-start | bytes 28311552 | tf_op jit(solution)/shard_map/reduce_scatter | solution.py:1622
  354.4 297.1 %reduce-scatter.8.cloned.1.call-start = ((), (), s32[]{:S(2)}) async-start(), calls=%async_computation.7 | async-start | bytes 9437184 | tf_op jit(solution)/shard_map/reduce_scatter | solution.py:1622
  522.6 25.0 %collective-permute-start.3 = (bf16[1024,512]{1,0:T(8,128)(2,1)S(1)}, bf16[1024,512]{1,0:T(8,128)(2,1)S(1)}, u32[]{:S(2)}, u32[]{:S(2)}) collective-permute-start(bf16[1024,512]{1,0:T(8,128)(2,1)S(1)} %get-tuple-element.144), channel_id=1, source_target_pairs={{1,0},{2,1},{3,2},{5,4},{6,5},{7,6},{9,8},{10,9},{11,10},{13,12},{... | collective-permute-start | bytes 3145736 | tf_op jit(solution)/shard_map/ppermute | solution.py:1600
  523.9 23.7 %collective-permute-start.2 = (bf16[1024,512]{1,0:T(8,128)(2,1)S(1)}, bf16[1024,512]{1,0:T(8,128)(2,1)}, u32[]{:S(2)}, u32[]{:S(2)}) collective-permute-start(bf16[1024,512]{1,0:T(8,128)(2,1)S(1)} %get-tuple-element.145), channel_id=1, source_target_pairs={{0,1},{1,2},{2,3},{4,5},{5,6},{6,7},{8,9},{9,10},{10,11},{12,13},{... | collective-permute-start | bytes 3145736 | tf_op jit(solution)/shard_map/ppermute | solution.py:1600
  555.6 27.0 %collective-permute-start.5 = (bf16[1024,512]{1,0:T(8,128)(2,1)}, bf16[1024,512]{1,0:T(8,128)(2,1)S(1)}, u32[]{:S(2)}, u32[]{:S(2)}) collective-permute-start(bf16[1024,512]{1,0:T(8,128)(2,1)} %get-tuple-element.142), channel_id=1, source_target_pairs={{1,0},{2,1},{3,2},{5,4},{6,5},{7,6},{9,8},{10,9},{11,10},{13,12},{... | collective-permute-start | bytes 3145736 | tf_op jit(solution)/shard_map/ppermute | solution.py:1600
  556.9 26.7 %collective-permute-start.4 = (bf16[1024,512]{1,0:T(8,128)(2,1)S(1)}, bf16[1024,512]{1,0:T(8,128)(2,1)S(1)}, u32[]{:S(2)}, u32[]{:S(2)}) collective-permute-start(bf16[1024,512]{1,0:T(8,128)(2,1)S(1)} %get-tuple-element.143), channel_id=1, source_target_pairs={{0,1},{1,2},{2,3},{4,5},{5,6},{6,7},{8,9},{9,10},{10,11},{12,13},{... | collective-permute-start | bytes 3145736 | tf_op jit(solution)/shard_map/ppermute | solution.py:1600
  583.6 9.5 %copy-start.2 = (f32[2,4,6]{2,1,0:T(4,128)S(1)}, f32[2,4,6]{2,1,0:T(4,128)}, u32[]{:S(2)}) copy-start(f32[2,4,6]{2,1,0:T(4,128)} %mix.9) | copy-start | bytes 580
  586.7 26.6 %collective-permute-start.7 = (bf16[1024,512]{1,0:T(8,128)(2,1)}, bf16[1024,512]{1,0:T(8,128)(2,1)S(1)}, u32[]{:S(2)}, u32[]{:S(2)}) collective-permute-start(bf16[1024,512]{1,0:T(8,128)(2,1)} %get-tuple-element.140), channel_id=1, source_target_pairs={{1,0},{2,1},{3,2},{5,4},{6,5},{7,6},{9,8},{10,9},{11,10},{13,12},{... | collective-permute-start | bytes 3145736 | tf_op jit(solution)/shard_map/ppermute | solution.py:1600
  588.0 26.2 %collective-permute-start.6 = (bf16[1024,512]{1,0:T(8,128)(2,1)S(1)}, bf16[1024,512]{1,0:T(8,128)(2,1)S(1)}, u32[]{:S(2)}, u32[]{:S(2)}) collective-permute-start(bf16[1024,512]{1,0:T(8,128)(2,1)S(1)} %get-tuple-element.141), channel_id=1, source_target_pairs={{0,1},{1,2},{2,3},{4,5},{5,6},{6,7},{8,9},{9,10},{10,11},{12,13},{... | collective-permute-start | bytes 3145736 | tf_op jit(solution)/shard_map/ppermute | solution.py:1600
  613.3 1.0 copy-start
  614.2 1.0 copy-start.1
  640.5 10.4 %copy-start.3 = (f32[2,4,6]{2,1,0:T(4,128)S(1)}, f32[2,4,6]{2,1,0:T(4,128)}, u32[]{:S(2)}) copy-start(f32[2,4,6]{2,1,0:T(4,128)} %mix.9) | copy-start | bytes 580
  640.5 10.4 %copy-start.5 = (f32[2,4,6]{2,1,0:T(4,128)S(1)}, f32[2,4,6]{2,1,0:T(4,128)}, u32[]{:S(2)}) copy-start(f32[2,4,6]{2,1,0:T(4,128)} %param.34) | copy-start | bytes 580
  640.5 10.4 %copy-start.6 = (f32[2,4,6]{2,1,0:T(4,128)S(1)}, f32[2,4,6]{2,1,0:T(4,128)}, u32[]{:S(2)}) copy-start(f32[2,4,6]{2,1,0:T(4,128)} %param.29) | copy-start | bytes 580
Sparse Core Ops, SparseCore 0:
  11.2 57.1 all-gather.2
  96.1 125.1 all-gather.4
  301.9 85.6 reduce-scatter.3
  391.5 160.6 reduce-scatter.5
  555.8 71.3 reduce-scatter.7

commit v5 on v4

--- a/solution.py
+++ b/solution.py
@@ -25,18 +25,6 @@
 LOG2E = 1.4426950408889634
 LANES = (((1,), (1,)), ((), ()))
 ROWS = (((0,), (0,)), ((), ()))
-
-
-def rope_tables(segments):
-    segments = segments[0]
-    length = segments.shape[0]
-    index = jnp.arange(length, dtype=jnp.int32)
-    before = jnp.concatenate([jnp.full((1,), -1, jnp.int32), segments[:-1]])
-    starts = jnp.where(segments != before, index, 0)
-    places = index - lax.cummax(starts)
-    rates = 10000.0 ** (-2.0 * jnp.arange(HEAD_DIM // 2).astype(jnp.float32) / HEAD_DIM)
-    angle = places[:, None].astype(jnp.float32) * rates
-    return (jnp.cos(angle), jnp.sin(angle))
 
 
 def line_exchange(
@@ -423,11 +411,16 @@
     grads_in,
     gate_in,
     down_in,
+    documents,
+    rates,
     whole_out,
     scale,
     branch_grad,
     products,
     packed,
+    column,
+    cosine,
+    sine,
     whole,
     grads,
     gate_up,
@@ -459,6 +452,23 @@
             for wait in waits:
                 wait.wait()
 
+        own_docs = documents[:, pl.ds(pl.multiple_of(rows.start // GROUP * GROUP, GROUP), GROUP)]
+        turned = jnp.broadcast_to(own_docs.astype(f32), (GROUP, GROUP)).T
+
+        @pl.when(lax.rem(rows.start, GROUP) == 0)
+        def _():
+            group = pl.ds(pl.multiple_of(rows.start, GROUP), GROUP)
+            docs = turned[:, :1]
+            shape = (GROUP, tokens)
+            index = lax.broadcasted_iota(jnp.int32, shape, 0) + rows.start
+            before = lax.broadcasted_iota(jnp.int32, shape, 1) < index
+            same = (docs == documents[...].astype(f32)) & before
+            place = jnp.sum(jnp.where(same, 1.0, 0.0), -1, keepdims=True)
+            angle = place * rates[...]
+            column[group, :] = docs
+            cosine[group, :] = jnp.cos(angle)
+            sine[group, :] = jnp.sin(angle)
+
         for piece in range((kinds + 1) * tiles):
 
             @pl.when(rows.start == piece * chunk)
@@ -488,13 +498,15 @@
     wait_stores()
 
 
-def norm_in(size, streams, grads, gate_up, down, mix, chunk=64, hop=(1, 0, 1)):
+def norm_in(size, streams, grads, gate_up, down, documents, mix, chunk=64, hop=(1, 0, 1)):
     _, tokens, width = streams.shape
     whole = jax.ShapeDtypeStruct((tokens, size * width), jnp.bfloat16)
+    half = HEAD_DIM // 2
+    rates = 10000.0 ** (-2.0 * jnp.arange(half).astype(f32) / HEAD_DIM)
     return call(
         functools.partial(norm_in_kernel, size, chunk, hop),
-        (mix, streams, grads, gate_up, down),
-        (SM, VM, pl.ANY, pl.ANY, pl.ANY),
+        (mix, streams, grads, gate_up, down, documents, rates[None]),
+        (SM, VM, pl.ANY, pl.ANY, pl.ANY, VM, VM),
         [
             whole,
             jax.ShapeDtypeStruct((tokens, 1), f32),
@@ -503,8 +515,11 @@
             jax.ShapeDtypeStruct(
                 (gate_up.shape[1], (gate_up.shape[0] + 1) * gate_up.shape[2]), jnp.bfloat16
             ),
+            jax.ShapeDtypeStruct((tokens, 1), f32),
+            jax.ShapeDtypeStruct((tokens, half), f32),
+            jax.ShapeDtypeStruct((tokens, half), f32),
         ],
-        (pl.ANY, VM, VM, VM, VM),
+        (pl.ANY,) + (VM,) * 7,
         held(whole, grads, gate_up, down)
         + [pltpu.SemaphoreType.DMA((3,)), pltpu.SemaphoreType.DMA((tokens // GROUP,))]
         + exchange_scratch(size, tokens, width, chunk, False, True),
@@ -744,6 +759,107 @@
     return total
 
 
+def back_sums_kernel(
+    size, partial_in, normal_in, first_sum, second_sum, partial, normal, facts, loads, sent, got
+):
+    tokens, features = partial.shape
+    groups = tokens // GROUP
+    me = lax.axis_index("col")
+
+    def rows_of(group):
+        return pl.ds(pl.multiple_of(group * GROUP, GROUP), GROUP)
+
+    def load(way, group):
+        source, target = ((partial_in, partial), (normal_in, normal))[way]
+        rows = rows_of(group)
+        return pltpu.make_async_copy(source.at[rows], target.at[rows], loads.at[way, group])
+
+    def start_load(group, carry):
+        load(0, group).start()
+        load(1, group).start()
+        return carry
+
+    lax.fori_loop(0, groups, start_load, 0)
+    barrier = pltpu.get_barrier_semaphore()
+    for member in range(size):
+
+        @pl.when(member != me)
+        def _():
+            pl.semaphore_signal(barrier, inc=1, device_id={"col": member}, device_id_type=MESH)
+
+    def own(group, carry):
+        load(0, group).wait()
+        load(1, group).wait()
+        rows = rows_of(group)
+        total = partial[rows, :].astype(f32)
+        one = jnp.sum(total, -1, keepdims=True)
+        two = jnp.sum(total * normal[rows, :].astype(f32), -1, keepdims=True)
+        lane = lax.broadcasted_iota(jnp.int32, (GROUP, 128), 1)
+        packed = jnp.where(lane == 0, one, jnp.where(lane == 1, two, 0.0))
+        facts[me, pl.ds(pl.multiple_of(group * 8, 8), 8)] = packed.T[:8]
+        return carry
+
+    lax.fori_loop(0, groups, own, 0)
+    pl.semaphore_wait(barrier, size - 1)
+
+    def fact_copy(place, member):
+        return pltpu.make_async_remote_copy(
+            src_ref=facts.at[place],
+            dst_ref=facts.at[place],
+            send_sem=sent.at[member],
+            recv_sem=got.at[place],
+            device_id={"col": member},
+            device_id_type=MESH,
+        )
+
+    for member in range(size):
+
+        @pl.when(member != me)
+        def _():
+            fact_copy(me, member).start()
+
+    for member in range(size):
+
+        @pl.when(member != me)
+        def _():
+            fact_copy(member, member).wait()
+
+    def conclude(group, carry):
+        fact_rows = pl.ds(pl.multiple_of(group * 8, 8), 8)
+        total = facts[0, fact_rows]
+        for place in range(1, size):
+            total = total + facts[place, fact_rows]
+        total = total * (1.0 / features)
+        turned = jnp.concatenate([total, jnp.zeros((GROUP - 8, 128), f32)], 0).T
+        first_sum[rows_of(group), :] = turned[:, :1]
+        second_sum[rows_of(group), :] = turned[:, 1:2]
+        return carry
+
+    lax.fori_loop(0, groups, conclude, 0)
+
+
+def back_sums(size, partial, normal):
+    tokens = partial.shape[0]
+    dma = pltpu.SemaphoreType.DMA
+    return call(
+        functools.partial(back_sums_kernel, size),
+        (partial, normal),
+        (pl.ANY, pl.ANY),
+        [jax.ShapeDtypeStruct((tokens, 1), f32)] * 2,
+        (VM, VM),
+        held(partial, normal)
+        + [
+            pltpu.VMEM((size, tokens // GROUP * 8, 128), f32),
+            dma((2, tokens // GROUP)),
+            dma((size,)),
+            dma((size,)),
+        ],
+        "back_sums",
+        6,
+        10**9,
+    )
+
+
 def back_in_kernel(
     size,
     partial_in,
@@ -751,6 +867,8 @@
     last_in,
     normal_in,
     scale,
+    first_sum,
+    second_sum,
     streams_in,
     streams_grads,
     other_products,
@@ -761,12 +879,9 @@
     last,
     normal,
     streams,
-    facts,
     products,
     shares,
     loads,
-    facts_sent,
-    facts_got,
     shares_sent,
     shares_got,
 ):
@@ -795,60 +910,15 @@
                     barrier, inc=1, device_id={axis: member}, device_id_type=MESH
                 )
 
-    for wait in waits[:4]:
+    products[...] = jnp.zeros_like(products)
+    for wait in waits:
         wait.wait()
 
-    def rows_of(group):
-        return pl.ds(pl.multiple_of(group * GROUP, GROUP), GROUP)
-
-    def sums(group, carry):
-        rows = rows_of(group)
+    def conclude(group, carry):
+        rows = pl.ds(pl.multiple_of(group * GROUP, GROUP), GROUP)
         total = share[rows, :].astype(f32) + first[rows, :].astype(f32) + last[rows, :].astype(f32)
-        inner[rows, :] = total
-        one = jnp.sum(total, -1, keepdims=True)
-        two = jnp.sum(total * normal[rows, :].astype(f32), -1, keepdims=True)
-        lane = lax.broadcasted_iota(jnp.int32, (GROUP, 128), 1)
-        packed = jnp.where(lane == 0, one, jnp.where(lane == 1, two, 0.0))
-        facts[me, pl.ds(pl.multiple_of(group * 8, 8), 8)] = packed.T[:8]
-        return carry
-
-    lax.fori_loop(0, groups, sums, 0)
-    pl.semaphore_wait(barrier, size - 1 + count_rows - 1)
-
-    def fact_copy(place, member):
-        return pltpu.make_async_remote_copy(
-            src_ref=facts.at[place],
-            dst_ref=facts.at[place],
-            send_sem=facts_sent.at[member],
-            recv_sem=facts_got.at[place],
-            device_id={"col": member},
-            device_id_type=MESH,
-        )
-
-    for member in range(size):
-
-        @pl.when(member != me)
-        def _():
-            fact_copy(me, member).start()
-
-    products[...] = jnp.zeros_like(products)
-    waits[4].wait()
-    for member in range(size):
-
-        @pl.when(member != me)
-        def _():
-            fact_copy(member, member).wait()
-
-    def conclude(group, carry):
-        rows = rows_of(group)
-        fact_rows = pl.ds(pl.multiple_of(group * 8, 8), 8)
-        total = facts[0, fact_rows]
-        for place in range(1, size):
-            total = total + facts[place, fact_rows]
-        total = total * (1.0 / (size * width))
-        turned = jnp.concatenate([total, jnp.zeros((GROUP - 8, 128), f32)], 0).T
         own = scale[rows, :] * (
-            inner[rows, :] - turned[:, :1] - turned[:, 1:2] * normal[rows, :].astype(f32)
+            total - first_sum[rows, :] - second_sum[rows, :] * normal[rows, :].astype(f32)
         )
         inner[rows, :] = own
         for i in range(count):
@@ -860,6 +930,7 @@
     total = jnp.concatenate([jnp.sum(jnp.sum(part, 1), -1, keepdims=True) for part in parts], 0)
     total = jnp.concatenate([total, jnp.zeros((128 - total.shape[0], 1), f32)], 0)
     total = jnp.broadcast_to(total, (128, 128)).T[:8]
+    pl.semaphore_wait(barrier, size - 1 + count_rows - 1)
     for axis, members, base in (("col", size, 0), ("row", count_rows, size)):
         here = lax.axis_index(axis)
 
@@ -892,15 +963,15 @@
     whole_products[...] = total
 
 
-def back_in(size, partial, first, last, normal, scale, streams, streams_grads, other_products):
+def back_in(size, partial, first, last, normal, scale, sums, streams, streams_grads, other_products):
     count, tokens, width = streams.shape
     own = -(-count // 8) * 8
     members = size + lax.axis_size("row")
     dma = pltpu.SemaphoreType.DMA
     return call(
         functools.partial(back_in_kernel, size),
-        (partial, first, last, normal, scale, streams, streams_grads, other_products),
-        (pl.ANY, pl.ANY, pl.ANY, pl.ANY, VM, pl.ANY, VM, VM),
+        (partial, first, last, normal, scale, *sums, streams, streams_grads, other_products),
+        (pl.ANY, pl.ANY, pl.ANY, pl.ANY, VM, VM, VM, pl.ANY, VM, VM),
         [
             jax.ShapeDtypeStruct((tokens, width), f32),
             jax.ShapeDtypeStruct((8, 128), f32),
@@ -908,12 +979,9 @@
         (VM, VM),
         held(first, first, last, first, streams)
         + [
-            pltpu.VMEM((size, tokens // GROUP * 8, 128), f32),
             pltpu.VMEM((own, 8, 128), f32),
             pltpu.VMEM((members, 8, 128), f32),
             dma((5,)),
-            dma((size,)),
-            dma((size,)),
             dma((members,)),
             dma((members,)),
         ],
@@ -1333,34 +1401,61 @@
     )
 
 
-def heads_kernel(grads, rows, out):
+def heads_kernel(ends, grads, rows, *refs):
     width = grads.shape[2]
     total = 0.0
     for k in range(grads.shape[0]):
         total = total + lax.dot_general(
             grads[k], rows[:, k * width : (k + 1) * width], LANES, preferred_element_type=f32
         )
-    out[...] = total.astype(jnp.bfloat16)
-
-
-def heads_product(grads, weights, tile=512):
+    total = total.astype(jnp.bfloat16)
+    if ends:
+        out, low, high = refs
+
+        @pl.when(pl.program_id(0) == 0)
+        def _():
+            low[...] = total
+
+        @pl.when(pl.program_id(0) == 1)
+        def _():
+            high[...] = total
+
+    else:
+        out = refs[1]
+    out[...] = total
+
+
+def heads_product(size, grads, weights, begun=None):
     count, tokens, width = grads.shape
     rows = weights.shape[0]
-    tile = min(tile, rows)
-    return tiled(
-        heads_kernel,
-        (rows // tile,),
-        (grads, weights),
-        [
+    tile = rows // size
+    ends = begun is None
+    place = (lambda j: j * (size - 1)) if ends else (lambda j: j + 1)
+    whole = jax.ShapeDtypeStruct((tokens, rows), jnp.bfloat16)
+    one = jax.ShapeDtypeStruct((tokens, tile), jnp.bfloat16)
+    own = pl.BlockSpec((tokens, tile), lambda j: (0, 0))
+    steps = 2 if ends else size - 2
+    return pl.pallas_call(
+        functools.partial(heads_kernel, ends),
+        grid=(steps,),
+        out_shape=[whole, one, one] if ends else whole,
+        in_specs=[
             pl.BlockSpec((count, tokens, width), lambda j: (0, 0, 0)),
-            pl.BlockSpec((tile, count * width), lambda j: (j, 0)),
-        ],
-        jax.ShapeDtypeStruct((tokens, rows), jnp.bfloat16),
-        pl.BlockSpec((tokens, tile), lambda j: (0, j)),
-        [],
-        2 * count * tokens * width * rows,
-        "heads_product",
-    )
+            pl.BlockSpec((tile, count * width), lambda j: (place(j), 0)),
+        ]
+        + ([] if ends else [pl.BlockSpec(memory_space=pl.ANY)]),
+        out_specs=[pl.BlockSpec((tokens, tile), lambda j: (0, place(j))), own, own]
+        if ends
+        else pl.BlockSpec((tokens, tile), lambda j: (0, place(j))),
+        input_output_aliases={} if ends else {2: 0},
+        compiler_params=pltpu.CompilerParams(vmem_limit_bytes=60 * 2**20),
+        cost_estimate=pl.CostEstimate(
+            flops=2 * count * tokens * width * steps * tile,
+            bytes_accessed=4 * tokens * rows,
+            transcendentals=0,
+        ),
+        name="heads_product",
+    )(*((grads, weights) if ends else (grads, weights, begun)))
 
 
 def fill_bias(bias, column, row):
@@ -1368,7 +1463,7 @@
     for start in range(0, bias.shape[0], tile):
         shape = (tile, bias.shape[1])
         index = lax.broadcasted_iota(jnp.int32, shape, 0) + start
-        allowed = (column[start : start + tile] == row[...]) & (
+        allowed = (column[start : start + tile] == row[...].astype(f32)) & (
             lax.broadcasted_iota(jnp.int32, shape, 1) <= index
         )
         bias[start : start + tile] = jnp.where(allowed, 0.0, MASKED)
@@ -1532,6 +1627,54 @@
     moment_new = MOMENTUM * moment + step_grad
     weight_new = weight - rate * (step_grad + MOMENTUM * moment_new)
     return (weight_new, moment_new, average + (weight_new - average) / (STEP + 1))
+
+
+def hyper_kernel(rate, products, mix, moment, average, new_mix, new_moment, new_average):
+    count = mix.shape[1]
+    span = range(count)
+    square = count * count
+    shared = [[products[0, i * count + j] for j in span] for i in span]
+    below = [products[0, square + i] for i in span]
+    branch = [products[0, square + count + j] for j in span]
+    outward = [products[0, square + 2 * count + j] for j in span]
+    both = products[0, square + 3 * count]
+    start = square + -(-(3 * count + 1) // 8) * 8
+    above = [products[0, start + i] for i in span]
+
+    def dot(left, right):
+        total = left[0] * right[0]
+        for a, b in zip(left[1:], right[1:]):
+            total = total + a * b
+        return total
+
+    for i in span:
+        rows_two = [[mix[1, j, 1 + k] for k in span] for j in span]
+        column_one = [mix[0, k, 1 + i] for k in span]
+        onto = mix[0, i, 1 + count]
+        one = [above[i]]
+        one = one + [dot(shared[i], rows_two[j]) + below[i] * mix[1, j, 0] for j in span]
+        one.append(dot(rows_two[i], branch) + mix[1, i, 0] * both)
+        two = [dot(column_one, below) + onto * both]
+        two = two + [
+            dot(column_one, [shared[k][j] for k in span]) + onto * branch[j] for j in span
+        ]
+        two.append(outward[i])
+        for layer, grads in ((0, one), (1, two)):
+            for j, grad in enumerate(grads):
+                at = (layer, i, j)
+                results = update(mix[at], grad, moment[at], average[at], rate)
+                new_mix[at], new_moment[at], new_average[at] = results
+
+
+def update_mix(products, mix, moment, average, rate):
+    place = pl.BlockSpec(memory_space=SM)
+    return pl.pallas_call(
+        functools.partial(hyper_kernel, rate),
+        out_shape=[jax.ShapeDtypeStruct(mix.shape, f32)] * 3,
+        in_specs=[place] * 4,
+        out_specs=[place] * 3,
+        name="update_mix",
+    )(products, mix, moment, average)
 
 
 def update_kernel(rate, turned, weight, grad, moment, average, *outs):
@@ -1581,7 +1724,7 @@
     return size, up, down
 
 
-def scatter_steps(partial):
+def scatter_steps(partial, low, high):
     size, up, down = line_ways()
     me = lax.axis_index("col")
     width = partial.shape[1] // size
@@ -1589,8 +1732,7 @@
     def share(place):
         return lax.dynamic_slice_in_dim(partial, place * width, width, 1)
 
-    first = share(jnp.minimum(me + size - 1, size - 1))
-    last = share(jnp.maximum(me - size + 1, 0))
+    first, last = high, low
     for step in range(1, size):
         if step > 1:
             first = share(jnp.minimum(me + size - step, size - 1)).astype(f32) + first.astype(f32)
@@ -1614,16 +1756,26 @@
     return moved
 
 
-def small_matmul(left, right):
-    return jnp.sum(left[:, :, None] * right[None, :, :], 1)
-
-
 def scatter_rows(grad):
     return lax.psum_scatter(grad, "row", scatter_dimension=0, tiled=True)
 
 
-def side_by_side(weights, turned):
-    return jnp.concatenate([weights[k] for k in range(weights.shape[0])] + [turned.T], 1)
+def pack_kernel(weights, turned, out):
+    count, _, columns = weights.shape
+    for k in range(count):
+        out[:, k * columns : (k + 1) * columns] = weights[k].astype(jnp.bfloat16)
+    out[:, count * columns :] = turned[...].T.astype(jnp.bfloat16)
+
+
+def pack(weights, turned):
+    count, rows, columns = weights.shape
+    return pl.pallas_call(
+        pack_kernel,
+        out_shape=jax.ShapeDtypeStruct((rows, count * columns + turned.shape[0]), jnp.bfloat16),
+        in_specs=[pl.BlockSpec(memory_space=VM)] * 2,
+        out_specs=pl.BlockSpec(memory_space=VM),
+        name="pack",
+    )(weights, turned)
 
 
 def per_device(
@@ -1649,17 +1801,12 @@
     size = lax.axis_size("col")
     low = jnp.bfloat16
     count, length, width = streams.shape
-    cosine, sine = rope_tables(segments)
-
-    def gather_rows(weights):
-        return lax.all_gather(weights.astype(low), "row", axis=0, tiled=True)
-
-    attention_weights = gather_rows(side_by_side(attention_in, attention_out))
-
-    one, two = hyper_mix[0], hyper_mix[1]
-    across_one, across_two = one[:, 1 : 1 + count], two[:, 1 : 1 + count]
-    whole_one, scale_one, grad_two, streams_grads, hidden_weights = norm_in(
-        size, streams, cotangent, gate_up, down_weights, hyper_mix
+
+    attention_weights = lax.all_gather(
+        pack(attention_in, attention_out), "row", axis=0, tiled=True
+    )
+    whole_one, scale_one, grad_two, streams_grads, hidden_weights, column, cosine, sine = norm_in(
+        size, streams, cotangent, gate_up, down_weights, segments, hyper_mix
     )
     hidden_weights = lax.all_gather(hidden_weights, "row", axis=0, tiled=True)
     heads = attention_in.shape[2]
@@ -1668,7 +1815,7 @@
     after = lax.ppermute(grad_two, "col", down)
     projected = product(whole_one, attention_weights, 0, 3 * heads, f32, heads, "project_in")
     queries, key_heads, value_heads, attended = attend_forward(
-        projected, cosine, sine, segments.T, segments
+        projected, cosine, sine, column, segments
     )
     attended, before, after = tie(attended, before, after)
     whole_two, scale_two, branch_one = norm_mid(
@@ -1696,18 +1843,18 @@
 
     grad_attended, branch_two = tie(grad_attended, branch_two)
     grad_heads = attend_back(
-        queries, key_heads, value_heads, grad_attended, cosine, sine, segments.T, segments
+        queries, key_heads, value_heads, grad_attended, cosine, sine, column, segments
     )
     tokens_all = length * lax.axis_size("row")
     token_scale = tokens_all ** (-0.5)
     model_rate = D ** (-0.5) * token_scale
-    partial_one = heads_product(grad_heads, attention_weights)
-    steps = scatter_steps(partial_one)
+    begun, low_share, high_share = heads_product(size, grad_heads, attention_weights)
+    partial_one = heads_product(size, grad_heads, attention_weights, begun)
+    steps = scatter_steps(partial_one, low_share, high_share)
     grad_attention = outer(
         whole_one, grad_heads, whole_grad_one, attended, name="outer_attention"
     )
     got, (grad_attention,) = advance(steps, None, grad_attention)
-    grad_attention, grad_hidden = tie(grad_attention, grad_hidden)
     grad_attention = scatter_rows(grad_attention)
     third = update_blocks(gate_up, grad_hidden, moment_gate_up, average_gate_up, model_rate, 0)
     fourth = update_blocks(
@@ -1728,7 +1875,8 @@
         branch_two,
         inner_two,
     )
-    got, (other_products,) = advance(steps, got, other_products)
+    sums = back_sums(size, partial_one, whole_one)
+    got, (other_products, *sums) = advance(steps, got, other_products, *sums)
     first_part, last_part = finish_line(steps, got)
     inner_one, products = back_in(
         size,
@@ -1737,41 +1885,14 @@
         last_part,
         whole_one,
         scale_one,
+        sums,
         streams,
         streams_grads,
         other_products,
     )
     grad_streams = grad_streams_of(hyper_mix, cotangent, inner_two, inner_one)
 
-    products = products[0]
-    streams_one = products[count * count + other_products.shape[0] :][:count]
-    cuts = [count * count, count, count, count, 1]
-    parts = []
-    start = 0
-    for cut in cuts:
-        parts.append(products[start : start + cut])
-        start = start + cut
-    streams_grads, streams_two, branch_grads, grads_branch, branch_inner = parts
-    streams_grads = streams_grads.reshape(count, count)
-    hyper_one = jnp.concatenate(
-        [
-            streams_one[:, None],
-            small_matmul(streams_grads, across_two.T) + streams_two[:, None] * two[None, :, 0],
-            small_matmul(across_two, branch_grads[:, None]) + (two[:, 0] * branch_inner)[:, None],
-        ],
-        1,
-    )
-    hyper_two = jnp.concatenate(
-        [
-            small_matmul(across_one.T, streams_two[:, None])
-            + (one[:, 1 + count] * branch_inner)[:, None],
-            small_matmul(across_one.T, streams_grads)
-            + one[:, 1 + count][:, None] * branch_grads[None, :],
-            grads_branch[:, None],
-        ],
-        1,
-    )
-    grad_hyper = jnp.stack([hyper_one, hyper_two])
+    products, grad_attention = tie(products, grad_attention)
     first = update_blocks(
         attention_in, grad_attention, moment_attention_in, average_attention_in, model_rate, 0
     )
@@ -1783,12 +1904,8 @@
         model_rate,
         attention_in.shape[0] * heads,
     )
-    fifth = update(
-        hyper_mix,
-        grad_hyper,
-        moment_hyper_mix,
-        average_hyper_mix,
-        0.05 * (tokens_all * D) ** (-0.5),
+    fifth = update_mix(
+        products, hyper_mix, moment_hyper_mix, average_hyper_mix, 0.05 * (tokens_all * D) ** (-0.5)
     )
     return (
         final,

time: 674 us -> 656 us (0.973)
  Pallas kernels: 584 us -> 604 us
  waiting for transfers between devices: 18 us -> 0.88 us
  other arithmetic: 15.5 us -> 7.14 us
  local copies, waits for them, and re-layouts: 9.86 us -> 2.45 us
    pallas_call x0 -> x4, Pallas kernels: none -> 19.9 us  [the longest x2 15.1 us: heads_product(): pl.pallas_call(functools.partial(heads_kernel, ends), grid=(steps,), out_...]
    pallas_call x4 -> x5, Pallas kernels: 360 us -> 371 us  [call(): pl.pallas_call(body, out_shape=outs, in_specs=[pl.BlockSpec(memory_space=...]
    ppermute x3, waiting for transfers between devices: 11.4 us -> 0.68 us  [scatter_steps(): lax.ppermute(last, 'col', down)]
    pallas_call x5 -> x4, Pallas kernels: 93.6 us -> 82.8 us  [tiled(): pl.pallas_call(body, grid=grid, out_shape=outs, in_specs=specs, out_specs...]
  transfers between devices with their start and end apart: 13 -> 13, of which waited for: 5 -> 1; matrix products, arithmetic and copies ran while one was open for 3% -> 1% of each run, Pallas kernels for 79% -> 82%
where the time goes in v5:
time: 656 us; the launch traced here: 649 us
  Pallas kernels  604 us (92%)
  starting transfers between devices  20.8 us (3%)
  between operations  14.3 us (2%)
  other arithmetic  7.14 us (1%)
    pallas_call x5, Pallas kernels, call(): pl.pallas_call(body, out_shape=outs, in_specs=[pl.BlockSpec(memory_space=...  371 us
    pallas_call x4, Pallas kernels, tiled(): pl.pallas_call(body, grid=grid, out_shape=outs, in_specs=specs, out_specs...  82.8 us
    pallas_call x1, Pallas kernels, gate_forward(): pl.pallas_call(functools.partial(gate_kernel, size, steps, chunks), grid=...  50.3 us
    pallas_call x4, Pallas kernels, update_blocks(): pl.pallas_call(functools.partial(update_kernel, rate, turned), grid=grid,...  27.4 us
    pallas_call x1, Pallas kernels, attend_back(): pl.pallas_call(functools.partial(attend_back_kernel, block), grid=(heads,...  18 us
    pallas_call x2, Pallas kernels, heads_product(): pl.pallas_call(functools.partial(heads_kernel, ends), grid=(steps,), out_...  15.1 us
    pallas_call x1, Pallas kernels, attend_forward(): pl.pallas_call(functools.partial(attend_forward_kernel, block), grid=(hea...  14.5 us
  transfers between devices with their start and end apart: 13, of which 1 were waited for; matrix products, arithmetic and copies ran while one was open for 1% of the time, Pallas kernels for 82%

profile of v5, /device:TPU:0, one launch (start us, length us, event | category | flops | bytes accessed | tf_op | source)
XLA Modules:
  0.0 649.2 jit_solution(4381070977092785616)
XLA Ops:
  10.5 85.5 %norm_in.1 = (bf16[1024,2048]{1,0:T(8,128)(2,1)}, f32[1024,1]{1,0:T(8,128)}, bf16[1024,512]{1,0:T(8,128)(2,1)}, f32[16,8,128]{2,1,0:T(8,128)}, bf16[256,6144]{1,...) custom-call(f32[2,4,6]{2,1,0:T(4,128)} %mix.11, bf16[4,1024,512]{2,1,0:T(8,128)(2,1)} %streams_in.3, ...), custom_call_target="tpu_custom_call" | custom-call | flops 99999997952 | bytes 23671232 | tf_op jit(solution)/shard_map/norm_in/pallas_call | solution.py:311
  98.5 4.6 collective-permute-start
  103.2 12.4 %project_in.1.query.key.value = f32[1024,1536]{1,0:T(8,128)} custom-call(bf16[1024,2048]{1,0:T(8,128)(2,1)} %get-tuple-element.89.left.normal_in, bf16[2048,2048]{1,0:T(8,128)(2,1)} %all-gather.3.cloned.1.call-done.right.rows_in.output_in.rows), custom_call_target="tpu_custom_call" | custom-call | flops 6442450944 | bytes 18874368 | tf_op jit(solution)/shard_map/project_in/pallas_call | solution.py:1087
  115.6 14.5 %attend_forward.1 = (bf16[1024,512]{1,0:T(8,128)(2,1)}, bf16[1024,512]{1,0:T(8,128)(2,1)}, bf16[1024,512]{1,0:T(8,128)(2,1)}, bf16[1024,512]{1,0:T(8,128)(2,1)}) custom-call(f32[1024,1536]{1,0:T(8,128)} %project_in.1.query.key.value, f32[1024,1536]{1,0:T(8,128)} %project_in.1.query.key.value, f32[1024,1536]{1,0:T(8,128)} %project_in.1.query.key.value, ...), custom_call_target="tpu_custom_call" | custom-call | tf_op jit(solution)/shard_map/attend_forward/pallas_call | solution.py:1535
  130.2 116.8 %norm_mid.1 = (bf16[1024,2048]{1,0:T(8,128)(2,1)}, f32[1024,1]{1,0:T(8,128)}, f32[1024,512]{1,0:T(8,128)}) custom-call(f32[2,4,6]{2,1,0:T(4,128)} %mix.11, bf16[1024,512]{1,0:T(8,128)(2,1)} %get-tuple-element.95.attended_in.other_right, bf16[2048,2048]{1,0:T(8,128)(2,1)} %all-gather.3.cloned.1.call-done.right.rows_in.output_in.rows, ...), custom_call_target="tpu_custom_call" | custom-call | flops 99999997952 | bytes 19927232 | tf_op jit(solution)/shard_map/norm_mid/pallas_call | solution.py:311
  247.0 50.3 %gate_forward.1 = (bf16[1024,2048]{1,0:T(8,128)(2,1)}, bf16[1024,2048]{1,0:T(8,128)(2,1)}, bf16[1024,2048]{1,0:T(8,128)(2,1)}, bf16[1024,2048]{1,0:T(8,128)(2,1)}, bf16[1024,2048]{1,0:T(8,128)(2,1)}) custom-call(bf16[1024,2048]{1,0:T(8,128)(2,1)} %get-tuple-element.97.whole.left.normal_in, ...), custom_call_target="tpu_custom_call" | custom-call | flops 25769803776 | bytes 25165824 | tf_op jit(solution)/shard_map/gate_forward/pallas_call | solution.py:1266
  297.6 15.5 %gate_back.1.right.gated_in = bf16[2,1024,2048]{2,1,0:T(8,128)(2,1)} custom-call(bf16[1024,2048]{1,0:T(8,128)(2,1)} %get-tuple-element.101.whole.other_left, bf16[2048,6144]{1,0:T(8,128)(2,1)} %all-gather.5.cloned.1.call-done.gate_rows.upper_rows.down_rows.rows.rows_in, bf16[1024,2048]{1,0:T(8,128)(2,1)} %get-tuple-element.102.by_gate, ...), custom_call_target="tpu_custom_call" | custom-call | flops 8589934592 | bytes 46137344 | tf_op jit(solution)/shard_map/gate_back/pallas_call | solution.py:1087
  313.2 36.9 %outer_hidden.1 = bf16[2048,6144]{1,0:T(8,128)(2,1)} custom-call(bf16[1024,2048]{1,0:T(8,128)(2,1)} %get-tuple-element.97.whole.left.normal_in, bf16[2,1024,2048]{2,1,0:T(8,128)(2,1)} %gate_back.1.right.gated_in, bf16[1024,2048]{1,0:T(8,128)(2,1)} %get-tuple-element.101.whole.other_left, bf16[1024,2048]{1,0:T(8,128)(2,1)} %get-tuple-element.104.other_right), custom_call_target="tpu_custom_call" | custom-call | flops 25769803776 | bytes 46137344 | tf_op jit(solution)/shard_map/outer_hidden/pallas_call | solution.py:1087
  350.1 137.4 %back_mid.1 = (bf16[1024,2048]{1,0:T(8,128)(2,1)}, f32[1024,512]{1,0:T(8,128)}, bf16[1024,512]{1,0:T(8,128)(2,1)}) custom-call(f32[2,4,6]{2,1,0:T(4,128)} %mix.11, bf16[2,1024,2048]{2,1,0:T(8,128)(2,1)} %gate_back.1.right.gated_in, bf16[2048,6144]{1,0:T(8,128)(2,1)} %all-gather.5.cloned.1.call-done.gate_rows.upper_rows.down_rows.rows.rows_in, ...), custom_call_target="tpu_custom_call" | custom-call | flops 1000000000 | bytes 57675968 | tf_op jit(solution)/shard_map/back_mid/pallas_call | solution.py:311
  487.5 18.0 %attend_back.1.grads.right = bf16[3,1024,512]{2,1,0:T(8,128)(2,1)} custom-call(bf16[1024,512]{1,0:T(8,128)(2,1)} %get-tuple-element.112.queries, bf16[1024,512]{1,0:T(8,128)(2,1)} %get-tuple-element.113.key_heads, bf16[1024,512]{1,0:T(8,128)(2,1)} %get-tuple-element.114.value_heads, bf16[1024,512]{1,0:T(8,128)(2,1)} %get-tuple-element.115.grad_result, ...), custom_call_target="tpu_custom_call" | custom-call | tf_op jit(solution)/shard_map/attend_back/pallas_call | solution.py:1612
  505.5 8.1 %heads_product.2 = (bf16[1024,2048]{1,0:T(8,128)(2,1)}, bf16[1024,512]{1,0:T(8,128)(2,1)}, bf16[1024,512]{1,0:T(8,128)(2,1)}) custom-call(bf16[3,1024,512]{2,1,0:T(8,128)(2,1)} %attend_back.1.grads.right, bf16[2048,2048]{1,0:T(8,128)(2,1)} %all-gather.3.cloned.1.call-done.right.rows_in.output_in.rows), custom_call_target="tpu_custom_call" | custom-call | flops 3221225472 | bytes 8388608 | tf_op jit(solution)/shard_map/heads_product/pallas_call | solution.py:1438
  516.2 18.0 %outer_attention.1 = bf16[2048,2048]{1,0:T(8,128)(2,1)} custom-call(bf16[1024,2048]{1,0:T(8,128)(2,1)} %get-tuple-element.89.left.normal_in, bf16[3,1024,512]{2,1,0:T(8,128)(2,1)} %attend_back.1.grads.right, bf16[1024,2048]{1,0:T(8,128)(2,1)} %get-tuple-element.119.other_left, bf16[1024,512]{1,0:T(8,128)(2,1)} %get-tuple-element.95.attended_in.other_right), custom_call_target="tpu_custom_call" | custom-call | flops 8589934592 | bytes 20971520 | tf_op jit(solution)/shard_map/outer_attention/pallas_call | solution.py:1087
  534.9 7.1 %heads_product.3.partial_in = bf16[1024,2048]{1,0:T(8,128)(2,1)} custom-call(bf16[3,1024,512]{2,1,0:T(8,128)(2,1)} %attend_back.1.grads.right, bf16[2048,2048]{1,0:T(8,128)(2,1)} %all-gather.3.cloned.1.call-done.right.rows_in.output_in.rows, bf16[1024,2048]{1,0:T(8,128)(2,1)} %get-tuple-element.116.refs_0_), custom_call_target="tpu_custom_call", output_to_operand_aliasing={{}: (2, {})} | custom-call | flops 3221225472 | bytes 8388608 | tf_op jit(solution)/shard_map/heads_product/pallas_call | solution.py:1438
  542.0 3.2 add_convert_fusion.2
  546.5 4.6 collective-permute-start.4
  551.1 6.3 update.5
  557.4 12.7 %update.4 = (f32[2,256,2048]{2,1,0:T(8,128)}, f32[2,256,2048]{2,1,0:T(8,128)}, f32[2,256,2048]{2,1,0:T(8,128)}) custom-call(f32[2,256,2048]{2,1,0:T(8,128)} %weight.4, bf16[256,6144]{1,0:T(8,128)(2,1)} %reduce-scatter.6.cloned.1.call-done.grad, f32[2,256,2048]{2,1,0:T(8,128)} %moment.5, f32[2,256,2048]{2,1,0:T(8,128)} %average.5), custom_call_target="tpu_custom_call" | custom-call | flops 10485760 | bytes 27262976 | tf_op jit(solution)/shard_map/update/pallas_call | solution.py:1702
  570.1 3.5 add_convert_fusion
  574.9 4.6 collective-permute-start.6
  579.5 10.9 %end_streams.1 = (bf16[4,1024,512]{2,1,0:T(8,128)(2,1)}, f32[16,8,128]{2,1,0:T(8,128)}) custom-call(f32[2,4,6]{2,1,0:T(4,128)} %mix.11, bf16[4,1024,512]{2,1,0:T(8,128)(2,1)} %streams_in.3, bf16[4,1024,512]{2,1,0:T(8,128)(2,1)} %grads.3, f32[1024,512]{1,0:T(8,128)} %get-tuple-element.96.branch_one, ...), custom_call_target="tpu_custom_call" | custom-call | flops 125829120 | bytes 18874368 | tf_op jit(solution)/shard_map/end_streams/pallas_call | solution.py:1038
  590.4 12.8 %back_sums.1 = (f32[1024,1]{1,0:T(8,128)}, f32[1024,1]{1,0:T(8,128)}) custom-call(bf16[1024,2048]{1,0:T(8,128)(2,1)} %heads_product.3.partial_in, bf16[1024,2048]{1,0:T(8,128)(2,1)} %get-tuple-element.89.left.normal_in), custom_call_target="tpu_custom_call" | custom-call | flops 1000000000 | bytes 8396800 | tf_op jit(solution)/shard_map/back_sums/pallas_call | solution.py:311
  604.6 18.9 %back_in.1 = (f32[1024,512]{1,0:T(8,128)}, f32[8,128]{1,0:T(8,128)}) custom-call(bf16[1024,2048]{1,0:T(8,128)(2,1)} %heads_product.3.partial_in, bf16[1024,512]{1,0:T(8,128)(2,1)} %copy-done.1, bf16[1024,512]{1,0:T(8,128)(2,1)} %copy-done, bf16[1024,2048]{1,0:T(8,128)(2,1)} %get-tuple-element.89.left.normal_in, f32[1024,1]{1,0:T(8,128)} %get-tuple-element.136.scale, ...), custom_call_target="tpu_custom_call" | custom-call | flops 1000000000 | bytes 16924672 | tf_op jit(solution)/shard_map/back_in/pallas_call | solution.py:311
  623.5 8.5 %grad_streams.1 = f32[4,1024,512]{2,1,0:T(8,128)} custom-call(f32[2,4,6]{2,1,0:T(4,128)} %mix.11, bf16[4,1024,512]{2,1,0:T(8,128)(2,1)} %grads.3, f32[1024,512]{1,0:T(8,128)} %get-tuple-element.110.inner_two, f32[1024,512]{1,0:T(8,128)} %get-tuple-element.141.inner_one), custom_call_target="tpu_custom_call" | custom-call | flops 20971520 | bytes 16777216 | tf_op jit(solution)/shard_map/grad_streams/pallas_call | solution.py:1071
  634.8 5.6 update.6
  (42 shorter events, 18.3 us)
Async XLA Ops:
  7.2 96.0 %all-gather.3.cloned.1.call-start = ((), (), s32[]{:S(2)}) async-start(), calls=%async_computation.3 | async-start | bytes 9437184 | tf_op jit(solution)/shard_map/all_gather | solution.py:1805
  9.9 237.1 %all-gather.5.cloned.1.call-start = ((), (), s32[]{:S(2)}) async-start(), calls=%async_computation.4 | async-start | bytes 28311552 | tf_op jit(solution)/shard_map/all_gather | solution.py:1811
  96.0 1.2 copy-start.2
  96.0 391.5 %reduce-scatter.4.cloned.1.call-start = ((), (), s32[]{:S(2)}) async-start(), calls=%async_computation.5 | async-start | bytes 5242880 | tf_op jit(solution)/shard_map/reduce_scatter | solution.py:1828
  97.2 32.9 %collective-permute-start.1 = (bf16[1024,512]{1,0:T(8,128)(2,1)S(1)}, bf16[1024,512]{1,0:T(8,128)(2,1)S(1)}, u32[]{:S(2)}, u32[]{:S(2)}) collective-permute-start(bf16[1024,512]{1,0:T(8,128)(2,1)S(1)} %copy-done.2), channel_id=1, source_target_pairs={{1,0},{2,1},{3,2},{5,4},{6,5},{7,6},{9,8},{10,9},{11,10},{13,12},{... | collective-permute-start | bytes 3145736 | tf_op jit(solution)/shard_map/ppermute | solution.py:1815
  98.5 31.6 %collective-permute-start = (bf16[1024,512]{1,0:T(8,128)(2,1)S(1)}, bf16[1024,512]{1,0:T(8,128)(2,1)S(1)}, u32[]{:S(2)}, u32[]{:S(2)}) collective-permute-start(bf16[1024,512]{1,0:T(8,128)(2,1)S(1)} %copy-done.2), channel_id=1, source_target_pairs={{0,1},{1,2},{2,3},{4,5},{5,6},{6,7},{8,9},{9,10},{10,11},{12,13},{... | collective-permute-start | bytes 3145736 | tf_op jit(solution)/shard_map/ppermute | solution.py:1814
  130.1 116.9 %copy-start.3 = (bf16[1024,512]{1,0:T(8,128)(2,1)}, bf16[1024,512]{1,0:T(8,128)(2,1)S(1)}, u32[]{:S(2)}) copy-start(bf16[1024,512]{1,0:T(8,128)(2,1)S(1)} %collective-permute-done.1.after_in) | copy-start | bytes 3145732
  130.2 116.9 %copy-start.4 = (bf16[1024,512]{1,0:T(8,128)(2,1)}, bf16[1024,512]{1,0:T(8,128)(2,1)S(1)}, u32[]{:S(2)}) copy-start(bf16[1024,512]{1,0:T(8,128)(2,1)S(1)} %collective-permute-done.before_in) | copy-start | bytes 3145732
  297.3 253.8 %reduce-scatter.6.cloned.1.call-start = ((), (), s32[]{:S(2)}) async-start(), calls=%async_computation.6 | async-start | bytes 28311552 | tf_op jit(solution)/shard_map/reduce_scatter | solution.py:1760
  350.1 273.4 %reduce-scatter.8.cloned.1.call-start = ((), (), s32[]{:S(2)}) async-start(), calls=%async_computation.7 | async-start | bytes 9437184 | tf_op jit(solution)/shard_map/reduce_scatter | solution.py:1760
  513.6 20.7 %collective-permute-start.2 = (bf16[1024,512]{1,0:T(8,128)(2,1)}, bf16[1024,512]{1,0:T(8,128)(2,1)S(1)}, u32[]{:S(2)}, u32[]{:S(2)}) collective-permute-start(bf16[1024,512]{1,0:T(8,128)(2,1)} %get-tuple-element.117), channel_id=1, source_target_pairs={{0,1},{1,2},{2,3},{4,5},{5,6},{6,7},{8,9},{9,10},{10,11},{12,13},{... | collective-permute-start | bytes 3145736 | tf_op jit(solution)/shard_map/ppermute | solution.py:1742
  514.9 20.0 %collective-permute-start.3 = (bf16[1024,512]{1,0:T(8,128)(2,1)}, bf16[1024,512]{1,0:T(8,128)(2,1)S(1)}, u32[]{:S(2)}, u32[]{:S(2)}) collective-permute-start(bf16[1024,512]{1,0:T(8,128)(2,1)} %get-tuple-element.118), channel_id=1, source_target_pairs={{1,0},{2,1},{3,2},{5,4},{6,5},{7,6},{9,8},{10,9},{11,10},{13,12},{... | collective-permute-start | bytes 3145736 | tf_op jit(solution)/shard_map/ppermute | solution.py:1742
  545.2 25.0 %collective-permute-start.5 = (bf16[1024,512]{1,0:T(8,128)(2,1)}, bf16[1024,512]{1,0:T(8,128)(2,1)S(1)}, u32[]{:S(2)}, u32[]{:S(2)}) collective-permute-start(bf16[1024,512]{1,0:T(8,128)(2,1)} %get-tuple-element.163), channel_id=1, source_target_pairs={{1,0},{2,1},{3,2},{5,4},{6,5},{7,6},{9,8},{10,9},{11,10},{13,12},{... | collective-permute-start | bytes 3145736 | tf_op jit(solution)/shard_map/ppermute | solution.py:1742
  546.5 23.7 %collective-permute-start.4 = (bf16[1024,512]{1,0:T(8,128)(2,1)S(1)}, bf16[1024,512]{1,0:T(8,128)(2,1)S(1)}, u32[]{:S(2)}, u32[]{:S(2)}) collective-permute-start(bf16[1024,512]{1,0:T(8,128)(2,1)S(1)} %get-tuple-element.164), channel_id=1, source_target_pairs={{0,1},{1,2},{2,3},{4,5},{5,6},{6,7},{8,9},{9,10},{10,11},{12,13},{... | collective-permute-start | bytes 3145736 | tf_op jit(solution)/shard_map/ppermute | solution.py:1742
  573.6 29.6 %collective-permute-start.7 = (bf16[1024,512]{1,0:T(8,128)(2,1)}, bf16[1024,512]{1,0:T(8,128)(2,1)S(1)}, u32[]{:S(2)}, u32[]{:S(2)}) collective-permute-start(bf16[1024,512]{1,0:T(8,128)(2,1)} %get-tuple-element.161), channel_id=1, source_target_pairs={{1,0},{2,1},{3,2},{5,4},{6,5},{7,6},{9,8},{10,9},{11,10},{13,12},{... | collective-permute-start | bytes 3145736 | tf_op jit(solution)/shard_map/ppermute | solution.py:1742
  574.9 28.4 %collective-permute-start.6 = (bf16[1024,512]{1,0:T(8,128)(2,1)}, bf16[1024,512]{1,0:T(8,128)(2,1)S(1)}, u32[]{:S(2)}, u32[]{:S(2)}) collective-permute-start(bf16[1024,512]{1,0:T(8,128)(2,1)} %get-tuple-element.162), channel_id=1, source_target_pairs={{0,1},{1,2},{2,3},{4,5},{5,6},{6,7},{8,9},{9,10},{10,11},{12,13},{... | collective-permute-start | bytes 3145736 | tf_op jit(solution)/shard_map/ppermute | solution.py:1742
  603.2 1.0 copy-start
  603.3 1.3 copy-start.1
Sparse Core Ops, SparseCore 0:
  10.5 57.0 all-gather.2
  96.2 125.3 all-gather.4
  297.5 85.2 reduce-scatter.3
  386.7 160.7 reduce-scatter.5
  551.8 71.5 reduce-scatter.7

commit v6 on v5

--- a/solution.py
+++ b/solution.py
@@ -861,45 +861,101 @@
 
 
 def back_in_kernel(
-    size,
-    partial_in,
-    first_in,
-    last_in,
-    normal_in,
-    scale,
-    first_sum,
-    second_sum,
-    streams_in,
-    streams_grads,
-    other_products,
-    inner,
-    whole_products,
+    place,
+    mix,
     share,
     first,
     last,
     normal,
+    scale,
+    first_sum,
+    second_sum,
     streams,
+    grads,
+    inner_two,
+    out,
     products,
-    shares,
-    loads,
-    shares_sent,
-    shares_got,
 ):
+    count = streams.shape[0]
+    through, in_two, _, _ = mixings(mix)
+
+    @pl.when(pl.program_id(0) == 0)
+    def _():
+        products[...] = jnp.zeros_like(products)
+
+    width = share.shape[1]
+
+    def slab(index, sums):
+        rows = pl.ds(pl.multiple_of(index * 16, 16), 16)
+        sums = list(sums)
+        shape = (16, 128)
+        rate = jnp.broadcast_to(scale[rows, :], shape)
+        one = jnp.broadcast_to(first_sum[rows, :], shape)
+        two = jnp.broadcast_to(second_sum[rows, :], shape)
+        for start in range(0, width, 128):
+            columns = slice(start, start + 128)
+            total = share[rows, columns].astype(f32) + first[rows, columns].astype(f32)
+            total = total + last[rows, columns].astype(f32)
+            own = rate * (total - one - two * normal[rows, columns].astype(f32))
+            below = inner_two[rows, columns]
+            above = [grads[k, rows, columns].astype(f32) for k in range(count)]
+            for i in range(count):
+                value = in_two[i] * below + mix[0, i, 0] * own
+                for k in range(count):
+                    value = value + through[i][k] * above[k]
+                out[i, rows, columns] = value
+                product = streams[i, rows, columns].astype(f32) * own
+                sums[i] = sums[i] + product[:8] + product[8:]
+        return tuple(sums)
+
+    sums = lax.fori_loop(0, share.shape[0] // 16, slab, (jnp.zeros((8, 128), f32),) * count)
+    for i in range(count):
+        products[i] = products[i] + sums[i]
+
+
+def back_in(mix, partial, first, last, normal, scale, sums, streams, grads, inner_two, tile=256):
     count, tokens, width = streams.shape
-    groups = tokens // GROUP
-    me = lax.axis_index("col")
+    used = -(-count // 8) * 8
+    many = pl.BlockSpec((count, tile, width), lambda i, place: (0, i, 0))
+    here = pl.BlockSpec((tile, width), lambda i, place: (i, place[0]))
+    own = pl.BlockSpec((tile, width), lambda i, place: (i, 0))
+    thin = pl.BlockSpec((tile, 1), lambda i, place: (i, 0))
+    return pl.pallas_call(
+        back_in_kernel,
+        grid_spec=pltpu.PrefetchScalarGridSpec(
+            num_scalar_prefetch=1,
+            grid=(tokens // tile,),
+            in_specs=[pl.BlockSpec(memory_space=SM), here, own, own, here, thin, thin, thin]
+            + [many, many, own],
+            out_specs=[many, pl.BlockSpec((used, 8, 128), lambda i, place: (0, 0, 0))],
+        ),
+        out_shape=[
+            jax.ShapeDtypeStruct(streams.shape, f32),
+            jax.ShapeDtypeStruct((used, 8, 128), f32),
+        ],
+        compiler_params=pltpu.CompilerParams(vmem_limit_bytes=60 * 2**20),
+        cost_estimate=pl.CostEstimate(
+            flops=20 * streams.size, bytes_accessed=11 * streams.size, transcendentals=0
+        ),
+        name="back_in",
+    )(
+        lax.axis_index("col").astype(jnp.int32)[None],
+        mix,
+        partial,
+        first,
+        last,
+        normal,
+        scale,
+        *sums,
+        streams,
+        grads,
+        inner_two,
+    )
+
+
+def sum_all_kernel(size, *refs):
+    parts, whole, shares, sent, got = refs[:-4], refs[-4], refs[-3], refs[-2], refs[-1]
     count_rows = lax.axis_size("row")
-    own_columns = pl.ds(pl.multiple_of(me * width, width), width)
-    waits = start_loads(
-        (
-            (partial_in.at[:, own_columns], share),
-            (first_in, first),
-            (last_in, last),
-            (normal_in.at[:, own_columns], normal),
-            (streams_in, streams),
-        ),
-        loads,
-    )
     barrier = pltpu.get_barrier_semaphore()
     for axis, members in (("col", size), ("row", count_rows)):
         for member in range(members):
@@ -910,24 +966,7 @@
                     barrier, inc=1, device_id={axis: member}, device_id_type=MESH
                 )
 
-    products[...] = jnp.zeros_like(products)
-    for wait in waits:
-        wait.wait()
-
-    def conclude(group, carry):
-        rows = pl.ds(pl.multiple_of(group * GROUP, GROUP), GROUP)
-        total = share[rows, :].astype(f32) + first[rows, :].astype(f32) + last[rows, :].astype(f32)
-        own = scale[rows, :] * (
-            total - first_sum[rows, :] - second_sum[rows, :] * normal[rows, :].astype(f32)
-        )
-        inner[rows, :] = own
-        for i in range(count):
-            products[i] = products[i] + tile_sum(streams[i, rows].astype(f32) * own)
-        return carry
-
-    lax.fori_loop(0, groups, conclude, 0)
-    parts = [streams_grads[...], other_products[...], products[...]]
-    total = jnp.concatenate([jnp.sum(jnp.sum(part, 1), -1, keepdims=True) for part in parts], 0)
+    total = jnp.concatenate([jnp.sum(jnp.sum(part[...], 1), -1, keepdims=True) for part in parts], 0)
     total = jnp.concatenate([total, jnp.zeros((128 - total.shape[0], 1), f32)], 0)
     total = jnp.broadcast_to(total, (128, 128)).T[:8]
     pl.semaphore_wait(barrier, size - 1 + count_rows - 1)
@@ -938,8 +977,8 @@
             return pltpu.make_async_remote_copy(
                 src_ref=shares.at[base + source],
                 dst_ref=shares.at[base + source],
-                send_sem=shares_sent.at[base + member],
-                recv_sem=shares_got.at[base + source],
+                send_sem=sent.at[base + member],
+                recv_sem=got.at[base + source],
                 device_id={axis: member},
                 device_id_type=MESH,
             )
@@ -960,35 +999,26 @@
         total = shares[base]
         for member in range(1, members):
             total = total + shares[base + member]
-    whole_products[...] = total
-
-
-def back_in(size, partial, first, last, normal, scale, sums, streams, streams_grads, other_products):
-    count, tokens, width = streams.shape
-    own = -(-count // 8) * 8
+    whole[...] = total
+
+
+def sum_all(size, *parts):
     members = size + lax.axis_size("row")
-    dma = pltpu.SemaphoreType.DMA
     return call(
-        functools.partial(back_in_kernel, size),
-        (partial, first, last, normal, scale, *sums, streams, streams_grads, other_products),
-        (pl.ANY, pl.ANY, pl.ANY, pl.ANY, VM, VM, VM, pl.ANY, VM, VM),
+        functools.partial(sum_all_kernel, size),
+        parts,
+        (VM,) * len(parts),
+        [jax.ShapeDtypeStruct((8, 128), f32)],
+        (VM,),
         [
-            jax.ShapeDtypeStruct((tokens, width), f32),
-            jax.ShapeDtypeStruct((8, 128), f32),
+            pltpu.VMEM((members, 8, 128), f32),
+            pltpu.SemaphoreType.DMA((members,)),
+            pltpu.SemaphoreType.DMA((members,)),
         ],
-        (VM, VM),
-        held(first, first, last, first, streams)
-        + [
-            pltpu.VMEM((own, 8, 128), f32),
-            pltpu.VMEM((members, 8, 128), f32),
-            dma((5,)),
-            dma((members,)),
-            dma((members,)),
-        ],
-        "back_in",
+        "sum_all",
         4,
         10**9,
-    )
+    )[0]
 
 
 def end_kernel(mix, streams, grads, branch_one, branch_two, inner_two, final, products):
@@ -1050,36 +1080,6 @@
         ),
         name="end_streams",
     )(mix, streams, grads, branch_one, branch_two, inner_two)
-
-
-def grad_kernel(mix, grads, inner_two, inner_one, out):
-    count = grads.shape[0]
-    through, in_two, _, _ = mixings(mix)
-    above = [grads[k].astype(f32) for k in range(count)]
-    below, own = inner_two[...], inner_one[...]
-    for i in range(count):
-        value = in_two[i] * below + mix[0, i, 0] * own
-        for k in range(count):
-            value = value + through[i][k] * above[k]
-        out[i] = value
-
-
-def grad_streams_of(mix, grads, inner_two, inner_one, tile=256):
-    count, tokens, width = grads.shape
-    many = pl.BlockSpec((count, tile, width), lambda i: (0, i, 0))
-    own = pl.BlockSpec((tile, width), lambda i: (i, 0))
-    return pl.pallas_call(
-        grad_kernel,
-        grid=(tokens // tile,),
-        out_shape=jax.ShapeDtypeStruct(grads.shape, f32),
-        in_specs=[pl.BlockSpec(memory_space=SM), many, own, own],
-        out_specs=many,
-        compiler_params=pltpu.CompilerParams(vmem_limit_bytes=60 * 2**20),
-        cost_estimate=pl.CostEstimate(
-            flops=10 * grads.size, bytes_accessed=8 * grads.size, transcendentals=0
-        ),
-        name="grad_streams",
-    )(mix, grads, inner_two, inner_one)
 
 
 def tiled(body, grid, operands, specs, outs, out_specs, scratch, flops, name):
@@ -1298,32 +1298,55 @@
     )(whole, weights, weights, weights, own, before, after)
 
 
-def gate_back_kernel(whole, rows, by_gate, by_upper, grads):
-    grad = jnp.dot(whole[...], rows[...], preferred_element_type=f32)
+def gate_back_kernel(
+    branch_grad, normal, rows, by_gate, by_upper, active, grads, weight_grads, turned_grad, turned
+):
+    @pl.when(pl.program_id(0) == 0)
+    def _():
+        turned[...] = normal[...].T
+        turned_grad[...] = branch_grad[...].T
+
+    grad = jnp.dot(branch_grad[...], rows[...], preferred_element_type=f32)
     grads[0] = (grad * by_gate[...].astype(f32)).astype(jnp.bfloat16)
     grads[1] = (grad * by_upper[...].astype(f32)).astype(jnp.bfloat16)
-
-
-def gate_back(whole, weights, by_gate, by_upper, tile=512):
-    tokens, features = whole.shape
+    pairs = ((turned, grads.at[0]), (turned, grads.at[1]), (turned_grad, active))
+    for place, (left, right) in enumerate(pairs):
+        weight_grads[place] = jnp.dot(
+            left[...], right[...], preferred_element_type=f32
+        ).astype(jnp.bfloat16)
+
+
+def gate_back(branch_grad, normal, weights, by_gate, by_upper, active, tile=256):
+    tokens, features = normal.shape
     hidden = weights.shape[1] // 3
     tile = min(tile, hidden)
     tiles = hidden // tile
+    whole = pl.BlockSpec(
+        (tokens, features), lambda j: (0, 0), pipeline_mode=pl.Buffered(buffer_count=1)
+    )
     part = pl.BlockSpec((tokens, tile), lambda j: (0, j))
     return tiled(
         gate_back_kernel,
         (tiles,),
-        (whole, weights, by_gate, by_upper),
+        (branch_grad, normal, weights, by_gate, by_upper, active),
         [
-            pl.BlockSpec((tokens, features), lambda j: (0, 0)),
+            whole,
+            whole,
             pl.BlockSpec((features, tile), lambda j: (0, 2 * tiles + j)),
             part,
             part,
+            part,
         ],
-        jax.ShapeDtypeStruct((2, tokens, hidden), jnp.bfloat16),
-        pl.BlockSpec((2, tokens, tile), lambda j: (0, 0, j)),
-        [],
-        2 * tokens * features * hidden,
+        [
+            jax.ShapeDtypeStruct((2, tokens, hidden), jnp.bfloat16),
+            jax.ShapeDtypeStruct((3, features, hidden), jnp.bfloat16),
+        ],
+        [
+            pl.BlockSpec((2, tokens, tile), lambda j: (0, 0, j)),
+            pl.BlockSpec((3, features, tile), lambda j: (0, 0, j)),
+        ],
+        [pltpu.VMEM((features, tokens), jnp.bfloat16)] * 2,
+        8 * tokens * features * hidden,
         "gate_back",
     )
 
@@ -1492,6 +1515,7 @@
     key_heads,
     value_heads,
     attended,
+    kept,
     bias,
 ):
     length = query.shape[0]
@@ -1514,9 +1538,9 @@
         probs = block_probs(
             queries[start:end], key_heads[first:end], bias[start:end, first:end]
         )
-        result = jnp.dot(
-            probs.astype(jnp.bfloat16), value_heads[first:end], preferred_element_type=f32
-        )
+        probs = probs.astype(jnp.bfloat16)
+        kept[start:end, first:end] = probs
+        result = jnp.dot(probs, value_heads[first:end], preferred_element_type=f32)
         attended[start:end, :] = result.astype(jnp.bfloat16)
 
 
@@ -1535,10 +1559,11 @@
     return pl.pallas_call(
         functools.partial(attend_forward_kernel, block),
         grid=(heads,),
-        out_shape=[jax.ShapeDtypeStruct((length, width), jnp.bfloat16)] * 4,
+        out_shape=[jax.ShapeDtypeStruct((length, width), jnp.bfloat16)] * 4
+        + [jax.ShapeDtypeStruct((heads, length, length), jnp.bfloat16)],
         in_specs=[head(0), head(heads), head(2 * heads)]
         + [fixed(array) for array in (cosine, sine, column, row)],
-        out_specs=[head(0)] * 4,
+        out_specs=[head(0)] * 4 + [pl.BlockSpec((None, length, length), lambda h: (h, 0, 0))],
         scratch_shapes=[pltpu.VMEM((length, length), f32)],
         compiler_params=pltpu.CompilerParams(vmem_limit_bytes=60 * 2**20),
         name="attend_forward",
@@ -1551,21 +1576,14 @@
     key_heads,
     value_heads,
     grad_result,
+    kept,
     cosine,
     sine,
-    column,
-    row,
     grads,
     key_sum,
     value_sum,
-    bias,
 ):
     length = queries.shape[0]
-
-    @pl.when(pl.program_id(0) == 0)
-    def _():
-        fill_bias(bias, column, row)
-
     key_sum[...] = jnp.zeros_like(key_sum)
     value_sum[...] = jnp.zeros_like(value_sum)
 
@@ -1580,7 +1598,8 @@
     for start in range(0, length, block):
         first, end = key_span(start, block)
         query, grad_part = queries[start:end], grad_result[start:end]
-        probs = block_probs(query, key_heads[first:end], bias[start:end, first:end])
+        lowered = kept[start:end, first:end]
+        probs = lowered.astype(f32)
         grad_probs = lax.dot_general(
             grad_part, value_heads[first:end], LANES, preferred_element_type=f32
         )
@@ -1594,13 +1613,13 @@
             grad_scores, query, ROWS, preferred_element_type=f32
         )
         value_sum[first:end, :] += lax.dot_general(
-            probs.astype(jnp.bfloat16), grad_part, ROWS, preferred_element_type=f32
+            lowered, grad_part, ROWS, preferred_element_type=f32
         )
     grads[1] = turn_back(key_sum[...], pl.ds(0, length), 1.0 / LOG2E)
     grads[2] = value_sum[...].astype(jnp.bfloat16)
 
 
-def attend_back(queries, key_heads, value_heads, grad_result, cosine, sine, column, row):
+def attend_back(queries, key_heads, value_heads, grad_result, kept, cosine, sine):
     length, width = queries.shape
     heads = width // HEAD_DIM
     block = min(256, length)
@@ -1613,13 +1632,13 @@
         functools.partial(attend_back_kernel, block),
         grid=(heads,),
         out_shape=jax.ShapeDtypeStruct((3, length, width), jnp.bfloat16),
-        in_specs=[head] * 4 + [fixed(array) for array in (cosine, sine, column, row)],
+        in_specs=[head] * 4
+        + [pl.BlockSpec((None, length, length), lambda h: (h, 0, 0)), fixed(cosine), fixed(sine)],
         out_specs=pl.BlockSpec((3, length, HEAD_DIM), lambda h: (0, 0, h)),
-        scratch_shapes=[pltpu.VMEM((length, HEAD_DIM), f32)] * 2
-        + [pltpu.VMEM((length, length), f32)],
+        scratch_shapes=[pltpu.VMEM((length, HEAD_DIM), f32)] * 2,
         compiler_params=pltpu.CompilerParams(vmem_limit_bytes=60 * 2**20),
         name="attend_back",
-    )(queries, key_heads, value_heads, grad_result, cosine, sine, column, row)
+    )(queries, key_heads, value_heads, grad_result, kept, cosine, sine)
 
 
 def update(weight, grad, moment, average, rate):
@@ -1686,19 +1705,24 @@
 
 def update_blocks(weight, grad, moment, average, rate, start):
     turned = weight.ndim == 2
-    rows = grad.shape[0]
+    parted = grad.ndim == 3
+    rows = grad.shape[-2]
     columns = weight.shape[0] if turned else weight.shape[2]
     tile = min(columns, 512)
     tiles = columns // tile
-    first = start // tile
+    lead = (None,) if parted else ()
+
+    def spot(k, j):
+        return (start + k, 0, j) if parted else (0, start // tile + k * tiles + j)
+
     if turned:
         grid = (tiles,)
         own = pl.BlockSpec((tile, rows), lambda j: (j, 0))
-        place = pl.BlockSpec((rows, tile), lambda j: (0, first + j))
+        place = pl.BlockSpec(lead + (rows, tile), lambda j: spot(0, j))
     else:
         grid = (weight.shape[0], tiles)
         own = pl.BlockSpec((None, rows, tile), lambda k, j: (k, 0, j))
-        place = pl.BlockSpec((rows, tile), lambda k, j: (0, first + k * tiles + j))
+        place = pl.BlockSpec(lead + (rows, tile), spot)
     return pl.pallas_call(
         functools.partial(update_kernel, rate, turned),
         grid=grid,
@@ -1814,7 +1838,7 @@
     before = lax.ppermute(grad_two, "col", up)
     after = lax.ppermute(grad_two, "col", down)
     projected = product(whole_one, attention_weights, 0, 3 * heads, f32, heads, "project_in")
-    queries, key_heads, value_heads, attended = attend_forward(
+    queries, key_heads, value_heads, attended, kept = attend_forward(
         projected, cosine, sine, column, segments
     )
     attended, before, after = tie(attended, before, after)
@@ -1826,10 +1850,10 @@
         size, whole_two, hidden_weights, grad_two, before, after
     )
     branch_two = lax.psum_scatter(partial_two, "col", scatter_dimension=1, tiled=True)
-    grad_gated = gate_back(whole_grad_two, hidden_weights, by_gate, by_upper)
-    grad_hidden = outer(whole_two, grad_gated, whole_grad_two, active, name="outer_hidden")
-    grad_hidden, grad_gated = tie(grad_hidden, grad_gated)
-    grad_hidden = scatter_rows(grad_hidden)
+    grad_gated, grad_hidden = gate_back(
+        whole_grad_two, whole_two, hidden_weights, by_gate, by_upper, active
+    )
+    grad_hidden = lax.psum_scatter(grad_hidden, "row", scatter_dimension=1, tiled=True)
     whole_grad_one, inner_two, grad_attended = back_mid(
         size,
         grad_gated,
@@ -1843,7 +1867,7 @@
 
     grad_attended, branch_two = tie(grad_attended, branch_two)
     grad_heads = attend_back(
-        queries, key_heads, value_heads, grad_attended, cosine, sine, column, segments
+        queries, key_heads, value_heads, grad_attended, kept, cosine, sine
     )
     tokens_all = length * lax.axis_size("row")
     token_scale = tokens_all ** (-0.5)
@@ -1863,7 +1887,7 @@
         moment_down_weights,
         average_down_weights,
         FF ** (-0.5) * token_scale,
-        gate_up.shape[0] * gate_up.shape[2],
+        gate_up.shape[0],
     )
     got, hidden = advance(steps, got, *third, *fourth)
     third, fourth = hidden[:3], hidden[3:]
@@ -1878,8 +1902,8 @@
     sums = back_sums(size, partial_one, whole_one)
     got, (other_products, *sums) = advance(steps, got, other_products, *sums)
     first_part, last_part = finish_line(steps, got)
-    inner_one, products = back_in(
-        size,
+    grad_streams, own_products = back_in(
+        hyper_mix,
         partial_one,
         first_part,
         last_part,
@@ -1887,11 +1911,10 @@
         scale_one,
         sums,
         streams,
-        streams_grads,
-        other_products,
-    )
-    grad_streams = grad_streams_of(hyper_mix, cotangent, inner_two, inner_one)
-
+        cotangent,
+        inner_two,
+    )
+    products = sum_all(size, streams_grads, other_products, own_products)
     products, grad_attention = tie(products, grad_attention)
     first = update_blocks(
         attention_in, grad_attention, moment_attention_in, average_attention_in, model_rate, 0

time: 656 us -> 645 us (0.983)
  Pallas kernels: 604 us -> 594 us
    pallas_call x5, Pallas kernels: 371 us -> 352 us  [call(): pl.pallas_call(body, out_shape=outs, in_specs=[pl.BlockSpec(memory_space=...]
    pallas_call x4 -> x3, Pallas kernels: 82.8 us -> 92.5 us  [tiled(): pl.pallas_call(body, grid=grid, out_shape=outs, in_specs=specs, out_specs...]
  transfers between devices with their start and end apart: 13 -> 13, of which waited for: 1 -> 0; matrix products, arithmetic and copies ran while one was open for 1% -> 1% of each run, Pallas kernels for 82% -> 83%
where the time goes in v6:
time: 645 us; the launch traced here: 639 us
  Pallas kernels  594 us (92%)
  starting transfers between devices  21.5 us (3%)
  between operations  14.3 us (2%)
  other arithmetic  6.93 us (1%)
    pallas_call x5, Pallas kernels, call(): pl.pallas_call(body, out_shape=outs, in_specs=[pl.BlockSpec(memory_space=...  352 us
    pallas_call x3, Pallas kernels, tiled(): pl.pallas_call(body, grid=grid, out_shape=outs, in_specs=specs, out_specs...  92.5 us
    pallas_call x1, Pallas kernels, gate_forward(): pl.pallas_call(functools.partial(gate_kernel, size, steps, chunks), grid=...  48.2 us
    pallas_call x4, Pallas kernels, update_blocks(): pl.pallas_call(functools.partial(update_kernel, rate, turned), grid=grid,...  27.9 us
    pallas_call x2, Pallas kernels, heads_product(): pl.pallas_call(functools.partial(heads_kernel, ends), grid=(steps,), out_...  16 us
    pallas_call x1, Pallas kernels, attend_forward(): pl.pallas_call(functools.partial(attend_forward_kernel, block), grid=(hea...  15.2 us
    pallas_call x1, Pallas kernels, attend_back(): pl.pallas_call(functools.partial(attend_back_kernel, block), grid=(heads,...  13.9 us
    pallas_call x1, Pallas kernels, back_in(): pl.pallas_call(back_in_kernel, grid_spec=pltpu.PrefetchScalarGridSpec(num...  13.1 us
  transfers between devices with their start and end apart: 13, of which 0 were waited for; matrix products, arithmetic and copies ran while one was open for 1% of the time, Pallas kernels for 83%

profile of v6, /device:TPU:0, one launch (start us, length us, event | category | flops | bytes accessed | tf_op | source)
XLA Modules:
  0.0 638.6 jit_solution(8946800069996978081)
XLA Ops:
  10.5 85.5 %norm_in.1 = (bf16[1024,2048]{1,0:T(8,128)(2,1)}, f32[1024,1]{1,0:T(8,128)}, bf16[1024,512]{1,0:T(8,128)(2,1)}, f32[16,8,128]{2,1,0:T(8,128)}, bf16[256,6144]{1,...) custom-call(f32[2,4,6]{2,1,0:T(4,128)} %mix.11, bf16[4,1024,512]{2,1,0:T(8,128)(2,1)} %streams.5, ...), custom_call_target="tpu_custom_call" | custom-call | flops 99999997952 | bytes 23671232 | tf_op jit(solution)/shard_map/norm_in/pallas_call | solution.py:311
  97.3 4.6 collective-permute-start
  102.0 12.7 %project_in.1.query.key.value = f32[1024,1536]{1,0:T(8,128)} custom-call(bf16[1024,2048]{1,0:T(8,128)(2,1)} %get-tuple-element.90.left.normal_in.normal, bf16[2048,2048]{1,0:T(8,128)(2,1)} %all-gather.3.cloned.1.call-done.right.rows_in.output_in.rows), custom_call_target="tpu_custom_call" | custom-call | flops 6442450944 | bytes 18874368 | tf_op jit(solution)/shard_map/project_in/pallas_call | solution.py:1087
  114.7 15.2 %attend_forward.1 = (bf16[1024,512]{1,0:T(8,128)(2,1)}, bf16[1024,512]{1,0:T(8,128)(2,1)}, bf16[1024,512]{1,0:T(8,128)(2,1)}, bf16[1024,512]{1,0:T(8,128)(2,1)}, bf16[4,1024,1024]{2,1,0:T(8,128)(2,1)}) custom-call(f32[1024,1536]{1,0:T(8,128)} %project_in.1.query.key.value, f32[1024,1536]{1,0:T(8,128)} %project_in.1.query.key.value, ...), custom_call_target="tpu_custom_call" | custom-call | tf_op jit(solution)/shard_map/attend_forward/pallas_call | solution.py:1559
  129.9 116.3 %norm_mid.1 = (bf16[1024,2048]{1,0:T(8,128)(2,1)}, f32[1024,1]{1,0:T(8,128)}, f32[1024,512]{1,0:T(8,128)}) custom-call(f32[2,4,6]{2,1,0:T(4,128)} %mix.11, bf16[1024,512]{1,0:T(8,128)(2,1)} %get-tuple-element.96.attended_in.other_right, bf16[2048,2048]{1,0:T(8,128)(2,1)} %all-gather.3.cloned.1.call-done.right.rows_in.output_in.rows, ...), custom_call_target="tpu_custom_call" | custom-call | flops 99999997952 | bytes 19927232 | tf_op jit(solution)/shard_map/norm_mid/pallas_call | solution.py:311
  246.3 48.2 %gate_forward.1 = (bf16[1024,2048]{1,0:T(8,128)(2,1)}, bf16[1024,2048]{1,0:T(8,128)(2,1)}, bf16[1024,2048]{1,0:T(8,128)(2,1)}, bf16[1024,2048]{1,0:T(8,128)(2,1)}, bf16[1024,2048]{1,0:T(8,128)(2,1)}) custom-call(bf16[1024,2048]{1,0:T(8,128)(2,1)} %get-tuple-element.98.whole.normal.normal_in, ...), custom_call_target="tpu_custom_call" | custom-call | flops 25769803776 | bytes 25165824 | tf_op jit(solution)/shard_map/gate_forward/pallas_call | solution.py:1266
  294.8 61.7 %gate_back.1 = (bf16[2,1024,2048]{2,1,0:T(8,128)(2,1)}, bf16[3,2048,2048]{2,1,0:T(8,128)(2,1)}) custom-call(bf16[1024,2048]{1,0:T(8,128)(2,1)} %get-tuple-element.102.branch_grad, bf16[1024,2048]{1,0:T(8,128)(2,1)} %get-tuple-element.98.whole.normal.normal_in, bf16[2048,6144]{1,0:T(8,128)(2,1)} %all-gather.5.cloned.1.call-done.gate_rows.upper_rows.down_rows.rows.rows_in, ...), custom_call_target="tpu_custom_call" | custom-call | flops 34359738368 | bytes 79691776 | tf_op jit(solution)/shard_map/gate_back/pallas_call | solution.py:1087
  356.6 128.3 %back_mid.1 = (bf16[1024,2048]{1,0:T(8,128)(2,1)}, f32[1024,512]{1,0:T(8,128)}, bf16[1024,512]{1,0:T(8,128)(2,1)}) custom-call(f32[2,4,6]{2,1,0:T(4,128)} %mix.11, bf16[2,1024,2048]{2,1,0:T(8,128)(2,1)} %get-tuple-element.106.gated_in, bf16[2048,6144]{1,0:T(8,128)(2,1)} %all-gather.5.cloned.1.call-done.gate_rows.upper_rows.down_rows.rows.rows_in, ...), custom_call_target="tpu_custom_call" | custom-call | flops 1000000000 | bytes 57675968 | tf_op jit(solution)/shard_map/back_mid/pallas_call | solution.py:311
  485.0 13.9 %attend_back.1.grads.right = bf16[3,1024,512]{2,1,0:T(8,128)(2,1)} custom-call(bf16[1024,512]{1,0:T(8,128)(2,1)} %get-tuple-element.113.queries, bf16[1024,512]{1,0:T(8,128)(2,1)} %get-tuple-element.114.key_heads, bf16[1024,512]{1,0:T(8,128)(2,1)} %get-tuple-element.115.value_heads, bf16[1024,512]{1,0:T(8,128)(2,1)} %get-tuple-element.116.grad_result, ...), custom_call_target="tpu_custom_call" | custom-call | tf_op jit(solution)/shard_map/attend_back/pallas_call | solution.py:1631
  498.9 8.9 %heads_product.2 = (bf16[1024,2048]{1,0:T(8,128)(2,1)}, bf16[1024,512]{1,0:T(8,128)(2,1)}, bf16[1024,512]{1,0:T(8,128)(2,1)}) custom-call(bf16[3,1024,512]{2,1,0:T(8,128)(2,1)} %attend_back.1.grads.right, bf16[2048,2048]{1,0:T(8,128)(2,1)} %all-gather.3.cloned.1.call-done.right.rows_in.output_in.rows), custom_call_target="tpu_custom_call" | custom-call | flops 3221225472 | bytes 8388608 | tf_op jit(solution)/shard_map/heads_product/pallas_call | solution.py:1461
  510.5 18.0 %outer_attention.1 = bf16[2048,2048]{1,0:T(8,128)(2,1)} custom-call(bf16[1024,2048]{1,0:T(8,128)(2,1)} %get-tuple-element.90.left.normal_in.normal, bf16[3,1024,512]{2,1,0:T(8,128)(2,1)} %attend_back.1.grads.right, bf16[1024,2048]{1,0:T(8,128)(2,1)} %get-tuple-element.121.other_left, bf16[1024,512]{1,0:T(8,128)(2,1)} %get-tuple-element.96.attended_in.other_right), custom_call_target="tpu_custom_call" | custom-call | flops 8589934592 | bytes 20971520 | tf_op jit(solution)/shard_map/outer_attention/pallas_call | solution.py:1087
  528.5 7.1 %heads_product.3.partial_in.share = bf16[1024,2048]{1,0:T(8,128)(2,1)} custom-call(bf16[3,1024,512]{2,1,0:T(8,128)(2,1)} %attend_back.1.grads.right, bf16[2048,2048]{1,0:T(8,128)(2,1)} %all-gather.3.cloned.1.call-done.right.rows_in.output_in.rows, bf16[1024,2048]{1,0:T(8,128)(2,1)} %get-tuple-element.118.refs_0_), custom_call_target="tpu_custom_call", output_to_operand_aliasing={{}: (2, {})} | custom-call | flops 3221225472 | bytes 8388608 | tf_op jit(solution)/shard_map/heads_product/pallas_call | solution.py:1461
  535.7 3.1 add_convert_fusion.2
  540.1 5.0 collective-permute-start.4
  545.1 7.2 %update.5 = (f32[2048,256]{1,0:T(8,128)}, f32[2048,256]{1,0:T(8,128)}, f32[2048,256]{1,0:T(8,128)}) custom-call(f32[2048,256]{1,0:T(8,128)} %weight.5, bf16[3,256,2048]{2,1,0:T(8,128)(2,1)} %reduce-scatter.6.cloned.1.call-done.grad, f32[2048,256]{1,0:T(8,128)} %moment.6, f32[2048,256]{1,0:T(8,128)} %average.6), custom_call_target="tpu_custom_call" | custom-call | flops 5242880 | bytes 13631488 | tf_op jit(solution)/shard_map/update/pallas_call | solution.py:1726
  552.3 12.3 %update.4 = (f32[2,256,2048]{2,1,0:T(8,128)}, f32[2,256,2048]{2,1,0:T(8,128)}, f32[2,256,2048]{2,1,0:T(8,128)}) custom-call(f32[2,256,2048]{2,1,0:T(8,128)} %weight.4, bf16[3,256,2048]{2,1,0:T(8,128)(2,1)} %reduce-scatter.6.cloned.1.call-done.grad, f32[2,256,2048]{2,1,0:T(8,128)} %moment.5, f32[2,256,2048]{2,1,0:T(8,128)} %average.5), custom_call_target="tpu_custom_call" | custom-call | flops 10485760 | bytes 27262976 | tf_op jit(solution)/shard_map/update/pallas_call | solution.py:1726
  564.6 3.3 add_convert_fusion
  569.1 5.0 collective-permute-start.6
  574.1 11.1 %end_streams.1 = (bf16[4,1024,512]{2,1,0:T(8,128)(2,1)}, f32[16,8,128]{2,1,0:T(8,128)}) custom-call(f32[2,4,6]{2,1,0:T(4,128)} %mix.11, bf16[4,1024,512]{2,1,0:T(8,128)(2,1)} %streams.5, bf16[4,1024,512]{2,1,0:T(8,128)(2,1)} %grads.3, f32[1024,512]{1,0:T(8,128)} %get-tuple-element.97.branch_one, ...), custom_call_target="tpu_custom_call" | custom-call | flops 125829120 | bytes 18874368 | tf_op jit(solution)/shard_map/end_streams/pallas_call | solution.py:1068
  585.2 10.0 %back_sums.1 = (f32[1024,1]{1,0:T(8,128)}, f32[1024,1]{1,0:T(8,128)}) custom-call(bf16[1024,2048]{1,0:T(8,128)(2,1)} %heads_product.3.partial_in.share, bf16[1024,2048]{1,0:T(8,128)(2,1)} %get-tuple-element.90.left.normal_in.normal), custom_call_target="tpu_custom_call" | custom-call | flops 1000000000 | bytes 8396800 | tf_op jit(solution)/shard_map/back_sums/pallas_call | solution.py:311
  596.5 13.1 %back_in.1 = (f32[4,1024,512]{2,1,0:T(8,128)}, f32[8,8,128]{2,1,0:T(8,128)}) custom-call(s32[1]{0:T(128)} %bitcast.place, f32[2,4,6]{2,1,0:T(4,128)} %mix.11, bf16[1024,2048]{1,0:T(8,128)(2,1)} %heads_product.3.partial_in.share, bf16[1024,512]{1,0:T(8,128)(2,1)} %copy-done.1, bf16[1024,512]{1,0:T(8,128)(2,1)} %copy-done, ...), custom_call_target="tpu_custom_call" | custom-call | flops 41943040 | bytes 23068672 | tf_op jit(solution)/shard_map/back_in/pallas_call | solution.py:923
  609.7 11.6 %sum_all.1.products = f32[8,128]{1,0:T(8,128)} custom-call(f32[16,8,128]{2,1,0:T(8,128)} %get-tuple-element.142.refs_0_, f32[16,8,128]{2,1,0:T(8,128)} %get-tuple-element.143.refs_1_, f32[8,8,128]{2,1,0:T(8,128)} %get-tuple-element.144.refs_2_), custom_call_target="tpu_custom_call" | custom-call | flops 1000000000 | bytes 167936 | tf_op jit(solution)/shard_map/sum_all/pallas_call | solution.py:311
  621.3 2.8 update.7
  624.2 5.6 update.6
  (39 shorter events, 13.7 us)
Async XLA Ops:
  7.2 94.8 %all-gather.3.cloned.1.call-start = ((), (), s32[]{:S(2)}) async-start(), calls=%async_computation.3 | async-start | bytes 9437184 | tf_op jit(solution)/shard_map/all_gather | solution.py:1829
  9.9 236.4 %all-gather.5.cloned.1.call-start = ((), (), s32[]{:S(2)}) async-start(), calls=%async_computation.4 | async-start | bytes 28311552 | tf_op jit(solution)/shard_map/all_gather | solution.py:1835
  96.0 389.0 %reduce-scatter.4.cloned.1.call-start = ((), (), s32[]{:S(2)}) async-start(), calls=%async_computation.5 | async-start | bytes 5242880 | tf_op jit(solution)/shard_map/reduce_scatter | solution.py:1852
  96.0 33.9 %collective-permute-start.1 = (bf16[1024,512]{1,0:T(8,128)(2,1)}, bf16[1024,512]{1,0:T(8,128)(2,1)S(1)}, u32[]{:S(2)}, u32[]{:S(2)}) collective-permute-start(bf16[1024,512]{1,0:T(8,128)(2,1)} %get-tuple-element.95.own_in), channel_id=1, source_target_pairs={{1,0},{2,1},{3,2},{5,4},{6,5},{7,6},{9,8},{10,9},{11,10},{13,12},{... | collective-permute-start | bytes 3145736 | tf_op jit(solution)/shard_map/ppermute | solution.py:1839
  97.3 32.6 %collective-permute-start = (bf16[1024,512]{1,0:T(8,128)(2,1)}, bf16[1024,512]{1,0:T(8,128)(2,1)S(1)}, u32[]{:S(2)}, u32[]{:S(2)}) collective-permute-start(bf16[1024,512]{1,0:T(8,128)(2,1)} %get-tuple-element.95.own_in), channel_id=1, source_target_pairs={{0,1},{1,2},{2,3},{4,5},{5,6},{6,7},{8,9},{9,10},{10,11},{12,13},{... | collective-permute-start | bytes 3145736 | tf_op jit(solution)/shard_map/ppermute | solution.py:1838
  129.9 116.4 %copy-start.2 = (bf16[1024,512]{1,0:T(8,128)(2,1)}, bf16[1024,512]{1,0:T(8,128)(2,1)S(1)}, u32[]{:S(2)}) copy-start(bf16[1024,512]{1,0:T(8,128)(2,1)S(1)} %collective-permute-done.1.after_in) | copy-start | bytes 3145732
  129.9 116.4 %copy-start.3 = (bf16[1024,512]{1,0:T(8,128)(2,1)}, bf16[1024,512]{1,0:T(8,128)(2,1)S(1)}, u32[]{:S(2)}) copy-start(bf16[1024,512]{1,0:T(8,128)(2,1)S(1)} %collective-permute-done.before_in) | copy-start | bytes 3145732
  294.5 250.6 %reduce-scatter.6.cloned.1.call-start = ((), (), s32[]{:S(2)}) async-start(), calls=%async_computation.6 | async-start | bytes 28311552 | tf_op jit(solution)/shard_map/reduce_scatter | solution.py:1856
  356.6 264.7 %reduce-scatter.8.cloned.1.call-start = ((), (), s32[]{:S(2)}) async-start(), calls=%async_computation.7 | async-start | bytes 9437184 | tf_op jit(solution)/shard_map/reduce_scatter | solution.py:1784
  507.8 20.7 %collective-permute-start.2 = (bf16[1024,512]{1,0:T(8,128)(2,1)}, bf16[1024,512]{1,0:T(8,128)(2,1)S(1)}, u32[]{:S(2)}, u32[]{:S(2)}) collective-permute-start(bf16[1024,512]{1,0:T(8,128)(2,1)} %get-tuple-element.119), channel_id=1, source_target_pairs={{0,1},{1,2},{2,3},{4,5},{5,6},{6,7},{8,9},{9,10},{10,11},{12,13},{... | collective-permute-start | bytes 3145736 | tf_op jit(solution)/shard_map/ppermute | solution.py:1766
  509.2 19.4 %collective-permute-start.3 = (bf16[1024,512]{1,0:T(8,128)(2,1)}, bf16[1024,512]{1,0:T(8,128)(2,1)S(1)}, u32[]{:S(2)}, u32[]{:S(2)}) collective-permute-start(bf16[1024,512]{1,0:T(8,128)(2,1)} %get-tuple-element.120), channel_id=1, source_target_pairs={{1,0},{2,1},{3,2},{5,4},{6,5},{7,6},{9,8},{10,9},{11,10},{13,12},{... | collective-permute-start | bytes 3145736 | tf_op jit(solution)/shard_map/ppermute | solution.py:1766
  538.8 25.8 %collective-permute-start.5 = (bf16[1024,512]{1,0:T(8,128)(2,1)}, bf16[1024,512]{1,0:T(8,128)(2,1)S(1)}, u32[]{:S(2)}, u32[]{:S(2)}) collective-permute-start(bf16[1024,512]{1,0:T(8,128)(2,1)} %get-tuple-element.165), channel_id=1, source_target_pairs={{1,0},{2,1},{3,2},{5,4},{6,5},{7,6},{9,8},{10,9},{11,10},{13,12},{... | collective-permute-start | bytes 3145736 | tf_op jit(solution)/shard_map/ppermute | solution.py:1766
  540.1 24.5 %collective-permute-start.4 = (bf16[1024,512]{1,0:T(8,128)(2,1)S(1)}, bf16[1024,512]{1,0:T(8,128)(2,1)S(1)}, u32[]{:S(2)}, u32[]{:S(2)}) collective-permute-start(bf16[1024,512]{1,0:T(8,128)(2,1)S(1)} %get-tuple-element.166), channel_id=1, source_target_pairs={{0,1},{1,2},{2,3},{4,5},{5,6},{6,7},{8,9},{9,10},{10,11},{12,13},{... | collective-permute-start | bytes 3145736 | tf_op jit(solution)/shard_map/ppermute | solution.py:1766
  567.9 27.4 %collective-permute-start.7 = (bf16[1024,512]{1,0:T(8,128)(2,1)}, bf16[1024,512]{1,0:T(8,128)(2,1)S(1)}, u32[]{:S(2)}, u32[]{:S(2)}) collective-permute-start(bf16[1024,512]{1,0:T(8,128)(2,1)} %get-tuple-element.163), channel_id=1, source_target_pairs={{1,0},{2,1},{3,2},{5,4},{6,5},{7,6},{9,8},{10,9},{11,10},{13,12},{... | collective-permute-start | bytes 3145736 | tf_op jit(solution)/shard_map/ppermute | solution.py:1766
  569.1 26.1 %collective-permute-start.6 = (bf16[1024,512]{1,0:T(8,128)(2,1)S(1)}, bf16[1024,512]{1,0:T(8,128)(2,1)S(1)}, u32[]{:S(2)}, u32[]{:S(2)}) collective-permute-start(bf16[1024,512]{1,0:T(8,128)(2,1)S(1)} %get-tuple-element.164), channel_id=1, source_target_pairs={{0,1},{1,2},{2,3},{4,5},{5,6},{6,7},{8,9},{9,10},{10,11},{12,13},{... | collective-permute-start | bytes 3145736 | tf_op jit(solution)/shard_map/ppermute | solution.py:1766
  595.2 1.0 copy-start
  595.2 1.3 copy-start.1
Sparse Core Ops, SparseCore 0:
  10.5 57.0 all-gather.2
  96.1 125.3 all-gather.4
  294.6 77.8 reduce-scatter.3
  376.4 160.7 reduce-scatter.5
  540.9 71.3 reduce-scatter.7

commit v7 on v6

--- a/solution.py
+++ b/solution.py
@@ -1351,15 +1351,18 @@
     )
 
 
-def outer_kernel(cut, left, right, other_left, other_right, out, turned):
+def outer_kernel(cut, left, right, other_in, other_right, out, turned, other_left, load):
     step = pl.program_id(0)
+    fetch = pltpu.make_async_copy(other_in, other_left, load.at[0])
 
     @pl.when(step == 0)
     def _():
+        fetch.start()
         turned[...] = left[...].T
 
     @pl.when(step == cut)
     def _():
+        fetch.wait()
         turned[...] = other_left[...].T
 
     @pl.when(step < cut)
@@ -1390,10 +1393,19 @@
         functools.partial(outer_kernel, cut),
         (cut + other,),
         (left, right, other_left, other_right),
-        [whole, spec, whole, pl.BlockSpec((tokens, tile), lambda j: (0, jnp.maximum(j - cut, 0)))],
+        [
+            whole,
+            spec,
+            pl.BlockSpec(memory_space=pl.ANY),
+            pl.BlockSpec((tokens, tile), lambda j: (0, jnp.maximum(j - cut, 0))),
+        ],
         jax.ShapeDtypeStruct((rows, (cut + other) * tile), jnp.bfloat16),
         pl.BlockSpec((rows, tile), lambda j: (0, j)),
-        [pltpu.VMEM((rows, tokens), jnp.bfloat16)],
+        [
+            pltpu.VMEM((rows, tokens), jnp.bfloat16),
+            pltpu.VMEM((tokens, rows), jnp.bfloat16),
+            pltpu.SemaphoreType.DMA((1,)),
+        ],
         2 * tokens * rows * (cut + other) * tile,
         name,
     )
@@ -1708,7 +1720,7 @@
     parted = grad.ndim == 3
     rows = grad.shape[-2]
     columns = weight.shape[0] if turned else weight.shape[2]
-    tile = min(columns, 512)
+    tile = min(columns, 1024 if turned else 2048)
     tiles = columns // tile
     lead = (None,) if parted else ()
 
@@ -1782,6 +1794,48 @@
 
 def scatter_rows(grad):
     return lax.psum_scatter(grad, "row", scatter_dimension=0, tiled=True)
+
+
+def attention_kernel(rate, last, *refs):
+    step = pl.program_id(0)
+    into, out = refs[:3], refs[3:6]
+    grad, turned_grad = refs[6:8]
+    results = refs[8:]
+
+    @pl.when(step < last)
+    def _():
+        weight, moment, average = [ref[...] for ref in into]
+        values = update(weight, grad[...].astype(f32), moment, average, rate)
+        for ref, value in zip(results[:3], values):
+            ref[...] = value
+
+    @pl.when(step == last)
+    def _():
+        weight, moment, average = [ref[...] for ref in out]
+        values = update(weight, turned_grad[...].astype(f32).T, moment, average, rate)
+        for ref, value in zip(results[3:], values):
+            ref[...] = value
+
+
+def update_attention(weight, moment, average, out_weight, out_moment, out_average, grad, rate):
+    count, rows, columns = weight.shape
+    own = pl.BlockSpec((None, rows, columns), lambda j: (jnp.minimum(j, count - 1), 0, 0))
+    whole = pl.BlockSpec(out_weight.shape, lambda j: (0, 0))
+    return pl.pallas_call(
+        functools.partial(attention_kernel, rate, count),
+        grid=(count + 1,),
+        out_shape=[jax.ShapeDtypeStruct(weight.shape, f32)] * 3
+        + [jax.ShapeDtypeStruct(out_weight.shape, f32)] * 3,
+        in_specs=[own] * 3
+        + [whole] * 3
+        + [
+            pl.BlockSpec((rows, columns), lambda j: (0, jnp.minimum(j, count - 1))),
+            pl.BlockSpec((rows, columns), lambda j: (0, count)),
+        ],
+        out_specs=[own] * 3 + [whole] * 3,
+        compiler_params=pltpu.CompilerParams(vmem_limit_bytes=60 * 2**20),
+        name="update_attention",
+    )(weight, moment, average, out_weight, out_moment, out_average, grad, grad)
 
 
 def pack_kernel(weights, turned, out):
@@ -1916,17 +1970,17 @@
     )
     products = sum_all(size, streams_grads, other_products, own_products)
     products, grad_attention = tie(products, grad_attention)
-    first = update_blocks(
-        attention_in, grad_attention, moment_attention_in, average_attention_in, model_rate, 0
-    )
-    second = update_blocks(
+    updated = update_attention(
+        attention_in,
+        moment_attention_in,
+        average_attention_in,
         attention_out,
-        grad_attention,
         moment_attention_out,
         average_attention_out,
+        grad_attention,
         model_rate,
-        attention_in.shape[0] * heads,
-    )
+    )
+    first, second = updated[:3], updated[3:]
     fifth = update_mix(
         products, hyper_mix, moment_hyper_mix, average_hyper_mix, 0.05 * (tokens_all * D) ** (-0.5)
     )

time: 645 us -> 641 us (level)
    pallas_call x4 -> x2, Pallas kernels: 27.9 us -> 19.2 us  [update_blocks(): pl.pallas_call(functools.partial(update_kernel, rate, turned), grid=grid,...]
    pallas_call x0 -> x1, Pallas kernels: none -> 7.23 us  [update_attention(): pl.pallas_call(functools.partial(attention_kernel, rate, count), grid=(co...]
  transfers between devices with their start and end apart: 13 -> 13, of which waited for: 0 -> 1; matrix products, arithmetic and copies ran while one was open for 1% -> 1% of each run, Pallas kernels for 83% -> 84%
where the time goes in v7:
time: 641 us; the launch traced here: 635 us
  Pallas kernels  591 us (92%)
  starting transfers between devices  21 us (3%)
  between operations  14.3 us (2%)
  other arithmetic  6.74 us (1%)
    pallas_call x5, Pallas kernels, call(): pl.pallas_call(body, out_shape=outs, in_specs=[pl.BlockSpec(memory_space=...  352 us
    pallas_call x3, Pallas kernels, tiled(): pl.pallas_call(body, grid=grid, out_shape=outs, in_specs=specs, out_specs...  91.5 us
    pallas_call x1, Pallas kernels, gate_forward(): pl.pallas_call(functools.partial(gate_kernel, size, steps, chunks), grid=...  48.2 us
    pallas_call x2, Pallas kernels, update_blocks(): pl.pallas_call(functools.partial(update_kernel, rate, turned), grid=grid,...  19.2 us
    pallas_call x2, Pallas kernels, heads_product(): pl.pallas_call(functools.partial(heads_kernel, ends), grid=(steps,), out_...  16.1 us
    pallas_call x1, Pallas kernels, attend_forward(): pl.pallas_call(functools.partial(attend_forward_kernel, block), grid=(hea...  15.2 us
    pallas_call x1, Pallas kernels, attend_back(): pl.pallas_call(functools.partial(attend_back_kernel, block), grid=(heads,...  13.9 us
  transfers between devices with their start and end apart: 13, of which 1 were waited for; matrix products, arithmetic and copies ran while one was open for 1% of the time, Pallas kernels for 84%

profile of v7, /device:TPU:0, one launch (start us, length us, event | category | flops | bytes accessed | tf_op | source)
XLA Modules:
  0.0 634.8 jit_solution(176945518268457216)
XLA Ops:
  7.2 2.6 pack.1
  10.5 85.5 %norm_in.1 = (bf16[1024,2048]{1,0:T(8,128)(2,1)}, f32[1024,1]{1,0:T(8,128)}, bf16[1024,512]{1,0:T(8,128)(2,1)}, f32[16,8,128]{2,1,0:T(8,128)}, bf16[256,6144]{1,...) custom-call(f32[2,4,6]{2,1,0:T(4,128)} %mix.11, bf16[4,1024,512]{2,1,0:T(8,128)(2,1)} %streams.5, ...), custom_call_target="tpu_custom_call" | custom-call | flops 99999997952 | bytes 23671232 | tf_op jit(solution)/shard_map/norm_in/pallas_call | solution.py:311
  97.3 4.6 collective-permute-start
  102.0 12.8 %project_in.1.query.key.value = f32[1024,1536]{1,0:T(8,128)} custom-call(bf16[1024,2048]{1,0:T(8,128)(2,1)} %get-tuple-element.90.left.normal_in.normal, bf16[2048,2048]{1,0:T(8,128)(2,1)} %all-gather.3.cloned.1.call-done.right.rows_in.output_in.rows), custom_call_target="tpu_custom_call" | custom-call | flops 6442450944 | bytes 18874368 | tf_op jit(solution)/shard_map/project_in/pallas_call | solution.py:1087
  114.8 15.2 %attend_forward.1 = (bf16[1024,512]{1,0:T(8,128)(2,1)}, bf16[1024,512]{1,0:T(8,128)(2,1)}, bf16[1024,512]{1,0:T(8,128)(2,1)}, bf16[1024,512]{1,0:T(8,128)(2,1)}, bf16[4,1024,1024]{2,1,0:T(8,128)(2,1)}) custom-call(f32[1024,1536]{1,0:T(8,128)} %project_in.1.query.key.value, f32[1024,1536]{1,0:T(8,128)} %project_in.1.query.key.value, ...), custom_call_target="tpu_custom_call" | custom-call | tf_op jit(solution)/shard_map/attend_forward/pallas_call | solution.py:1571
  130.0 116.3 %norm_mid.1 = (bf16[1024,2048]{1,0:T(8,128)(2,1)}, f32[1024,1]{1,0:T(8,128)}, f32[1024,512]{1,0:T(8,128)}) custom-call(f32[2,4,6]{2,1,0:T(4,128)} %mix.11, bf16[1024,512]{1,0:T(8,128)(2,1)} %get-tuple-element.96.attended_in.other_right, bf16[2048,2048]{1,0:T(8,128)(2,1)} %all-gather.3.cloned.1.call-done.right.rows_in.output_in.rows, ...), custom_call_target="tpu_custom_call" | custom-call | flops 99999997952 | bytes 19927232 | tf_op jit(solution)/shard_map/norm_mid/pallas_call | solution.py:311
  246.4 48.2 %gate_forward.1 = (bf16[1024,2048]{1,0:T(8,128)(2,1)}, bf16[1024,2048]{1,0:T(8,128)(2,1)}, bf16[1024,2048]{1,0:T(8,128)(2,1)}, bf16[1024,2048]{1,0:T(8,128)(2,1)}, bf16[1024,2048]{1,0:T(8,128)(2,1)}) custom-call(bf16[1024,2048]{1,0:T(8,128)(2,1)} %get-tuple-element.98.whole.normal.normal_in, ...), custom_call_target="tpu_custom_call" | custom-call | flops 25769803776 | bytes 25165824 | tf_op jit(solution)/shard_map/gate_forward/pallas_call | solution.py:1266
  295.0 61.7 %gate_back.1 = (bf16[2,1024,2048]{2,1,0:T(8,128)(2,1)}, bf16[3,2048,2048]{2,1,0:T(8,128)(2,1)}) custom-call(bf16[1024,2048]{1,0:T(8,128)(2,1)} %get-tuple-element.102.branch_grad, bf16[1024,2048]{1,0:T(8,128)(2,1)} %get-tuple-element.98.whole.normal.normal_in, bf16[2048,6144]{1,0:T(8,128)(2,1)} %all-gather.5.cloned.1.call-done.gate_rows.upper_rows.down_rows.rows.rows_in, ...), custom_call_target="tpu_custom_call" | custom-call | flops 34359738368 | bytes 79691776 | tf_op jit(solution)/shard_map/gate_back/pallas_call | solution.py:1087
  356.8 128.3 %back_mid.1 = (bf16[1024,2048]{1,0:T(8,128)(2,1)}, f32[1024,512]{1,0:T(8,128)}, bf16[1024,512]{1,0:T(8,128)(2,1)}) custom-call(f32[2,4,6]{2,1,0:T(4,128)} %mix.11, bf16[2,1024,2048]{2,1,0:T(8,128)(2,1)} %get-tuple-element.106.gated_in, bf16[2048,6144]{1,0:T(8,128)(2,1)} %all-gather.5.cloned.1.call-done.gate_rows.upper_rows.down_rows.rows.rows_in, ...), custom_call_target="tpu_custom_call" | custom-call | flops 1000000000 | bytes 57675968 | tf_op jit(solution)/shard_map/back_mid/pallas_call | solution.py:311
  485.1 13.9 %attend_back.1.grads.right = bf16[3,1024,512]{2,1,0:T(8,128)(2,1)} custom-call(bf16[1024,512]{1,0:T(8,128)(2,1)} %get-tuple-element.113.queries, bf16[1024,512]{1,0:T(8,128)(2,1)} %get-tuple-element.114.key_heads, bf16[1024,512]{1,0:T(8,128)(2,1)} %get-tuple-element.115.value_heads, bf16[1024,512]{1,0:T(8,128)(2,1)} %get-tuple-element.116.grad_result, ...), custom_call_target="tpu_custom_call" | custom-call | tf_op jit(solution)/shard_map/attend_back/pallas_call | solution.py:1643
  499.0 8.9 %heads_product.2 = (bf16[1024,2048]{1,0:T(8,128)(2,1)}, bf16[1024,512]{1,0:T(8,128)(2,1)}, bf16[1024,512]{1,0:T(8,128)(2,1)}) custom-call(bf16[3,1024,512]{2,1,0:T(8,128)(2,1)} %attend_back.1.grads.right, bf16[2048,2048]{1,0:T(8,128)(2,1)} %all-gather.3.cloned.1.call-done.right.rows_in.output_in.rows), custom_call_target="tpu_custom_call" | custom-call | flops 3221225472 | bytes 8388608 | tf_op jit(solution)/shard_map/heads_product/pallas_call | solution.py:1473
  510.6 16.9 %outer_attention.1 = bf16[2048,2048]{1,0:T(8,128)(2,1)} custom-call(bf16[1024,2048]{1,0:T(8,128)(2,1)} %get-tuple-element.90.left.normal_in.normal, bf16[3,1024,512]{2,1,0:T(8,128)(2,1)} %attend_back.1.grads.right, bf16[1024,2048]{1,0:T(8,128)(2,1)} %get-tuple-element.121.other_in, bf16[1024,512]{1,0:T(8,128)(2,1)} %get-tuple-element.96.attended_in.other_right), custom_call_target="tpu_custom_call" | custom-call | flops 8589934592 | bytes 20971520 | tf_op jit(solution)/shard_map/outer_attention/pallas_call | solution.py:1087
  527.7 7.2 %heads_product.3.partial_in.share = bf16[1024,2048]{1,0:T(8,128)(2,1)} custom-call(bf16[3,1024,512]{2,1,0:T(8,128)(2,1)} %attend_back.1.grads.right, bf16[2048,2048]{1,0:T(8,128)(2,1)} %all-gather.3.cloned.1.call-done.right.rows_in.output_in.rows, bf16[1024,2048]{1,0:T(8,128)(2,1)} %get-tuple-element.118.refs_0_), custom_call_target="tpu_custom_call", output_to_operand_aliasing={{}: (2, {})} | custom-call | flops 3221225472 | bytes 8388608 | tf_op jit(solution)/shard_map/heads_product/pallas_call | solution.py:1473
  534.9 3.1 add_convert_fusion.2
  539.3 4.8 collective-permute-start.4
  544.1 6.6 %update.3 = (f32[2048,256]{1,0:T(8,128)}, f32[2048,256]{1,0:T(8,128)}, f32[2048,256]{1,0:T(8,128)}) custom-call(f32[2048,256]{1,0:T(8,128)} %weight.3, bf16[3,256,2048]{2,1,0:T(8,128)(2,1)} %reduce-scatter.6.cloned.1.call-done.grad, f32[2048,256]{1,0:T(8,128)} %moment.4, f32[2048,256]{1,0:T(8,128)} %average.4), custom_call_target="tpu_custom_call" | custom-call | flops 5242880 | bytes 13631488 | tf_op jit(solution)/shard_map/update/pallas_call | solution.py:1738
  550.7 12.6 %update.2 = (f32[2,256,2048]{2,1,0:T(8,128)}, f32[2,256,2048]{2,1,0:T(8,128)}, f32[2,256,2048]{2,1,0:T(8,128)}) custom-call(f32[2,256,2048]{2,1,0:T(8,128)} %weight.2, bf16[3,256,2048]{2,1,0:T(8,128)(2,1)} %reduce-scatter.6.cloned.1.call-done.grad, f32[2,256,2048]{2,1,0:T(8,128)} %moment.3, f32[2,256,2048]{2,1,0:T(8,128)} %average.3), custom_call_target="tpu_custom_call" | custom-call | flops 10485760 | bytes 27262976 | tf_op jit(solution)/shard_map/update/pallas_call | solution.py:1738
  563.3 3.1 add_convert_fusion
  567.7 4.6 collective-permute-start.6
  572.3 10.8 %end_streams.1 = (bf16[4,1024,512]{2,1,0:T(8,128)(2,1)}, f32[16,8,128]{2,1,0:T(8,128)}) custom-call(f32[2,4,6]{2,1,0:T(4,128)} %mix.11, bf16[4,1024,512]{2,1,0:T(8,128)(2,1)} %streams.5, bf16[4,1024,512]{2,1,0:T(8,128)(2,1)} %grads.3, f32[1024,512]{1,0:T(8,128)} %get-tuple-element.97.branch_one, ...), custom_call_target="tpu_custom_call" | custom-call | flops 125829120 | bytes 18874368 | tf_op jit(solution)/shard_map/end_streams/pallas_call | solution.py:1068
  583.1 10.3 %back_sums.1 = (f32[1024,1]{1,0:T(8,128)}, f32[1024,1]{1,0:T(8,128)}) custom-call(bf16[1024,2048]{1,0:T(8,128)(2,1)} %heads_product.3.partial_in.share, bf16[1024,2048]{1,0:T(8,128)(2,1)} %get-tuple-element.90.left.normal_in.normal), custom_call_target="tpu_custom_call" | custom-call | flops 1000000000 | bytes 8396800 | tf_op jit(solution)/shard_map/back_sums/pallas_call | solution.py:311
  594.7 12.5 %back_in.1 = (f32[4,1024,512]{2,1,0:T(8,128)}, f32[8,8,128]{2,1,0:T(8,128)}) custom-call(s32[1]{0:T(128)} %bitcast.place, f32[2,4,6]{2,1,0:T(4,128)} %mix.11, bf16[1024,2048]{1,0:T(8,128)(2,1)} %heads_product.3.partial_in.share, bf16[1024,512]{1,0:T(8,128)(2,1)} %copy-done.1, bf16[1024,512]{1,0:T(8,128)(2,1)} %copy-done, ...), custom_call_target="tpu_custom_call" | custom-call | flops 41943040 | bytes 23068672 | tf_op jit(solution)/shard_map/back_in/pallas_call | solution.py:923
  607.3 11.5 %sum_all.1.products = f32[8,128]{1,0:T(8,128)} custom-call(f32[16,8,128]{2,1,0:T(8,128)} %get-tuple-element.142.refs_0_, f32[16,8,128]{2,1,0:T(8,128)} %get-tuple-element.143.refs_1_, f32[8,8,128]{2,1,0:T(8,128)} %get-tuple-element.144.refs_2_), custom_call_target="tpu_custom_call" | custom-call | flops 1000000000 | bytes 167936 | tf_op jit(solution)/shard_map/sum_all/pallas_call | solution.py:311
  620.9 7.2 %update_attention.1 = (f32[3,256,512]{2,1,0:T(8,128)}, f32[3,256,512]{2,1,0:T(8,128)}, f32[3,256,512]{2,1,0:T(8,128)}, f32[512,256]{1,0:T(8,128)}, f32[512,256]{1,0:T(8,128)}, /*index=5*/f32[512,256]{1,0:T(8,128)}) custom-call(f32[3,256,512]{2,1,0:T(8,128)} %refs_0_.1, f32[3,256,512]{2,1,0:T(8,128)} %refs_1_.1, f32[3,256,512]{2,1,0:T(8,128)} %refs_2_.1, ...), custom_call_target="tpu_custom_call" | custom-call | tf_op jit(solution)/shard_map/update_attention/pallas_call | solution.py:1824
  (38 shorter events, 11.2 us)
Async XLA Ops:
  7.2 94.8 %all-gather.3.cloned.1.call-start = ((), (), s32[]{:S(2)}) async-start(), calls=%async_computation.3 | async-start | bytes 9437184 | tf_op jit(solution)/shard_map/all_gather | solution.py:1883
  9.9 236.5 %all-gather.5.cloned.1.call-start = ((), (), s32[]{:S(2)}) async-start(), calls=%async_computation.4 | async-start | bytes 28311552 | tf_op jit(solution)/shard_map/all_gather | solution.py:1889
  96.0 389.2 %reduce-scatter.4.cloned.1.call-start = ((), (), s32[]{:S(2)}) async-start(), calls=%async_computation.5 | async-start | bytes 5242880 | tf_op jit(solution)/shard_map/reduce_scatter | solution.py:1906
  96.0 34.0 %collective-permute-start.1 = (bf16[1024,512]{1,0:T(8,128)(2,1)}, bf16[1024,512]{1,0:T(8,128)(2,1)S(1)}, u32[]{:S(2)}, u32[]{:S(2)}) collective-permute-start(bf16[1024,512]{1,0:T(8,128)(2,1)} %get-tuple-element.95.own_in), channel_id=1, source_target_pairs={{1,0},{2,1},{3,2},{5,4},{6,5},{7,6},{9,8},{10,9},{11,10},{13,12},{... | collective-permute-start | bytes 3145736 | tf_op jit(solution)/shard_map/ppermute | solution.py:1893
  97.3 32.7 %collective-permute-start = (bf16[1024,512]{1,0:T(8,128)(2,1)}, bf16[1024,512]{1,0:T(8,128)(2,1)S(1)}, u32[]{:S(2)}, u32[]{:S(2)}) collective-permute-start(bf16[1024,512]{1,0:T(8,128)(2,1)} %get-tuple-element.95.own_in), channel_id=1, source_target_pairs={{0,1},{1,2},{2,3},{4,5},{5,6},{6,7},{8,9},{9,10},{10,11},{12,13},{... | collective-permute-start | bytes 3145736 | tf_op jit(solution)/shard_map/ppermute | solution.py:1892
  130.0 116.4 %copy-start.2 = (bf16[1024,512]{1,0:T(8,128)(2,1)}, bf16[1024,512]{1,0:T(8,128)(2,1)S(1)}, u32[]{:S(2)}) copy-start(bf16[1024,512]{1,0:T(8,128)(2,1)S(1)} %collective-permute-done.1.after_in) | copy-start | bytes 3145732
  130.0 116.3 %copy-start.3 = (bf16[1024,512]{1,0:T(8,128)(2,1)}, bf16[1024,512]{1,0:T(8,128)(2,1)S(1)}, u32[]{:S(2)}) copy-start(bf16[1024,512]{1,0:T(8,128)(2,1)S(1)} %collective-permute-done.before_in) | copy-start | bytes 3145732
  294.6 249.5 %reduce-scatter.6.cloned.1.call-start = ((), (), s32[]{:S(2)}) async-start(), calls=%async_computation.6 | async-start | bytes 28311552 | tf_op jit(solution)/shard_map/reduce_scatter | solution.py:1910
  356.7 262.0 %reduce-scatter.8.cloned.1.call-start = ((), (), s32[]{:S(2)}) async-start(), calls=%async_computation.7 | async-start | bytes 9437184 | tf_op jit(solution)/shard_map/reduce_scatter | solution.py:1796
  508.0 19.6 %collective-permute-start.2 = (bf16[1024,512]{1,0:T(8,128)(2,1)}, bf16[1024,512]{1,0:T(8,128)(2,1)S(1)}, u32[]{:S(2)}, u32[]{:S(2)}) collective-permute-start(bf16[1024,512]{1,0:T(8,128)(2,1)} %get-tuple-element.119), channel_id=1, source_target_pairs={{0,1},{1,2},{2,3},{4,5},{5,6},{6,7},{8,9},{9,10},{10,11},{12,13},{... | collective-permute-start | bytes 3145736 | tf_op jit(solution)/shard_map/ppermute | solution.py:1778
  509.3 18.3 %collective-permute-start.3 = (bf16[1024,512]{1,0:T(8,128)(2,1)}, bf16[1024,512]{1,0:T(8,128)(2,1)S(1)}, u32[]{:S(2)}, u32[]{:S(2)}) collective-permute-start(bf16[1024,512]{1,0:T(8,128)(2,1)} %get-tuple-element.120), channel_id=1, source_target_pairs={{1,0},{2,1},{3,2},{5,4},{6,5},{7,6},{9,8},{10,9},{11,10},{13,12},{... | collective-permute-start | bytes 3145736 | tf_op jit(solution)/shard_map/ppermute | solution.py:1778
  538.0 25.3 %collective-permute-start.5 = (bf16[1024,512]{1,0:T(8,128)(2,1)}, bf16[1024,512]{1,0:T(8,128)(2,1)S(1)}, u32[]{:S(2)}, u32[]{:S(2)}) collective-permute-start(bf16[1024,512]{1,0:T(8,128)(2,1)} %get-tuple-element.165), channel_id=1, source_target_pairs={{1,0},{2,1},{3,2},{5,4},{6,5},{7,6},{9,8},{10,9},{11,10},{13,12},{... | collective-permute-start | bytes 3145736 | tf_op jit(solution)/shard_map/ppermute | solution.py:1778
  539.3 24.0 %collective-permute-start.4 = (bf16[1024,512]{1,0:T(8,128)(2,1)S(1)}, bf16[1024,512]{1,0:T(8,128)(2,1)S(1)}, u32[]{:S(2)}, u32[]{:S(2)}) collective-permute-start(bf16[1024,512]{1,0:T(8,128)(2,1)S(1)} %get-tuple-element.166), channel_id=1, source_target_pairs={{0,1},{1,2},{2,3},{4,5},{5,6},{6,7},{8,9},{9,10},{10,11},{12,13},{... | collective-permute-start | bytes 3145736 | tf_op jit(solution)/shard_map/ppermute | solution.py:1778
  566.4 27.0 %collective-permute-start.7 = (bf16[1024,512]{1,0:T(8,128)(2,1)}, bf16[1024,512]{1,0:T(8,128)(2,1)S(1)}, u32[]{:S(2)}, u32[]{:S(2)}) collective-permute-start(bf16[1024,512]{1,0:T(8,128)(2,1)} %get-tuple-element.163), channel_id=1, source_target_pairs={{1,0},{2,1},{3,2},{5,4},{6,5},{7,6},{9,8},{10,9},{11,10},{13,12},{... | collective-permute-start | bytes 3145736 | tf_op jit(solution)/shard_map/ppermute | solution.py:1778
  567.7 25.7 %collective-permute-start.6 = (bf16[1024,512]{1,0:T(8,128)(2,1)S(1)}, bf16[1024,512]{1,0:T(8,128)(2,1)S(1)}, u32[]{:S(2)}, u32[]{:S(2)}) collective-permute-start(bf16[1024,512]{1,0:T(8,128)(2,1)S(1)} %get-tuple-element.164), channel_id=1, source_target_pairs={{0,1},{1,2},{2,3},{4,5},{5,6},{6,7},{8,9},{9,10},{10,11},{12,13},{... | collective-permute-start | bytes 3145736 | tf_op jit(solution)/shard_map/ppermute | solution.py:1778
  593.4 1.0 copy-start
  593.5 1.3 copy-start.1
Sparse Core Ops, SparseCore 0:
  10.5 57.0 all-gather.2
  96.1 125.3 all-gather.4
  294.8 77.8 reduce-scatter.3
  376.6 160.7 reduce-scatter.5
  541.1 71.3 reduce-scatter.7
